TPU v7x, 32 devices: a whole 2x2x4 slice. The times are simulated.
32 devices in a mesh: rep: 8 (over z, y), shard: 4 (over x, core).
Axes of the slice: x: 2, y: 2, z: 4, core: 2. Of those that a mesh axis runs over, the one named last changes fastest.
Arguments:
- tokens: bfloat16 [8192, 1024], P(('rep', 'shard')), may hold values from -6 to 6
- segment_ids: int32 [8, 1024], P('rep'), may hold values from 0 to 4, as said below
- ln1_gain: bfloat16 [1024], P('shard'), may hold values from 0.099609375 to 1.8984375
- w_qkv: bfloat16 [1024, 3072], P('shard'), may hold values from -0.1875 to 0.1875
- w_out: bfloat16 [1024, 1024], P('shard'), may hold values from -1.5 to 1.5
- ln2_gain: bfloat16 [1024], P('shard'), may hold values from 0.099609375 to 1.8984375
- w_in: bfloat16 [1024, 5248], P('shard'), may hold values from -0.1875 to 0.1875
- w_down: bfloat16 [2624, 1024], P('shard'), may hold values from -0.125 to 0.125
- cotangent: bfloat16 [8192, 1024], P(('rep', 'shard')), may hold values from -6 to 6
Outputs:
- activations: bfloat16 [8192, 1024], P(('rep', 'shard'))
- input_grad: float32 [8192, 1024], P(('rep', 'shard'))
- ln1_grad: float32 [1024], P('shard')
- qkv_grad: float32 [1024, 3072], P('shard')
- out_grad: float32 [1024, 1024], P('shard')
- ln2_grad: float32 [1024], P('shard')
- in_grad: float32 [1024, 5248], P('shard')
- down_grad: float32 [2624, 1024], P('shard')
Inputs may be any that keep to these rules, and one draw needn't show every extreme that they name: `segment_ids`: along each packed sequence the numbers never fall; one document covers every position from some position under 256 to some position at or over 1024 - 255; the other documents lie before or after it.
All inputs are finite; a program needn't handle non-finite values.
Results may differ from a plain program's by a relative error of at most 0.018.
Values may be sent and summed in bfloat16 or wider, within the bound.
No kernel may reach another device: no remote copies, remote signals or barrier semaphores. Data moves between devices by JAX's collectives and lax.ppermute only.
A program may use at most 192 MiB of HBM per device.

v0:
```python
import functools
import math

import jax
import jax.numpy as jnp
from jax import lax
from jax.experimental import pallas as pl
from jax.experimental.pallas import tpu as pltpu
from jax.sharding import PartitionSpec as P

HEADS = 16
HEAD_DIM = 64
HALF = 64
QB = 128
LANES = 128

norm_epsilon = 1e-05
rope_base = 10000.0
masked_score = -1e30

F32 = jnp.float32
BF16 = jnp.bfloat16
VMEM_LIMIT = 52 << 20


def bits_of(axis):
    return lax.axis_size(axis).bit_length() - 1


def bit_of(axis, bit):
    return (lax.axis_index(axis) >> bit) & 1


def swap(x, axis, bit):
    size = lax.axis_size(axis)
    return lax.ppermute(x, axis, [(i, i ^ (1 << bit)) for i in range(size)])


def gather_list(x, axis):
    blocks = {0: x}
    for bit in reversed(range(bits_of(axis))):
        for j in list(blocks):
            blocks[j | 1 << bit] = swap(blocks[j], axis, bit)
    return [blocks[j] for j in range(len(blocks))]


def scatter_bits(blocks, axis, bits):
    blocks = dict(blocks)
    for bit in bits:
        for j in [j for j in blocks if j >> bit & 1]:
            got = swap(blocks.pop(j).astype(BF16), axis, bit)
            k = j ^ (1 << bit)
            blocks[k] = blocks[k].astype(F32) + got.astype(F32)
    return blocks


def scatter_sum_list(blocks, axis):
    return scatter_bits(enumerate(blocks), axis, range(bits_of(axis)))[0]


def half_by_replica(x, dim, bit):
    shape = x.shape
    x = x.reshape(shape[:dim] + (2, shape[dim] // 2) + shape[dim + 1 :])
    return lax.dynamic_index_in_dim(x, bit_of("rep", bit), dim, keepdims=False)


def gather_weight(x, rep_bit):
    top = bits_of("shard") - 1
    got = swap(half_by_replica(x, 0, rep_bit), "shard", top)
    pieces = [(0, None, x), (1 << top, 0, got), (1 << top, 1, swap(got, "rep", rep_bit))]
    for bit in reversed(range(top)):
        pieces += [(j | 1 << bit, h, swap(a, "shard", bit)) for j, h, a in pieces]
    return pieces


def split_weight(x, rep_bit):
    me = lax.axis_index("shard")
    top = bits_of("shard") - 1

    def part_for(a, bit):
        start = ((me & (a.shape[0] - 1)) >> bit ^ 1) << bit
        return lax.dynamic_slice_in_dim(a, start, 1 << bit)

    got = swap(half_by_replica(part_for(x, top), 1, rep_bit), "shard", top)
    pieces = [(0, None, x), (1 << top, 0, got), (1 << top, 1, swap(got, "rep", rep_bit))]
    for bit in reversed(range(top)):
        pieces += [(j | 1 << bit, h, swap(part_for(a, bit), "shard", bit)) for j, h, a in pieces]
    return pieces


def replica_reduce(keep, send, order, gates=()):
    for step, bit in enumerate(order):
        got = swap(send, "rep", bit)
        if step < len(gates):
            got = after(got, gates[step])

        def total(a, b):
            return (keep[a:b].astype(F32) + got[a:b].astype(F32)).astype(BF16)

        size = keep.shape[0]
        if size == 1:
            return total(0, 1)[0]
        keep, send = total(0, size // 2), total(size // 2, size)


def replica_spread(x, order):
    now = x[None]
    for bit in reversed(order[1:]):
        now = jnp.concatenate([now, swap(now, "rep", bit)])
    return now, swap(now, "rep", order[0])


def turn(x, n):
    pieces = {0: x}
    for bit in reversed(range(n.bit_length() - 1)):
        for j in list(pieces):
            half = pieces[j].shape[0] // 2
            pieces[j | 1 << bit] = swap(pieces[j][half:], "shard", bit)
            pieces[j] = pieces[j][:half]
    return jnp.concatenate([pieces[j] for j in range(n)])


def slot_mask(slot, order):
    count = len(order)
    return sum(((slot >> (count - 1 - i)) & 1) << bit for i, bit in enumerate(order))


def slot_of(mask, order):
    count = len(order)
    return sum(((mask >> bit) & 1) << (count - 1 - i) for i, bit in enumerate(order))


def dot(a, b, dims):
    return lax.dot_general(a, b, (dims, ((), ())), preferred_element_type=F32)


def normalise(values):
    centred = values - jnp.mean(values, axis=-1, keepdims=True)
    scale = lax.rsqrt(jnp.mean(centred * centred, axis=-1, keepdims=True) + norm_epsilon)
    return centred * scale, scale


def weight_copies(pieces, refs, target, me, sems, rep, rep_bit, by_owner, rows):
    copies = []
    for i, ((j, half, shape), ref) in enumerate(zip(pieces, refs)):
        start = (me ^ j if by_owner else j) * rows
        count = rows
        if half is not None:
            count = rows // 2
            start = start + (((rep >> rep_bit) & 1) ^ half) * count
        source = ref.at[me & (shape[0] - 1)] if len(shape) == 3 else ref
        place = target.at[pl.ds(pl.multiple_of(start, count), count), :]
        copies.append(pltpu.make_async_copy(source, place, sems.at[i]))
    return copies


def partner(x):
    width = x.shape[-1]
    lane = lax.broadcasted_iota(jnp.int32, x.shape, 1)
    front = (lane % HEAD_DIM) < HEAD_DIM // 2
    return jnp.where(
        front,
        pltpu.roll(x, width - HEAD_DIM // 2, 1),
        pltpu.roll(x, HEAD_DIM // 2, 1),
    )


def head_masks(heads, width):
    lane = lax.broadcasted_iota(jnp.int32, (QB, width), 1) // HEAD_DIM
    return [lane == h for h in range(heads)]


def stack_heads(x, masks):
    x = x.astype(F32)
    return jnp.concatenate([jnp.where(m, x, 0.0) for m in masks], axis=0).astype(BF16)


def merge_heads(x, masks):
    total = None
    for h, m in enumerate(masks):
        part = jnp.where(m, x[h * QB : (h + 1) * QB], 0.0)
        total = part if total is None else total + part
    return total


def window_bias(ids_q, ids_k):
    row = lax.broadcasted_iota(jnp.int32, (QB, QB + 2 * HALF), 0)
    col = lax.broadcasted_iota(jnp.int32, (QB, QB + 2 * HALF), 1)
    ids_q = jnp.concatenate([ids_q] * ((QB + 2 * HALF) // LANES), axis=1)
    allowed = (col >= row) & (col <= row + 2 * HALF) & (ids_q == ids_k)
    return jnp.where(allowed, 0.0, masked_score)


def block_probs(stacked_q, keys, bias, heads):
    scores = dot(stacked_q, keys, ((1,), (1,)))
    rows, cols = scores.shape
    scores = (scores.reshape(heads, QB, cols) + bias[None]).reshape(rows, cols)
    weights = jnp.exp(scores - jnp.max(scores, axis=-1, keepdims=True))
    return weights * (1.0 / jnp.sum(weights, axis=-1, keepdims=True))


def column_chunk(ref, chunk, cols):
    if cols >= LANES:
        return ref[:, pl.ds(pl.multiple_of(chunk * cols, cols), cols)]
    per = LANES // cols
    tile = ref[:, pl.ds(pl.multiple_of(chunk // per * LANES, LANES), LANES)]
    result = tile
    for k in range(1, per):
        result = jnp.where(chunk % per == k, pltpu.roll(tile, LANES - k * cols, 1), result)
    return result


def row_chunk(ref, chunk, rows, start):
    if rows % 8 == 0:
        return ref[pl.ds(pl.multiple_of(chunk * rows, rows), rows), start : start + LANES]
    per = 8 // rows
    tile = ref[pl.ds(pl.multiple_of(chunk // per * 8, 8), 8), start : start + LANES]
    result = tile[:rows]
    for k in range(1, per):
        result = jnp.where(chunk % per == k, tile[k * rows : (k + 1) * rows], result)
    return result


def take_columns(ref, offset, valid, size):
    begin = offset // LANES * LANES
    end = -(-(offset + valid) // LANES) * LANES
    x = ref[:, begin:end].astype(F32)
    if offset != begin:
        x = pltpu.roll(x, end - offset, 1)
    x = x[:, :size]
    if valid != size:
        lane = lax.broadcasted_iota(jnp.int32, x.shape, 1)
        x = jnp.where(lane < valid, x, 0.0)
    return x


def split_kernel(n, blocks, valid, size, gain_ref, w_ref, out_ref):
    gain = gain_ref[...]
    for owner in range(n):
        for b in range(blocks):
            x = take_columns(w_ref, (b * n + owner) * valid, valid, size)
            out_ref[owner, :, b * size : (b + 1) * size] = (x * gain).astype(BF16)


def split_columns(w, gain, n, blocks, valid, size):
    rows, cols = w.shape
    step = min(rows, 64)
    return pl.pallas_call(
        functools.partial(split_kernel, n, blocks, valid, size),
        grid=(rows // step,),
        in_specs=[
            pl.BlockSpec((step, 1), lambda i: (i, 0)),
            pl.BlockSpec((step, cols), lambda i: (i, 0)),
        ],
        out_specs=pl.BlockSpec((n, step, blocks * size), lambda i: (0, i, 0)),
        out_shape=jax.ShapeDtypeStruct((n, rows, blocks * size), BF16),
        compiler_params=pltpu.CompilerParams(vmem_limit_bytes=24 << 20),
        name="split_columns",
    )(gain, w)


def attention_kernel(
    pieces, rep_bit, n, heads, place_ref, cos_ref, sin_ref, idq_ref, idk_ref, *refs
):
    tok_refs, refs = refs[:n], refs[n:]
    piece_refs, refs = refs[: len(pieces)], refs[len(pieces) :]
    q_ref, k_ref, v_ref, out_ref, normed_ref, w_ref, sems = refs
    seq, width = q_ref.shape
    rows = seq // n
    me, rep = place_ref[0], place_ref[1]
    copies = weight_copies(
        pieces, piece_refs, w_ref, me, sems, rep, rep_bit, True, w_ref.shape[0] // n
    )
    for c in copies:
        c.start()
    edge = jnp.zeros((HALF, width), BF16)
    for ref in (k_ref, v_ref):
        ref[0:HALF, :] = edge
        ref[seq + HALF : seq + 2 * HALF, :] = edge
    for c in copies:
        c.wait()
    for j in range(n):
        start = (me ^ j) * rows
        at = pl.ds(pl.multiple_of(start, rows), rows)
        shifted = pl.ds(pl.multiple_of(start + HALF, HALF), rows)
        hat, _ = normalise(tok_refs[j][...].astype(F32))
        normed = hat.astype(BF16)
        normed_ref[at, :] = normed
        qkv = jnp.dot(normed, w_ref[...], preferred_element_type=F32)
        cos, sin = cos_ref[at, :], sin_ref[at, :]
        q, k = qkv[:, 0:width], qkv[:, width : 2 * width]
        rotated = (q * cos + partner(q) * sin).astype(BF16)
        q_ref[at, :] = (rotated.astype(F32) * (1.0 / math.sqrt(HEAD_DIM))).astype(BF16)
        k_ref[shifted, :] = (k * cos + partner(k) * sin).astype(BF16)
        v_ref[shifted, :] = qkv[:, 2 * width : 3 * width].astype(BF16)
    masks = head_masks(heads, width)

    def attend(i, carry):
        at = pl.ds(pl.multiple_of(i * QB, QB), QB)
        window = pl.ds(pl.multiple_of(i * QB, QB), QB + 2 * HALF)
        bias = window_bias(idq_ref[at, :], idk_ref[0:1, window])
        probs = block_probs(stack_heads(q_ref[at, :], masks), k_ref[window, :], bias, heads)
        mixed = jnp.dot(probs.astype(BF16), v_ref[window, :], preferred_element_type=F32)
        out_ref[at, :] = merge_heads(mixed, masks).astype(BF16)
        return carry

    lax.fori_loop(0, seq // QB, attend, 0)


def feed_forward_kernel(out_pieces, in_pieces, out_bit, in_bit, n, place_ref, *refs):
    tok_refs, refs = refs[:n], refs[n:]
    cot_refs, refs = refs[:n], refs[n:]
    att_refs, refs = refs[:n], refs[n:]
    out_refs, refs = refs[: len(out_pieces)], refs[len(out_pieces) :]
    in_refs, refs = refs[: len(in_pieces)], refs[len(in_pieces) :]
    down_ref, hidden_out, normed_out, act_out, dup_out, *refs = refs
    dnormed_outs, refs = refs[:n], refs[n:]
    tok, cot, att, w_out, w_in, w_down, hidden_own, normed, act, dup, dnormed = refs[:11]
    out_sems, in_sems, att_sems, tok_sems, cot_sems, down_sem, sems = refs[11:]
    me, rep = place_ref[0], place_ref[1]
    rows, model = tok_refs[0].shape
    padded = w_down.shape[0]
    given = down_ref.shape[0]
    if given != padded:
        w_down[given:padded, :] = jnp.zeros((padded - given, model), BF16)
    down_copy = pltpu.make_async_copy(down_ref, w_down.at[0:given, :], down_sem)
    copy = pltpu.make_async_copy
    att_copies = [copy(att_refs[j], att.at[j], att_sems.at[j]) for j in range(n)]
    tok_copies = [copy(tok_refs[j], tok.at[j], tok_sems.at[j]) for j in range(n)]
    cot_copies = [copy(cot_refs[j], cot.at[j], cot_sems.at[j]) for j in range(n)]
    part = model // n
    out_copies = weight_copies(out_pieces, out_refs, w_out, me, out_sems, rep, out_bit, False, part)
    in_copies = weight_copies(in_pieces, in_refs, w_in, me, in_sems, rep, in_bit, True, part)
    for c in att_copies + tok_copies[:1] + out_copies + in_copies + [down_copy]:
        c.start()
    for c in cot_copies[:1] + tok_copies[1:] + cot_copies[1:]:
        c.start()
    for c in att_copies + out_copies:
        c.wait()
    sent = []
    for j in range(n):
        at = pl.ds(pl.multiple_of((me ^ j) * rows, rows), rows)
        here = slice(j * rows, (j + 1) * rows)
        tok_copies[j].wait()
        hidden = tok[j].astype(F32)
        for i in range(n):
            hidden = hidden + jnp.dot(
                att[i, at, :], w_out[i * part : (i + 1) * part, :], preferred_element_type=F32
            )
        if j == 0:
            hidden_own[...] = hidden
        hat, _ = normalise(hidden)
        low = hat.astype(BF16)
        normed[here, :] = low
        if j == 0:
            for c in in_copies + [down_copy]:
                c.wait()
        up = jnp.dot(low, w_in[...], preferred_element_type=F32)
        gate, lin = up[:, :padded], up[:, padded:]
        phi = 0.5 + 0.5 * lax.erf(gate * (1.0 / math.sqrt(2.0)))
        gelu = gate * phi
        slope = phi + gate * jnp.exp(gate * gate * -0.5) * (1.0 / math.sqrt(2.0 * math.pi))
        act_low = (gelu * lin).astype(BF16)
        act[here, :] = act_low
        cot_copies[j].wait()
        dact = dot(cot[j], w_down[...], ((1,), (1,)))
        dup[here, :padded] = (dact * lin * slope).astype(BF16)
        dup[here, padded:] = (dact * gelu).astype(BF16)
        dnormed[j] = dot(dup[here, :], w_in[...], ((1,), (1,))).astype(BF16)
        sent += [
            copy(dnormed.at[j], dnormed_outs[j], sems.at[4 * j]),
            copy(normed.at[here, :], normed_out.at[here, :], sems.at[4 * j + 1]),
            copy(act.at[here, :], act_out.at[here, :], sems.at[4 * j + 2]),
            copy(dup.at[here, :], dup_out.at[here, :], sems.at[4 * j + 3]),
        ]
        for c in sent[-4:]:
            c.start()
    sent.append(copy(hidden_own, hidden_out, sems.at[4 * n]))
    sent[-1].start()
    for c in sent:
        c.wait()


def store_slots(keep_ref, send_ref, rep, order, write):
    half = keep_ref.shape[0]
    for slot in range(2 * half):
        target = keep_ref if slot < half else send_ref
        write(target, slot % half, rep ^ slot_mask(slot, order))


def up_tiles(ff):
    return 2 * (ff // LANES) + 1


def down_kernel(n, ff, far, place_ref, act, w_down, *refs):
    cot_refs, refs = refs[:n], refs[n:]
    keep, send, *refs = refs
    mlp_refs, refs = refs[:n], refs[n:]
    (down_sum,) = refs
    rows, model = cot_refs[0].shape
    cols = model // (2 * keep.shape[0])
    total = None
    for j in range(n):
        term = dot(act[j * rows : (j + 1) * rows, :], cot_refs[j][...], ((0,), (0,)))
        total = term if total is None else total + term
    down_sum[...] = total

    def write(target, slot, c):
        target[slot] = column_chunk(down_sum, c, cols)[:ff].astype(BF16)

    store_slots(keep, send, place_ref[1], far, write)
    given = w_down.shape[0]
    for j in range(n):
        low = act[j * rows : (j + 1) * rows, 0:given]
        mlp_refs[j][...] = jnp.dot(low, w_down[...], preferred_element_type=F32).astype(BF16)


def in_kernel(n, ff, near, place_ref, normed, dup, keep, send, in_sum):
    me, rep = place_ref[0], place_ref[1]
    part = normed.shape[1] // n
    padded = dup.shape[1] // 2
    chunk = keep.shape[2]
    tiles = up_tiles(ff)
    whole, rest = ff // LANES, ff % LANES
    for owner in range(n):
        block = dot(normed[:, owner * part : (owner + 1) * part], dup[...], ((0,), (0,)))
        in_sum[:, : 2 * padded] = block
        first = block[:, whole * LANES : (whole + 1) * LANES]
        second = block[:, padded + whole * LANES : padded + (whole + 1) * LANES]
        lane = lax.broadcasted_iota(jnp.int32, first.shape, 1)
        both = jnp.where(lane < rest, first, pltpu.roll(second, rest, 1))
        in_sum[:, 2 * padded :] = both
        base = (me ^ owner) * tiles
        starts = [t * LANES for t in range(whole)] + [padded + t * LANES for t in range(whole)]
        starts.append(2 * padded)

        def write(target, slot, c):
            for t, s in enumerate(starts):
                target[slot, base + t] = row_chunk(in_sum, c, chunk, s).astype(BF16)

        store_slots(keep, send, rep, near, write)


def add_kernel(a_ref, b_ref, c_ref, d_ref, mine_ref, other_ref):
    mine_ref[...] = a_ref[...].astype(F32) + b_ref[...].astype(F32)
    other_ref[...] = (c_ref[...].astype(F32) + d_ref[...].astype(F32)).astype(BF16)


def norm_back_kernel(mine, got, hidden, cotangent, dhidden, dproj):
    hat, scale = normalise(hidden[...])
    e = mine[...] + got[...].astype(F32)
    value = cotangent[...].astype(F32) + norm_backward(e, hat, scale)
    dhidden[...] = value
    dproj[...] = value.astype(BF16)


def attention_back_kernel(n, heads, far, place_ref, *refs):
    dproj_refs, refs = refs[:n], refs[n:]
    w_out, att, q_ref, k_ref, v_ref, cos_ref, sin_ref, idq_ref, idk_ref, *refs = refs
    dqkv, out_keep, out_send, da, dk, dv, out_sum = refs
    me, rep = place_ref[0], place_ref[1]
    seq, width = q_ref.shape
    rows, model = dproj_refs[0].shape
    part = model // n
    dk[...] = jnp.zeros_like(dk)
    dv[...] = jnp.zeros_like(dv)
    head_cols = heads * HEAD_DIM
    total = None
    for j in range(n):
        at = pl.ds(pl.multiple_of((me ^ j) * rows, rows), rows)
        dproj = dproj_refs[j][...]
        da[at, 0:head_cols] = dot(dproj, w_out[...], ((1,), (1,))).astype(BF16)
        term = dot(att[at, :], dproj, ((0,), (0,)))
        total = term if total is None else total + term
    if head_cols != width:
        da[:, head_cols:] = jnp.zeros((seq, width - head_cols), BF16)
    out_sum[...] = total[0:part]
    cols = model // (2 * out_keep.shape[0])

    def write_out(target, slot, c):
        target[slot] = column_chunk(out_sum, c, cols).astype(BF16)

    store_slots(out_keep, out_send, rep, far, write_out)
    masks = head_masks(heads, width)

    def back(i, carry):
        at = pl.ds(pl.multiple_of(i * QB, QB), QB)
        window = pl.ds(pl.multiple_of(i * QB, QB), QB + 2 * HALF)
        bias = window_bias(idq_ref[at, :], idk_ref[0:1, window])
        queries = stack_heads(q_ref[at, :], masks)
        keys = k_ref[window, :]
        probs = block_probs(queries, keys, bias, heads)
        grads = stack_heads(da[at, :], masks)
        dprobs = dot(grads, v_ref[window, :], ((1,), (1,)))
        delta = jnp.sum(probs * dprobs, axis=-1, keepdims=True)
        dscores = (probs * (dprobs - delta)).astype(BF16)
        dq = merge_heads(jnp.dot(dscores, keys, preferred_element_type=F32), masks)
        dq = dq * (1.0 / math.sqrt(HEAD_DIM))
        cos, sin = cos_ref[at, :], sin_ref[at, :]
        dqkv[at, 0:width] = (dq * cos - partner(dq) * sin).astype(BF16)
        dk[window, :] += dot(dscores, queries, ((0,), (0,)))
        dv[window, :] += dot(probs.astype(BF16), grads, ((0,), (0,)))
        return carry

    lax.fori_loop(0, seq // QB, back, 0)

    def finish(i, carry):
        at = pl.ds(pl.multiple_of(i * QB, QB), QB)
        shifted = pl.ds(pl.multiple_of(i * QB + HALF, HALF), QB)
        cos, sin = cos_ref[at, :], sin_ref[at, :]
        g = dk[shifted, :]
        dqkv[at, width : 2 * width] = (g * cos - partner(g) * sin).astype(BF16)
        dqkv[at, 2 * width : 3 * width] = dv[shifted, :].astype(BF16)
        return carry

    lax.fori_loop(0, seq // QB, finish, 0)


def qkv_kernel(n, near, place_ref, normed, dqkv, keep, send, qkv_sum):
    me, rep = place_ref[0], place_ref[1]
    part = normed.shape[1] // n
    chunk = keep.shape[2]
    tiles = dqkv.shape[1] // LANES
    for owner in range(n):
        qkv_sum[...] = dot(normed[:, owner * part : (owner + 1) * part], dqkv[...], ((0,), (0,)))
        base = (me ^ owner) * tiles

        def write(target, slot, c):
            for t in range(tiles):
                target[slot, base + t] = row_chunk(qkv_sum, c, chunk, t * LANES).astype(BF16)

        store_slots(keep, send, rep, near, write)


def project_back_kernel(n, place_ref, dqkv, w_qkv, *out_refs):
    rows = out_refs[0].shape[0]
    for j in range(n):
        at = pl.ds(pl.multiple_of((place_ref[0] ^ j) * rows, rows), rows)
        out_refs[j][...] = dot(dqkv[at, :], w_qkv[...], ((1,), (1,))).astype(BF16)


def place_piece(canvas, piece, offset, valid):
    shift = offset % LANES
    height, size = piece.shape
    count = -(-(shift + valid) // LANES)
    if count * LANES > size:
        piece = jnp.concatenate([piece, jnp.zeros((height, count * LANES - size), F32)], axis=1)
    if shift:
        piece = pltpu.roll(piece, shift, 1)
    lane = lax.broadcasted_iota(jnp.int32, (height, LANES), 1)
    for t in range(count):
        tile = piece[:, t * LANES : (t + 1) * LANES]
        low, high = shift - t * LANES, shift + valid - t * LANES
        if low > 0 or high < LANES:
            tile = jnp.where((lane >= low) & (lane < high), tile, 0.0)
        index = offset // LANES + t
        canvas[index] = tile if index not in canvas else canvas[index] + tile


def columns_out_kernel(
    n, ff, head_cols, width, order, count, place_ref, gain_ref, w_ref, *refs
):
    me, rep = place_ref[0], place_ref[1]
    *parts, out_ref, ln_ref = refs
    tiles = count // n
    if len(parts) == 1:

        def read(index):
            return parts[0][index]

    else:
        half = parts[0].shape[0]
        slot = slot_of(rep ^ pl.program_id(0), order)
        at = slot & (half - 1)

        def read(index):
            return jnp.where(slot < half, parts[0][at, index], parts[1][at, index])

    canvas = {}
    for owner in range(n):
        base = (me ^ owner) * tiles

        def tile(t):
            return read(base + t).astype(F32)

        if ff:
            whole, rest = ff // LANES, ff % LANES
            last = tile(2 * whole)
            gate = jnp.concatenate([tile(t) for t in range(whole)] + [last], axis=1)
            last = pltpu.roll(last, LANES - rest, 1)
            lin = jnp.concatenate([tile(whole + t) for t in range(whole)] + [last], axis=1)
            place_piece(canvas, gate, owner * ff, ff)
            place_piece(canvas, lin, (n + owner) * ff, ff)
        else:
            per = width // LANES
            for b in range(3):
                piece = jnp.concatenate([tile(b * per + t) for t in range(per)], axis=1)
                place_piece(canvas, piece, (b * n + owner) * head_cols, head_cols)
    gain = gain_ref[...]
    total = None
    for index, value in canvas.items():
        at = slice(index * LANES, (index + 1) * LANES)
        term = value * w_ref[:, at].astype(F32)
        total = term if total is None else total + term
        out_ref[:, at] = value * gain
    ln_ref[...] = jnp.sum(total, axis=1, keepdims=True)


def columns_out(place, parts, weight, gain, n, tiles, order, ff=0, head_cols=0, width=0):
    now, got = parts
    chunk = now.shape[2]
    part, cols = weight.shape
    count = part // chunk
    if got is None:
        parts = [now]
        part_specs = [pl.BlockSpec((None, tiles, chunk, LANES), lambda i: (i, 0, 0, 0))]
    else:
        part_specs = [pl.BlockSpec(now.shape, lambda i: (0, 0, 0, 0))] * 2
    total, ln = pl.pallas_call(
        functools.partial(columns_out_kernel, n, ff, head_cols, width, order, tiles),
        grid=(count,),
        in_specs=[
            pl.BlockSpec(memory_space=pltpu.SMEM),
            pl.BlockSpec((None, chunk, 1), lambda i: (i, 0, 0)),
            pl.BlockSpec((None, chunk, cols), lambda i: (i, 0, 0)),
            *part_specs,
        ],
        out_specs=[
            pl.BlockSpec((None, chunk, cols), lambda i: (i, 0, 0)),
            pl.BlockSpec((None, chunk, 1), lambda i: (i, 0, 0)),
        ],
        out_shape=[
            jax.ShapeDtypeStruct((count, chunk, cols), F32),
            jax.ShapeDtypeStruct((count, chunk, 1), F32),
        ],
        compiler_params=pltpu.CompilerParams(vmem_limit_bytes=32 << 20),
        name="columns_out",
    )(place, gain.reshape(count, chunk, 1), weight.reshape(count, chunk, cols), *parts)
    return total.reshape(part, cols), ln.reshape(part)


def rows_out_kernel(order, cols, place_ref, *refs):
    *parts, out_ref = refs
    rep = place_ref[1]

    def chunk(c):
        if len(parts) == 1:
            return parts[0][c].astype(F32)
        half = parts[0].shape[0]
        slot = slot_of(rep ^ c, order)
        at = slot & (half - 1)
        return jnp.where(slot < half, parts[0][at], parts[1][at]).astype(F32)

    count = out_ref.shape[1] // cols
    if cols >= LANES:
        for c in range(count):
            out_ref[:, c * cols : (c + 1) * cols] = chunk(c)
    else:
        per = LANES // cols
        lane = lax.broadcasted_iota(jnp.int32, out_ref.shape[:1] + (LANES,), 1) // cols
        for t in range(count // per):
            value = chunk(per * t)
            for k in range(1, per):
                value = jnp.where(lane == k, pltpu.roll(chunk(per * t + k), k * cols, 1), value)
            out_ref[:, t * LANES : (t + 1) * LANES] = value


def rows_out(place, parts, model, order):
    now, got = parts
    count = now.shape[0]
    if got is None:
        parts = [now]
    else:
        count = 2 * count
    return pl.pallas_call(
        functools.partial(rows_out_kernel, order, model // count),
        in_specs=[pl.BlockSpec(memory_space=pltpu.SMEM)]
        + [pl.BlockSpec(memory_space=pltpu.VMEM)] * len(parts),
        out_shape=jax.ShapeDtypeStruct((now.shape[1], model), F32),
        compiler_params=pltpu.CompilerParams(vmem_limit_bytes=32 << 20),
        name="rows_out",
    )(place, *parts)


def ordered(kernel, first, count):
    def body(*refs):
        kernel(*refs[:first], *refs[first + count :])

    return body


def work(flops):
    return pl.CostEstimate(flops=int(flops), bytes_accessed=1 << 22, transcendentals=0)


SMEM_SPEC = pl.BlockSpec(memory_space=pltpu.SMEM)
VMEM_SPEC = pl.BlockSpec(memory_space=pltpu.VMEM)
ANY_SPEC = pl.BlockSpec(memory_space=pl.ANY)


def norm_backward(grad_hat, normed, scale):
    return (
        grad_hat
        - jnp.mean(grad_hat, axis=-1, keepdims=True)
        - normed * jnp.mean(grad_hat * normed, axis=-1, keepdims=True)
    ) * scale


def after(value, *earlier):
    return lax.optimization_barrier((value,) + earlier)[0]


def shards(tokens, segment_ids, ln1_gain, w_qkv, w_out, ln2_gain, w_in, w_down, cotangent):
    n = lax.axis_size("shard")
    replicas = lax.axis_size("rep")
    me = lax.axis_index("shard")
    place = jnp.stack([me, lax.axis_index("rep")]).astype(jnp.int32)
    rows, model = tokens.shape
    seq = rows * n
    part = model // n
    ff = w_down.shape[0]
    heads = HEADS // n
    head_cols = heads * HEAD_DIM
    width = max(LANES, head_cols)
    padded = -(-ff // LANES) * LANES
    near = list(range(bits_of("rep")))
    far = near[1:2] + near[:1] + near[2:]
    shape = jax.ShapeDtypeStruct
    params = pltpu.CompilerParams(vmem_limit_bytes=VMEM_LIMIT)

    gain1 = ln1_gain.astype(F32)[:, None]
    gain2 = ln2_gain.astype(F32)[:, None]
    qkv_to = split_columns(w_qkv, gain1, n, 3, head_cols, width)
    in_to = split_columns(w_in, gain2, n, 2, ff, padded)
    qkv_pieces = split_weight(qkv_to, 0)

    def fetched(pieces):
        return [a for j, h, a in pieces if j == n // 2 and h == 0]

    toks = gather_list(after(tokens, *fetched(qkv_pieces)), "shard")
    out_pieces = gather_weight(after(w_out, toks[n // 2]), 0)
    in_pieces = split_weight(after(in_to, toks[n // 2]), 1)
    cots = gather_list(after(cotangent, *fetched(in_pieces)), "shard")

    lane = jnp.arange(width, dtype=jnp.int32) % HEAD_DIM
    half = HEAD_DIM // 2
    frequency = jnp.exp(-math.log(rope_base) * 2.0 * (lane % half).astype(F32) / HEAD_DIM)
    angles = jnp.arange(seq, dtype=F32)[:, None] * frequency[None, :]
    sign = jnp.where(lane < half, -1.0, 1.0)
    ids = segment_ids[0]
    tables = (
        jnp.cos(angles),
        jnp.sin(angles) * sign[None, :],
        jnp.broadcast_to(ids[:, None], (seq, LANES)),
        jnp.pad(ids, (HALF, HALF), constant_values=-1)[None],
    )

    def about(pieces):
        return [(j, h, a.shape) for j, h, a in pieces]

    queries, keys, values, attended, normed1, qkv_w = pl.pallas_call(
        functools.partial(attention_kernel, about(qkv_pieces), 0, n, heads),
        in_specs=[SMEM_SPEC] + [VMEM_SPEC] * (4 + n) + [ANY_SPEC] * len(qkv_pieces),
        out_shape=(
            shape((seq, width), BF16),
            shape((seq + 2 * HALF, width), BF16),
            shape((seq + 2 * HALF, width), BF16),
            shape((seq, width), BF16),
            shape((seq, model), BF16),
            shape((model, 3 * width), BF16),
        ),
        scratch_shapes=[pltpu.SemaphoreType.DMA((len(qkv_pieces),))],
        compiler_params=params,
        cost_estimate=work(40 * seq * model * width),
        name="attention",
    )(place, *tables, *toks, *[a for _, _, a in qkv_pieces])

    atts = gather_list(attended[:, :head_cols], "shard")
    blocks = [shape((rows, model), BF16)] * n
    hidden, normed2, act, dup, *dnormed2_blocks = pl.pallas_call(
        functools.partial(
            feed_forward_kernel, about(out_pieces), about(in_pieces), 0, 1, n
        ),
        in_specs=[SMEM_SPEC]
        + [ANY_SPEC] * (3 * n + len(out_pieces) + len(in_pieces) + 1),
        out_specs=[ANY_SPEC] * (4 + n),
        out_shape=[
            shape((rows, model), F32),
            shape((seq, model), BF16),
            shape((seq, padded), BF16),
            shape((seq, 2 * padded), BF16),
        ]
        + blocks,
        scratch_shapes=[
            pltpu.VMEM((n, rows, model), BF16),
            pltpu.VMEM((n, rows, model), BF16),
            pltpu.VMEM((n, seq, head_cols), BF16),
            pltpu.VMEM((model, model), BF16),
            pltpu.VMEM((model, 2 * padded), BF16),
            pltpu.VMEM((padded, model), BF16),
            pltpu.VMEM((rows, model), F32),
            pltpu.VMEM((seq, model), BF16),
            pltpu.VMEM((seq, padded), BF16),
            pltpu.VMEM((seq, 2 * padded), BF16),
            pltpu.VMEM((n, rows, model), BF16),
            pltpu.SemaphoreType.DMA((len(out_pieces),)),
            pltpu.SemaphoreType.DMA((len(in_pieces),)),
            pltpu.SemaphoreType.DMA((n,)),
            pltpu.SemaphoreType.DMA((n,)),
            pltpu.SemaphoreType.DMA((n,)),
            pltpu.SemaphoreType.DMA,
            pltpu.SemaphoreType.DMA((4 * n + 1,)),
        ],
        compiler_params=params,
        cost_estimate=work(26 * seq * model * padded),
        name="feed_forward",
    )(
        place,
        *toks,
        *cots,
        *atts,
        *[a for _, _, a in out_pieces],
        *[a for _, _, a in in_pieces],
        jnp.pad(w_down, ((0, -ff % 16), (0, 0))),
    )
    slots = replicas // 2
    chunk = part // replicas
    lanes = max(LANES, model // replicas)
    tiles = up_tiles(ff)
    in_shape = shape((slots, n * tiles, chunk, LANES), BF16)
    down_shape = shape((slots, ff, lanes), BF16)

    in_keep, in_send = pl.pallas_call(
        functools.partial(in_kernel, n, ff, near),
        in_specs=[SMEM_SPEC] + [VMEM_SPEC] * 2,
        out_shape=[in_shape, in_shape],
        scratch_shapes=[pltpu.VMEM((part, 2 * padded + LANES), F32)],
        compiler_params=params,
        cost_estimate=work(8 * seq * model * padded),
        name="in_gradient",
    )(place, normed2, dup)

    top = bits_of("shard") - 1
    sums = scatter_bits(enumerate(dnormed2_blocks), "shard", range(top - 1))
    low, high = 1 << (top - 1), 1 << top
    mine, other = pl.pallas_call(
        ordered(add_kernel, 4, 1),
        in_specs=[VMEM_SPEC] * 4 + [ANY_SPEC],
        out_shape=[shape((rows, model), F32), shape((rows, model), BF16)],
        compiler_params=pltpu.CompilerParams(vmem_limit_bytes=16 << 20),
        name="near_sum",
    )(
        sums[0],
        swap(sums[low].astype(BF16), "shard", top - 1),
        sums[high],
        swap(sums[low | high].astype(BF16), "shard", top - 1),
        in_keep,
    )
    down_keep, down_send, *mlp_blocks = pl.pallas_call(
        ordered(functools.partial(down_kernel, n, ff, far), 3 + n, 1),
        in_specs=[SMEM_SPEC] + [VMEM_SPEC] * (2 + n) + [ANY_SPEC],
        out_shape=[down_shape, down_shape] + blocks,
        scratch_shapes=[pltpu.VMEM((padded, model), F32)],
        compiler_params=params,
        cost_estimate=work(8 * seq * model * padded),
        name="down_gradient",
    )(place, act, jnp.pad(w_down, ((0, -ff % 16), (0, 0))), *cots, other)
    dhidden, dproj = pl.pallas_call(
        ordered(norm_back_kernel, 4, 1),
        in_specs=[VMEM_SPEC] * 4 + [ANY_SPEC],
        out_shape=[shape((rows, model), F32), shape((rows, model), BF16)],
        compiler_params=pltpu.CompilerParams(vmem_limit_bytes=24 << 20),
        name="norm_back",
    )(mine, swap(other, "shard", top), hidden, cotangent, down_keep)
    dprojs = gather_list(dproj, "shard")

    out_shape = shape((slots, part, lanes), BF16)
    dqkv, out_keep, out_send = pl.pallas_call(
        functools.partial(attention_back_kernel, n, heads, far),
        in_specs=[SMEM_SPEC] + [VMEM_SPEC] * (n + 9),
        out_shape=[shape((seq, 3 * width), BF16), out_shape, out_shape],
        scratch_shapes=[
            pltpu.VMEM((seq, width), BF16),
            pltpu.VMEM((seq + 2 * HALF, width), F32),
            pltpu.VMEM((seq + 2 * HALF, width), F32),
            pltpu.VMEM((part, model), F32),
        ],
        compiler_params=params,
        cost_estimate=work(40 * seq * model * width),
        name="attention_back",
    )(place, *dprojs, w_out, attended, queries, keys, values, *tables)

    mlp_blocks = [after(b, dprojs[n // 2]) for b in mlp_blocks]
    mlp = scatter_sum_list(mlp_blocks, "shard")
    output = (hidden + mlp).astype(BF16)

    qkv_tiles = 3 * width // LANES
    qkv_shape = shape((slots, n * qkv_tiles, chunk, LANES), BF16)
    qkv_keep, qkv_send = pl.pallas_call(
        functools.partial(qkv_kernel, n, near),
        in_specs=[SMEM_SPEC] + [VMEM_SPEC] * 2,
        out_shape=[qkv_shape, qkv_shape],
        scratch_shapes=[pltpu.VMEM((part, 3 * width), F32)],
        compiler_params=params,
        cost_estimate=work(12 * seq * model * width),
        name="qkv_gradient",
    )(place, normed1, dqkv)
    dnormed1_blocks = pl.pallas_call(
        ordered(functools.partial(project_back_kernel, n), 3, 1),
        in_specs=[SMEM_SPEC] + [VMEM_SPEC] * 2 + [ANY_SPEC],
        out_shape=blocks,
        compiler_params=params,
        cost_estimate=work(6 * seq * model * width),
        name="project_back",
    )(place, dqkv, qkv_w, qkv_keep)
    dnormed1 = scatter_sum_list(dnormed1_blocks, "shard")
    hat1, scale1 = normalise(tokens.astype(F32))
    input_grad = dhidden + norm_backward(dnormed1, hat1, scale1)

    def turned(share, tiles):
        return turn(share.reshape(n, tiles, chunk, LANES), n).reshape(n * tiles, chunk, LANES)

    in_share = turned(replica_reduce(in_keep, in_send, near, [dproj, dqkv]), tiles)
    down_share = replica_reduce(down_keep, down_send, far, [dproj, dqkv])
    down_share = jnp.pad(down_share, ((0, -ff % chunk), (0, 0))).reshape(-1, chunk, LANES)
    both = lax.all_gather(jnp.concatenate([in_share, down_share]), "rep", axis=0)
    down_all = both[:, n * tiles :].reshape(replicas, -1, LANES)[:, :ff]

    out_pair = replica_spread(replica_reduce(out_keep, out_send, far), far)
    qkv_share = turned(replica_reduce(qkv_keep, qkv_send, near), qkv_tiles)
    qkv_pair = replica_spread(qkv_share, near)

    in_total, ln2_total = columns_out(place, (both, None), w_in, gain2, n, n * tiles, near, ff=ff)
    down_total = rows_out(place, (down_all, None), model, far)
    out_total = rows_out(place, out_pair, model, far)
    qkv_total, ln1_total = columns_out(
        place,
        qkv_pair,
        w_qkv,
        gain1,
        n,
        n * qkv_tiles,
        near,
        head_cols=head_cols,
        width=width,
    )
    return (
        output,
        input_grad,
        ln1_total,
        qkv_total,
        out_total,
        ln2_total,
        in_total,
        down_total,
    )


def solution(mesh):
    return jax.shard_map(
        shards,
        mesh=mesh,
        in_specs=(
            P(("rep", "shard"), None),
            P("rep", None),
            P("shard"),
            P("shard", None),
            P("shard", None),
            P("shard"),
            P("shard", None),
            P("shard", None),
            P(("rep", "shard"), None),
        ),
        out_specs=(
            P(("rep", "shard"), None),
            P(("rep", "shard"), None),
            P("shard"),
            P("shard", None),
            P("shard", None),
            P("shard"),
            P("shard", None),
            P("shard", None),
        ),
        check_vma=False,
    )
```

profile of v0, /device:TPU:0, one launch (start us, length us, event | category | flops | bytes accessed | tf_op | source)
XLA Modules:
  0.0 393.8 jit_solution(15081360021424365683)
XLA Ops:
  11.4 3.0 collective-permute-start
  14.4 9.1 %collective-permute-done.refs_5_ = bf16[2,128,768]{2,1,0:T(8,128)(2,1)S(1)} collective-permute-done((bf16[2,128,768]{2,1,0:T(8,128)(2,1)S(1)}, bf16[2,128,768]{2,1,0:T(8,128)(2,1)S(1)}, u32[]{:S(2)}, u32[]{:S(2)}) %collective-permute-start) | collective-permute-done | bytes 393248 | tf_op jit(solution)/shard_map/ppermute | solution.py:36
  31.8 5.2 %collective-permute-done.2.refs_2_ = bf16[256,1024]{1,0:T(8,128)(2,1)} collective-permute-done((bf16[256,1024]{1,0:T(8,128)(2,1)}, bf16[256,1024]{1,0:T(8,128)(2,1)}, u32[]{:S(2)}, u32[]{:S(2)}) %collective-permute-start.2) | collective-permute-done | bytes 524320 | tf_op jit(solution)/shard_map/ppermute | solution.py:36
  40.8 4.8 %sine_multiply_fusion = (f32[1024,256]{1,0:T(8,128)}, f32[1024,256]{1,0:T(8,128)}) fusion(f32[256]{0:T(256)S(1)} %get-tuple-element.130, f32[256]{0:T(256)S(1)} %get-tuple-element.131), kind=kLoop, calls=%fused_computation.17 | loop fusion | flops 524288 | bytes 2099200 | tf_op jit(solution)/shard_map/mul | solution.py:753
  51.1 12.0 %collective-permute-done.15.refs_13_ = bf16[128,1024]{1,0:T(8,128)(2,1)S(1)} collective-permute-done((bf16[128,1024]{1,0:T(8,128)(2,1)S(1)}, bf16[128,1024]{1,0:T(8,128)(2,1)S(1)}, u32[]{:S(2)}, u32[]{:S(2)}) %collective-permute-start.15) | collective-permute-done | bytes 262176 | tf_op jit(solution)/shard_map/ppermute | solution.py:36
  66.8 13.9 %attention.1 = (bf16[1024,256]{1,0:T(8,128)(2,1)}, bf16[1152,256]{1,0:T(8,128)(2,1)}, bf16[1152,256]{1,0:T(8,128)(2,1)}, bf16[1024,256]{1,0:T(8,128)(2,1)}, bf16...) custom-call(s32[2]{0:T(128)S(1)} %pad_add_fusion.place_ref.refs_0_, f32[1024,256]{1,0:T(8,128)} %get-tuple-element.129.cos_ref.refs_9_, ...), custom_call_target="tpu_custom_call" | custom-call | flops 10737418240 | bytes 4194304 | tf_op jit(solution)/shard_map/attention/pallas_call | solution.py:761
  85.2 10.5 %collective-permute-done.13.refs_10_ = bf16[1024,256]{1,0:T(8,128)(2,1)S(1)} collective-permute-done((bf16[1024,256]{1,0:T(8,128)(2,1)}, bf16[1024,256]{1,0:T(8,128)(2,1)S(1)}, u32[]{:S(2)}, u32[]{:S(2)}) %collective-permute-start.13) | collective-permute-done | bytes 524320 | tf_op jit(solution)/shard_map/ppermute | solution.py:36
  95.7 10.5 %collective-permute-done.6.refs_6_.refs_5_ = bf16[256,1024]{1,0:T(8,128)(2,1)S(1)} collective-permute-done((bf16[256,1024]{1,0:T(8,128)(2,1)S(1)}, bf16[256,1024]{1,0:T(8,128)(2,1)S(1)}, u32[]{:S(2)}, u32[]{:S(2)}) %collective-permute-start.6) | collective-permute-done | bytes 524320 | tf_op jit(solution)/shard_map/ppermute | solution.py:36
  109.7 22.0 %feed_forward.1 = (f32[256,1024]{1,0:T(8,128)}, bf16[1024,1024]{1,0:T(8,128)(2,1)}, bf16[1024,768]{1,0:T(8,128)(2,1)}, bf16[1024,1536]{1,0:T(8,128)(2,1)}, bf16[...) custom-call(s32[2]{0:T(128)S(1)} %pad_add_fusion.place_ref.refs_0_, ...), custom_call_target="tpu_custom_call" | custom-call | flops 20937965568 | bytes 4194304 | tf_op jit(solution)/shard_map/feed_forward/pallas_call | solution.py:780
  132.2 7.7 %in_gradient.1 = (bf16[4,44,32,128]{3,2,1,0:T(8,128)(2,1)S(1)}, bf16[4,44,32,128]{3,2,1,0:T(8,128)(2,1)}) custom-call(s32[2]{0:T(128)S(1)} %pad_add_fusion.place_ref.refs_0_, bf16[1024,1024]{1,0:T(8,128)(2,1)} %get-tuple-element.70.normed, bf16[1024,1536]{1,0:T(8,128)(2,1)} %get-tuple-element.71.dup), custom_call_target="tpu_custom_call" | custom-call | flops 6442450944 | bytes 4194304 | tf_op jit(solution)/shard_map/in_gradient/pallas_call | solution.py:833
  142.2 7.2 %down_gradient.1 = (bf16[4,656,128]{2,1,0:T(8,128)(2,1)}, bf16[4,656,128]{2,1,0:T(8,128)(2,1)}, bf16[256,1024]{1,0:T(8,128)(2,1)S(1)}, bf16[256,1024]{1,0:T(8,12...) custom-call(s32[2]{0:T(128)S(1)} %pad_add_fusion.place_ref.refs_0_, ...), custom_call_target="tpu_custom_call" | custom-call | flops 6442450944 | bytes 4194304 | tf_op jit(solution)/shard_map/down_gradient/pallas_call | solution.py:859
  150.6 3.8 collective-permute-done.26.refs_1_
  157.8 9.2 %collective-permute-done.57 = bf16[4,656,128]{2,1,0:T(8,128)(2,1)S(1)} collective-permute-done((bf16[4,656,128]{2,1,0:T(8,128)(2,1)}, bf16[4,656,128]{2,1,0:T(8,128)(2,1)S(1)}, u32[]{:S(2)}, u32[]{:S(2)}) %collective-permute-start.57) | collective-permute-done | bytes 671776 | tf_op jit(solution)/shard_map/ppermute | solution.py:36
  171.0 3.7 collective-permute-done.51
  177.7 14.5 %attention_back.1 = (bf16[1024,768]{1,0:T(8,128)(2,1)}, bf16[4,256,128]{2,1,0:T(8,128)(2,1)S(1)}, bf16[4,256,128]{2,1,0:T(8,128)(2,1)}) custom-call(s32[2]{0:T(128)S(1)} %pad_add_fusion.place_ref.refs_0_, bf16[256,1024]{1,0:T(8,128)(2,1)S(1)} %get-tuple-element.77.refs_0_, bf16[256,1024]{1,0:T(8,128)(2,1)S(1)} %collective-permute-done.31.refs_1_, ...), custom_call_target="tpu_custom_call" | custom-call | flops 10737418240 | bytes 4194304 | tf_op jit(solution)/shard_map/attention_back/pallas_call | solution.py:878
  193.2 2.6 collective-permute-start.53
  196.3 18.1 %collective-permute-done.53 = bf16[1,44,32,128]{3,2,1,0:T(8,128)(2,1)S(1)} collective-permute-done((bf16[1,44,32,128]{3,2,1,0:T(8,128)(2,1)S(1)}, bf16[1,44,32,128]{3,2,1,0:T(8,128)(2,1)S(1)}, u32[]{:S(2)}, u32[]{:S(2)}) %collective-permute-start.53) | collective-permute-done | bytes 360480 | tf_op jit(solution)/shard_map/ppermute | solution.py:36
  216.2 3.9 collective-permute-done.55
  223.6 5.0 %qkv_gradient.1 = (bf16[4,24,32,128]{3,2,1,0:T(8,128)(2,1)S(1)}, bf16[4,24,32,128]{3,2,1,0:T(8,128)(2,1)}) custom-call(s32[2]{0:T(128)S(1)} %pad_add_fusion.place_ref.refs_0_, bf16[1024,1024]{1,0:T(8,128)(2,1)} %get-tuple-element.91.normed, bf16[1024,768]{1,0:T(8,128)(2,1)} %get-tuple-element.89.dqkv.refs_1_), custom_call_target="tpu_custom_call" | custom-call | flops 3221225472 | bytes 4194304 | tf_op jit(solution)/shard_map/qkv_gradient/pallas_call | solution.py:899
  231.9 4.7 %project_back.1 = (bf16[256,1024]{1,0:T(8,128)(2,1)S(1)}, bf16[256,1024]{1,0:T(8,128)(2,1)S(1)}, bf16[256,1024]{1,0:T(8,128)(2,1)S(1)}, bf16[256,1024]{1,0:T(8,128)(2,1)}) custom-call(s32[2]{0:T(128)S(1)} %pad_add_fusion.place_ref.refs_0_, bf16[1024,768]{1,0:T(8,128)(2,1)} %get-tuple-element.89.dqkv.refs_1_, bf16[1024,768]{1,0:T(8,128)(2,1)} %get-tuple-element.90.refs_2_, ...), custom_call_target="tpu_custom_call" | custom-call | flops 1610612736 | bytes 4194304 | tf_op jit(solution)/shard_map/project_back/pallas_call | solution.py:908
  236.7 14.5 %collective-permute-done.45 = bf16[4,256,128]{2,1,0:T(8,128)(2,1)} collective-permute-done((bf16[4,256,128]{2,1,0:T(8,128)(2,1)}, bf16[4,256,128]{2,1,0:T(8,128)(2,1)}, u32[]{:S(2)}, u32[]{:S(2)}) %collective-permute-start.45) | collective-permute-done | bytes 262176 | tf_op jit(solution)/shard_map/ppermute | solution.py:36
  252.3 2.8 collective-permute-done.36
  261.3 25.4 %collective-permute-done.37 = bf16[2,24,32,128]{3,2,1,0:T(8,128)(2,1)S(1)} collective-permute-done((bf16[2,24,32,128]{3,2,1,0:T(8,128)(2,1)S(1)}, bf16[2,24,32,128]{3,2,1,0:T(8,128)(2,1)S(1)}, u32[]{:S(2)}, u32[]{:S(2)}) %collective-permute-start.37) | collective-permute-done | bytes 393248 | tf_op jit(solution)/shard_map/ppermute | solution.py:36
  289.9 20.0 %collective-permute-done.38 = bf16[1,24,32,128]{3,2,1,0:T(8,128)(2,1)S(1)} collective-permute-done((bf16[1,24,32,128]{3,2,1,0:T(8,128)(2,1)S(1)}, bf16[1,24,32,128]{3,2,1,0:T(8,128)(2,1)S(1)}, u32[]{:S(2)}, u32[]{:S(2)}) %collective-permute-start.38) | collective-permute-done | bytes 196640 | tf_op jit(solution)/shard_map/ppermute | solution.py:36
  311.6 3.1 collective-permute-done.40
  317.8 10.8 %collective-permute-done.42 = bf16[1,24,32,128]{3,2,1,0:T(8,128)(2,1)S(1)} collective-permute-done((bf16[1,24,32,128]{3,2,1,0:T(8,128)(2,1)S(1)}, bf16[1,24,32,128]{3,2,1,0:T(8,128)(2,1)S(1)}, u32[]{:S(2)}, u32[]{:S(2)}) %collective-permute-start.42) | collective-permute-done | bytes 196640 | tf_op jit(solution)/shard_map/ppermute | solution.py:36
  332.9 13.1 %collective-permute-done.50.refs_1_ = bf16[4,256,128]{2,1,0:T(8,128)(2,1)S(1)} collective-permute-done((bf16[4,256,128]{2,1,0:T(8,128)(2,1)S(1)}, bf16[4,256,128]{2,1,0:T(8,128)(2,1)S(1)}, u32[]{:S(2)}, u32[]{:S(2)}) %collective-permute-start.50) | collective-permute-done | bytes 262176 | tf_op jit(solution)/shard_map/ppermute | solution.py:36
  351.6 14.6 %collective-permute-done.44.refs_1_ = bf16[4,24,32,128]{3,2,1,0:T(8,128)(2,1)S(1)} collective-permute-done((bf16[4,24,32,128]{3,2,1,0:T(8,128)(2,1)S(1)}, bf16[4,24,32,128]{3,2,1,0:T(8,128)(2,1)S(1)}, u32[]{:S(2)}, u32[]{:S(2)}) %collective-permute-start.44) | collective-permute-done | bytes 786464 | tf_op jit(solution)/shard_map/ppermute | solution.py:36
  366.2 4.4 %columns_out.2 = (f32[8,32,3072]{2,1,0:T(8,128)}, f32[8,32,1]{2,1,0:T(8,128)S(1)}) custom-call(s32[2]{0:T(128)S(1)} %pad_add_fusion.place_ref.refs_0_, f32[8,32,1]{2,1,0:T(8,128)S(1)} %reshape_broadcast_in_dim.8.gain_ref, bf16[8,32,3072]{2,1,0:T(8,128)(2,1)S(1)} %bitcast.30, bf16[4,24,32,128]{3,2,1,0:T(8,128)(2,1)S(1)} %pad_maximum_fusion.refs_0_, ...), custom_call_target="tpu_custom_call" | custom-call | tf_op jit(solution)/shard_map/columns_out/pallas_call | solution.py:619
  371.4 2.7 slice.222
  376.2 5.8 %columns_out.3 = (f32[8,32,5248]{2,1,0:T(8,128)}, f32[8,32,1]{2,1,0:T(8,128)S(1)}) custom-call(s32[2]{0:T(128)S(1)} %pad_add_fusion.place_ref.refs_0_, f32[8,32,1]{2,1,0:T(8,128)S(1)} %reshape_broadcast_in_dim.9.gain_ref, bf16[8,32,5248]{2,1,0:T(8,128)(2,1)S(1)} %bitcast.27, bf16[8,65,32,128]{3,2,1,0:T(8,128)(2,1)S(1)} %bitcast.29), custom_call_target="tpu_custom_call" | custom-call | tf_op jit(solution)/shard_map/columns_out/pallas_call | solution.py:619
  384.2 2.4 rows_out.3
  (256 shorter events, 88.0 us)
Async XLA Ops:
  7.2 364.2 %all-gather.3.cloned.1.call-start = ((), (), s32[]{:S(2)}) async-start(), calls=%async_computation | async-start | bytes 4792320 | tf_op jit(solution)/shard_map/all_gather | solution.py:926
  27.0 19.3 %collective-permute-start.9 = (bf16[1,256,768]{2,1,0:T(8,128)(2,1)}, bf16[1,256,768]{2,1,0:T(8,128)(2,1)}, u32[]{:S(2)}, u32[]{:S(2)}) collective-permute-start(bf16[1,256,768]{2,1,0:T(8,128)(2,1)} %constant_dynamic-slice_fusion.5), channel_id=1, source_target_pairs={{0,1},{1,0},{2,3},{3,2},{4,5},{5,4},{6,7},{7,6},{8,9},{9,8},{10,11... | collective-permute-start | bytes 1179656 | tf_op jit(solution)/shard_map/ppermute | solution.py:36
  30.2 17.2 %collective-permute-start.8 = (bf16[2,128,768]{2,1,0:T(8,128)(2,1)S(1)}, bf16[2,128,768]{2,1,0:T(8,128)(2,1)}, u32[]{:S(2)}, u32[]{:S(2)}) collective-permute-start(bf16[2,128,768]{2,1,0:T(8,128)(2,1)S(1)} %collective-permute-done.refs_5_), channel_id=1, source_target_pairs={{0,4},{4,0},{8,12},{12,8},{16,20},{20,16},{24,28},{28,24},{1,5},{5... | collective-permute-start | bytes 1179656 | tf_op jit(solution)/shard_map/ppermute | solution.py:36
  39.4 24.8 %collective-permute-start.4 = (bf16[2,128,1536]{2,1,0:T(8,128)(2,1)}, bf16[2,128,1536]{2,1,0:T(8,128)(2,1)}, u32[]{:S(2)}, u32[]{:S(2)}) collective-permute-start(bf16[2,128,1536]{2,1,0:T(8,128)(2,1)} %dynamic-slice_bitcast_fusion), channel_id=1, source_target_pairs={{0,2},{1,3},{2,0},{3,1},{4,6},{5,7},{6,4},{7,5},{8,10},{9,11},{10,... | collective-permute-start | bytes 2359304 | tf_op jit(solution)/shard_map/ppermute | solution.py:36
  45.8 18.4 %collective-permute-start.3 = (bf16[256,1024]{1,0:T(8,128)(2,1)}, bf16[256,1024]{1,0:T(8,128)(2,1)S(1)}, u32[]{:S(2)}, u32[]{:S(2)}) collective-permute-start(bf16[256,1024]{1,0:T(8,128)(2,1)} %collective-permute-done.2.refs_2_), channel_id=1, source_target_pairs={{0,1},{1,0},{2,3},{3,2},{4,5},{5,4},{6,7},{7,6},{8,9},{9,8},{10,11... | collective-permute-start | bytes 1572872 | tf_op jit(solution)/shard_map/ppermute | solution.py:36
  50.5 32.3 %collective-permute-start.17 = (bf16[256,1024]{1,0:T(8,128)(2,1)S(1)}, bf16[256,1024]{1,0:T(8,128)(2,1)S(1)}, u32[]{:S(2)}, u32[]{:S(2)}) collective-permute-start(bf16[256,1024]{1,0:T(8,128)(2,1)S(1)} %copy-done.26), channel_id=1, source_target_pairs={{0,1},{1,0},{2,3},{3,2},{4,5},{5,4},{6,7},{7,6},{8,9},{9,8},{10,11... | collective-permute-start | bytes 1572872 | tf_op jit(solution)/shard_map/ppermute | solution.py:36
  50.9 31.9 %collective-permute-start.21 = (bf16[1,256,1536]{2,1,0:T(8,128)(2,1)S(1)}, bf16[1,256,1536]{2,1,0:T(8,128)(2,1)S(1)}, u32[]{:S(2)}, u32[]{:S(2)}) collective-permute-start(bf16[1,256,1536]{2,1,0:T(8,128)(2,1)S(1)} %constant_dynamic-slice_fusion.2), channel_id=1, source_target_pairs={{0,1},{1,0},{2,3},{3,2},{4,5},{5,4},{6,7},{7,6},{8,9},{9,8},{10,11... | collective-permute-start | bytes 2359304 | tf_op jit(solution)/shard_map/ppermute | solution.py:36
  63.0 17.7 %collective-permute-start.16 = (bf16[128,1024]{1,0:T(8,128)(2,1)S(1)}, bf16[128,1024]{1,0:T(8,128)(2,1)S(1)}, u32[]{:S(2)}, u32[]{:S(2)}) collective-permute-start(bf16[128,1024]{1,0:T(8,128)(2,1)S(1)} %collective-permute-done.15.refs_13_), channel_id=1, source_target_pairs={{0,4},{4,0},{8,12},{12,8},{16,20},{20,16},{24,28},{28,24},{1,5},{5... | collective-permute-start | bytes 786440 | tf_op jit(solution)/shard_map/ppermute | solution.py:36
  64.1 18.1 %collective-permute-start.18 = (bf16[128,1024]{1,0:T(8,128)(2,1)S(1)}, bf16[128,1024]{1,0:T(8,128)(2,1)S(1)}, u32[]{:S(2)}, u32[]{:S(2)}) collective-permute-start(bf16[128,1024]{1,0:T(8,128)(2,1)S(1)} %collective-permute-done.15.refs_13_), channel_id=1, source_target_pairs={{0,1},{1,0},{2,3},{3,2},{4,5},{5,4},{6,7},{7,6},{8,9},{9,8},{10,11... | collective-permute-start | bytes 786440 | tf_op jit(solution)/shard_map/ppermute | solution.py:36
  64.2 42.0 %collective-permute-start.20 = (bf16[2,128,1536]{2,1,0:T(8,128)(2,1)}, bf16[2,128,1536]{2,1,0:T(8,128)(2,1)S(1)}, u32[]{:S(2)}, u32[]{:S(2)}) collective-permute-start(bf16[2,128,1536]{2,1,0:T(8,128)(2,1)} %collective-permute-done.4.refs_19_), channel_id=1, source_target_pairs={{0,8},{4,12},{8,0},{12,4},{16,24},{20,28},{24,16},{28,20},{1,9},{5... | collective-permute-start | bytes 2359304 | tf_op jit(solution)/shard_map/ppermute | solution.py:36
  82.2 23.9 %collective-permute-start.6 = (bf16[256,1024]{1,0:T(8,128)(2,1)S(1)}, bf16[256,1024]{1,0:T(8,128)(2,1)S(1)}, u32[]{:S(2)}, u32[]{:S(2)}) collective-permute-start(bf16[256,1024]{1,0:T(8,128)(2,1)S(1)} %copy-done.17), channel_id=1, source_target_pairs={{0,2},{1,3},{2,0},{3,1},{4,6},{5,7},{6,4},{7,5},{8,10},{9,11},{10,... | collective-permute-start | bytes 1572872 | tf_op jit(solution)/shard_map/ppermute | solution.py:36
  82.8 24.0 %collective-permute-start.12 = (bf16[1024,256]{1,0:T(8,128)(2,1)}, bf16[1024,256]{1,0:T(8,128)(2,1)S(1)}, u32[]{:S(2)}, u32[]{:S(2)}) collective-permute-start(bf16[1024,256]{1,0:T(8,128)(2,1)} %get-tuple-element.62.refs_8_.refs_5_), channel_id=1, source_target_pairs={{0,1},{1,0},{2,3},{3,2},{4,5},{5,4},{6,7},{7,6},{8,9},{9,8},{10,11... | collective-permute-start | bytes 1572872 | tf_op jit(solution)/shard_map/ppermute | solution.py:36
  85.1 21.8 %collective-permute-start.5 = (bf16[256,1024]{1,0:T(8,128)(2,1)S(1)}, bf16[256,1024]{1,0:T(8,128)(2,1)S(1)}, u32[]{:S(2)}, u32[]{:S(2)}) collective-permute-start(bf16[256,1024]{1,0:T(8,128)(2,1)S(1)} %copy-done.17), channel_id=1, source_target_pairs={{0,1},{1,0},{2,3},{3,2},{4,5},{5,4},{6,7},{7,6},{8,9},{9,8},{10,11... | collective-permute-start | bytes 1572872 | tf_op jit(solution)/shard_map/ppermute | solution.py:36
  139.9 34.7 %collective-permute-start.51 = (bf16[4,44,32,128]{3,2,1,0:T(8,128)(2,1)}, bf16[4,44,32,128]{3,2,1,0:T(8,128)(2,1)}, u32[]{:S(2)}, u32[]{:S(2)}) collective-permute-start(bf16[4,44,32,128]{3,2,1,0:T(8,128)(2,1)} %get-tuple-element.102), channel_id=1, source_target_pairs={{0,4},{4,0},{8,12},{12,8},{16,20},{20,16},{24,28},{28,24},{1,5},{5... | collective-permute-start | bytes 4325384 | tf_op jit(solution)/shard_map/ppermute | solution.py:36
  150.2 16.8 %collective-permute-start.57 = (bf16[4,656,128]{2,1,0:T(8,128)(2,1)}, bf16[4,656,128]{2,1,0:T(8,128)(2,1)S(1)}, u32[]{:S(2)}, u32[]{:S(2)}) collective-permute-start(bf16[4,656,128]{2,1,0:T(8,128)(2,1)} %get-tuple-element.105), channel_id=1, source_target_pairs={{0,8},{4,12},{8,0},{12,4},{16,24},{20,28},{24,16},{28,20},{1,9},{5... | collective-permute-start | bytes 2015240 | tf_op jit(solution)/shard_map/ppermute | solution.py:36
  157.8 19.1 %collective-permute-start.31 = (bf16[256,1024]{1,0:T(8,128)(2,1)S(1)}, bf16[256,1024]{1,0:T(8,128)(2,1)S(1)}, u32[]{:S(2)}, u32[]{:S(2)}) collective-permute-start(bf16[256,1024]{1,0:T(8,128)(2,1)S(1)} %get-tuple-element.77.refs_0_), channel_id=1, source_target_pairs={{0,1},{1,0},{2,3},{3,2},{4,5},{5,4},{6,7},{7,6},{8,9},{9,8},{10,11... | collective-permute-start | bytes 1572872 | tf_op jit(solution)/shard_map/ppermute | solution.py:36
  169.4 26.5 %collective-permute-start.58 = (bf16[2,656,128]{2,1,0:T(8,128)(2,1)S(1)}, bf16[2,656,128]{2,1,0:T(8,128)(2,1)S(1)}, u32[]{:S(2)}, u32[]{:S(2)}) collective-permute-start(bf16[2,656,128]{2,1,0:T(8,128)(2,1)S(1)} %get-tuple-element.116), channel_id=1, source_target_pairs={{0,4},{4,0},{8,12},{12,8},{16,20},{20,16},{24,28},{28,24},{1,5},{5... | collective-permute-start | bytes 1007624 | tf_op jit(solution)/shard_map/ppermute | solution.py:36
  193.2 21.2 %collective-permute-start.53 = (bf16[1,44,32,128]{3,2,1,0:T(8,128)(2,1)S(1)}, bf16[1,44,32,128]{3,2,1,0:T(8,128)(2,1)S(1)}, u32[]{:S(2)}, u32[]{:S(2)}) collective-permute-start(bf16[1,44,32,128]{3,2,1,0:T(8,128)(2,1)S(1)} %add_convert_fusion.8), channel_id=1, source_target_pairs={{0,16},{4,20},{8,24},{12,28},{16,0},{20,4},{24,8},{28,12},{1,17},{... | collective-permute-start | bytes 1081352 | tf_op jit(solution)/shard_map/ppermute | solution.py:36
  195.9 24.3 %collective-permute-start.59 = (bf16[1,656,128]{2,1,0:T(8,128)(2,1)S(1)}, bf16[1,656,128]{2,1,0:T(8,128)(2,1)S(1)}, u32[]{:S(2)}, u32[]{:S(2)}) collective-permute-start(bf16[1,656,128]{2,1,0:T(8,128)(2,1)S(1)} %add_convert_fusion.16), channel_id=1, source_target_pairs={{0,16},{4,20},{8,24},{12,28},{16,0},{20,4},{24,8},{28,12},{1,17},{... | collective-permute-start | bytes 503816 | tf_op jit(solution)/shard_map/ppermute | solution.py:36
  229.5 25.6 %collective-permute-start.36 = (bf16[4,24,32,128]{3,2,1,0:T(8,128)(2,1)}, bf16[4,24,32,128]{3,2,1,0:T(8,128)(2,1)}, u32[]{:S(2)}, u32[]{:S(2)}) collective-permute-start(bf16[4,24,32,128]{3,2,1,0:T(8,128)(2,1)} %get-tuple-element.97), channel_id=1, source_target_pairs={{0,4},{4,0},{8,12},{12,8},{16,20},{20,16},{24,28},{28,24},{1,5},{5... | collective-permute-start | bytes 2359304 | tf_op jit(solution)/shard_map/ppermute | solution.py:36
  230.8 20.4 %collective-permute-start.45 = (bf16[4,256,128]{2,1,0:T(8,128)(2,1)}, bf16[4,256,128]{2,1,0:T(8,128)(2,1)}, u32[]{:S(2)}, u32[]{:S(2)}) collective-permute-start(bf16[4,256,128]{2,1,0:T(8,128)(2,1)} %get-tuple-element.101), channel_id=1, source_target_pairs={{0,8},{4,12},{8,0},{12,4},{16,24},{20,28},{24,16},{28,20},{1,9},{5... | collective-permute-start | bytes 786440 | tf_op jit(solution)/shard_map/ppermute | solution.py:36
  231.4 98.3 %collective-permute-start.28 = (bf16[256,1024]{1,0:T(8,128)(2,1)}, bf16[256,1024]{1,0:T(8,128)(2,1)S(1)}, u32[]{:S(2)}, u32[]{:S(2)}) collective-permute-start(bf16[256,1024]{1,0:T(8,128)(2,1)} %copy-done.21), channel_id=1, source_target_pairs={{0,1},{1,0},{2,3},{3,2},{4,5},{5,4},{6,7},{7,6},{8,9},{9,8},{10,11... | collective-permute-start | bytes 1572872 | tf_op jit(solution)/shard_map/ppermute | solution.py:36
  231.4 26.1 %collective-permute-start.29 = (bf16[256,1024]{1,0:T(8,128)(2,1)}, bf16[256,1024]{1,0:T(8,128)(2,1)S(1)}, u32[]{:S(2)}, u32[]{:S(2)}) collective-permute-start(bf16[256,1024]{1,0:T(8,128)(2,1)} %get-tuple-element.84), channel_id=1, source_target_pairs={{0,1},{1,0},{2,3},{3,2},{4,5},{5,4},{6,7},{7,6},{8,9},{9,8},{10,11... | collective-permute-start | bytes 1572872 | tf_op jit(solution)/shard_map/ppermute | solution.py:36
  236.6 80.9 %collective-permute-start.34 = (bf16[256,1024]{1,0:T(8,128)(2,1)}, bf16[256,1024]{1,0:T(8,128)(2,1)S(1)}, u32[]{:S(2)}, u32[]{:S(2)}) collective-permute-start(bf16[256,1024]{1,0:T(8,128)(2,1)} %get-tuple-element.96), channel_id=1, source_target_pairs={{0,1},{1,0},{2,3},{3,2},{4,5},{5,4},{6,7},{7,6},{8,9},{9,8},{10,11... | collective-permute-start | bytes 1572872 | tf_op jit(solution)/shard_map/ppermute | solution.py:36
  251.2 98.4 %collective-permute-start.33 = (bf16[256,1024]{1,0:T(8,128)(2,1)S(1)}, bf16[256,1024]{1,0:T(8,128)(2,1)S(1)}, u32[]{:S(2)}, u32[]{:S(2)}) collective-permute-start(bf16[256,1024]{1,0:T(8,128)(2,1)S(1)} %get-tuple-element.94), channel_id=1, source_target_pairs={{0,1},{1,0},{2,3},{3,2},{4,5},{5,4},{6,7},{7,6},{8,9},{9,8},{10,11... | collective-permute-start | bytes 1572872 | tf_op jit(solution)/shard_map/ppermute | solution.py:36
  257.6 29.1 %collective-permute-start.37 = (bf16[2,24,32,128]{3,2,1,0:T(8,128)(2,1)S(1)}, bf16[2,24,32,128]{3,2,1,0:T(8,128)(2,1)S(1)}, u32[]{:S(2)}, u32[]{:S(2)}) collective-permute-start(bf16[2,24,32,128]{3,2,1,0:T(8,128)(2,1)S(1)} %get-tuple-element.115), channel_id=1, source_target_pairs={{0,8},{4,12},{8,0},{12,4},{16,24},{20,28},{24,16},{28,20},{1,9},{5... | collective-permute-start | bytes 1179656 | tf_op jit(solution)/shard_map/ppermute | solution.py:36
  260.1 27.4 %collective-permute-start.47 = (bf16[1,256,128]{2,1,0:T(8,128)(2,1)S(1)}, bf16[1,256,128]{2,1,0:T(8,128)(2,1)S(1)}, u32[]{:S(2)}, u32[]{:S(2)}) collective-permute-start(bf16[1,256,128]{2,1,0:T(8,128)(2,1)S(1)} %add_convert_fusion.21), channel_id=1, source_target_pairs={{0,16},{4,20},{8,24},{12,28},{16,0},{20,4},{24,8},{28,12},{1,17},{... | collective-permute-start | bytes 196616 | tf_op jit(solution)/shard_map/ppermute | solution.py:36
  286.8 23.1 %collective-permute-start.38 = (bf16[1,24,32,128]{3,2,1,0:T(8,128)(2,1)S(1)}, bf16[1,24,32,128]{3,2,1,0:T(8,128)(2,1)S(1)}, u32[]{:S(2)}, u32[]{:S(2)}) collective-permute-start(bf16[1,24,32,128]{3,2,1,0:T(8,128)(2,1)S(1)} %add_convert_fusion.13), channel_id=1, source_target_pairs={{0,16},{4,20},{8,24},{12,28},{16,0},{20,4},{24,8},{28,12},{1,17},{... | collective-permute-start | bytes 589832 | tf_op jit(solution)/shard_map/ppermute | solution.py:36
  287.5 27.2 %collective-permute-start.48 = (bf16[1,256,128]{2,1,0:T(8,128)(2,1)S(1)}, bf16[1,256,128]{2,1,0:T(8,128)(2,1)S(1)}, u32[]{:S(2)}, u32[]{:S(2)}) collective-permute-start(bf16[1,256,128]{2,1,0:T(8,128)(2,1)S(1)} %add_convert_fusion.20), channel_id=1, source_target_pairs={{0,16},{4,20},{8,24},{12,28},{16,0},{20,4},{24,8},{28,12},{1,17},{... | collective-permute-start | bytes 196616 | tf_op jit(solution)/shard_map/ppermute | solution.py:36
  328.6 21.0 %collective-permute-start.35 = (bf16[256,1024]{1,0:T(8,128)(2,1)S(1)}, bf16[256,1024]{1,0:T(8,128)(2,1)S(1)}, u32[]{:S(2)}, u32[]{:S(2)}) collective-permute-start(bf16[256,1024]{1,0:T(8,128)(2,1)S(1)} %add_convert_fusion.2), channel_id=1, source_target_pairs={{0,2},{1,3},{2,0},{3,1},{4,6},{5,7},{6,4},{7,5},{8,10},{9,11},{10,... | collective-permute-start | bytes 1572872 | tf_op jit(solution)/shard_map/ppermute | solution.py:36
  329.6 18.1 %collective-permute-start.43 = (bf16[2,24,32,128]{3,2,1,0:T(8,128)(2,1)S(1)}, bf16[2,24,32,128]{3,2,1,0:T(8,128)(2,1)S(1)}, u32[]{:S(2)}, u32[]{:S(2)}) collective-permute-start(bf16[2,24,32,128]{3,2,1,0:T(8,128)(2,1)S(1)} %pad_maximum_fusion.2), channel_id=1, source_target_pairs={{0,8},{4,12},{8,0},{12,4},{16,24},{20,28},{24,16},{28,20},{1,9},{5... | collective-permute-start | bytes 1179656 | tf_op jit(solution)/shard_map/ppermute | solution.py:36
  347.8 18.4 %collective-permute-start.44 = (bf16[4,24,32,128]{3,2,1,0:T(8,128)(2,1)S(1)}, bf16[4,24,32,128]{3,2,1,0:T(8,128)(2,1)S(1)}, u32[]{:S(2)}, u32[]{:S(2)}) collective-permute-start(bf16[4,24,32,128]{3,2,1,0:T(8,128)(2,1)S(1)} %pad_maximum_fusion.refs_0_), channel_id=1, source_target_pairs={{0,4},{4,0},{8,12},{12,8},{16,20},{20,16},{24,28},{28,24},{1,5},{5... | collective-permute-start | bytes 2359304 | tf_op jit(solution)/shard_map/ppermute | solution.py:36
  (71 other events, 623.4 us)
Sparse Core Ops, SparseCore 0:
  222.5 90.4 all-gather.2
where the time goes:
time: 400 us; the launch traced here: 394 us
  waiting for transfers between devices  201 us (50%)
  Pallas kernels  92 us (23%)
  starting transfers between devices  43.2 us (11%)
  local copies, waits for them, and re-layouts  25.9 us (6%)
  other arithmetic  16.8 us (4%)
  between operations  15.3 us (4%)
    ppermute x60, waiting for transfers between devices, swap(): return lax.ppermute(x, axis, [(i, i ^ 1 << bit) for i in range(size)])  201 us
    ppermute x60, starting transfers between devices, swap(): return lax.ppermute(x, axis, [(i, i ^ 1 << bit) for i in range(size)])  43.2 us
    pallas_call x1, Pallas kernels, shards(): pl.pallas_call(functools.partial(feed_forward_kernel, about(out_pieces),...  22 us
    pallas_call x1, Pallas kernels, shards(): pl.pallas_call(functools.partial(attention_back_kernel, n, heads, far), i...  14.5 us
    pallas_call x1, Pallas kernels, shards(): pl.pallas_call(functools.partial(attention_kernel, about(qkv_pieces), 0,...  13.9 us
    unnamed x84, local copies, waits for them, and re-layouts  10.3 us
    pallas_call x2, Pallas kernels, columns_out(): pl.pallas_call(functools.partial(columns_out_kernel, n, ff, head_cols, wi...  10.2 us
  transfers between devices with their start and end apart: 61, of which 27 were waited for; matrix products, arithmetic and copies ran while one was open for 7% of the time, Pallas kernels for 16%

commit v1 on v0

--- a/solution.py
+++ b/solution.py
@@ -58,22 +58,36 @@
     return scatter_bits(enumerate(blocks), axis, range(bits_of(axis)))[0]
 
 
-def half_by_replica(x, dim, bit):
+def parity():
+    return bit_of("rep", 0) ^ bit_of("rep", 1)
+
+
+def half_by_replica(x, dim):
     shape = x.shape
     x = x.reshape(shape[:dim] + (2, shape[dim] // 2) + shape[dim + 1 :])
-    return lax.dynamic_index_in_dim(x, bit_of("rep", bit), dim, keepdims=False)
-
-
-def gather_weight(x, rep_bit):
+    return lax.dynamic_index_in_dim(x, parity(), dim, keepdims=False)
+
+
+def fetch_far(send, dim, top, gate):
+    got = swap(half_by_replica(send, dim), "shard", top)
+    kept = got if gate is None else after(got, gate())
+    first, second = jnp.split(kept, 2, axis=dim)
+    return [
+        (1 << top, 0, got),
+        (1 << top, 1, swap(first, "rep", 0)),
+        (1 << top, 2, swap(second, "rep", 1)),
+    ]
+
+
+def gather_weight(x, gate=None):
     top = bits_of("shard") - 1
-    got = swap(half_by_replica(x, 0, rep_bit), "shard", top)
-    pieces = [(0, None, x), (1 << top, 0, got), (1 << top, 1, swap(got, "rep", rep_bit))]
+    pieces = [(0, None, x)] + fetch_far(x, 0, top, gate)
     for bit in reversed(range(top)):
         pieces += [(j | 1 << bit, h, swap(a, "shard", bit)) for j, h, a in pieces]
     return pieces
 
 
-def split_weight(x, rep_bit):
+def split_weight(x, gate=None):
     me = lax.axis_index("shard")
     top = bits_of("shard") - 1
 
@@ -81,8 +95,7 @@
         start = ((me & (a.shape[0] - 1)) >> bit ^ 1) << bit
         return lax.dynamic_slice_in_dim(a, start, 1 << bit)
 
-    got = swap(half_by_replica(part_for(x, top), 1, rep_bit), "shard", top)
-    pieces = [(0, None, x), (1 << top, 0, got), (1 << top, 1, swap(got, "rep", rep_bit))]
+    pieces = [(0, None, x)] + fetch_far(part_for(x, top), 1, top, gate)
     for bit in reversed(range(top)):
         pieces += [(j | 1 << bit, h, swap(part_for(a, bit), "shard", bit)) for j, h, a in pieces]
     return pieces
@@ -140,14 +153,16 @@
     return centred * scale, scale
 
 
-def weight_copies(pieces, refs, target, me, sems, rep, rep_bit, by_owner, rows):
+def weight_copies(pieces, refs, target, me, sems, rep, by_owner, rows):
     copies = []
     for i, ((j, half, shape), ref) in enumerate(zip(pieces, refs)):
         start = (me ^ j if by_owner else j) * rows
         count = rows
         if half is not None:
-            count = rows // 2
-            start = start + (((rep >> rep_bit) & 1) ^ half) * count
+            own = (rep ^ (rep >> 1)) & 1
+            count = rows // 2 if half == 0 else rows // 4
+            start = start + (own if half == 0 else 1 - own) * (rows // 2)
+            start = start + (rows // 4 if half == 2 else 0)
         source = ref.at[me & (shape[0] - 1)] if len(shape) == 3 else ref
         place = target.at[pl.ds(pl.multiple_of(start, count), count), :]
         copies.append(pltpu.make_async_copy(source, place, sems.at[i]))
@@ -260,7 +275,7 @@
 
 
 def attention_kernel(
-    pieces, rep_bit, n, heads, place_ref, cos_ref, sin_ref, idq_ref, idk_ref, *refs
+    pieces, n, heads, place_ref, cos_ref, sin_ref, idq_ref, idk_ref, *refs
 ):
     tok_refs, refs = refs[:n], refs[n:]
     piece_refs, refs = refs[: len(pieces)], refs[len(pieces) :]
@@ -269,7 +284,7 @@
     rows = seq // n
     me, rep = place_ref[0], place_ref[1]
     copies = weight_copies(
-        pieces, piece_refs, w_ref, me, sems, rep, rep_bit, True, w_ref.shape[0] // n
+        pieces, piece_refs, w_ref, me, sems, rep, True, w_ref.shape[0] // n
     )
     for c in copies:
         c.start()
@@ -307,33 +322,23 @@
     lax.fori_loop(0, seq // QB, attend, 0)
 
 
-def feed_forward_kernel(out_pieces, in_pieces, out_bit, in_bit, n, place_ref, *refs):
+def up_kernel(out_pieces, in_pieces, n, place_ref, *refs):
     tok_refs, refs = refs[:n], refs[n:]
-    cot_refs, refs = refs[:n], refs[n:]
     att_refs, refs = refs[:n], refs[n:]
     out_refs, refs = refs[: len(out_pieces)], refs[len(out_pieces) :]
     in_refs, refs = refs[: len(in_pieces)], refs[len(in_pieces) :]
-    down_ref, hidden_out, normed_out, act_out, dup_out, *refs = refs
-    dnormed_outs, refs = refs[:n], refs[n:]
-    tok, cot, att, w_out, w_in, w_down, hidden_own, normed, act, dup, dnormed = refs[:11]
-    out_sems, in_sems, att_sems, tok_sems, cot_sems, down_sem, sems = refs[11:]
+    hidden_out, normed_out, up_out, in_out, *refs = refs
+    tok, att, w_out, w_in, hidden_own, normed, up, *refs = refs
+    out_sems, in_sems, att_sems, tok_sems, sems = refs
     me, rep = place_ref[0], place_ref[1]
     rows, model = tok_refs[0].shape
-    padded = w_down.shape[0]
-    given = down_ref.shape[0]
-    if given != padded:
-        w_down[given:padded, :] = jnp.zeros((padded - given, model), BF16)
-    down_copy = pltpu.make_async_copy(down_ref, w_down.at[0:given, :], down_sem)
     copy = pltpu.make_async_copy
     att_copies = [copy(att_refs[j], att.at[j], att_sems.at[j]) for j in range(n)]
     tok_copies = [copy(tok_refs[j], tok.at[j], tok_sems.at[j]) for j in range(n)]
-    cot_copies = [copy(cot_refs[j], cot.at[j], cot_sems.at[j]) for j in range(n)]
     part = model // n
-    out_copies = weight_copies(out_pieces, out_refs, w_out, me, out_sems, rep, out_bit, False, part)
-    in_copies = weight_copies(in_pieces, in_refs, w_in, me, in_sems, rep, in_bit, True, part)
-    for c in att_copies + tok_copies[:1] + out_copies + in_copies + [down_copy]:
-        c.start()
-    for c in cot_copies[:1] + tok_copies[1:] + cot_copies[1:]:
+    out_copies = weight_copies(out_pieces, out_refs, w_out, me, out_sems, rep, False, part)
+    in_copies = weight_copies(in_pieces, in_refs, w_in, me, in_sems, rep, True, part)
+    for c in att_copies + tok_copies[:1] + out_copies + in_copies + tok_copies[1:]:
         c.start()
     for c in att_copies + out_copies:
         c.wait()
@@ -349,34 +354,74 @@
             )
         if j == 0:
             hidden_own[...] = hidden
+            sent.append(copy(hidden_own, hidden_out, sems.at[2 * n]))
+            sent[-1].start()
         hat, _ = normalise(hidden)
         low = hat.astype(BF16)
         normed[here, :] = low
         if j == 0:
-            for c in in_copies + [down_copy]:
+            for c in in_copies:
                 c.wait()
-        up = jnp.dot(low, w_in[...], preferred_element_type=F32)
-        gate, lin = up[:, :padded], up[:, padded:]
+            sent.append(copy(w_in, in_out, sems.at[2 * n + 1]))
+            sent[-1].start()
+        up[here, :] = jnp.dot(low, w_in[...], preferred_element_type=F32)
+        sent += [
+            copy(normed.at[here, :], normed_out.at[here, :], sems.at[2 * j]),
+            copy(up.at[here, :], up_out.at[here, :], sems.at[2 * j + 1]),
+        ]
+        for c in sent[-2:]:
+            c.start()
+    for c in sent:
+        c.wait()
+
+
+def dup_kernel(n, up_ref, w_in_ref, down_ref, *refs):
+    cot_refs, refs = refs[:n], refs[n:]
+    act_out, dup_out, *refs = refs
+    dnormed_outs, refs = refs[:n], refs[n:]
+    up, cot, w_in, w_down, act, dup, dnormed, in_sem, down_sem, up_sems, cot_sems, sems = refs
+    rows, model = cot_refs[0].shape
+    padded = w_down.shape[0]
+    given = down_ref.shape[0]
+    if given != padded:
+        w_down[given:padded, :] = jnp.zeros((padded - given, model), BF16)
+    copy = pltpu.make_async_copy
+    down_copy = copy(down_ref, w_down.at[0:given, :], down_sem)
+    in_copy = copy(w_in_ref, w_in, in_sem)
+    cot_copies = [copy(cot_refs[j], cot.at[j], cot_sems.at[j]) for j in range(n)]
+    up_copies = []
+    for j in range(n):
+        here = slice(j * rows, (j + 1) * rows)
+        up_copies.append(copy(up_ref.at[here, :], up.at[here, :], up_sems.at[j]))
+    for c in [up_copies[0], cot_copies[0], down_copy, in_copy]:
+        c.start()
+    for c in up_copies[1:] + cot_copies[1:]:
+        c.start()
+    sent = []
+    for j in range(n):
+        here = slice(j * rows, (j + 1) * rows)
+        up_copies[j].wait()
+        gate, lin = up[here, :padded], up[here, padded:]
         phi = 0.5 + 0.5 * lax.erf(gate * (1.0 / math.sqrt(2.0)))
         gelu = gate * phi
         slope = phi + gate * jnp.exp(gate * gate * -0.5) * (1.0 / math.sqrt(2.0 * math.pi))
-        act_low = (gelu * lin).astype(BF16)
-        act[here, :] = act_low
+        act[here, :] = (gelu * lin).astype(BF16)
         cot_copies[j].wait()
+        if j == 0:
+            down_copy.wait()
         dact = dot(cot[j], w_down[...], ((1,), (1,)))
         dup[here, :padded] = (dact * lin * slope).astype(BF16)
         dup[here, padded:] = (dact * gelu).astype(BF16)
+        if j == 0:
+            in_copy.wait()
         dnormed[j] = dot(dup[here, :], w_in[...], ((1,), (1,))).astype(BF16)
         sent += [
-            copy(dnormed.at[j], dnormed_outs[j], sems.at[4 * j]),
-            copy(normed.at[here, :], normed_out.at[here, :], sems.at[4 * j + 1]),
-            copy(act.at[here, :], act_out.at[here, :], sems.at[4 * j + 2]),
-            copy(dup.at[here, :], dup_out.at[here, :], sems.at[4 * j + 3]),
+            copy(dnormed.at[j], dnormed_outs[j], sems.at[3 * j]),
+            copy(act.at[here, :], act_out.at[here, :], sems.at[3 * j + 1]),
+            copy(dup.at[here, :], dup_out.at[here, :], sems.at[3 * j + 2]),
         ]
-        for c in sent[-4:]:
+        for c in sent[-3:]:
             c.start()
-    sent.append(copy(hidden_own, hidden_out, sems.at[4 * n]))
-    sent[-1].start()
     for c in sent:
         c.wait()
 
@@ -415,30 +460,33 @@
         mlp_refs[j][...] = jnp.dot(low, w_down[...], preferred_element_type=F32).astype(BF16)
 
 
-def in_kernel(n, ff, near, place_ref, normed, dup, keep, send, in_sum):
+def in_kernel(n, ff, counts, orders, place_ref, normed, dup, *refs):
+    flows, in_sum = refs[:-1], refs[-1]
     me, rep = place_ref[0], place_ref[1]
     part = normed.shape[1] // n
     padded = dup.shape[1] // 2
-    chunk = keep.shape[2]
-    tiles = up_tiles(ff)
     whole, rest = ff // LANES, ff % LANES
+    starts = [t * LANES for t in range(whole)] + [padded + t * LANES for t in range(whole)]
+    starts.append(2 * padded)
     for owner in range(n):
         block = dot(normed[:, owner * part : (owner + 1) * part], dup[...], ((0,), (0,)))
         in_sum[:, : 2 * padded] = block
         first = block[:, whole * LANES : (whole + 1) * LANES]
         second = block[:, padded + whole * LANES : padded + (whole + 1) * LANES]
         lane = lax.broadcasted_iota(jnp.int32, first.shape, 1)
-        both = jnp.where(lane < rest, first, pltpu.roll(second, rest, 1))
-        in_sum[:, 2 * padded :] = both
-        base = (me ^ owner) * tiles
-        starts = [t * LANES for t in range(whole)] + [padded + t * LANES for t in range(whole)]
-        starts.append(2 * padded)
-
-        def write(target, slot, c):
-            for t, s in enumerate(starts):
-                target[slot, base + t] = row_chunk(in_sum, c, chunk, s).astype(BF16)
-
-        store_slots(keep, send, rep, near, write)
+        in_sum[:, 2 * padded :] = jnp.where(lane < rest, first, pltpu.roll(second, rest, 1))
+        begin = 0
+        for f, (count, order) in enumerate(zip(counts, orders)):
+            keep, send = flows[2 * f], flows[2 * f + 1]
+            chunk = keep.shape[2]
+
+            def write(target, slot, c):
+                for t in range(count):
+                    value = row_chunk(in_sum, c, chunk, starts[begin + t])
+                    target[slot, (me ^ owner) * count + t] = value.astype(BF16)
+
+            store_slots(keep, send, rep, order, write)
+            begin += count
 
 
 def add_kernel(a_ref, b_ref, c_ref, d_ref, mine_ref, other_ref):
@@ -557,31 +605,25 @@
         canvas[index] = tile if index not in canvas else canvas[index] + tile
 
 
-def columns_out_kernel(
-    n, ff, head_cols, width, order, count, place_ref, gain_ref, w_ref, *refs
-):
+def columns_out_kernel(n, ff, head_cols, width, counts, orders, place_ref, gain_ref, w_ref, *refs):
     me, rep = place_ref[0], place_ref[1]
     *parts, out_ref, ln_ref = refs
-    tiles = count // n
-    if len(parts) == 1:
-
-        def read(index):
-            return parts[0][index]
-
-    else:
-        half = parts[0].shape[0]
-        slot = slot_of(rep ^ pl.program_id(0), order)
+    half = parts[0].shape[0]
+    slots = [slot_of(rep ^ pl.program_id(0), order) for order in orders]
+
+    def read(owner, t):
+        f = 0
+        while t >= counts[f]:
+            t -= counts[f]
+            f += 1
+        slot, index = slots[f], (me ^ owner) * counts[f] + t
         at = slot & (half - 1)
-
-        def read(index):
-            return jnp.where(slot < half, parts[0][at, index], parts[1][at, index])
+        now, got = parts[2 * f][at, index], parts[2 * f + 1][at, index]
+        return jnp.where(slot < half, now, got).astype(F32)
 
     canvas = {}
     for owner in range(n):
-        base = (me ^ owner) * tiles
-
-        def tile(t):
-            return read(base + t).astype(F32)
+        tile = functools.partial(read, owner)
 
         if ff:
             whole, rest = ff // LANES, ff % LANES
@@ -606,18 +648,14 @@
     ln_ref[...] = jnp.sum(total, axis=1, keepdims=True)
 
 
-def columns_out(place, parts, weight, gain, n, tiles, order, ff=0, head_cols=0, width=0):
-    now, got = parts
-    chunk = now.shape[2]
+def columns_out(place, pairs, counts, orders, weight, gain, n, ff=0, head_cols=0, width=0):
+    parts = [a for pair in pairs for a in pair]
+    chunk = parts[0].shape[2]
     part, cols = weight.shape
     count = part // chunk
-    if got is None:
-        parts = [now]
-        part_specs = [pl.BlockSpec((None, tiles, chunk, LANES), lambda i: (i, 0, 0, 0))]
-    else:
-        part_specs = [pl.BlockSpec(now.shape, lambda i: (0, 0, 0, 0))] * 2
+    part_specs = [pl.BlockSpec(a.shape, lambda i: (0, 0, 0, 0)) for a in parts]
     total, ln = pl.pallas_call(
-        functools.partial(columns_out_kernel, n, ff, head_cols, width, order, tiles),
+        functools.partial(columns_out_kernel, n, ff, head_cols, width, counts, orders),
         grid=(count,),
         in_specs=[
             pl.BlockSpec(memory_space=pltpu.SMEM),
@@ -732,15 +770,9 @@
     gain2 = ln2_gain.astype(F32)[:, None]
     qkv_to = split_columns(w_qkv, gain1, n, 3, head_cols, width)
     in_to = split_columns(w_in, gain2, n, 2, ff, padded)
-    qkv_pieces = split_weight(qkv_to, 0)
-
-    def fetched(pieces):
-        return [a for j, h, a in pieces if j == n // 2 and h == 0]
-
-    toks = gather_list(after(tokens, *fetched(qkv_pieces)), "shard")
-    out_pieces = gather_weight(after(w_out, toks[n // 2]), 0)
-    in_pieces = split_weight(after(in_to, toks[n // 2]), 1)
-    cots = gather_list(after(cotangent, *fetched(in_pieces)), "shard")
+    qkv_pieces = split_weight(qkv_to)
+
+    toks = gather_list(tokens, "shard")
 
     lane = jnp.arange(width, dtype=jnp.int32) % HEAD_DIM
     half = HEAD_DIM // 2
@@ -759,7 +791,7 @@
         return [(j, h, a.shape) for j, h, a in pieces]
 
     queries, keys, values, attended, normed1, qkv_w = pl.pallas_call(
-        functools.partial(attention_kernel, about(qkv_pieces), 0, n, heads),
+        functools.partial(attention_kernel, about(qkv_pieces), n, heads),
         in_specs=[SMEM_SPEC] + [VMEM_SPEC] * (4 + n) + [ANY_SPEC] * len(qkv_pieces),
         out_shape=(
             shape((seq, width), BF16),
@@ -775,77 +807,83 @@
         name="attention",
     )(place, *tables, *toks, *[a for _, _, a in qkv_pieces])
 
+    def once_attended():
+        return attended
+
+    far_done = [toks[n // 2], qkv_pieces[1][2]]
+    out_pieces = gather_weight(after(w_out, *far_done), once_attended)
+    in_pieces = split_weight(after(in_to, *far_done), once_attended)
     atts = gather_list(attended[:, :head_cols], "shard")
+    cots = gather_list(after(cotangent, atts[n // 2]), "shard")
     blocks = [shape((rows, model), BF16)] * n
-    hidden, normed2, act, dup, *dnormed2_blocks = pl.pallas_call(
-        functools.partial(
-            feed_forward_kernel, about(out_pieces), about(in_pieces), 0, 1, n
-        ),
-        in_specs=[SMEM_SPEC]
-        + [ANY_SPEC] * (3 * n + len(out_pieces) + len(in_pieces) + 1),
-        out_specs=[ANY_SPEC] * (4 + n),
+    hidden, normed2, up, in_w = pl.pallas_call(
+        functools.partial(up_kernel, about(out_pieces), about(in_pieces), n),
+        in_specs=[SMEM_SPEC] + [ANY_SPEC] * (2 * n + len(out_pieces) + len(in_pieces)),
+        out_specs=[ANY_SPEC] * 4,
         out_shape=[
             shape((rows, model), F32),
             shape((seq, model), BF16),
-            shape((seq, padded), BF16),
-            shape((seq, 2 * padded), BF16),
-        ]
-        + blocks,
+            shape((seq, 2 * padded), F32),
+            shape((model, 2 * padded), BF16),
+        ],
         scratch_shapes=[
-            pltpu.VMEM((n, rows, model), BF16),
             pltpu.VMEM((n, rows, model), BF16),
             pltpu.VMEM((n, seq, head_cols), BF16),
             pltpu.VMEM((model, model), BF16),
             pltpu.VMEM((model, 2 * padded), BF16),
-            pltpu.VMEM((padded, model), BF16),
             pltpu.VMEM((rows, model), F32),
             pltpu.VMEM((seq, model), BF16),
-            pltpu.VMEM((seq, padded), BF16),
-            pltpu.VMEM((seq, 2 * padded), BF16),
-            pltpu.VMEM((n, rows, model), BF16),
+            pltpu.VMEM((seq, 2 * padded), F32),
             pltpu.SemaphoreType.DMA((len(out_pieces),)),
             pltpu.SemaphoreType.DMA((len(in_pieces),)),
             pltpu.SemaphoreType.DMA((n,)),
             pltpu.SemaphoreType.DMA((n,)),
-            pltpu.SemaphoreType.DMA((n,)),
-            pltpu.SemaphoreType.DMA,
-            pltpu.SemaphoreType.DMA((4 * n + 1,)),
+            pltpu.SemaphoreType.DMA((2 * n + 2,)),
         ],
         compiler_params=params,
-        cost_estimate=work(26 * seq * model * padded),
-        name="feed_forward",
-    )(
-        place,
-        *toks,
-        *cots,
-        *atts,
-        *[a for _, _, a in out_pieces],
-        *[a for _, _, a in in_pieces],
-        jnp.pad(w_down, ((0, -ff % 16), (0, 0))),
-    )
+        cost_estimate=work(12 * seq * model * padded),
+        name="up_projection",
+    )(place, *toks, *atts, *[a for _, _, a in out_pieces], *[a for _, _, a in in_pieces])
+    down_w = jnp.pad(w_down, ((0, -ff % 16), (0, 0)))
+    act, dup, *dnormed2_blocks = pl.pallas_call(
+        functools.partial(dup_kernel, n),
+        in_specs=[ANY_SPEC] * (3 + n),
+        out_specs=[ANY_SPEC] * (2 + n),
+        out_shape=[shape((seq, padded), BF16), shape((seq, 2 * padded), BF16)] + blocks,
+        scratch_shapes=[
+            pltpu.VMEM((seq, 2 * padded), F32),
+            pltpu.VMEM((n, rows, model), BF16),
+            pltpu.VMEM((model, 2 * padded), BF16),
+            pltpu.VMEM((padded, model), BF16),
+            pltpu.VMEM((seq, padded), BF16),
+            pltpu.VMEM((seq, 2 * padded), BF16),
+            pltpu.VMEM((n, rows, model), BF16),
+            pltpu.SemaphoreType.DMA,
+            pltpu.SemaphoreType.DMA,
+            pltpu.SemaphoreType.DMA((n,)),
+            pltpu.SemaphoreType.DMA((n,)),
+            pltpu.SemaphoreType.DMA((3 * n,)),
+        ],
+        compiler_params=params,
+        cost_estimate=work(14 * seq * model * padded),
+        name="dup",
+    )(up, in_w, down_w, *cots)
+
     slots = replicas // 2
     chunk = part // replicas
     lanes = max(LANES, model // replicas)
     tiles = up_tiles(ff)
-    in_shape = shape((slots, n * tiles, chunk, LANES), BF16)
+    in_counts = [tiles - tiles // 2, tiles // 2]
+    orders = [near, far]
+    in_shapes = [shape((slots, n * c, chunk, LANES), BF16) for c in in_counts for _ in range(2)]
     down_shape = shape((slots, ff, lanes), BF16)
-
-    in_keep, in_send = pl.pallas_call(
-        functools.partial(in_kernel, n, ff, near),
-        in_specs=[SMEM_SPEC] + [VMEM_SPEC] * 2,
-        out_shape=[in_shape, in_shape],
-        scratch_shapes=[pltpu.VMEM((part, 2 * padded + LANES), F32)],
-        compiler_params=params,
-        cost_estimate=work(8 * seq * model * padded),
-        name="in_gradient",
-    )(place, normed2, dup)
 
     top = bits_of("shard") - 1
     sums = scatter_bits(enumerate(dnormed2_blocks), "shard", range(top - 1))
     low, high = 1 << (top - 1), 1 << top
     mine, other = pl.pallas_call(
-        ordered(add_kernel, 4, 1),
-        in_specs=[VMEM_SPEC] * 4 + [ANY_SPEC],
+        add_kernel,
+        in_specs=[VMEM_SPEC] * 4,
         out_shape=[shape((rows, model), F32), shape((rows, model), BF16)],
         compiler_params=pltpu.CompilerParams(vmem_limit_bytes=16 << 20),
         name="near_sum",
@@ -854,30 +892,38 @@
         swap(sums[low].astype(BF16), "shard", top - 1),
         sums[high],
         swap(sums[low | high].astype(BF16), "shard", top - 1),
-        in_keep,
     )
+    in_flows = pl.pallas_call(
+        ordered(functools.partial(in_kernel, n, ff, in_counts, orders), 3, 1),
+        in_specs=[SMEM_SPEC] + [VMEM_SPEC] * 2 + [ANY_SPEC],
+        out_shape=in_shapes,
+        scratch_shapes=[pltpu.VMEM((part, 2 * padded + LANES), F32)],
+        compiler_params=params,
+        cost_estimate=work(8 * seq * model * padded),
+        name="in_gradient",
+    )(place, normed2, dup, other)
+    dhidden, dproj = pl.pallas_call(
+        ordered(norm_back_kernel, 4, 1),
+        in_specs=[VMEM_SPEC] * 4 + [ANY_SPEC],
+        out_shape=[shape((rows, model), F32), shape((rows, model), BF16)],
+        compiler_params=pltpu.CompilerParams(vmem_limit_bytes=24 << 20),
+        name="norm_back",
+    )(mine, swap(other, "shard", top), hidden, cotangent, in_flows[0])
     down_keep, down_send, *mlp_blocks = pl.pallas_call(
-        ordered(functools.partial(down_kernel, n, ff, far), 3 + n, 1),
+        ordered(functools.partial(down_kernel, n, ff, near), 3 + n, 1),
         in_specs=[SMEM_SPEC] + [VMEM_SPEC] * (2 + n) + [ANY_SPEC],
         out_shape=[down_shape, down_shape] + blocks,
         scratch_shapes=[pltpu.VMEM((padded, model), F32)],
         compiler_params=params,
         cost_estimate=work(8 * seq * model * padded),
         name="down_gradient",
-    )(place, act, jnp.pad(w_down, ((0, -ff % 16), (0, 0))), *cots, other)
-    dhidden, dproj = pl.pallas_call(
-        ordered(norm_back_kernel, 4, 1),
-        in_specs=[VMEM_SPEC] * 4 + [ANY_SPEC],
-        out_shape=[shape((rows, model), F32), shape((rows, model), BF16)],
-        compiler_params=pltpu.CompilerParams(vmem_limit_bytes=24 << 20),
-        name="norm_back",
-    )(mine, swap(other, "shard", top), hidden, cotangent, down_keep)
+    )(place, act, down_w, *cots, dproj)
     dprojs = gather_list(dproj, "shard")
 
     out_shape = shape((slots, part, lanes), BF16)
     dqkv, out_keep, out_send = pl.pallas_call(
-        functools.partial(attention_back_kernel, n, heads, far),
-        in_specs=[SMEM_SPEC] + [VMEM_SPEC] * (n + 9),
+        ordered(functools.partial(attention_back_kernel, n, heads, near), n + 10, 1),
+        in_specs=[SMEM_SPEC] + [VMEM_SPEC] * (n + 9) + [ANY_SPEC],
         out_shape=[shape((seq, 3 * width), BF16), out_shape, out_shape],
         scratch_shapes=[
             pltpu.VMEM((seq, width), BF16),
@@ -888,7 +934,7 @@
         compiler_params=params,
         cost_estimate=work(40 * seq * model * width),
         name="attention_back",
-    )(place, *dprojs, w_out, attended, queries, keys, values, *tables)
+    )(place, *dprojs, w_out, attended, queries, keys, values, *tables, down_keep)
 
     mlp_blocks = [after(b, dprojs[n // 2]) for b in mlp_blocks]
     mlp = scatter_sum_list(mlp_blocks, "shard")
@@ -920,27 +966,29 @@
     def turned(share, tiles):
         return turn(share.reshape(n, tiles, chunk, LANES), n).reshape(n * tiles, chunk, LANES)
 
-    in_share = turned(replica_reduce(in_keep, in_send, near, [dproj, dqkv]), tiles)
-    down_share = replica_reduce(down_keep, down_send, far, [dproj, dqkv])
-    down_share = jnp.pad(down_share, ((0, -ff % chunk), (0, 0))).reshape(-1, chunk, LANES)
-    both = lax.all_gather(jnp.concatenate([in_share, down_share]), "rep", axis=0)
-    down_all = both[:, n * tiles :].reshape(replicas, -1, LANES)[:, :ff]
-
-    out_pair = replica_spread(replica_reduce(out_keep, out_send, far), far)
+    gates = [dqkv, qkv_keep, dnormed1_blocks[0]]
+    in_pairs = []
+    for f, (count, order) in enumerate(zip(in_counts, orders)):
+        share = replica_reduce(in_flows[2 * f], in_flows[2 * f + 1], order, gates)
+        in_pairs.append(replica_spread(turned(share, count), order))
+    down_pair = replica_spread(replica_reduce(down_keep, down_send, near, gates), near)
+    out_pair = replica_spread(replica_reduce(out_keep, out_send, near), near)
     qkv_share = turned(replica_reduce(qkv_keep, qkv_send, near), qkv_tiles)
     qkv_pair = replica_spread(qkv_share, near)
 
-    in_total, ln2_total = columns_out(place, (both, None), w_in, gain2, n, n * tiles, near, ff=ff)
-    down_total = rows_out(place, (down_all, None), model, far)
-    out_total = rows_out(place, out_pair, model, far)
+    in_total, ln2_total = columns_out(
+        place, in_pairs, in_counts, orders, w_in, gain2, n, ff=ff
+    )
+    down_total = rows_out(place, down_pair, model, near)
+    out_total = rows_out(place, out_pair, model, near)
     qkv_total, ln1_total = columns_out(
         place,
-        qkv_pair,
+        [qkv_pair],
+        [qkv_tiles],
+        [near],
         w_qkv,
         gain1,
         n,
-        n * qkv_tiles,
-        near,
         head_cols=head_cols,
         width=width,
     )

time: 400 us -> 375 us (0.938)
  waiting for transfers between devices: 201 us -> 160 us
  starting transfers between devices: 43.2 us -> 67.9 us
  between operations: 15.3 us -> 2.02 us
  local copies, waits for them, and re-layouts: 25.9 us -> 18.4 us
  other arithmetic: 16.8 us -> 23.1 us
  Pallas kernels: 92 us -> 96.8 us
    ppermute x60 -> x81, waiting for transfers between devices: 201 us -> 160 us  [swap(): return lax.ppermute(x, axis, [(i, i ^ 1 << bit) for i in range(size)])]
    ppermute x60 -> x81, starting transfers between devices: 43.2 us -> 67.9 us  [swap(): return lax.ppermute(x, axis, [(i, i ^ 1 << bit) for i in range(size)])]
    pallas_call x6 -> x7, Pallas kernels: 65.3 us -> 70.4 us  [the longest x1 14.5 us: shards(): pl.pallas_call(ordered(functools.partial(attention_back_kernel, n, heads,...]
    dynamic_slice x8 -> x10, local copies, waits for them, and re-layouts: 6.51 us -> 2.11 us  [part_for(): return lax.dynamic_slice_in_dim(a, start, 1 << bit)]
    slice x2 -> x0, local copies, waits for them, and re-layouts: 4.07 us -> none  [shards(): down_all = both[:, n * tiles:].reshape(replicas, -1, LANES)[:, :ff]]
    convert_element_type x11 -> x15, other arithmetic: 4.94 us -> 8.9 us  [total(): return (keep[a:b].astype(F32) + got[a:b].astype(F32)).astype(BF16)]
    unnamed x84 -> x76, local copies, waits for them, and re-layouts: 10.3 us -> 10.9 us
  transfers between devices with their start and end apart: 61 -> 81, of which waited for: 27 -> 30; matrix products, arithmetic and copies ran while one was open for 7% -> 8% of each run, Pallas kernels for 16% -> 21%
where the time goes in v1:
time: 375 us; the launch traced here: 368 us
  waiting for transfers between devices  160 us (43%)
  Pallas kernels  96.8 us (26%)
  starting transfers between devices  67.9 us (18%)
  other arithmetic  23.1 us (6%)
  local copies, waits for them, and re-layouts  18.4 us (5%)
    ppermute x81, waiting for transfers between devices, swap(): return lax.ppermute(x, axis, [(i, i ^ 1 << bit) for i in range(size)])  160 us
    ppermute x81, starting transfers between devices, swap(): return lax.ppermute(x, axis, [(i, i ^ 1 << bit) for i in range(size)])  67.9 us
    pallas_call x1, Pallas kernels, shards(): pl.pallas_call(ordered(functools.partial(attention_back_kernel, n, heads,...  14.5 us
    pallas_call x1, Pallas kernels, shards(): pl.pallas_call(functools.partial(attention_kernel, about(qkv_pieces), n,...  14 us
    pallas_call x1, Pallas kernels, shards(): pl.pallas_call(functools.partial(dup_kernel, n), in_specs=[ANY_SPEC] * (3...  14 us
    pallas_call x1, Pallas kernels, shards(): pl.pallas_call(functools.partial(up_kernel, about(out_pieces), about(in_p...  11.7 us
    unnamed x76, local copies, waits for them, and re-layouts  10.9 us
    pallas_call x2, Pallas kernels, columns_out(): pl.pallas_call(functools.partial(columns_out_kernel, n, ff, head_cols, wi...  10.9 us
  transfers between devices with their start and end apart: 81, of which 30 were waited for; matrix products, arithmetic and copies ran while one was open for 8% of the time, Pallas kernels for 21%

profile of v1, /device:TPU:0, one launch (start us, length us, event | category | flops | bytes accessed | tf_op | source)
XLA Modules:
  0.0 368.5 jit_solution(17696459113323340825)
XLA Ops:
  0.6 3.0 collective-permute-start.1
  11.0 4.8 %sine_multiply_fusion = (f32[1024,256]{1,0:T(8,128)}, f32[1024,256]{1,0:T(8,128)}) fusion(f32[256]{0:T(256)S(1)} %get-tuple-element.162, f32[256]{0:T(256)S(1)} %get-tuple-element.163), kind=kLoop, calls=%fused_computation.15 | loop fusion | flops 524288 | bytes 2099200 | tf_op jit(solution)/shard_map/mul | solution.py:785
  17.5 6.7 %collective-permute-done.3.refs_5_ = bf16[2,128,768]{2,1,0:T(8,128)(2,1)S(1)} collective-permute-done((bf16[2,128,768]{2,1,0:T(8,128)(2,1)}, bf16[2,128,768]{2,1,0:T(8,128)(2,1)S(1)}, u32[]{:S(2)}, u32[]{:S(2)}) %collective-permute-start.3) | collective-permute-done | bytes 393248 | tf_op jit(solution)/shard_map/ppermute | solution.py:36
  35.5 14.0 %attention.1 = (bf16[1024,256]{1,0:T(8,128)(2,1)}, bf16[1152,256]{1,0:T(8,128)(2,1)}, bf16[1152,256]{1,0:T(8,128)(2,1)}, bf16[1024,256]{1,0:T(8,128)(2,1)}, bf16...) custom-call(s32[2]{0:T(128)S(1)} %pad_add_fusion.place_ref.refs_0_, f32[1024,256]{1,0:T(8,128)} %get-tuple-element.161.cos_ref.refs_10_, ...), custom_call_target="tpu_custom_call" | custom-call | flops 10737418240 | bytes 4194304 | tf_op jit(solution)/shard_map/attention/pallas_call | solution.py:793
  49.5 8.0 %collective-permute-done.13.refs_9_ = bf16[128,1024]{1,0:T(8,128)(2,1)S(1)} collective-permute-done((bf16[128,1024]{1,0:T(8,128)(2,1)S(1)}, bf16[128,1024]{1,0:T(8,128)(2,1)S(1)}, u32[]{:S(2)}, u32[]{:S(2)}) %collective-permute-start.13) | collective-permute-done | bytes 262176 | tf_op jit(solution)/shard_map/ppermute | solution.py:36
  68.1 4.8 %collective-permute-done.11.refs_6_ = bf16[1024,256]{1,0:T(8,128)(2,1)S(1)} collective-permute-done((bf16[1024,256]{1,0:T(8,128)(2,1)}, bf16[1024,256]{1,0:T(8,128)(2,1)S(1)}, u32[]{:S(2)}, u32[]{:S(2)}) %collective-permute-start.11) | collective-permute-done | bytes 524320 | tf_op jit(solution)/shard_map/ppermute | solution.py:36
  76.0 7.0 %collective-permute-done.22.refs_19_ = bf16[2,64,1536]{2,1,0:T(8,128)(2,1)S(1)} collective-permute-done((bf16[2,64,1536]{2,1,0:T(8,128)(2,1)S(1)}, bf16[2,64,1536]{2,1,0:T(8,128)(2,1)S(1)}, u32[]{:S(2)}, u32[]{:S(2)}) %collective-permute-start.22) | collective-permute-done | bytes 393248 | tf_op jit(solution)/shard_map/ppermute | solution.py:36
  87.3 11.7 %up_projection.1 = (f32[256,1024]{1,0:T(8,128)}, bf16[1024,1024]{1,0:T(8,128)(2,1)}, f32[1024,1536]{1,0:T(8,128)}, bf16[1024,1536]{1,0:T(8,128)(2,1)}) custom-call(s32[2]{0:T(128)S(1)} %pad_add_fusion.place_ref.refs_0_, bf16[256,1024]{1,0:T(8,128)(2,1)} %refs_0_.3, bf16[256,1024]{1,0:T(8,128)(2,1)} %collective-permute-done.refs_1_, ...), custom_call_target="tpu_custom_call" | custom-call | flops 9663676416 | bytes 4194304 | tf_op jit(solution)/shard_map/up_projection/pallas_call | solution.py:819
  100.0 14.0 %dup.1 = (bf16[1024,768]{1,0:T(8,128)(2,1)}, bf16[1024,1536]{1,0:T(8,128)(2,1)}, bf16[256,1024]{1,0:T(8,128)(2,1)S(1)}, bf16[256,1024]{1,0:T(8,128)(2,1)}, bf16[...) custom-call(f32[1024,1536]{1,0:T(8,128)} %get-tuple-element.75.up_ref, ...), custom_call_target="tpu_custom_call" | custom-call | flops 11274289152 | bytes 4194304 | tf_op jit(solution)/shard_map/dup/pallas_call | solution.py:848
  122.4 7.5 %in_gradient.1 = (bf16[4,24,32,128]{3,2,1,0:T(8,128)(2,1)}, bf16[4,24,32,128]{3,2,1,0:T(8,128)(2,1)}, bf16[4,20,32,128]{3,2,1,0:T(8,128)(2,1)S(1)}, bf16[4,20,32,128]{3,2,1,0:T(8,128)(2,1)S(1)}) custom-call(s32[2]{0:T(128)S(1)} %pad_add_fusion.place_ref.refs_0_, bf16[1024,1024]{1,0:T(8,128)(2,1)} %get-tuple-element.85.refs_1_, ...), custom_call_target="tpu_custom_call" | custom-call | flops 6442450944 | bytes 4194304 | tf_op jit(solution)/shard_map/in_gradient/pallas_call | solution.py:896
  129.9 5.3 %collective-permute-done.32.refs_1_ = bf16[256,1024]{1,0:T(8,128)(2,1)S(1)} collective-permute-done((bf16[256,1024]{1,0:T(8,128)(2,1)S(1)}, bf16[256,1024]{1,0:T(8,128)(2,1)S(1)}, u32[]{:S(2)}, u32[]{:S(2)}) %collective-permute-start.32) | collective-permute-done | bytes 524320 | tf_op jit(solution)/shard_map/ppermute | solution.py:36
  140.8 9.9 %collective-permute-done.33.refs_3_ = bf16[256,1024]{1,0:T(8,128)(2,1)S(1)} collective-permute-done((bf16[256,1024]{1,0:T(8,128)(2,1)S(1)}, bf16[256,1024]{1,0:T(8,128)(2,1)S(1)}, u32[]{:S(2)}, u32[]{:S(2)}) %collective-permute-start.33) | collective-permute-done | bytes 524320 | tf_op jit(solution)/shard_map/ppermute | solution.py:36
  150.6 7.2 %down_gradient.1 = (bf16[4,656,128]{2,1,0:T(8,128)(2,1)}, bf16[4,656,128]{2,1,0:T(8,128)(2,1)}, bf16[256,1024]{1,0:T(8,128)(2,1)S(1)}, bf16[256,1024]{1,0:T(8,12...) custom-call(s32[2]{0:T(128)S(1)} %pad_add_fusion.place_ref.refs_0_, ...), custom_call_target="tpu_custom_call" | custom-call | flops 6442450944 | bytes 4194304 | tf_op jit(solution)/shard_map/down_gradient/pallas_call | solution.py:912
  161.1 14.5 %attention_back.1 = (bf16[1024,768]{1,0:T(8,128)(2,1)}, bf16[4,256,128]{2,1,0:T(8,128)(2,1)S(1)}, bf16[4,256,128]{2,1,0:T(8,128)(2,1)S(1)}) custom-call(s32[2]{0:T(128)S(1)} %pad_add_fusion.place_ref.refs_0_, bf16[256,1024]{1,0:T(8,128)(2,1)S(1)} %copy-done.18, bf16[256,1024]{1,0:T(8,128)(2,1)S(1)} %collective-permute-done.37.refs_2_, ...), custom_call_target="tpu_custom_call" | custom-call | flops 10737418240 | bytes 4194304 | tf_op jit(solution)/shard_map/attention_back/pallas_call | solution.py:924
  183.2 4.0 %qkv_gradient.1 = (bf16[4,24,32,128]{3,2,1,0:T(8,128)(2,1)S(1)}, bf16[4,24,32,128]{3,2,1,0:T(8,128)(2,1)S(1)}) custom-call(s32[2]{0:T(128)S(1)} %pad_add_fusion.place_ref.refs_0_, bf16[1024,1024]{1,0:T(8,128)(2,1)} %get-tuple-element.104.normed, bf16[1024,768]{1,0:T(8,128)(2,1)} %get-tuple-element.102.dqkv.refs_1_), custom_call_target="tpu_custom_call" | custom-call | flops 3221225472 | bytes 4194304 | tf_op jit(solution)/shard_map/qkv_gradient/pallas_call | solution.py:945
  189.5 4.6 %project_back.1 = (bf16[256,1024]{1,0:T(8,128)(2,1)S(1)}, bf16[256,1024]{1,0:T(8,128)(2,1)S(1)}, bf16[256,1024]{1,0:T(8,128)(2,1)S(1)}, bf16[256,1024]{1,0:T(8,128)(2,1)}) custom-call(s32[2]{0:T(128)S(1)} %pad_add_fusion.place_ref.refs_0_, bf16[1024,768]{1,0:T(8,128)(2,1)} %get-tuple-element.102.dqkv.refs_1_, bf16[1024,768]{1,0:T(8,128)(2,1)} %get-tuple-element.103.refs_2_, ...), custom_call_target="tpu_custom_call" | custom-call | flops 1610612736 | bytes 4194304 | tf_op jit(solution)/shard_map/project_back/pallas_call | solution.py:954
  206.4 3.6 collective-permute-done.53
  211.6 8.8 %collective-permute-done.68 = bf16[1,20,32,128]{3,2,1,0:T(8,128)(2,1)S(1)} collective-permute-done((bf16[1,20,32,128]{3,2,1,0:T(8,128)(2,1)S(1)}, bf16[1,20,32,128]{3,2,1,0:T(8,128)(2,1)S(1)}, u32[]{:S(2)}, u32[]{:S(2)}) %collective-permute-start.68) | collective-permute-done | bytes 163872 | tf_op jit(solution)/shard_map/ppermute | solution.py:36
  221.5 7.4 %collective-permute-done.77 = bf16[1,656,128]{2,1,0:T(8,128)(2,1)S(1)} collective-permute-done((bf16[1,656,128]{2,1,0:T(8,128)(2,1)S(1)}, bf16[1,656,128]{2,1,0:T(8,128)(2,1)S(1)}, u32[]{:S(2)}, u32[]{:S(2)}) %collective-permute-start.77) | collective-permute-done | bytes 167968 | tf_op jit(solution)/shard_map/ppermute | solution.py:36
  236.7 8.2 %collective-permute-done.54 = bf16[1,256,128]{2,1,0:T(8,128)(2,1)S(1)} collective-permute-done((bf16[1,256,128]{2,1,0:T(8,128)(2,1)S(1)}, bf16[1,256,128]{2,1,0:T(8,128)(2,1)S(1)}, u32[]{:S(2)}, u32[]{:S(2)}) %collective-permute-start.54) | collective-permute-done | bytes 65568 | tf_op jit(solution)/shard_map/ppermute | solution.py:36
  251.4 9.3 %collective-permute-done.78 = bf16[1,656,128]{2,1,0:T(8,128)(2,1)S(1)} collective-permute-done((bf16[1,656,128]{2,1,0:T(8,128)(2,1)S(1)}, bf16[1,656,128]{2,1,0:T(8,128)(2,1)S(1)}, u32[]{:S(2)}, u32[]{:S(2)}) %collective-permute-start.78) | collective-permute-done | bytes 167968 | tf_op jit(solution)/shard_map/ppermute | solution.py:36
  260.8 3.4 collective-permute-start.72
  265.8 14.5 %collective-permute-done.44 = bf16[1,24,32,128]{3,2,1,0:T(8,128)(2,1)S(1)} collective-permute-done((bf16[1,24,32,128]{3,2,1,0:T(8,128)(2,1)S(1)}, bf16[1,24,32,128]{3,2,1,0:T(8,128)(2,1)S(1)}, u32[]{:S(2)}, u32[]{:S(2)}) %collective-permute-start.44) | collective-permute-done | bytes 196640 | tf_op jit(solution)/shard_map/ppermute | solution.py:36
  282.0 3.1 collective-permute-done.46
  292.9 6.1 %collective-permute-done.63 = bf16[1,24,32,128]{3,2,1,0:T(8,128)(2,1)S(1)} collective-permute-done((bf16[1,24,32,128]{3,2,1,0:T(8,128)(2,1)S(1)}, bf16[1,24,32,128]{3,2,1,0:T(8,128)(2,1)S(1)}, u32[]{:S(2)}, u32[]{:S(2)}) %collective-permute-start.63) | collective-permute-done | bytes 196640 | tf_op jit(solution)/shard_map/ppermute | solution.py:36
  300.5 6.9 %collective-permute-done.48 = bf16[1,24,32,128]{3,2,1,0:T(8,128)(2,1)S(1)} collective-permute-done((bf16[1,24,32,128]{3,2,1,0:T(8,128)(2,1)S(1)}, bf16[1,24,32,128]{3,2,1,0:T(8,128)(2,1)S(1)}, u32[]{:S(2)}, u32[]{:S(2)}) %collective-permute-start.48) | collective-permute-done | bytes 196640 | tf_op jit(solution)/shard_map/ppermute | solution.py:36
  311.5 7.8 %collective-permute-done.64 = bf16[2,24,32,128]{3,2,1,0:T(8,128)(2,1)S(1)} collective-permute-done((bf16[2,24,32,128]{3,2,1,0:T(8,128)(2,1)S(1)}, bf16[2,24,32,128]{3,2,1,0:T(8,128)(2,1)S(1)}, u32[]{:S(2)}, u32[]{:S(2)}) %collective-permute-start.64) | collective-permute-done | bytes 393248 | tf_op jit(solution)/shard_map/ppermute | solution.py:36
  320.8 6.0 %collective-permute-done.49 = bf16[2,24,32,128]{3,2,1,0:T(8,128)(2,1)S(1)} collective-permute-done((bf16[2,24,32,128]{3,2,1,0:T(8,128)(2,1)S(1)}, bf16[2,24,32,128]{3,2,1,0:T(8,128)(2,1)S(1)}, u32[]{:S(2)}, u32[]{:S(2)}) %collective-permute-start.49) | collective-permute-done | bytes 393248 | tf_op jit(solution)/shard_map/ppermute | solution.py:36
  332.7 11.3 %collective-permute-done.74.refs_3_ = bf16[4,20,32,128]{3,2,1,0:T(8,128)(2,1)S(1)} collective-permute-done((bf16[4,20,32,128]{3,2,1,0:T(8,128)(2,1)S(1)}, bf16[4,20,32,128]{3,2,1,0:T(8,128)(2,1)S(1)}, u32[]{:S(2)}, u32[]{:S(2)}) %collective-permute-start.74) | collective-permute-done | bytes 655392 | tf_op jit(solution)/shard_map/ppermute | solution.py:36
  344.5 5.8 %columns_out.3 = (f32[8,32,5248]{2,1,0:T(8,128)}, f32[8,32,1]{2,1,0:T(8,128)S(1)}) custom-call(s32[2]{0:T(128)S(1)} %pad_add_fusion.place_ref.refs_0_, f32[8,32,1]{2,1,0:T(8,128)S(1)} %copy-done.13, bf16[8,32,5248]{2,1,0:T(8,128)(2,1)S(1)} %bitcast.24, bf16[4,24,32,128]{3,2,1,0:T(8,128)(2,1)S(1)} %pad_maximum_fusion.1.refs_0_, ...), custom_call_target="tpu_custom_call" | custom-call | tf_op jit(solution)/shard_map/columns_out/pallas_call | solution.py:657
  352.7 7.2 %collective-permute-done.50.refs_1_ = bf16[4,24,32,128]{3,2,1,0:T(8,128)(2,1)} collective-permute-done((bf16[4,24,32,128]{3,2,1,0:T(8,128)(2,1)S(1)}, bf16[4,24,32,128]{3,2,1,0:T(8,128)(2,1)}, u32[]{:S(2)}, u32[]{:S(2)}) %collective-permute-start.50) | collective-permute-done | bytes 786464 | tf_op jit(solution)/shard_map/ppermute | solution.py:36
  362.2 5.1 %columns_out.2 = (f32[8,32,3072]{2,1,0:T(8,128)}, f32[8,32,1]{2,1,0:T(8,128)S(1)}) custom-call(s32[2]{0:T(128)S(1)} %pad_add_fusion.place_ref.refs_0_, f32[8,32,1]{2,1,0:T(8,128)S(1)} %copy-done.12, bf16[8,32,3072]{2,1,0:T(8,128)(2,1)S(1)} %bitcast.25, bf16[4,24,32,128]{3,2,1,0:T(8,128)(2,1)S(1)} %pad_maximum_fusion.refs_0_, ...), custom_call_target="tpu_custom_call" | custom-call | tf_op jit(solution)/shard_map/columns_out/pallas_call | solution.py:657
  (302 shorter events, 124.9 us)
Async XLA Ops:
  0.6 27.0 %collective-permute-start.1 = (bf16[256,1024]{1,0:T(8,128)(2,1)}, bf16[256,1024]{1,0:T(8,128)(2,1)}, u32[]{:S(2)}, u32[]{:S(2)}) collective-permute-start(bf16[256,1024]{1,0:T(8,128)(2,1)} %refs_0_.3), channel_id=1, source_target_pairs={{0,2},{1,3},{2,0},{3,1},{4,6},{5,7},{6,4},{7,5},{8,10},{9,11},{10,... | collective-permute-start | bytes 1572872 | tf_op jit(solution)/shard_map/ppermute | solution.py:36
  3.6 28.7 %collective-permute-start = (bf16[256,1024]{1,0:T(8,128)(2,1)}, bf16[256,1024]{1,0:T(8,128)(2,1)}, u32[]{:S(2)}, u32[]{:S(2)}) collective-permute-start(bf16[256,1024]{1,0:T(8,128)(2,1)} %refs_0_.3), channel_id=1, source_target_pairs={{0,1},{1,0},{2,3},{3,2},{4,5},{5,4},{6,7},{7,6},{8,9},{9,8},{10,11... | collective-permute-start | bytes 1572872 | tf_op jit(solution)/shard_map/ppermute | solution.py:36
  10.5 21.3 %collective-permute-start.6 = (bf16[1,256,768]{2,1,0:T(8,128)(2,1)}, bf16[1,256,768]{2,1,0:T(8,128)(2,1)}, u32[]{:S(2)}, u32[]{:S(2)}) collective-permute-start(bf16[1,256,768]{2,1,0:T(8,128)(2,1)} %constant_dynamic-slice_fusion.8), channel_id=1, source_target_pairs={{0,1},{1,0},{2,3},{3,2},{4,5},{5,4},{6,7},{7,6},{8,9},{9,8},{10,11... | collective-permute-start | bytes 1179656 | tf_op jit(solution)/shard_map/ppermute | solution.py:36
  32.4 31.8 %collective-permute-start.20 = (bf16[2,128,1536]{2,1,0:T(8,128)(2,1)S(1)}, bf16[2,128,1536]{2,1,0:T(8,128)(2,1)S(1)}, u32[]{:S(2)}, u32[]{:S(2)}) collective-permute-start(bf16[2,128,1536]{2,1,0:T(8,128)(2,1)S(1)} %dynamic-slice_bitcast_fusion), channel_id=1, source_target_pairs={{0,2},{1,3},{2,0},{3,1},{4,6},{5,7},{6,4},{7,5},{8,10},{9,11},{10,... | collective-permute-start | bytes 2359304 | tf_op jit(solution)/shard_map/ppermute | solution.py:36
  33.9 23.6 %collective-permute-start.13 = (bf16[128,1024]{1,0:T(8,128)(2,1)S(1)}, bf16[128,1024]{1,0:T(8,128)(2,1)S(1)}, u32[]{:S(2)}, u32[]{:S(2)}) collective-permute-start(bf16[128,1024]{1,0:T(8,128)(2,1)S(1)} %dynamic-slice_bitcast_fusion.2), channel_id=1, source_target_pairs={{0,2},{1,3},{2,0},{3,1},{4,6},{5,7},{6,4},{7,5},{8,10},{9,11},{10,... | collective-permute-start | bytes 786440 | tf_op jit(solution)/shard_map/ppermute | solution.py:36
  65.0 18.0 %collective-permute-start.23 = (bf16[1,256,1536]{2,1,0:T(8,128)(2,1)S(1)}, bf16[1,256,1536]{2,1,0:T(8,128)(2,1)S(1)}, u32[]{:S(2)}, u32[]{:S(2)}) collective-permute-start(bf16[1,256,1536]{2,1,0:T(8,128)(2,1)S(1)} %constant_dynamic-slice_fusion.3), channel_id=1, source_target_pairs={{0,1},{1,0},{2,3},{3,2},{4,5},{5,4},{6,7},{7,6},{8,9},{9,8},{10,11... | collective-permute-start | bytes 2359304 | tf_op jit(solution)/shard_map/ppermute | solution.py:36
  138.9 39.3 %collective-permute-start.66 = (bf16[4,20,32,128]{3,2,1,0:T(8,128)(2,1)S(1)}, bf16[4,20,32,128]{3,2,1,0:T(8,128)(2,1)}, u32[]{:S(2)}, u32[]{:S(2)}) collective-permute-start(bf16[4,20,32,128]{3,2,1,0:T(8,128)(2,1)S(1)} %get-tuple-element.120), channel_id=1, source_target_pairs={{0,8},{4,12},{8,0},{12,4},{16,24},{20,28},{24,16},{28,20},{1,9},{5... | collective-permute-start | bytes 1966088 | tf_op jit(solution)/shard_map/ppermute | solution.py:36
  139.4 42.0 %collective-permute-start.57 = (bf16[4,24,32,128]{3,2,1,0:T(8,128)(2,1)}, bf16[4,24,32,128]{3,2,1,0:T(8,128)(2,1)S(1)}, u32[]{:S(2)}, u32[]{:S(2)}) collective-permute-start(bf16[4,24,32,128]{3,2,1,0:T(8,128)(2,1)} %get-tuple-element.115), channel_id=1, source_target_pairs={{0,4},{4,0},{8,12},{12,8},{16,20},{20,16},{24,28},{28,24},{1,5},{5... | collective-permute-start | bytes 2359304 | tf_op jit(solution)/shard_map/ppermute | solution.py:36
  140.8 18.5 %collective-permute-start.37 = (bf16[256,1024]{1,0:T(8,128)(2,1)S(1)}, bf16[256,1024]{1,0:T(8,128)(2,1)S(1)}, u32[]{:S(2)}, u32[]{:S(2)}) collective-permute-start(bf16[256,1024]{1,0:T(8,128)(2,1)S(1)} %get-tuple-element.88.refs_7_.refs_1_), channel_id=1, source_target_pairs={{0,1},{1,0},{2,3},{3,2},{4,5},{5,4},{6,7},{7,6},{8,9},{9,8},{10,11... | collective-permute-start | bytes 1572872 | tf_op jit(solution)/shard_map/ppermute | solution.py:36
  157.8 17.8 %collective-permute-start.75 = (bf16[4,656,128]{2,1,0:T(8,128)(2,1)}, bf16[4,656,128]{2,1,0:T(8,128)(2,1)}, u32[]{:S(2)}, u32[]{:S(2)}) collective-permute-start(bf16[4,656,128]{2,1,0:T(8,128)(2,1)} %get-tuple-element.126), channel_id=1, source_target_pairs={{0,4},{4,0},{8,12},{12,8},{16,20},{20,16},{24,28},{28,24},{1,5},{5... | collective-permute-start | bytes 2015240 | tf_op jit(solution)/shard_map/ppermute | solution.py:36
  159.2 70.6 %collective-permute-start.34 = (bf16[256,1024]{1,0:T(8,128)(2,1)S(1)}, bf16[256,1024]{1,0:T(8,128)(2,1)}, u32[]{:S(2)}, u32[]{:S(2)}) collective-permute-start(bf16[256,1024]{1,0:T(8,128)(2,1)S(1)} %get-tuple-element.92), channel_id=1, source_target_pairs={{0,1},{1,0},{2,3},{3,2},{4,5},{5,4},{6,7},{7,6},{8,9},{9,8},{10,11... | collective-permute-start | bytes 1572872 | tf_op jit(solution)/shard_map/ppermute | solution.py:36
  159.3 28.0 %collective-permute-start.35 = (bf16[256,1024]{1,0:T(8,128)(2,1)}, bf16[256,1024]{1,0:T(8,128)(2,1)}, u32[]{:S(2)}, u32[]{:S(2)}) collective-permute-start(bf16[256,1024]{1,0:T(8,128)(2,1)} %get-tuple-element.96), channel_id=1, source_target_pairs={{0,1},{1,0},{2,3},{3,2},{4,5},{5,4},{6,7},{7,6},{8,9},{9,8},{10,11... | collective-permute-start | bytes 1572872 | tf_op jit(solution)/shard_map/ppermute | solution.py:36
  177.7 19.9 %collective-permute-start.76 = (bf16[2,656,128]{2,1,0:T(8,128)(2,1)}, bf16[2,656,128]{2,1,0:T(8,128)(2,1)}, u32[]{:S(2)}, u32[]{:S(2)}) collective-permute-start(bf16[2,656,128]{2,1,0:T(8,128)(2,1)} %get-tuple-element.136), channel_id=1, source_target_pairs={{0,8},{4,12},{8,0},{12,4},{16,24},{20,28},{24,16},{28,20},{1,9},{5... | collective-permute-start | bytes 1007624 | tf_op jit(solution)/shard_map/ppermute | solution.py:36
  180.3 16.4 %collective-permute-start.67 = (bf16[2,20,32,128]{3,2,1,0:T(8,128)(2,1)}, bf16[2,20,32,128]{3,2,1,0:T(8,128)(2,1)}, u32[]{:S(2)}, u32[]{:S(2)}) collective-permute-start(bf16[2,20,32,128]{3,2,1,0:T(8,128)(2,1)} %get-tuple-element.138), channel_id=1, source_target_pairs={{0,4},{4,0},{8,12},{12,8},{16,20},{20,16},{24,28},{28,24},{1,5},{5... | collective-permute-start | bytes 983048 | tf_op jit(solution)/shard_map/ppermute | solution.py:36
  181.6 18.7 %collective-permute-start.58 = (bf16[2,24,32,128]{3,2,1,0:T(8,128)(2,1)S(1)}, bf16[2,24,32,128]{3,2,1,0:T(8,128)(2,1)S(1)}, u32[]{:S(2)}, u32[]{:S(2)}) collective-permute-start(bf16[2,24,32,128]{3,2,1,0:T(8,128)(2,1)S(1)} %get-tuple-element.132), channel_id=1, source_target_pairs={{0,8},{4,12},{8,0},{12,4},{16,24},{20,28},{24,16},{28,20},{1,9},{5... | collective-permute-start | bytes 1179656 | tf_op jit(solution)/shard_map/ppermute | solution.py:36
  195.9 49.8 %collective-permute-start.42 = (bf16[4,24,32,128]{3,2,1,0:T(8,128)(2,1)S(1)}, bf16[4,24,32,128]{3,2,1,0:T(8,128)(2,1)S(1)}, u32[]{:S(2)}, u32[]{:S(2)}) collective-permute-start(bf16[4,24,32,128]{3,2,1,0:T(8,128)(2,1)S(1)} %get-tuple-element.110), channel_id=1, source_target_pairs={{0,4},{4,0},{8,12},{12,8},{16,20},{20,16},{24,28},{28,24},{1,5},{5... | collective-permute-start | bytes 2359304 | tf_op jit(solution)/shard_map/ppermute | solution.py:36
  196.6 38.4 %collective-permute-start.40 = (bf16[256,1024]{1,0:T(8,128)(2,1)}, bf16[256,1024]{1,0:T(8,128)(2,1)S(1)}, u32[]{:S(2)}, u32[]{:S(2)}) collective-permute-start(bf16[256,1024]{1,0:T(8,128)(2,1)} %get-tuple-element.109), channel_id=1, source_target_pairs={{0,1},{1,0},{2,3},{3,2},{4,5},{5,4},{6,7},{7,6},{8,9},{9,8},{10,11... | collective-permute-start | bytes 1572872 | tf_op jit(solution)/shard_map/ppermute | solution.py:36
  200.3 29.7 %collective-permute-start.36 = (bf16[256,1024]{1,0:T(8,128)(2,1)S(1)}, bf16[256,1024]{1,0:T(8,128)(2,1)S(1)}, u32[]{:S(2)}, u32[]{:S(2)}) collective-permute-start(bf16[256,1024]{1,0:T(8,128)(2,1)S(1)} %add_convert_fusion.2), channel_id=1, source_target_pairs={{0,2},{1,3},{2,0},{3,1},{4,6},{5,7},{6,4},{7,5},{8,10},{9,11},{10,... | collective-permute-start | bytes 1572872 | tf_op jit(solution)/shard_map/ppermute | solution.py:36
  228.9 80.7 %collective-permute-start.39 = (bf16[256,1024]{1,0:T(8,128)(2,1)S(1)}, bf16[256,1024]{1,0:T(8,128)(2,1)S(1)}, u32[]{:S(2)}, u32[]{:S(2)}) collective-permute-start(bf16[256,1024]{1,0:T(8,128)(2,1)S(1)} %get-tuple-element.107), channel_id=1, source_target_pairs={{0,1},{1,0},{2,3},{3,2},{4,5},{5,4},{6,7},{7,6},{8,9},{9,8},{10,11... | collective-permute-start | bytes 1572872 | tf_op jit(solution)/shard_map/ppermute | solution.py:36
  245.9 18.2 %collective-permute-start.43 = (bf16[2,24,32,128]{3,2,1,0:T(8,128)(2,1)S(1)}, bf16[2,24,32,128]{3,2,1,0:T(8,128)(2,1)S(1)}, u32[]{:S(2)}, u32[]{:S(2)}) collective-permute-start(bf16[2,24,32,128]{3,2,1,0:T(8,128)(2,1)S(1)} %get-tuple-element.135), channel_id=1, source_target_pairs={{0,8},{4,12},{8,0},{12,4},{16,24},{20,28},{24,16},{28,20},{1,9},{5... | collective-permute-start | bytes 1179656 | tf_op jit(solution)/shard_map/ppermute | solution.py:36
  248.1 17.5 %collective-permute-start.61 = (bf16[2,6,32,128]{3,2,1,0:T(8,128)(2,1)S(1)}, bf16[2,6,32,128]{3,2,1,0:T(8,128)(2,1)S(1)}, u32[]{:S(2)}, u32[]{:S(2)}) collective-permute-start(bf16[2,6,32,128]{3,2,1,0:T(8,128)(2,1)S(1)} %bitcast.38), channel_id=1, source_target_pairs={{0,2},{1,3},{2,0},{3,1},{4,6},{5,7},{6,4},{7,5},{8,10},{9,11},{10,... | collective-permute-start | bytes 294920 | tf_op jit(solution)/shard_map/ppermute | solution.py:36
  251.4 33.7 %collective-permute-start.60 = (bf16[1,6,32,128]{3,2,1,0:T(8,128)(2,1)S(1)}, bf16[1,6,32,128]{3,2,1,0:T(8,128)(2,1)S(1)}, u32[]{:S(2)}, u32[]{:S(2)}) collective-permute-start(bf16[1,6,32,128]{3,2,1,0:T(8,128)(2,1)S(1)} %get-tuple-element.149), channel_id=1, source_target_pairs={{0,1},{1,0},{2,3},{3,2},{4,5},{5,4},{6,7},{7,6},{8,9},{9,8},{10,11... | collective-permute-start | bytes 147464 | tf_op jit(solution)/shard_map/ppermute | solution.py:36
  260.8 27.4 %collective-permute-start.72 = (bf16[1,20,32,128]{3,2,1,0:T(8,128)(2,1)S(1)}, bf16[1,20,32,128]{3,2,1,0:T(8,128)(2,1)S(1)}, u32[]{:S(2)}, u32[]{:S(2)}) collective-permute-start(bf16[1,20,32,128]{3,2,1,0:T(8,128)(2,1)S(1)} %bitcast.34), channel_id=1, source_target_pairs={{0,16},{4,20},{8,24},{12,28},{16,0},{20,4},{24,8},{28,12},{1,17},{... | collective-permute-start | bytes 491528 | tf_op jit(solution)/shard_map/ppermute | solution.py:36
  264.2 26.0 %collective-permute-start.56 = (bf16[4,256,128]{2,1,0:T(8,128)(2,1)S(1)}, bf16[4,256,128]{2,1,0:T(8,128)(2,1)S(1)}, u32[]{:S(2)}, u32[]{:S(2)}) collective-permute-start(bf16[4,256,128]{2,1,0:T(8,128)(2,1)S(1)} %pad_maximum_fusion.8.refs_0_), channel_id=1, source_target_pairs={{0,4},{4,0},{8,12},{12,8},{16,20},{20,16},{24,28},{28,24},{1,5},{5... | collective-permute-start | bytes 786440 | tf_op jit(solution)/shard_map/ppermute | solution.py:36
  286.6 24.5 %collective-permute-start.41 = (bf16[256,1024]{1,0:T(8,128)(2,1)S(1)}, bf16[256,1024]{1,0:T(8,128)(2,1)S(1)}, u32[]{:S(2)}, u32[]{:S(2)}) collective-permute-start(bf16[256,1024]{1,0:T(8,128)(2,1)S(1)} %add_convert_fusion), channel_id=1, source_target_pairs={{0,2},{1,3},{2,0},{3,1},{4,6},{5,7},{6,4},{7,5},{8,10},{9,11},{10,... | collective-permute-start | bytes 1572872 | tf_op jit(solution)/shard_map/ppermute | solution.py:36
  288.1 19.3 %collective-permute-start.79 = (bf16[2,656,128]{2,1,0:T(8,128)(2,1)S(1)}, bf16[2,656,128]{2,1,0:T(8,128)(2,1)S(1)}, u32[]{:S(2)}, u32[]{:S(2)}) collective-permute-start(bf16[2,656,128]{2,1,0:T(8,128)(2,1)S(1)} %pad_maximum_fusion.6), channel_id=1, source_target_pairs={{0,8},{4,12},{8,0},{12,4},{16,24},{20,28},{24,16},{28,20},{1,9},{5... | collective-permute-start | bytes 1007624 | tf_op jit(solution)/shard_map/ppermute | solution.py:36
  290.2 17.1 %collective-permute-start.48 = (bf16[1,24,32,128]{3,2,1,0:T(8,128)(2,1)S(1)}, bf16[1,24,32,128]{3,2,1,0:T(8,128)(2,1)S(1)}, u32[]{:S(2)}, u32[]{:S(2)}) collective-permute-start(bf16[1,24,32,128]{3,2,1,0:T(8,128)(2,1)S(1)} %bitcast.30), channel_id=1, source_target_pairs={{0,16},{4,20},{8,24},{12,28},{16,0},{20,4},{24,8},{28,12},{1,17},{... | collective-permute-start | bytes 589832 | tf_op jit(solution)/shard_map/ppermute | solution.py:36
  299.1 29.3 %collective-permute-start.73 = (bf16[2,20,32,128]{3,2,1,0:T(8,128)(2,1)S(1)}, bf16[2,20,32,128]{3,2,1,0:T(8,128)(2,1)S(1)}, u32[]{:S(2)}, u32[]{:S(2)}) collective-permute-start(bf16[2,20,32,128]{3,2,1,0:T(8,128)(2,1)S(1)} %pad_maximum_fusion.7), channel_id=1, source_target_pairs={{0,4},{4,0},{8,12},{12,8},{16,20},{20,16},{24,28},{28,24},{1,5},{5... | collective-permute-start | bytes 983048 | tf_op jit(solution)/shard_map/ppermute | solution.py:36
  307.4 19.4 %collective-permute-start.49 = (bf16[2,24,32,128]{3,2,1,0:T(8,128)(2,1)S(1)}, bf16[2,24,32,128]{3,2,1,0:T(8,128)(2,1)S(1)}, u32[]{:S(2)}, u32[]{:S(2)}) collective-permute-start(bf16[2,24,32,128]{3,2,1,0:T(8,128)(2,1)S(1)} %pad_maximum_fusion.4), channel_id=1, source_target_pairs={{0,8},{4,12},{8,0},{12,4},{16,24},{20,28},{24,16},{28,20},{1,9},{5... | collective-permute-start | bytes 1179656 | tf_op jit(solution)/shard_map/ppermute | solution.py:36
  309.6 20.7 %collective-permute-start.80 = (bf16[4,656,128]{2,1,0:T(8,128)(2,1)S(1)}, bf16[4,656,128]{2,1,0:T(8,128)(2,1)S(1)}, u32[]{:S(2)}, u32[]{:S(2)}) collective-permute-start(bf16[4,656,128]{2,1,0:T(8,128)(2,1)S(1)} %pad_maximum_fusion.2.refs_0_), channel_id=1, source_target_pairs={{0,4},{4,0},{8,12},{12,8},{16,20},{20,16},{24,28},{28,24},{1,5},{5... | collective-permute-start | bytes 2015240 | tf_op jit(solution)/shard_map/ppermute | solution.py:36
  319.4 25.1 %collective-permute-start.65 = (bf16[4,24,32,128]{3,2,1,0:T(8,128)(2,1)S(1)}, bf16[4,24,32,128]{3,2,1,0:T(8,128)(2,1)S(1)}, u32[]{:S(2)}, u32[]{:S(2)}) collective-permute-start(bf16[4,24,32,128]{3,2,1,0:T(8,128)(2,1)S(1)} %pad_maximum_fusion.1.refs_0_), channel_id=1, source_target_pairs={{0,4},{4,0},{8,12},{12,8},{16,20},{20,16},{24,28},{28,24},{1,5},{5... | collective-permute-start | bytes 2359304 | tf_op jit(solution)/shard_map/ppermute | solution.py:36
  326.9 33.0 %collective-permute-start.50 = (bf16[4,24,32,128]{3,2,1,0:T(8,128)(2,1)S(1)}, bf16[4,24,32,128]{3,2,1,0:T(8,128)(2,1)}, u32[]{:S(2)}, u32[]{:S(2)}) collective-permute-start(bf16[4,24,32,128]{3,2,1,0:T(8,128)(2,1)S(1)} %pad_maximum_fusion.refs_0_), channel_id=1, source_target_pairs={{0,4},{4,0},{8,12},{12,8},{16,20},{20,16},{24,28},{28,24},{1,5},{5... | collective-permute-start | bytes 2359304 | tf_op jit(solution)/shard_map/ppermute | solution.py:36
  (87 other events, 702.1 us)

commit v2 on v1

--- a/solution.py
+++ b/solution.py
@@ -101,26 +101,55 @@
     return pieces
 
 
+def add_halves(keep, got):
+    def total(a, b):
+        return (keep[a:b].astype(F32) + got[a:b].astype(F32)).astype(BF16)
+
+    size = keep.shape[0]
+    if size == 1:
+        return total(0, 1), None
+    return total(0, size // 2), total(size // 2, size)
+
+
+def gated(value, gates, step):
+    return after(value, *gates[step]) if step < len(gates) else value
+
+
 def replica_reduce(keep, send, order, gates=()):
     for step, bit in enumerate(order):
-        got = swap(send, "rep", bit)
-        if step < len(gates):
-            got = after(got, gates[step])
-
-        def total(a, b):
-            return (keep[a:b].astype(F32) + got[a:b].astype(F32)).astype(BF16)
-
-        size = keep.shape[0]
-        if size == 1:
-            return total(0, 1)[0]
-        keep, send = total(0, size // 2), total(size // 2, size)
-
-
-def replica_spread(x, order):
-    now = x[None]
-    for bit in reversed(order[1:]):
+        keep, send = add_halves(keep, gated(swap(send, "rep", bit), gates, step))
+    return keep[0]
+
+
+class PairReduce:
+    def __init__(self, p, q, orders):
+        self.p, self.q, self.orders = p, q, orders
+
+    def step(self, i, gates=()):
+        p, q = self.p, self.q
+        got_p = swap(p[1], "rep", self.orders[0][i])
+        got_q = swap(q[1], "rep", self.orders[1][i])
+        if gates:
+            got_p, got_q = after(got_p, *gates), after(got_q, *gates)
+        self.p, self.q = add_halves(p[0], got_p), add_halves(q[0], got_q)
+
+    def finish(self, gates=()):
+        rows = self.p[0].shape[1]
+        keep, send = (jnp.concatenate(x, axis=1) for x in zip(self.p, self.q))
+        share = replica_reduce(keep, send, self.orders[0][2:], gates)
+        return share[:rows], share[rows:]
+
+
+def pair_gather(p, q, orders):
+    rows = p.shape[0]
+    now = jnp.concatenate([p, q])[None]
+    for bit in reversed(orders[0][2:]):
         now = jnp.concatenate([now, swap(now, "rep", bit)])
-    return now, swap(now, "rep", order[0])
+    pairs = []
+    for x, order in zip((now[:, :rows], now[:, rows:]), orders):
+        x = jnp.concatenate([x, swap(x, "rep", order[1])])
+        pairs.append((x, swap(x, "rep", order[0])))
+    return pairs
 
 
 def turn(x, n):
@@ -319,7 +348,7 @@
         out_ref[at, :] = merge_heads(mixed, masks).astype(BF16)
         return carry
 
-    lax.fori_loop(0, seq // QB, attend, 0)
+    lax.fori_loop(0, seq // QB, attend, 0, unroll=2)
 
 
 def up_kernel(out_pieces, in_pieces, n, place_ref, *refs):
@@ -460,6 +489,21 @@
         mlp_refs[j][...] = jnp.dot(low, w_down[...], preferred_element_type=F32).astype(BF16)
 
 
+def write_flows(total, starts, counts, orders, flows, index, rep):
+    begin = 0
+    for f, (count, order) in enumerate(zip(counts, orders)):
+        keep, send = flows[2 * f], flows[2 * f + 1]
+        chunk = keep.shape[2]
+
+        def write(target, slot, c):
+            for t in range(count):
+                value = row_chunk(total, c, chunk, starts[begin + t])
+                target[slot, index * count + t] = value.astype(BF16)
+
+        store_slots(keep, send, rep, order, write)
+        begin += count
+
+
 def in_kernel(n, ff, counts, orders, place_ref, normed, dup, *refs):
     flows, in_sum = refs[:-1], refs[-1]
     me, rep = place_ref[0], place_ref[1]
@@ -475,18 +519,7 @@
         second = block[:, padded + whole * LANES : padded + (whole + 1) * LANES]
         lane = lax.broadcasted_iota(jnp.int32, first.shape, 1)
         in_sum[:, 2 * padded :] = jnp.where(lane < rest, first, pltpu.roll(second, rest, 1))
-        begin = 0
-        for f, (count, order) in enumerate(zip(counts, orders)):
-            keep, send = flows[2 * f], flows[2 * f + 1]
-            chunk = keep.shape[2]
-
-            def write(target, slot, c):
-                for t in range(count):
-                    value = row_chunk(in_sum, c, chunk, starts[begin + t])
-                    target[slot, (me ^ owner) * count + t] = value.astype(BF16)
-
-            store_slots(keep, send, rep, order, write)
-            begin += count
+        write_flows(in_sum, starts, counts, orders, flows, me ^ owner, rep)
 
 
 def add_kernel(a_ref, b_ref, c_ref, d_ref, mine_ref, other_ref):
@@ -550,7 +583,7 @@
         dv[window, :] += dot(probs.astype(BF16), grads, ((0,), (0,)))
         return carry
 
-    lax.fori_loop(0, seq // QB, back, 0)
+    lax.fori_loop(0, seq // QB, back, 0, unroll=2)
 
     def finish(i, carry):
         at = pl.ds(pl.multiple_of(i * QB, QB), QB)
@@ -564,20 +597,14 @@
     lax.fori_loop(0, seq // QB, finish, 0)
 
 
-def qkv_kernel(n, near, place_ref, normed, dqkv, keep, send, qkv_sum):
+def qkv_kernel(n, counts, orders, place_ref, normed, dqkv, *refs):
+    flows, qkv_sum = refs[:-1], refs[-1]
     me, rep = place_ref[0], place_ref[1]
     part = normed.shape[1] // n
-    chunk = keep.shape[2]
-    tiles = dqkv.shape[1] // LANES
+    starts = [t * LANES for t in range(sum(counts))]
     for owner in range(n):
         qkv_sum[...] = dot(normed[:, owner * part : (owner + 1) * part], dqkv[...], ((0,), (0,)))
-        base = (me ^ owner) * tiles
-
-        def write(target, slot, c):
-            for t in range(tiles):
-                target[slot, base + t] = row_chunk(qkv_sum, c, chunk, t * LANES).astype(BF16)
-
-        store_slots(keep, send, rep, near, write)
+        write_flows(qkv_sum, starts, counts, orders, flows, me ^ owner, rep)
 
 
 def project_back_kernel(n, place_ref, dqkv, w_qkv, *out_refs):
@@ -677,17 +704,16 @@
     return total.reshape(part, cols), ln.reshape(part)
 
 
-def rows_out_kernel(order, cols, place_ref, *refs):
+def rows_out_kernel(order, cols, skip, place_ref, *refs):
     *parts, out_ref = refs
     rep = place_ref[1]
 
     def chunk(c):
-        if len(parts) == 1:
-            return parts[0][c].astype(F32)
         half = parts[0].shape[0]
         slot = slot_of(rep ^ c, order)
         at = slot & (half - 1)
-        return jnp.where(slot < half, parts[0][at], parts[1][at]).astype(F32)
+        rows = slice(skip, skip + out_ref.shape[0])
+        return jnp.where(slot < half, parts[0][at, rows], parts[1][at, rows]).astype(F32)
 
     count = out_ref.shape[1] // cols
     if cols >= LANES:
@@ -703,21 +729,15 @@
             out_ref[:, t * LANES : (t + 1) * LANES] = value
 
 
-def rows_out(place, parts, model, order):
-    now, got = parts
-    count = now.shape[0]
-    if got is None:
-        parts = [now]
-    else:
-        count = 2 * count
+def rows_out(place, pair, skip, rows, model, order):
     return pl.pallas_call(
-        functools.partial(rows_out_kernel, order, model // count),
+        functools.partial(rows_out_kernel, order, model // (2 * pair[0].shape[0]), skip),
         in_specs=[pl.BlockSpec(memory_space=pltpu.SMEM)]
-        + [pl.BlockSpec(memory_space=pltpu.VMEM)] * len(parts),
-        out_shape=jax.ShapeDtypeStruct((now.shape[1], model), F32),
+        + [pl.BlockSpec(memory_space=pltpu.VMEM)] * 2,
+        out_shape=jax.ShapeDtypeStruct((rows, model), F32),
         compiler_params=pltpu.CompilerParams(vmem_limit_bytes=32 << 20),
         name="rows_out",
-    )(place, *parts)
+    )(place, *pair)
 
 
 def ordered(kernel, first, count):
@@ -807,13 +827,14 @@
         name="attention",
     )(place, *tables, *toks, *[a for _, _, a in qkv_pieces])
 
+    atts = gather_list(attended[:, :head_cols], "shard")
+
     def once_attended():
-        return attended
+        return atts[1]
 
     far_done = [toks[n // 2], qkv_pieces[1][2]]
     out_pieces = gather_weight(after(w_out, *far_done), once_attended)
     in_pieces = split_weight(after(in_to, *far_done), once_attended)
-    atts = gather_list(attended[:, :head_cols], "shard")
     cots = gather_list(after(cotangent, atts[n // 2]), "shard")
     blocks = [shape((rows, model), BF16)] * n
     hidden, normed2, up, in_w = pl.pallas_call(
@@ -873,7 +894,8 @@
     chunk = part // replicas
     lanes = max(LANES, model // replicas)
     tiles = up_tiles(ff)
-    in_counts = [tiles - tiles // 2, tiles // 2]
+    second = max(1, tiles * 3 // 11)
+    in_counts = [tiles - second, second]
     orders = [near, far]
     in_shapes = [shape((slots, n * c, chunk, LANES), BF16) for c in in_counts for _ in range(2)]
     down_shape = shape((slots, ff, lanes), BF16)
@@ -902,6 +924,11 @@
         cost_estimate=work(8 * seq * model * padded),
         name="in_gradient",
     )(place, normed2, dup, other)
+    def flow_rows(a):
+        return a.reshape(a.shape[0], -1, LANES)
+
+    in_flows = [flow_rows(a) for a in in_flows]
+    in_reduce = PairReduce(in_flows[:2], in_flows[2:], orders)
     dhidden, dproj = pl.pallas_call(
         ordered(norm_back_kernel, 4, 1),
         in_specs=[VMEM_SPEC] * 4 + [ANY_SPEC],
@@ -910,7 +937,7 @@
         name="norm_back",
     )(mine, swap(other, "shard", top), hidden, cotangent, in_flows[0])
     down_keep, down_send, *mlp_blocks = pl.pallas_call(
-        ordered(functools.partial(down_kernel, n, ff, near), 3 + n, 1),
+        ordered(functools.partial(down_kernel, n, ff, far), 3 + n, 1),
         in_specs=[SMEM_SPEC] + [VMEM_SPEC] * (2 + n) + [ANY_SPEC],
         out_shape=[down_shape, down_shape] + blocks,
         scratch_shapes=[pltpu.VMEM((padded, model), F32)],
@@ -919,11 +946,12 @@
         name="down_gradient",
     )(place, act, down_w, *cots, dproj)
     dprojs = gather_list(dproj, "shard")
+    in_reduce.step(0, [dprojs[n // 2]])
 
     out_shape = shape((slots, part, lanes), BF16)
     dqkv, out_keep, out_send = pl.pallas_call(
-        ordered(functools.partial(attention_back_kernel, n, heads, near), n + 10, 1),
-        in_specs=[SMEM_SPEC] + [VMEM_SPEC] * (n + 9) + [ANY_SPEC],
+        ordered(functools.partial(attention_back_kernel, n, heads, far), n + 10, 3),
+        in_specs=[SMEM_SPEC] + [VMEM_SPEC] * (n + 9) + [ANY_SPEC] * 3,
         out_shape=[shape((seq, 3 * width), BF16), out_shape, out_shape],
         scratch_shapes=[
             pltpu.VMEM((seq, width), BF16),
@@ -934,23 +962,25 @@
         compiler_params=params,
         cost_estimate=work(40 * seq * model * width),
         name="attention_back",
-    )(place, *dprojs, w_out, attended, queries, keys, values, *tables, down_keep)
+    )(place, *dprojs, w_out, attended, queries, keys, values, *tables, down_keep, in_reduce.p[1], in_reduce.q[1])
 
     mlp_blocks = [after(b, dprojs[n // 2]) for b in mlp_blocks]
     mlp = scatter_sum_list(mlp_blocks, "shard")
     output = (hidden + mlp).astype(BF16)
 
     qkv_tiles = 3 * width // LANES
-    qkv_shape = shape((slots, n * qkv_tiles, chunk, LANES), BF16)
-    qkv_keep, qkv_send = pl.pallas_call(
-        functools.partial(qkv_kernel, n, near),
-        in_specs=[SMEM_SPEC] + [VMEM_SPEC] * 2,
-        out_shape=[qkv_shape, qkv_shape],
+    qkv_counts = [qkv_tiles - qkv_tiles // 3, qkv_tiles // 3]
+    in_reduce.step(1, [dqkv])
+    qkv_flows = pl.pallas_call(
+        ordered(functools.partial(qkv_kernel, n, qkv_counts, orders), 3, 2),
+        in_specs=[SMEM_SPEC] + [VMEM_SPEC] * 2 + [ANY_SPEC] * 2,
+        out_shape=[shape((slots, n * c, chunk, LANES), BF16) for c in qkv_counts for _ in range(2)],
         scratch_shapes=[pltpu.VMEM((part, 3 * width), F32)],
         compiler_params=params,
         cost_estimate=work(12 * seq * model * width),
         name="qkv_gradient",
-    )(place, normed1, dqkv)
+    )(place, normed1, dqkv, in_reduce.p[1], in_reduce.q[1])
+    qkv_flows = [flow_rows(a) for a in qkv_flows]
     dnormed1_blocks = pl.pallas_call(
         ordered(functools.partial(project_back_kernel, n), 3, 1),
         in_specs=[SMEM_SPEC] + [VMEM_SPEC] * 2 + [ANY_SPEC],
@@ -958,34 +988,53 @@
         compiler_params=params,
         cost_estimate=work(6 * seq * model * width),
         name="project_back",
-    )(place, dqkv, qkv_w, qkv_keep)
+    )(place, dqkv, qkv_w, qkv_flows[0])
     dnormed1 = scatter_sum_list(dnormed1_blocks, "shard")
     hat1, scale1 = normalise(tokens.astype(F32))
     input_grad = dhidden + norm_backward(dnormed1, hat1, scale1)
 
-    def turned(share, tiles):
-        return turn(share.reshape(n, tiles, chunk, LANES), n).reshape(n * tiles, chunk, LANES)
-
-    gates = [dqkv, qkv_keep, dnormed1_blocks[0]]
-    in_pairs = []
-    for f, (count, order) in enumerate(zip(in_counts, orders)):
-        share = replica_reduce(in_flows[2 * f], in_flows[2 * f + 1], order, gates)
-        in_pairs.append(replica_spread(turned(share, count), order))
-    down_pair = replica_spread(replica_reduce(down_keep, down_send, near, gates), near)
-    out_pair = replica_spread(replica_reduce(out_keep, out_send, near), near)
-    qkv_share = turned(replica_reduce(qkv_keep, qkv_send, near), qkv_tiles)
-    qkv_pair = replica_spread(qkv_share, near)
+    def turned(p, q, counts):
+        sizes = [c * chunk for c in counts]
+        whole = jnp.concatenate([p.reshape(n, sizes[0], LANES), q.reshape(n, sizes[1], LANES)], 1)
+        whole = turn(whole, n)
+        return whole[:, : sizes[0]].reshape(-1, LANES), whole[:, sizes[0] :].reshape(-1, LANES)
+
+    def tiles_of(pair, count):
+        rows = n * count * chunk
+        return [a[:, :rows].reshape(a.shape[0], n * count, chunk, LANES) for a in pair]
+
+    attention_done = [qkv_flows[0], dnormed1_blocks[0]]
+    down_share = replica_reduce(down_keep, down_send, far, [[dqkv], attention_done])
+    in_p, in_q = turned(*in_reduce.finish([attention_done]), in_counts)
+    in_p, in_q = pair_gather(jnp.concatenate([in_p, down_share]), in_q, orders)
+
+    split = qkv_flows[2].shape[1]
+    qkv_q = [jnp.concatenate(x, axis=1) for x in zip(qkv_flows[2:], (out_keep, out_send))]
+    qkv_reduce = PairReduce(qkv_flows[:2], qkv_q, orders)
+    qkv_reduce.step(0)
+    qkv_reduce.step(1)
+    qkv_p, qkv_q = qkv_reduce.finish()
+    out_share = qkv_q[split:]
+    qkv_p, qkv_q = turned(qkv_p, qkv_q[:split], qkv_counts)
+    qkv_p, qkv_q = pair_gather(qkv_p, jnp.concatenate([qkv_q, out_share]), orders)
 
     in_total, ln2_total = columns_out(
-        place, in_pairs, in_counts, orders, w_in, gain2, n, ff=ff
+        place,
+        [tiles_of(in_p, in_counts[0]), tiles_of(in_q, in_counts[1])],
+        in_counts,
+        orders,
+        w_in,
+        gain2,
+        n,
+        ff=ff,
     )
-    down_total = rows_out(place, down_pair, model, near)
-    out_total = rows_out(place, out_pair, model, near)
+    down_total = rows_out(place, in_p, n * in_counts[0] * chunk, ff, model, near)
+    out_total = rows_out(place, qkv_q, split, part, model, far)
     qkv_total, ln1_total = columns_out(
         place,
-        [qkv_pair],
-        [qkv_tiles],
-        [near],
+        [tiles_of(qkv_p, qkv_counts[0]), tiles_of(qkv_q, qkv_counts[1])],
+        qkv_counts,
+        orders,
         w_qkv,
         gain1,
         n,

time: 375 us -> 395 us (1.053)
  waiting for transfers between devices: 160 us -> 188 us
  starting transfers between devices: 67.9 us -> 51 us
  other arithmetic: 23.1 us -> 30.1 us
    ppermute x81 -> x71, waiting for transfers between devices: 160 us -> 188 us  [swap(): return lax.ppermute(x, axis, [(i, i ^ 1 << bit) for i in range(size)])]
    ppermute x81 -> x71, starting transfers between devices: 67.9 us -> 51 us  [swap(): return lax.ppermute(x, axis, [(i, i ^ 1 << bit) for i in range(size)])]
    concatenate x10 -> x14, other arithmetic: 0.47 us -> 5.13 us  [the longest x6 3.34 us: pair_gather(): x = jnp.concatenate([x, swap(x, 'rep', order[1])])]
    convert_element_type x15 -> x12, other arithmetic: 8.9 us -> 10.2 us  [total(): return (keep[a:b].astype(F32) + got[a:b].astype(F32)).astype(BF16)]
    unnamed x76 -> x84, local copies, waits for them, and re-layouts: 10.9 us -> 11.5 us
  transfers between devices with their start and end apart: 81 -> 71, of which waited for: 30 -> 25; matrix products, arithmetic and copies ran while one was open for 8% -> 10% of each run, Pallas kernels for 21% -> 18%
where the time goes in v2:
time: 395 us; the launch traced here: 388 us
  waiting for transfers between devices  188 us (48%)
  Pallas kernels  94.9 us (24%)
  starting transfers between devices  51 us (13%)
  other arithmetic  30.1 us (8%)
  local copies, waits for them, and re-layouts  21.9 us (6%)
    ppermute x71, waiting for transfers between devices, swap(): return lax.ppermute(x, axis, [(i, i ^ 1 << bit) for i in range(size)])  188 us
    ppermute x71, starting transfers between devices, swap(): return lax.ppermute(x, axis, [(i, i ^ 1 << bit) for i in range(size)])  51 us
    pallas_call x1, Pallas kernels, shards(): pl.pallas_call(functools.partial(dup_kernel, n), in_specs=[ANY_SPEC] * (3...  14.1 us
    pallas_call x1, Pallas kernels, shards(): pl.pallas_call(ordered(functools.partial(attention_back_kernel, n, heads,...  13.5 us
    pallas_call x1, Pallas kernels, shards(): pl.pallas_call(functools.partial(attention_kernel, about(qkv_pieces), n,...  12.7 us
    pallas_call x1, Pallas kernels, shards(): pl.pallas_call(functools.partial(up_kernel, about(out_pieces), about(in_p...  12 us
    unnamed x84, local copies, waits for them, and re-layouts  11.5 us
    pallas_call x2, Pallas kernels, columns_out(): pl.pallas_call(functools.partial(columns_out_kernel, n, ff, head_cols, wi...  10.9 us
  transfers between devices with their start and end apart: 71, of which 25 were waited for; matrix products, arithmetic and copies ran while one was open for 10% of the time, Pallas kernels for 18%

profile of v2, /device:TPU:0, one launch (start us, length us, event | category | flops | bytes accessed | tf_op | source)
XLA Modules:
  0.0 388.0 jit_solution(2166601578578640253)
XLA Ops:
  0.6 3.0 collective-permute-start.1
  10.9 4.8 %sine_multiply_fusion = (f32[1024,256]{1,0:T(8,128)}, f32[1024,256]{1,0:T(8,128)}) fusion(f32[256]{0:T(256)S(1)} %get-tuple-element.172, f32[256]{0:T(256)S(1)} %get-tuple-element.173), kind=kLoop, calls=%fused_computation.25 | loop fusion | flops 524288 | bytes 2099200 | tf_op jit(solution)/shard_map/mul | solution.py:805
  17.4 6.8 %collective-permute-done.3.refs_5_ = bf16[2,128,768]{2,1,0:T(8,128)(2,1)S(1)} collective-permute-done((bf16[2,128,768]{2,1,0:T(8,128)(2,1)}, bf16[2,128,768]{2,1,0:T(8,128)(2,1)S(1)}, u32[]{:S(2)}, u32[]{:S(2)}) %collective-permute-start.3) | collective-permute-done | bytes 393248 | tf_op jit(solution)/shard_map/ppermute | solution.py:36
  27.9 2.5 collective-permute-done.4.refs_6_
  35.0 12.7 %attention.1 = (bf16[1024,256]{1,0:T(8,128)(2,1)}, bf16[1152,256]{1,0:T(8,128)(2,1)}, bf16[1152,256]{1,0:T(8,128)(2,1)}, bf16[1024,256]{1,0:T(8,128)(2,1)}, bf16...) custom-call(s32[2]{0:T(128)S(1)} %pad_add_fusion.place_ref.refs_0_, f32[1024,256]{1,0:T(8,128)} %get-tuple-element.171.cos_ref.refs_10_, ...), custom_call_target="tpu_custom_call" | custom-call | flops 10737418240 | bytes 4194304 | tf_op jit(solution)/shard_map/attention/pallas_call | solution.py:813
  49.6 7.9 %collective-permute-done.13.refs_9_ = bf16[128,1024]{1,0:T(8,128)(2,1)S(1)} collective-permute-done((bf16[128,1024]{1,0:T(8,128)(2,1)S(1)}, bf16[128,1024]{1,0:T(8,128)(2,1)S(1)}, u32[]{:S(2)}, u32[]{:S(2)}) %collective-permute-start.13) | collective-permute-done | bytes 262176 | tf_op jit(solution)/shard_map/ppermute | solution.py:36
  60.0 12.1 %collective-permute-done.11.refs_6_ = bf16[1024,256]{1,0:T(8,128)(2,1)} collective-permute-done((bf16[1024,256]{1,0:T(8,128)(2,1)S(1)}, bf16[1024,256]{1,0:T(8,128)(2,1)}, u32[]{:S(2)}, u32[]{:S(2)}) %collective-permute-start.11) | collective-permute-done | bytes 524320 | tf_op jit(solution)/shard_map/ppermute | solution.py:36
  76.9 2.9 collective-permute-done.14.refs_10_
  80.2 3.3 collective-permute-done.22.refs_19_
  93.6 12.0 %up_projection.1 = (f32[256,1024]{1,0:T(8,128)}, bf16[1024,1024]{1,0:T(8,128)(2,1)}, f32[1024,1536]{1,0:T(8,128)}, bf16[1024,1536]{1,0:T(8,128)(2,1)}) custom-call(s32[2]{0:T(128)S(1)} %pad_add_fusion.place_ref.refs_0_, bf16[256,1024]{1,0:T(8,128)(2,1)} %refs_0_.3, bf16[256,1024]{1,0:T(8,128)(2,1)} %collective-permute-done.refs_1_, ...), custom_call_target="tpu_custom_call" | custom-call | flops 9663676416 | bytes 4194304 | tf_op jit(solution)/shard_map/up_projection/pallas_call | solution.py:840
  106.6 14.1 %dup.1 = (bf16[1024,768]{1,0:T(8,128)(2,1)}, bf16[1024,1536]{1,0:T(8,128)(2,1)}, bf16[256,1024]{1,0:T(8,128)(2,1)S(1)}, bf16[256,1024]{1,0:T(8,128)(2,1)S(1)}, b...) custom-call(f32[1024,1536]{1,0:T(8,128)} %get-tuple-element.75.up_ref, ...), custom_call_target="tpu_custom_call" | custom-call | flops 11274289152 | bytes 4194304 | tf_op jit(solution)/shard_map/dup/pallas_call | solution.py:869
  125.4 7.6 %in_gradient.1 = (bf16[4,32,32,128]{3,2,1,0:T(8,128)(2,1)}, bf16[4,32,32,128]{3,2,1,0:T(8,128)(2,1)}, bf16[4,12,32,128]{3,2,1,0:T(8,128)(2,1)S(1)}, bf16[4,12,32,128]{3,2,1,0:T(8,128)(2,1)S(1)}) custom-call(s32[2]{0:T(128)S(1)} %pad_add_fusion.place_ref.refs_0_, bf16[1024,1024]{1,0:T(8,128)(2,1)} %get-tuple-element.85.refs_1_, ...), custom_call_target="tpu_custom_call" | custom-call | flops 6442450944 | bytes 4194304 | tf_op jit(solution)/shard_map/in_gradient/pallas_call | solution.py:918
  140.3 7.0 %down_gradient.1 = (bf16[4,656,128]{2,1,0:T(8,128)(2,1)}, bf16[4,656,128]{2,1,0:T(8,128)(2,1)}, bf16[256,1024]{1,0:T(8,128)(2,1)S(1)}, bf16[256,1024]{1,0:T(8,12...) custom-call(s32[2]{0:T(128)S(1)} %pad_add_fusion.place_ref.refs_0_, ...), custom_call_target="tpu_custom_call" | custom-call | flops 6442450944 | bytes 4194304 | tf_op jit(solution)/shard_map/down_gradient/pallas_call | solution.py:939
  148.9 3.3 collective-permute-done.33.refs_3_
  152.3 7.5 %collective-permute-done.39 = bf16[4,1024,128]{2,1,0:T(8,128)(2,1)} collective-permute-done((bf16[4,1024,128]{2,1,0:T(8,128)(2,1)}, bf16[4,1024,128]{2,1,0:T(8,128)(2,1)}, u32[]{:S(2)}, u32[]{:S(2)}) %collective-permute-start.39) | collective-permute-done | bytes 1048608 | tf_op jit(solution)/shard_map/ppermute | solution.py:36
  164.2 13.5 %attention_back.1 = (bf16[1024,768]{1,0:T(8,128)(2,1)}, bf16[4,256,128]{2,1,0:T(8,128)(2,1)S(1)}, bf16[4,256,128]{2,1,0:T(8,128)(2,1)S(1)}) custom-call(s32[2]{0:T(128)S(1)} %pad_add_fusion.place_ref.refs_0_, bf16[256,1024]{1,0:T(8,128)(2,1)S(1)} %copy-done.19, bf16[256,1024]{1,0:T(8,128)(2,1)S(1)} %collective-permute-done.37.refs_2_, ...), custom_call_target="tpu_custom_call" | custom-call | flops 10737418240 | bytes 4194304 | tf_op jit(solution)/shard_map/attention_back/pallas_call | solution.py:952
  182.9 2.6 collective-permute-start.59
  185.5 4.0 %qkv_gradient.1 = (bf16[4,16,32,128]{3,2,1,0:T(8,128)(2,1)S(1)}, bf16[4,16,32,128]{3,2,1,0:T(8,128)(2,1)S(1)}, bf16[4,8,32,128]{3,2,1,0:T(8,128)(2,1)S(1)}, bf16[4,8,32,128]{3,2,1,0:T(8,128)(2,1)S(1)}) custom-call(s32[2]{0:T(128)S(1)} %pad_add_fusion.place_ref.refs_0_, bf16[1024,1024]{1,0:T(8,128)(2,1)} %get-tuple-element.109.refs_1_, ...), custom_call_target="tpu_custom_call" | custom-call | flops 3221225472 | bytes 4194304 | tf_op jit(solution)/shard_map/qkv_gradient/pallas_call | solution.py:974
  194.8 4.6 %project_back.1 = (bf16[256,1024]{1,0:T(8,128)(2,1)S(1)}, bf16[256,1024]{1,0:T(8,128)(2,1)S(1)}, bf16[256,1024]{1,0:T(8,128)(2,1)S(1)}, bf16[256,1024]{1,0:T(8,128)(2,1)}) custom-call(s32[2]{0:T(128)S(1)} %pad_add_fusion.place_ref.refs_0_, bf16[1024,768]{1,0:T(8,128)(2,1)} %get-tuple-element.107.refs_2_.refs_1_, ...), custom_call_target="tpu_custom_call" | custom-call | flops 1610612736 | bytes 4194304 | tf_op jit(solution)/shard_map/project_back/pallas_call | solution.py:984
  203.7 9.0 %collective-permute-done.65 = bf16[1,656,128]{2,1,0:T(8,128)(2,1)S(1)} collective-permute-done((bf16[1,656,128]{2,1,0:T(8,128)(2,1)S(1)}, bf16[1,656,128]{2,1,0:T(8,128)(2,1)S(1)}, u32[]{:S(2)}, u32[]{:S(2)}) %collective-permute-start.65) | collective-permute-done | bytes 167968 | tf_op jit(solution)/shard_map/ppermute | solution.py:36
  217.3 14.7 %collective-permute-done.61 = bf16[2,352,128]{2,1,0:T(8,128)(2,1)S(1)} collective-permute-done((bf16[2,352,128]{2,1,0:T(8,128)(2,1)S(1)}, bf16[2,352,128]{2,1,0:T(8,128)(2,1)S(1)}, u32[]{:S(2)}, u32[]{:S(2)}) %collective-permute-start.61) | collective-permute-done | bytes 180256 | tf_op jit(solution)/shard_map/ppermute | solution.py:36
  235.3 6.8 %collective-permute-done.47 = bf16[2,512,128]{2,1,0:T(8,128)(2,1)S(1)} collective-permute-done((bf16[2,512,128]{2,1,0:T(8,128)(2,1)S(1)}, bf16[2,512,128]{2,1,0:T(8,128)(2,1)S(1)}, u32[]{:S(2)}, u32[]{:S(2)}) %collective-permute-start.47) | collective-permute-done | bytes 262176 | tf_op jit(solution)/shard_map/ppermute | solution.py:36
  242.7 3.2 collective-permute-start.66
  248.3 31.2 %collective-permute-done.50 = bf16[1,1024,128]{2,1,0:T(8,128)(2,1)S(1)} collective-permute-done((bf16[1,1024,128]{2,1,0:T(8,128)(2,1)S(1)}, bf16[1,1024,128]{2,1,0:T(8,128)(2,1)S(1)}, u32[]{:S(2)}, u32[]{:S(2)}) %collective-permute-start.50) | collective-permute-done | bytes 262176 | tf_op jit(solution)/shard_map/ppermute | solution.py:36
  281.6 3.1 collective-permute-done.52
  286.1 14.2 %collective-permute-done.67 = bf16[2,1680,128]{2,1,0:T(8,128)(2,1)S(1)} collective-permute-done((bf16[2,1680,128]{2,1,0:T(8,128)(2,1)S(1)}, bf16[2,1680,128]{2,1,0:T(8,128)(2,1)S(1)}, u32[]{:S(2)}, u32[]{:S(2)}) %collective-permute-start.67) | collective-permute-done | bytes 860192 | tf_op jit(solution)/shard_map/ppermute | solution.py:36
  305.7 9.7 %collective-permute-done.54 = bf16[1,1024,128]{2,1,0:T(8,128)(2,1)S(1)} collective-permute-done((bf16[1,1024,128]{2,1,0:T(8,128)(2,1)S(1)}, bf16[1,1024,128]{2,1,0:T(8,128)(2,1)S(1)}, u32[]{:S(2)}, u32[]{:S(2)}) %collective-permute-start.54) | collective-permute-done | bytes 262176 | tf_op jit(solution)/shard_map/ppermute | solution.py:36
  317.1 29.5 %collective-permute-done.69 = bf16[2,384,128]{2,1,0:T(8,128)(2,1)S(1)} collective-permute-done((bf16[2,384,128]{2,1,0:T(8,128)(2,1)S(1)}, bf16[2,384,128]{2,1,0:T(8,128)(2,1)S(1)}, u32[]{:S(2)}, u32[]{:S(2)}) %collective-permute-start.69) | collective-permute-done | bytes 196640 | tf_op jit(solution)/shard_map/ppermute | solution.py:36
  353.5 12.1 %collective-permute-done.58.refs_1_ = bf16[4,512,128]{2,1,0:T(8,128)(2,1)S(1)} collective-permute-done((bf16[4,512,128]{2,1,0:T(8,128)(2,1)S(1)}, bf16[4,512,128]{2,1,0:T(8,128)(2,1)S(1)}, u32[]{:S(2)}, u32[]{:S(2)}) %collective-permute-start.58) | collective-permute-done | bytes 524320 | tf_op jit(solution)/shard_map/ppermute | solution.py:36
  365.7 4.5 %columns_out.2 = (f32[8,32,3072]{2,1,0:T(8,128)}, f32[8,32,1]{2,1,0:T(8,128)S(1)}) custom-call(s32[2]{0:T(128)S(1)} %pad_add_fusion.place_ref.refs_0_, f32[8,32,1]{2,1,0:T(8,128)S(1)} %reshape_broadcast_in_dim.8.gain_ref, bf16[8,32,3072]{2,1,0:T(8,128)(2,1)S(1)} %bitcast.68, bf16[4,16,32,128]{3,2,1,0:T(8,128)(2,1)S(1)} %bitcast.72, ...), custom_call_target="tpu_custom_call" | custom-call | tf_op jit(solution)/shard_map/columns_out/pallas_call | solution.py:684
  376.5 6.5 %columns_out.3 = (f32[8,32,5248]{2,1,0:T(8,128)}, f32[8,32,1]{2,1,0:T(8,128)S(1)}) custom-call(s32[2]{0:T(128)S(1)} %pad_add_fusion.place_ref.refs_0_, f32[8,32,1]{2,1,0:T(8,128)S(1)} %reshape_broadcast_in_dim.9.gain_ref, bf16[8,32,5248]{2,1,0:T(8,128)(2,1)S(1)} %bitcast.67, bf16[4,32,32,128]{3,2,1,0:T(8,128)(2,1)S(1)} %bitcast.69, ...), custom_call_target="tpu_custom_call" | custom-call | tf_op jit(solution)/shard_map/columns_out/pallas_call | solution.py:684
  383.7 3.9 %rows_out.3 = f32[656,1024]{1,0:T(8,128)} custom-call(s32[2]{0:T(128)S(1)} %pad_add_fusion.place_ref.refs_0_, bf16[4,1680,128]{2,1,0:T(8,128)(2,1)} %pad_maximum_fusion.refs_0_, bf16[4,1680,128]{2,1,0:T(8,128)(2,1)} %collective-permute-done.68.refs_1_), custom_call_target="tpu_custom_call" | custom-call | tf_op jit(solution)/shard_map/rows_out/pallas_call | solution.py:733
  (301 shorter events, 105.4 us)
Async XLA Ops:
  0.6 27.0 %collective-permute-start.1 = (bf16[256,1024]{1,0:T(8,128)(2,1)}, bf16[256,1024]{1,0:T(8,128)(2,1)}, u32[]{:S(2)}, u32[]{:S(2)}) collective-permute-start(bf16[256,1024]{1,0:T(8,128)(2,1)} %refs_0_.3), channel_id=1, source_target_pairs={{0,2},{1,3},{2,0},{3,1},{4,6},{5,7},{6,4},{7,5},{8,10},{9,11},{10,... | collective-permute-start | bytes 1572872 | tf_op jit(solution)/shard_map/ppermute | solution.py:36
  3.6 28.7 %collective-permute-start = (bf16[256,1024]{1,0:T(8,128)(2,1)}, bf16[256,1024]{1,0:T(8,128)(2,1)}, u32[]{:S(2)}, u32[]{:S(2)}) collective-permute-start(bf16[256,1024]{1,0:T(8,128)(2,1)} %refs_0_.3), channel_id=1, source_target_pairs={{0,1},{1,0},{2,3},{3,2},{4,5},{5,4},{6,7},{7,6},{8,9},{9,8},{10,11... | collective-permute-start | bytes 1572872 | tf_op jit(solution)/shard_map/ppermute | solution.py:36
  10.5 21.3 %collective-permute-start.6 = (bf16[1,256,768]{2,1,0:T(8,128)(2,1)}, bf16[1,256,768]{2,1,0:T(8,128)(2,1)}, u32[]{:S(2)}, u32[]{:S(2)}) collective-permute-start(bf16[1,256,768]{2,1,0:T(8,128)(2,1)} %constant_dynamic-slice_fusion.8), channel_id=1, source_target_pairs={{0,1},{1,0},{2,3},{3,2},{4,5},{5,4},{6,7},{7,6},{8,9},{9,8},{10,11... | collective-permute-start | bytes 1179656 | tf_op jit(solution)/shard_map/ppermute | solution.py:36
  32.4 25.2 %collective-permute-start.20 = (bf16[2,128,1536]{2,1,0:T(8,128)(2,1)S(1)}, bf16[2,128,1536]{2,1,0:T(8,128)(2,1)S(1)}, u32[]{:S(2)}, u32[]{:S(2)}) collective-permute-start(bf16[2,128,1536]{2,1,0:T(8,128)(2,1)S(1)} %dynamic-slice_bitcast_fusion), channel_id=1, source_target_pairs={{0,2},{1,3},{2,0},{3,1},{4,6},{5,7},{6,4},{7,5},{8,10},{9,11},{10,... | collective-permute-start | bytes 2359304 | tf_op jit(solution)/shard_map/ppermute | solution.py:36
  49.0 24.8 %collective-permute-start.16 = (bf16[256,1024]{1,0:T(8,128)(2,1)S(1)}, bf16[256,1024]{1,0:T(8,128)(2,1)S(1)}, u32[]{:S(2)}, u32[]{:S(2)}) collective-permute-start(bf16[256,1024]{1,0:T(8,128)(2,1)S(1)} %copy-done.28), channel_id=1, source_target_pairs={{0,1},{1,0},{2,3},{3,2},{4,5},{5,4},{6,7},{7,6},{8,9},{9,8},{10,11... | collective-permute-start | bytes 1572872 | tf_op jit(solution)/shard_map/ppermute | solution.py:36
  49.1 25.4 %collective-permute-start.23 = (bf16[1,256,1536]{2,1,0:T(8,128)(2,1)S(1)}, bf16[1,256,1536]{2,1,0:T(8,128)(2,1)S(1)}, u32[]{:S(2)}, u32[]{:S(2)}) collective-permute-start(bf16[1,256,1536]{2,1,0:T(8,128)(2,1)S(1)} %constant_dynamic-slice_fusion.3), channel_id=1, source_target_pairs={{0,1},{1,0},{2,3},{3,2},{4,5},{5,4},{6,7},{7,6},{8,9},{9,8},{10,11... | collective-permute-start | bytes 2359304 | tf_op jit(solution)/shard_map/ppermute | solution.py:36
  57.5 16.1 %collective-permute-start.17 = (bf16[128,1024]{1,0:T(8,128)(2,1)S(1)}, bf16[128,1024]{1,0:T(8,128)(2,1)S(1)}, u32[]{:S(2)}, u32[]{:S(2)}) collective-permute-start(bf16[128,1024]{1,0:T(8,128)(2,1)S(1)} %collective-permute-done.13.refs_9_), channel_id=1, source_target_pairs={{0,1},{1,0},{2,3},{3,2},{4,5},{5,4},{6,7},{7,6},{8,9},{9,8},{10,11... | collective-permute-start | bytes 786440 | tf_op jit(solution)/shard_map/ppermute | solution.py:36
  59.2 16.9 %collective-permute-start.21 = (bf16[2,64,1536]{2,1,0:T(8,128)(2,1)S(1)}, bf16[2,64,1536]{2,1,0:T(8,128)(2,1)S(1)}, u32[]{:S(2)}, u32[]{:S(2)}) collective-permute-start(bf16[2,64,1536]{2,1,0:T(8,128)(2,1)S(1)} %get-tuple-element.143), channel_id=1, source_target_pairs={{0,4},{4,0},{8,12},{12,8},{16,20},{20,16},{24,28},{28,24},{1,5},{5... | collective-permute-start | bytes 1179656 | tf_op jit(solution)/shard_map/ppermute | solution.py:36
  89.2 16.4 %collective-permute-start.27 = (bf16[256,1024]{1,0:T(8,128)(2,1)S(1)}, bf16[256,1024]{1,0:T(8,128)(2,1)S(1)}, u32[]{:S(2)}, u32[]{:S(2)}) collective-permute-start(bf16[256,1024]{1,0:T(8,128)(2,1)S(1)} %copy-done.11), channel_id=1, source_target_pairs={{0,1},{1,0},{2,3},{3,2},{4,5},{5,4},{6,7},{7,6},{8,9},{9,8},{10,11... | collective-permute-start | bytes 1572872 | tf_op jit(solution)/shard_map/ppermute | solution.py:36
  134.6 25.1 %collective-permute-start.39 = (bf16[4,1024,128]{2,1,0:T(8,128)(2,1)}, bf16[4,1024,128]{2,1,0:T(8,128)(2,1)}, u32[]{:S(2)}, u32[]{:S(2)}) collective-permute-start(bf16[4,1024,128]{2,1,0:T(8,128)(2,1)} %bitcast.106), channel_id=1, source_target_pairs={{0,4},{4,0},{8,12},{12,8},{16,20},{20,16},{24,28},{28,24},{1,5},{5... | collective-permute-start | bytes 3145736 | tf_op jit(solution)/shard_map/ppermute | solution.py:36
  140.3 23.0 %collective-permute-start.37 = (bf16[256,1024]{1,0:T(8,128)(2,1)S(1)}, bf16[256,1024]{1,0:T(8,128)(2,1)S(1)}, u32[]{:S(2)}, u32[]{:S(2)}) collective-permute-start(bf16[256,1024]{1,0:T(8,128)(2,1)S(1)} %get-tuple-element.88.refs_7_.refs_1_), channel_id=1, source_target_pairs={{0,1},{1,0},{2,3},{3,2},{4,5},{5,4},{6,7},{7,6},{8,9},{9,8},{10,11... | collective-permute-start | bytes 1572872 | tf_op jit(solution)/shard_map/ppermute | solution.py:36
  147.4 30.3 %collective-permute-start.63 = (bf16[4,656,128]{2,1,0:T(8,128)(2,1)}, bf16[4,656,128]{2,1,0:T(8,128)(2,1)S(1)}, u32[]{:S(2)}, u32[]{:S(2)}) collective-permute-start(bf16[4,656,128]{2,1,0:T(8,128)(2,1)} %get-tuple-element.125), channel_id=1, source_target_pairs={{0,8},{4,12},{8,0},{12,4},{16,24},{20,28},{24,16},{28,20},{1,9},{5... | collective-permute-start | bytes 2015240 | tf_op jit(solution)/shard_map/ppermute | solution.py:36
  159.9 20.1 %collective-permute-start.42 = (bf16[2,384,128]{2,1,0:T(8,128)(2,1)S(1)}, bf16[2,384,128]{2,1,0:T(8,128)(2,1)}, u32[]{:S(2)}, u32[]{:S(2)}) collective-permute-start(bf16[2,384,128]{2,1,0:T(8,128)(2,1)S(1)} %get-tuple-element.157.refs_16_), channel_id=1, source_target_pairs={{0,4},{4,0},{8,12},{12,8},{16,20},{20,16},{24,28},{28,24},{1,5},{5... | collective-permute-start | bytes 589832 | tf_op jit(solution)/shard_map/ppermute | solution.py:36
  162.9 17.0 %collective-permute-start.41 = (bf16[2,1024,128]{2,1,0:T(8,128)(2,1)}, bf16[2,1024,128]{2,1,0:T(8,128)(2,1)}, u32[]{:S(2)}, u32[]{:S(2)}) collective-permute-start(bf16[2,1024,128]{2,1,0:T(8,128)(2,1)} %get-tuple-element.139.refs_15_), channel_id=1, source_target_pairs={{0,8},{4,12},{8,0},{12,4},{16,24},{20,28},{24,16},{28,20},{1,9},{5... | collective-permute-start | bytes 1572872 | tf_op jit(solution)/shard_map/ppermute | solution.py:36
  163.4 82.6 %collective-permute-start.34 = (bf16[256,1024]{1,0:T(8,128)(2,1)S(1)}, bf16[256,1024]{1,0:T(8,128)(2,1)}, u32[]{:S(2)}, u32[]{:S(2)}) collective-permute-start(bf16[256,1024]{1,0:T(8,128)(2,1)S(1)} %get-tuple-element.92), channel_id=1, source_target_pairs={{0,1},{1,0},{2,3},{3,2},{4,5},{5,4},{6,7},{7,6},{8,9},{9,8},{10,11... | collective-permute-start | bytes 1572872 | tf_op jit(solution)/shard_map/ppermute | solution.py:36
  163.4 27.7 %collective-permute-start.35 = (bf16[256,1024]{1,0:T(8,128)(2,1)}, bf16[256,1024]{1,0:T(8,128)(2,1)S(1)}, u32[]{:S(2)}, u32[]{:S(2)}) collective-permute-start(bf16[256,1024]{1,0:T(8,128)(2,1)} %get-tuple-element.96), channel_id=1, source_target_pairs={{0,1},{1,0},{2,3},{3,2},{4,5},{5,4},{6,7},{7,6},{8,9},{9,8},{10,11... | collective-permute-start | bytes 1572872 | tf_op jit(solution)/shard_map/ppermute | solution.py:36
  178.6 20.8 %collective-permute-start.64 = (bf16[2,656,128]{2,1,0:T(8,128)(2,1)}, bf16[2,656,128]{2,1,0:T(8,128)(2,1)}, u32[]{:S(2)}, u32[]{:S(2)}) collective-permute-start(bf16[2,656,128]{2,1,0:T(8,128)(2,1)} %get-tuple-element.132), channel_id=1, source_target_pairs={{0,4},{4,0},{8,12},{12,8},{16,20},{20,16},{24,28},{28,24},{1,5},{5... | collective-permute-start | bytes 1007624 | tf_op jit(solution)/shard_map/ppermute | solution.py:36
  182.9 19.6 %collective-permute-start.59 = (bf16[1,1408,128]{2,1,0:T(8,128)(2,1)}, bf16[1,1408,128]{2,1,0:T(8,128)(2,1)}, u32[]{:S(2)}, u32[]{:S(2)}) collective-permute-start(bf16[1,1408,128]{2,1,0:T(8,128)(2,1)} %pad_maximum_fusion.5), channel_id=1, source_target_pairs={{0,16},{4,20},{8,24},{12,28},{16,0},{20,4},{24,8},{28,12},{1,17},{... | collective-permute-start | bytes 1081352 | tf_op jit(solution)/shard_map/ppermute | solution.py:36
  189.6 24.9 %collective-permute-start.46 = (bf16[4,512,128]{2,1,0:T(8,128)(2,1)S(1)}, bf16[4,512,128]{2,1,0:T(8,128)(2,1)}, u32[]{:S(2)}, u32[]{:S(2)}) collective-permute-start(bf16[4,512,128]{2,1,0:T(8,128)(2,1)S(1)} %bitcast.79), channel_id=1, source_target_pairs={{0,4},{4,0},{8,12},{12,8},{16,20},{20,16},{24,28},{28,24},{1,5},{5... | collective-permute-start | bytes 1572872 | tf_op jit(solution)/shard_map/ppermute | solution.py:36
  191.9 40.1 %collective-permute-start.48 = (bf16[4,512,128]{2,1,0:T(8,128)(2,1)}, bf16[4,512,128]{2,1,0:T(8,128)(2,1)}, u32[]{:S(2)}, u32[]{:S(2)}) collective-permute-start(bf16[4,512,128]{2,1,0:T(8,128)(2,1)} %pad_maximum_fusion.2), channel_id=1, source_target_pairs={{0,8},{4,12},{8,0},{12,4},{16,24},{20,28},{24,16},{28,20},{1,9},{5... | collective-permute-start | bytes 1572872 | tf_op jit(solution)/shard_map/ppermute | solution.py:36
  212.7 72.1 %collective-permute-start.43 = (bf16[256,1024]{1,0:T(8,128)(2,1)S(1)}, bf16[256,1024]{1,0:T(8,128)(2,1)S(1)}, u32[]{:S(2)}, u32[]{:S(2)}) collective-permute-start(bf16[256,1024]{1,0:T(8,128)(2,1)S(1)} %get-tuple-element.114), channel_id=1, source_target_pairs={{0,1},{1,0},{2,3},{3,2},{4,5},{5,4},{6,7},{7,6},{8,9},{9,8},{10,11... | collective-permute-start | bytes 1572872 | tf_op jit(solution)/shard_map/ppermute | solution.py:36
  213.7 32.4 %collective-permute-start.36 = (bf16[256,1024]{1,0:T(8,128)(2,1)S(1)}, bf16[256,1024]{1,0:T(8,128)(2,1)S(1)}, u32[]{:S(2)}, u32[]{:S(2)}) collective-permute-start(bf16[256,1024]{1,0:T(8,128)(2,1)S(1)} %add_convert_fusion.2), channel_id=1, source_target_pairs={{0,2},{1,3},{2,0},{3,1},{4,6},{5,7},{6,4},{7,5},{8,10},{9,11},{10,... | collective-permute-start | bytes 1572872 | tf_op jit(solution)/shard_map/ppermute | solution.py:36
  214.5 17.5 %collective-permute-start.61 = (bf16[2,352,128]{2,1,0:T(8,128)(2,1)S(1)}, bf16[2,352,128]{2,1,0:T(8,128)(2,1)S(1)}, u32[]{:S(2)}, u32[]{:S(2)}) collective-permute-start(bf16[2,352,128]{2,1,0:T(8,128)(2,1)S(1)} %pad_maximum_fusion.10), channel_id=1, source_target_pairs={{0,2},{1,3},{2,0},{3,1},{4,6},{5,7},{6,4},{7,5},{8,10},{9,11},{10,... | collective-permute-start | bytes 540680 | tf_op jit(solution)/shard_map/ppermute | solution.py:36
  242.1 42.7 %collective-permute-start.45 = (bf16[256,1024]{1,0:T(8,128)(2,1)S(1)}, bf16[256,1024]{1,0:T(8,128)(2,1)S(1)}, u32[]{:S(2)}, u32[]{:S(2)}) collective-permute-start(bf16[256,1024]{1,0:T(8,128)(2,1)S(1)} %add_convert_fusion), channel_id=1, source_target_pairs={{0,2},{1,3},{2,0},{3,1},{4,6},{5,7},{6,4},{7,5},{8,10},{9,11},{10,... | collective-permute-start | bytes 1572872 | tf_op jit(solution)/shard_map/ppermute | solution.py:36
  242.7 36.9 %collective-permute-start.66 = (bf16[1,2064,128]{2,1,0:T(8,128)(2,1)S(1)}, bf16[1,2064,128]{2,1,0:T(8,128)(2,1)S(1)}, u32[]{:S(2)}, u32[]{:S(2)}) collective-permute-start(bf16[1,2064,128]{2,1,0:T(8,128)(2,1)S(1)} %maximum_bitcast_fusion), channel_id=1, source_target_pairs={{0,16},{4,20},{8,24},{12,28},{16,0},{20,4},{24,8},{28,12},{1,17},{... | collective-permute-start | bytes 1585160 | tf_op jit(solution)/shard_map/ppermute | solution.py:36
  246.0 33.5 %collective-permute-start.50 = (bf16[1,1024,128]{2,1,0:T(8,128)(2,1)S(1)}, bf16[1,1024,128]{2,1,0:T(8,128)(2,1)S(1)}, u32[]{:S(2)}, u32[]{:S(2)}) collective-permute-start(bf16[1,1024,128]{2,1,0:T(8,128)(2,1)S(1)} %pad_maximum_fusion.8), channel_id=1, source_target_pairs={{0,16},{4,20},{8,24},{12,28},{16,0},{20,4},{24,8},{28,12},{1,17},{... | collective-permute-start | bytes 786440 | tf_op jit(solution)/shard_map/ppermute | solution.py:36
  279.7 20.6 %collective-permute-start.67 = (bf16[2,1680,128]{2,1,0:T(8,128)(2,1)S(1)}, bf16[2,1680,128]{2,1,0:T(8,128)(2,1)S(1)}, u32[]{:S(2)}, u32[]{:S(2)}) collective-permute-start(bf16[2,1680,128]{2,1,0:T(8,128)(2,1)S(1)} %fusion.13), channel_id=1, source_target_pairs={{0,8},{4,12},{8,0},{12,4},{16,24},{20,28},{24,16},{28,20},{1,9},{5... | collective-permute-start | bytes 2580488 | tf_op jit(solution)/shard_map/ppermute | solution.py:36
  301.6 73.5 %collective-permute-start.68 = (bf16[4,1680,128]{2,1,0:T(8,128)(2,1)}, bf16[4,1680,128]{2,1,0:T(8,128)(2,1)}, u32[]{:S(2)}, u32[]{:S(2)}) collective-permute-start(bf16[4,1680,128]{2,1,0:T(8,128)(2,1)} %pad_maximum_fusion.refs_0_), channel_id=1, source_target_pairs={{0,4},{4,0},{8,12},{12,8},{16,20},{20,16},{24,28},{28,24},{1,5},{5... | collective-permute-start | bytes 5160968 | tf_op jit(solution)/shard_map/ppermute | solution.py:36
  304.3 42.3 %collective-permute-start.69 = (bf16[2,384,128]{2,1,0:T(8,128)(2,1)S(1)}, bf16[2,384,128]{2,1,0:T(8,128)(2,1)S(1)}, u32[]{:S(2)}, u32[]{:S(2)}) collective-permute-start(bf16[2,384,128]{2,1,0:T(8,128)(2,1)S(1)} %pad_maximum_fusion.9), channel_id=1, source_target_pairs={{0,4},{4,0},{8,12},{12,8},{16,20},{20,16},{24,28},{28,24},{1,5},{5... | collective-permute-start | bytes 589832 | tf_op jit(solution)/shard_map/ppermute | solution.py:36
  315.5 34.3 %collective-permute-start.57 = (bf16[2,512,128]{2,1,0:T(8,128)(2,1)S(1)}, bf16[2,512,128]{2,1,0:T(8,128)(2,1)S(1)}, u32[]{:S(2)}, u32[]{:S(2)}) collective-permute-start(bf16[2,512,128]{2,1,0:T(8,128)(2,1)S(1)} %get-tuple-element.144), channel_id=1, source_target_pairs={{0,4},{4,0},{8,12},{12,8},{16,20},{20,16},{24,28},{28,24},{1,5},{5... | collective-permute-start | bytes 786440 | tf_op jit(solution)/shard_map/ppermute | solution.py:36
  316.9 33.3 %collective-permute-start.55 = (bf16[2,512,128]{2,1,0:T(8,128)(2,1)S(1)}, bf16[2,512,128]{2,1,0:T(8,128)(2,1)S(1)}, u32[]{:S(2)}, u32[]{:S(2)}) collective-permute-start(bf16[2,512,128]{2,1,0:T(8,128)(2,1)S(1)} %get-tuple-element.145), channel_id=1, source_target_pairs={{0,8},{4,12},{8,0},{12,4},{16,24},{20,28},{24,16},{28,20},{1,9},{5... | collective-permute-start | bytes 786440 | tf_op jit(solution)/shard_map/ppermute | solution.py:36
  347.4 29.1 %collective-permute-start.70 = (bf16[4,384,128]{2,1,0:T(8,128)(2,1)}, bf16[4,384,128]{2,1,0:T(8,128)(2,1)}, u32[]{:S(2)}, u32[]{:S(2)}) collective-permute-start(bf16[4,384,128]{2,1,0:T(8,128)(2,1)} %pad_maximum_fusion.4), channel_id=1, source_target_pairs={{0,8},{4,12},{8,0},{12,4},{16,24},{20,28},{24,16},{28,20},{1,9},{5... | collective-permute-start | bytes 1179656 | tf_op jit(solution)/shard_map/ppermute | solution.py:36
  (81 other events, 676.8 us)

commit v3 on v2

--- a/solution.py
+++ b/solution.py
@@ -36,26 +36,44 @@
     return lax.ppermute(x, axis, [(i, i ^ (1 << bit)) for i in range(size)])
 
 
-def gather_list(x, axis):
-    blocks = {0: x}
-    for bit in reversed(range(bits_of(axis))):
-        for j in list(blocks):
-            blocks[j | 1 << bit] = swap(blocks[j], axis, bit)
-    return [blocks[j] for j in range(len(blocks))]
-
-
-def scatter_bits(blocks, axis, bits):
-    blocks = dict(blocks)
-    for bit in bits:
-        for j in [j for j in blocks if j >> bit & 1]:
-            got = swap(blocks.pop(j).astype(BF16), axis, bit)
-            k = j ^ (1 << bit)
-            blocks[k] = blocks[k].astype(F32) + got.astype(F32)
-    return blocks
-
-
-def scatter_sum_list(blocks, axis):
-    return scatter_bits(enumerate(blocks), axis, range(bits_of(axis)))[0]
+def add_halves(keep, got):
+    def total(a, b):
+        return (keep[a:b].astype(F32) + got[a:b].astype(F32)).astype(BF16)
+
+    size = keep.shape[0]
+    if size == 1:
+        return total(0, 1), None
+    return total(0, size // 2), total(size // 2, size)
+
+
+def block_order(n):
+    bits = n.bit_length() - 1
+    return [sum(((k >> b) & 1) << (bits - 1 - b) for b in range(bits)) for k in range(n)]
+
+
+class Group:
+    def __init__(self, array, held):
+        self.array, self.held = array, held
+
+
+def join(groups, bit, arrays, axis):
+    held, start = [], 0
+    for group in groups:
+        held += [(j | 1 << bit, code, start + first, rows) for j, code, first, rows in group.held]
+        start += group.array.shape[axis]
+    array = arrays[0] if len(arrays) == 1 else jnp.concatenate(arrays, axis=axis)
+    return Group(swap(array, "shard", bit), held)
+
+
+def gather_rows(x, gate=None):
+    rows = x.shape[0]
+    groups = [Group(x, [(0, None, 0, rows)])]
+    for bit in reversed(range(bits_of("shard"))):
+        arrays = [g.array for g in groups]
+        if gate is not None and len(arrays) > 1:
+            arrays[-1] = after(arrays[-1], *gate())
+        groups = groups + [join(groups, bit, arrays, 0)]
+    return groups
 
 
 def parity():
@@ -70,21 +88,22 @@
 
 def fetch_far(send, dim, top, gate):
     got = swap(half_by_replica(send, dim), "shard", top)
-    kept = got if gate is None else after(got, gate())
+    kept = got if gate is None else after(got, gate)
     first, second = jnp.split(kept, 2, axis=dim)
+    size = got.shape[dim]
     return [
-        (1 << top, 0, got),
-        (1 << top, 1, swap(first, "rep", 0)),
-        (1 << top, 2, swap(second, "rep", 1)),
+        Group(got, [(1 << top, 0, 0, size)]),
+        Group(swap(first, "rep", 0), [(1 << top, 1, 0, size // 2)]),
+        Group(swap(second, "rep", 1), [(1 << top, 2, 0, size // 2)]),
     ]
 
 
 def gather_weight(x, gate=None):
     top = bits_of("shard") - 1
-    pieces = [(0, None, x)] + fetch_far(x, 0, top, gate)
+    groups = [Group(x, [(0, None, 0, x.shape[0])])] + fetch_far(x, 0, top, gate)
     for bit in reversed(range(top)):
-        pieces += [(j | 1 << bit, h, swap(a, "shard", bit)) for j, h, a in pieces]
-    return pieces
+        groups = groups + [join(groups, bit, [g.array for g in groups], 0)]
+    return groups
 
 
 def split_weight(x, gate=None):
@@ -95,20 +114,10 @@
         start = ((me & (a.shape[0] - 1)) >> bit ^ 1) << bit
         return lax.dynamic_slice_in_dim(a, start, 1 << bit)
 
-    pieces = [(0, None, x)] + fetch_far(part_for(x, top), 1, top, gate)
+    groups = [Group(x, [(0, None, 0, x.shape[1])])] + fetch_far(part_for(x, top), 1, top, gate)
     for bit in reversed(range(top)):
-        pieces += [(j | 1 << bit, h, swap(part_for(a, bit), "shard", bit)) for j, h, a in pieces]
-    return pieces
-
-
-def add_halves(keep, got):
-    def total(a, b):
-        return (keep[a:b].astype(F32) + got[a:b].astype(F32)).astype(BF16)
-
-    size = keep.shape[0]
-    if size == 1:
-        return total(0, 1), None
-    return total(0, size // 2), total(size // 2, size)
+        groups = groups + [join(groups, bit, [part_for(g.array, bit) for g in groups], 1)]
+    return groups
 
 
 def gated(value, gates, step):
@@ -119,6 +128,13 @@
     for step, bit in enumerate(order):
         keep, send = add_halves(keep, gated(swap(send, "rep", bit), gates, step))
     return keep[0]
+
+
+def replica_spread(x, order):
+    now = x[None]
+    for bit in reversed(order[1:]):
+        now = jnp.concatenate([now, swap(now, "rep", bit)])
+    return now, swap(now, "rep", order[0])
 
 
 class PairReduce:
@@ -153,13 +169,16 @@
 
 
 def turn(x, n):
-    pieces = {0: x}
+    x = x[:, None]
     for bit in reversed(range(n.bit_length() - 1)):
-        for j in list(pieces):
-            half = pieces[j].shape[0] // 2
-            pieces[j | 1 << bit] = swap(pieces[j][half:], "shard", bit)
-            pieces[j] = pieces[j][:half]
-    return jnp.concatenate([pieces[j] for j in range(n)])
+        half = x.shape[0] // 2
+        x = jnp.concatenate([x[:half], swap(x[half:], "shard", bit)], axis=1)
+    return x[0]
+
+
+def from_place(j, n):
+    bits = n.bit_length() - 1
+    return sum(((j >> b) & 1) << (bits - 1 - b) for b in range(bits))
 
 
 def slot_mask(slot, order):
@@ -182,19 +201,39 @@
     return centred * scale, scale
 
 
-def weight_copies(pieces, refs, target, me, sems, rep, by_owner, rows):
+def held_of(groups):
+    return [(g.held, g.array.shape) for g in groups]
+
+
+def arrays_of(groups):
+    return [g.array for g in groups]
+
+
+def pieces_of(held):
+    return sum(len(h) for h, _ in held)
+
+
+def blocks_of(held, refs):
+    found = {}
+    for (pieces, _), ref in zip(held, refs):
+        for j, _, first, rows in pieces:
+            found[j] = ref.at[first : first + rows, :]
+    return [found[j] for j in range(len(found))]
+
+
+def weight_copies(held, refs, target, me, sems, rep, by_owner, rows):
     copies = []
-    for i, ((j, half, shape), ref) in enumerate(zip(pieces, refs)):
-        start = (me ^ j if by_owner else j) * rows
-        count = rows
-        if half is not None:
-            own = (rep ^ (rep >> 1)) & 1
-            count = rows // 2 if half == 0 else rows // 4
-            start = start + (own if half == 0 else 1 - own) * (rows // 2)
-            start = start + (rows // 4 if half == 2 else 0)
+    own = (rep ^ (rep >> 1)) & 1
+    for (pieces, shape), ref in zip(held, refs):
         source = ref.at[me & (shape[0] - 1)] if len(shape) == 3 else ref
-        place = target.at[pl.ds(pl.multiple_of(start, count), count), :]
-        copies.append(pltpu.make_async_copy(source, place, sems.at[i]))
+        for j, code, first, count in pieces:
+            start = (me ^ j if by_owner else j) * rows
+            if code is not None:
+                start = start + (own if code == 0 else 1 - own) * (rows // 2)
+                start = start + (rows // 4 if code == 2 else 0)
+            place = target.at[pl.ds(pl.multiple_of(start, count), count), :]
+            sem = sems.at[len(copies)]
+            copies.append(pltpu.make_async_copy(source.at[first : first + count, :], place, sem))
     return copies
 
 
@@ -304,16 +343,16 @@
 
 
 def attention_kernel(
-    pieces, n, heads, place_ref, cos_ref, sin_ref, idq_ref, idk_ref, *refs
+    tok_held, held, n, heads, place_ref, cos_ref, sin_ref, idq_ref, idk_ref, *refs
 ):
-    tok_refs, refs = refs[:n], refs[n:]
-    piece_refs, refs = refs[: len(pieces)], refs[len(pieces) :]
+    tok_refs, refs = blocks_of(tok_held, refs), refs[len(tok_held) :]
+    piece_refs, refs = refs[: len(held)], refs[len(held) :]
     q_ref, k_ref, v_ref, out_ref, normed_ref, w_ref, sems = refs
     seq, width = q_ref.shape
     rows = seq // n
     me, rep = place_ref[0], place_ref[1]
     copies = weight_copies(
-        pieces, piece_refs, w_ref, me, sems, rep, True, w_ref.shape[0] // n
+        held, piece_refs, w_ref, me, sems, rep, True, w_ref.shape[0] // n
     )
     for c in copies:
         c.start()
@@ -351,11 +390,11 @@
     lax.fori_loop(0, seq // QB, attend, 0, unroll=2)
 
 
-def up_kernel(out_pieces, in_pieces, n, place_ref, *refs):
-    tok_refs, refs = refs[:n], refs[n:]
-    att_refs, refs = refs[:n], refs[n:]
-    out_refs, refs = refs[: len(out_pieces)], refs[len(out_pieces) :]
-    in_refs, refs = refs[: len(in_pieces)], refs[len(in_pieces) :]
+def up_kernel(tok_held, att_held, out_held, in_held, n, place_ref, *refs):
+    tok_refs, refs = blocks_of(tok_held, refs), refs[len(tok_held) :]
+    att_refs, refs = blocks_of(att_held, refs), refs[len(att_held) :]
+    out_refs, refs = refs[: len(out_held)], refs[len(out_held) :]
+    in_refs, refs = refs[: len(in_held)], refs[len(in_held) :]
     hidden_out, normed_out, up_out, in_out, *refs = refs
     tok, att, w_out, w_in, hidden_own, normed, up, *refs = refs
     out_sems, in_sems, att_sems, tok_sems, sems = refs
@@ -365,8 +404,8 @@
     att_copies = [copy(att_refs[j], att.at[j], att_sems.at[j]) for j in range(n)]
     tok_copies = [copy(tok_refs[j], tok.at[j], tok_sems.at[j]) for j in range(n)]
     part = model // n
-    out_copies = weight_copies(out_pieces, out_refs, w_out, me, out_sems, rep, False, part)
-    in_copies = weight_copies(in_pieces, in_refs, w_in, me, in_sems, rep, True, part)
+    out_copies = weight_copies(out_held, out_refs, w_out, me, out_sems, rep, False, part)
+    in_copies = weight_copies(in_held, in_refs, w_in, me, in_sems, rep, True, part)
     for c in att_copies + tok_copies[:1] + out_copies + in_copies + tok_copies[1:]:
         c.start()
     for c in att_copies + out_copies:
@@ -404,10 +443,9 @@
         c.wait()
 
 
-def dup_kernel(n, up_ref, w_in_ref, down_ref, *refs):
-    cot_refs, refs = refs[:n], refs[n:]
-    act_out, dup_out, *refs = refs
-    dnormed_outs, refs = refs[:n], refs[n:]
+def dup_kernel(cot_held, n, up_ref, w_in_ref, down_ref, *refs):
+    cot_refs, refs = blocks_of(cot_held, refs), refs[len(cot_held) :]
+    act_out, dup_out, keep_out, send_out, *refs = refs
     up, cot, w_in, w_down, act, dup, dnormed, in_sem, down_sem, up_sems, cot_sems, sems = refs
     rows, model = cot_refs[0].shape
     padded = w_down.shape[0]
@@ -427,8 +465,11 @@
     for c in up_copies[1:] + cot_copies[1:]:
         c.start()
     sent = []
+    order = block_order(n)
     for j in range(n):
         here = slice(j * rows, (j + 1) * rows)
+        place = order.index(j)
+        target = (keep_out if place < n // 2 else send_out).at[place % (n // 2)]
         up_copies[j].wait()
         gate, lin = up[here, :padded], up[here, padded:]
         phi = 0.5 + 0.5 * lax.erf(gate * (1.0 / math.sqrt(2.0)))
@@ -445,7 +486,7 @@
             in_copy.wait()
         dnormed[j] = dot(dup[here, :], w_in[...], ((1,), (1,))).astype(BF16)
         sent += [
-            copy(dnormed.at[j], dnormed_outs[j], sems.at[3 * j]),
+            copy(dnormed.at[j], target, sems.at[3 * j]),
             copy(act.at[here, :], act_out.at[here, :], sems.at[3 * j + 1]),
             copy(dup.at[here, :], dup_out.at[here, :], sems.at[3 * j + 2]),
         ]
@@ -466,11 +507,16 @@
     return 2 * (ff // LANES) + 1
 
 
-def down_kernel(n, ff, far, place_ref, act, w_down, *refs):
-    cot_refs, refs = refs[:n], refs[n:]
-    keep, send, *refs = refs
-    mlp_refs, refs = refs[:n], refs[n:]
-    (down_sum,) = refs
+def put_block(keep, send, j, value):
+    half = keep.shape[0]
+    place = block_order(2 * half).index(j)
+    target = keep if place < half else send
+    target[place % half] = value.astype(BF16)
+
+
+def down_kernel(cot_held, n, ff, order, place_ref, act, w_down, *refs):
+    cot_refs, refs = blocks_of(cot_held, refs), refs[len(cot_held) :]
+    keep, send, mlp_keep, mlp_send, down_sum = refs
     rows, model = cot_refs[0].shape
     cols = model // (2 * keep.shape[0])
     total = None
@@ -482,11 +528,11 @@
     def write(target, slot, c):
         target[slot] = column_chunk(down_sum, c, cols)[:ff].astype(BF16)
 
-    store_slots(keep, send, place_ref[1], far, write)
+    store_slots(keep, send, place_ref[1], order, write)
     given = w_down.shape[0]
     for j in range(n):
         low = act[j * rows : (j + 1) * rows, 0:given]
-        mlp_refs[j][...] = jnp.dot(low, w_down[...], preferred_element_type=F32).astype(BF16)
+        put_block(mlp_keep, mlp_send, j, jnp.dot(low, w_down[...], preferred_element_type=F32))
 
 
 def write_flows(total, starts, counts, orders, flows, index, rep):
@@ -522,9 +568,35 @@
         write_flows(in_sum, starts, counts, orders, flows, me ^ owner, rep)
 
 
-def add_kernel(a_ref, b_ref, c_ref, d_ref, mine_ref, other_ref):
-    mine_ref[...] = a_ref[...].astype(F32) + b_ref[...].astype(F32)
-    other_ref[...] = (c_ref[...].astype(F32) + d_ref[...].astype(F32)).astype(BF16)
+def add_kernel(keep_ref, got_ref, mine_ref, other_ref):
+    mine_ref[...] = keep_ref[0].astype(F32) + got_ref[0].astype(F32)
+    other_ref[...] = (keep_ref[1].astype(F32) + got_ref[1].astype(F32)).astype(BF16)
+
+
+def near_sums(keep, send, name):
+    bits = bits_of("shard")
+    for bit in range(bits - 2):
+        keep, send = add_halves(keep, swap(send, "shard", bit))
+    _, rows, model = keep.shape
+    return pl.pallas_call(
+        add_kernel,
+        out_shape=[
+            jax.ShapeDtypeStruct((rows, model), F32),
+            jax.ShapeDtypeStruct((rows, model), BF16),
+        ],
+        compiler_params=pltpu.CompilerParams(vmem_limit_bytes=16 << 20),
+        name=name,
+    )(keep, swap(send, "shard", bits - 2))
+
+
+def output_kernel(mine, got, hidden, out_ref):
+    out_ref[...] = (hidden[...] + mine[...] + got[...].astype(F32)).astype(BF16)
+
+
+def input_kernel(mine, got, tokens, dhidden, out_ref):
+    hat, scale = normalise(tokens[...].astype(F32))
+    e = mine[...] + got[...].astype(F32)
+    out_ref[...] = dhidden[...] + norm_backward(e, hat, scale)
 
 
 def norm_back_kernel(mine, got, hidden, cotangent, dhidden, dproj):
@@ -535,8 +607,8 @@
     dproj[...] = value.astype(BF16)
 
 
-def attention_back_kernel(n, heads, far, place_ref, *refs):
-    dproj_refs, refs = refs[:n], refs[n:]
+def attention_back_kernel(held, n, heads, order, place_ref, *refs):
+    dproj_refs, refs = blocks_of(held, refs), refs[len(held) :]
     w_out, att, q_ref, k_ref, v_ref, cos_ref, sin_ref, idq_ref, idk_ref, *refs = refs
     dqkv, out_keep, out_send, da, dk, dv, out_sum = refs
     me, rep = place_ref[0], place_ref[1]
@@ -561,7 +633,7 @@
     def write_out(target, slot, c):
         target[slot] = column_chunk(out_sum, c, cols).astype(BF16)
 
-    store_slots(out_keep, out_send, rep, far, write_out)
+    store_slots(out_keep, out_send, rep, order, write_out)
     masks = head_masks(heads, width)
 
     def back(i, carry):
@@ -607,11 +679,11 @@
         write_flows(qkv_sum, starts, counts, orders, flows, me ^ owner, rep)
 
 
-def project_back_kernel(n, place_ref, dqkv, w_qkv, *out_refs):
-    rows = out_refs[0].shape[0]
+def project_back_kernel(n, place_ref, dqkv, w_qkv, keep, send):
+    rows = keep.shape[1]
     for j in range(n):
         at = pl.ds(pl.multiple_of((place_ref[0] ^ j) * rows, rows), rows)
-        out_refs[j][...] = dot(dqkv[at, :], w_qkv[...], ((1,), (1,))).astype(BF16)
+        put_block(keep, send, j, dot(dqkv[at, :], w_qkv[...], ((1,), (1,))))
 
 
 def place_piece(canvas, piece, offset, valid):
@@ -643,7 +715,7 @@
         while t >= counts[f]:
             t -= counts[f]
             f += 1
-        slot, index = slots[f], (me ^ owner) * counts[f] + t
+        slot, index = slots[f], from_place(me ^ owner, n) * counts[f] + t
         at = slot & (half - 1)
         now, got = parts[2 * f][at, index], parts[2 * f + 1][at, index]
         return jnp.where(slot < half, now, got).astype(F32)
@@ -790,9 +862,9 @@
     gain2 = ln2_gain.astype(F32)[:, None]
     qkv_to = split_columns(w_qkv, gain1, n, 3, head_cols, width)
     in_to = split_columns(w_in, gain2, n, 2, ff, padded)
-    qkv_pieces = split_weight(qkv_to)
-
-    toks = gather_list(tokens, "shard")
+    toks = gather_rows(tokens)
+    qkv_groups = split_weight(qkv_to)
+    out_groups = gather_weight(w_out)
 
     lane = jnp.arange(width, dtype=jnp.int32) % HEAD_DIM
     half = HEAD_DIM // 2
@@ -807,12 +879,15 @@
         jnp.pad(ids, (HALF, HALF), constant_values=-1)[None],
     )
 
-    def about(pieces):
-        return [(j, h, a.shape) for j, h, a in pieces]
-
     queries, keys, values, attended, normed1, qkv_w = pl.pallas_call(
-        functools.partial(attention_kernel, about(qkv_pieces), n, heads),
-        in_specs=[SMEM_SPEC] + [VMEM_SPEC] * (4 + n) + [ANY_SPEC] * len(qkv_pieces),
+        ordered(
+            functools.partial(attention_kernel, held_of(toks), held_of(qkv_groups), n, heads),
+            5 + len(toks) + len(qkv_groups),
+            2,
+        ),
+        in_specs=[SMEM_SPEC]
+        + [VMEM_SPEC] * (4 + len(toks))
+        + [ANY_SPEC] * (len(qkv_groups) + 2),
         out_shape=(
             shape((seq, width), BF16),
             shape((seq + 2 * HALF, width), BF16),
@@ -821,25 +896,21 @@
             shape((seq, model), BF16),
             shape((model, 3 * width), BF16),
         ),
-        scratch_shapes=[pltpu.SemaphoreType.DMA((len(qkv_pieces),))],
+        scratch_shapes=[pltpu.SemaphoreType.DMA((pieces_of(held_of(qkv_groups)),))],
         compiler_params=params,
         cost_estimate=work(40 * seq * model * width),
         name="attention",
-    )(place, *tables, *toks, *[a for _, _, a in qkv_pieces])
-
-    atts = gather_list(attended[:, :head_cols], "shard")
-
-    def once_attended():
-        return atts[1]
-
-    far_done = [toks[n // 2], qkv_pieces[1][2]]
-    out_pieces = gather_weight(after(w_out, *far_done), once_attended)
-    in_pieces = split_weight(after(in_to, *far_done), once_attended)
-    cots = gather_list(after(cotangent, atts[n // 2]), "shard")
-    blocks = [shape((rows, model), BF16)] * n
+    )(place, *tables, *arrays_of(toks + qkv_groups + out_groups[2:4]))
+
+    far_done = [toks[1].array, qkv_groups[1].array, out_groups[1].array]
+    in_groups = split_weight(after(in_to, *far_done), attended)
+    atts = gather_rows(attended[:, :head_cols])
+    block_shape = shape((n // 2, rows, model), BF16)
     hidden, normed2, up, in_w = pl.pallas_call(
-        functools.partial(up_kernel, about(out_pieces), about(in_pieces), n),
-        in_specs=[SMEM_SPEC] + [ANY_SPEC] * (2 * n + len(out_pieces) + len(in_pieces)),
+        functools.partial(
+            up_kernel, held_of(toks), held_of(atts), held_of(out_groups), held_of(in_groups), n
+        ),
+        in_specs=[SMEM_SPEC] + [ANY_SPEC] * len(toks + atts + out_groups + in_groups),
         out_specs=[ANY_SPEC] * 4,
         out_shape=[
             shape((rows, model), F32),
@@ -855,8 +926,8 @@
             pltpu.VMEM((rows, model), F32),
             pltpu.VMEM((seq, model), BF16),
             pltpu.VMEM((seq, 2 * padded), F32),
-            pltpu.SemaphoreType.DMA((len(out_pieces),)),
-            pltpu.SemaphoreType.DMA((len(in_pieces),)),
+            pltpu.SemaphoreType.DMA((pieces_of(held_of(out_groups)),)),
+            pltpu.SemaphoreType.DMA((pieces_of(held_of(in_groups)),)),
             pltpu.SemaphoreType.DMA((n,)),
             pltpu.SemaphoreType.DMA((n,)),
             pltpu.SemaphoreType.DMA((2 * n + 2,)),
@@ -864,13 +935,14 @@
         compiler_params=params,
         cost_estimate=work(12 * seq * model * padded),
         name="up_projection",
-    )(place, *toks, *atts, *[a for _, _, a in out_pieces], *[a for _, _, a in in_pieces])
+    )(place, *arrays_of(toks + atts + out_groups + in_groups))
+    cots = gather_rows(after(cotangent, atts[1].array), lambda: (up,))
     down_w = jnp.pad(w_down, ((0, -ff % 16), (0, 0)))
-    act, dup, *dnormed2_blocks = pl.pallas_call(
-        functools.partial(dup_kernel, n),
-        in_specs=[ANY_SPEC] * (3 + n),
-        out_specs=[ANY_SPEC] * (2 + n),
-        out_shape=[shape((seq, padded), BF16), shape((seq, 2 * padded), BF16)] + blocks,
+    act, dup, dnormed2_keep, dnormed2_send = pl.pallas_call(
+        functools.partial(dup_kernel, held_of(cots), n),
+        in_specs=[ANY_SPEC] * (3 + len(cots)),
+        out_specs=[ANY_SPEC] * 4,
+        out_shape=[shape((seq, padded), BF16), shape((seq, 2 * padded), BF16)] + [block_shape] * 2,
         scratch_shapes=[
             pltpu.VMEM((seq, 2 * padded), F32),
             pltpu.VMEM((n, rows, model), BF16),
@@ -888,33 +960,22 @@
         compiler_params=params,
         cost_estimate=work(14 * seq * model * padded),
         name="dup",
-    )(up, in_w, down_w, *cots)
+    )(up, in_w, down_w, *arrays_of(cots))
 
     slots = replicas // 2
     chunk = part // replicas
     lanes = max(LANES, model // replicas)
     tiles = up_tiles(ff)
-    second = max(1, tiles * 3 // 11)
-    in_counts = [tiles - second, second]
     orders = [near, far]
+    in_counts = [tiles - tiles // 2, tiles // 2]
     in_shapes = [shape((slots, n * c, chunk, LANES), BF16) for c in in_counts for _ in range(2)]
     down_shape = shape((slots, ff, lanes), BF16)
-
     top = bits_of("shard") - 1
-    sums = scatter_bits(enumerate(dnormed2_blocks), "shard", range(top - 1))
-    low, high = 1 << (top - 1), 1 << top
-    mine, other = pl.pallas_call(
-        add_kernel,
-        in_specs=[VMEM_SPEC] * 4,
-        out_shape=[shape((rows, model), F32), shape((rows, model), BF16)],
-        compiler_params=pltpu.CompilerParams(vmem_limit_bytes=16 << 20),
-        name="near_sum",
-    )(
-        sums[0],
-        swap(sums[low].astype(BF16), "shard", top - 1),
-        sums[high],
-        swap(sums[low | high].astype(BF16), "shard", top - 1),
-    )
+
+    def flow_rows(a):
+        return a.reshape(a.shape[0], -1, LANES)
+
+    mine, other = near_sums(dnormed2_keep, dnormed2_send, "near_sum_2")
     in_flows = pl.pallas_call(
         ordered(functools.partial(in_kernel, n, ff, in_counts, orders), 3, 1),
         in_specs=[SMEM_SPEC] + [VMEM_SPEC] * 2 + [ANY_SPEC],
@@ -924,9 +985,6 @@
         cost_estimate=work(8 * seq * model * padded),
         name="in_gradient",
     )(place, normed2, dup, other)
-    def flow_rows(a):
-        return a.reshape(a.shape[0], -1, LANES)
-
     in_flows = [flow_rows(a) for a in in_flows]
     in_reduce = PairReduce(in_flows[:2], in_flows[2:], orders)
     dhidden, dproj = pl.pallas_call(
@@ -936,22 +994,27 @@
         compiler_params=pltpu.CompilerParams(vmem_limit_bytes=24 << 20),
         name="norm_back",
     )(mine, swap(other, "shard", top), hidden, cotangent, in_flows[0])
-    down_keep, down_send, *mlp_blocks = pl.pallas_call(
-        ordered(functools.partial(down_kernel, n, ff, far), 3 + n, 1),
-        in_specs=[SMEM_SPEC] + [VMEM_SPEC] * (2 + n) + [ANY_SPEC],
-        out_shape=[down_shape, down_shape] + blocks,
+    down_keep, down_send, mlp_keep, mlp_send = pl.pallas_call(
+        ordered(functools.partial(down_kernel, held_of(cots), n, ff, far), 3 + len(cots), 1),
+        in_specs=[SMEM_SPEC] + [VMEM_SPEC] * (2 + len(cots)) + [ANY_SPEC],
+        out_shape=[down_shape] * 2 + [block_shape] * 2,
         scratch_shapes=[pltpu.VMEM((padded, model), F32)],
         compiler_params=params,
         cost_estimate=work(8 * seq * model * padded),
         name="down_gradient",
-    )(place, act, down_w, *cots, dproj)
-    dprojs = gather_list(dproj, "shard")
-    in_reduce.step(0, [dprojs[n // 2]])
+    )(place, act, down_w, *arrays_of(cots), dproj)
+    dprojs = gather_rows(dproj)
+    mlp_mine, mlp_other = near_sums(mlp_keep, mlp_send, "near_sum_mlp")
+    in_reduce.step(0, [dprojs[1].array])
 
     out_shape = shape((slots, part, lanes), BF16)
     dqkv, out_keep, out_send = pl.pallas_call(
-        ordered(functools.partial(attention_back_kernel, n, heads, far), n + 10, 3),
-        in_specs=[SMEM_SPEC] + [VMEM_SPEC] * (n + 9) + [ANY_SPEC] * 3,
+        ordered(
+            functools.partial(attention_back_kernel, held_of(dprojs), n, heads, far),
+            len(dprojs) + 10,
+            3,
+        ),
+        in_specs=[SMEM_SPEC] + [VMEM_SPEC] * (len(dprojs) + 9) + [ANY_SPEC] * 3,
         out_shape=[shape((seq, 3 * width), BF16), out_shape, out_shape],
         scratch_shapes=[
             pltpu.VMEM((seq, width), BF16),
@@ -962,36 +1025,56 @@
         compiler_params=params,
         cost_estimate=work(40 * seq * model * width),
         name="attention_back",
-    )(place, *dprojs, w_out, attended, queries, keys, values, *tables, down_keep, in_reduce.p[1], in_reduce.q[1])
-
-    mlp_blocks = [after(b, dprojs[n // 2]) for b in mlp_blocks]
-    mlp = scatter_sum_list(mlp_blocks, "shard")
-    output = (hidden + mlp).astype(BF16)
+    )(
+        place,
+        *arrays_of(dprojs),
+        w_out,
+        attended,
+        queries,
+        keys,
+        values,
+        *tables,
+        mlp_other,
+        in_reduce.p[1],
+        in_reduce.q[1],
+    )
 
     qkv_tiles = 3 * width // LANES
     qkv_counts = [qkv_tiles - qkv_tiles // 3, qkv_tiles // 3]
     in_reduce.step(1, [dqkv])
+    down_reduce = add_halves(down_keep, after(swap(down_send, "rep", far[0]), dqkv))
     qkv_flows = pl.pallas_call(
-        ordered(functools.partial(qkv_kernel, n, qkv_counts, orders), 3, 2),
-        in_specs=[SMEM_SPEC] + [VMEM_SPEC] * 2 + [ANY_SPEC] * 2,
+        ordered(functools.partial(qkv_kernel, n, qkv_counts, orders), 3, 3),
+        in_specs=[SMEM_SPEC] + [VMEM_SPEC] * 2 + [ANY_SPEC] * 3,
         out_shape=[shape((slots, n * c, chunk, LANES), BF16) for c in qkv_counts for _ in range(2)],
         scratch_shapes=[pltpu.VMEM((part, 3 * width), F32)],
         compiler_params=params,
         cost_estimate=work(12 * seq * model * width),
         name="qkv_gradient",
-    )(place, normed1, dqkv, in_reduce.p[1], in_reduce.q[1])
+    )(place, normed1, dqkv, in_reduce.p[1], in_reduce.q[1], down_reduce[1])
     qkv_flows = [flow_rows(a) for a in qkv_flows]
-    dnormed1_blocks = pl.pallas_call(
+    output = pl.pallas_call(
+        ordered(output_kernel, 3, 1),
+        in_specs=[VMEM_SPEC] * 3 + [ANY_SPEC],
+        out_shape=shape((rows, model), BF16),
+        compiler_params=pltpu.CompilerParams(vmem_limit_bytes=16 << 20),
+        name="output",
+    )(mlp_mine, swap(mlp_other, "shard", top), hidden, qkv_flows[0])
+    dnormed1_keep, dnormed1_send = pl.pallas_call(
         ordered(functools.partial(project_back_kernel, n), 3, 1),
         in_specs=[SMEM_SPEC] + [VMEM_SPEC] * 2 + [ANY_SPEC],
-        out_shape=blocks,
+        out_shape=[block_shape] * 2,
         compiler_params=params,
         cost_estimate=work(6 * seq * model * width),
         name="project_back",
-    )(place, dqkv, qkv_w, qkv_flows[0])
-    dnormed1 = scatter_sum_list(dnormed1_blocks, "shard")
-    hat1, scale1 = normalise(tokens.astype(F32))
-    input_grad = dhidden + norm_backward(dnormed1, hat1, scale1)
+    )(place, dqkv, qkv_w, output)
+    mine, other = near_sums(dnormed1_keep, dnormed1_send, "near_sum_1")
+    input_grad = pl.pallas_call(
+        input_kernel,
+        out_shape=shape((rows, model), F32),
+        compiler_params=pltpu.CompilerParams(vmem_limit_bytes=24 << 20),
+        name="input_grad",
+    )(mine, swap(other, "shard", top), tokens, dhidden)
 
     def turned(p, q, counts):
         sizes = [c * chunk for c in counts]
@@ -1000,23 +1083,22 @@
         return whole[:, : sizes[0]].reshape(-1, LANES), whole[:, sizes[0] :].reshape(-1, LANES)
 
     def tiles_of(pair, count):
-        rows = n * count * chunk
-        return [a[:, :rows].reshape(a.shape[0], n * count, chunk, LANES) for a in pair]
-
-    attention_done = [qkv_flows[0], dnormed1_blocks[0]]
-    down_share = replica_reduce(down_keep, down_send, far, [[dqkv], attention_done])
-    in_p, in_q = turned(*in_reduce.finish([attention_done]), in_counts)
-    in_p, in_q = pair_gather(jnp.concatenate([in_p, down_share]), in_q, orders)
+        size = n * count * chunk
+        return [a[:, :size].reshape(a.shape[0], n * count, chunk, LANES) for a in pair]
+
+    in_p, in_q = turned(*in_reduce.finish([[other]]), in_counts)
+    in_p, in_q = pair_gather(in_p, in_q, orders)
+    down_share = replica_reduce(*down_reduce, far[1:], [[other]])
+    down_pair = replica_spread(down_share, far)
 
     split = qkv_flows[2].shape[1]
     qkv_q = [jnp.concatenate(x, axis=1) for x in zip(qkv_flows[2:], (out_keep, out_send))]
-    qkv_reduce = PairReduce(qkv_flows[:2], qkv_q, orders)
-    qkv_reduce.step(0)
-    qkv_reduce.step(1)
-    qkv_p, qkv_q = qkv_reduce.finish()
-    out_share = qkv_q[split:]
-    qkv_p, qkv_q = turned(qkv_p, qkv_q[:split], qkv_counts)
-    qkv_p, qkv_q = pair_gather(qkv_p, jnp.concatenate([qkv_q, out_share]), orders)
+    att_reduce = PairReduce(qkv_flows[:2], qkv_q, orders)
+    att_reduce.step(0, [other])
+    att_reduce.step(1, [input_grad])
+    att_p, att_q = att_reduce.finish()
+    qkv_p, qkv_q = turned(att_p, att_q[:split], qkv_counts)
+    att_p, att_q = pair_gather(qkv_p, jnp.concatenate([qkv_q, att_q[split:]]), orders)
 
     in_total, ln2_total = columns_out(
         place,
@@ -1028,11 +1110,11 @@
         n,
         ff=ff,
     )
-    down_total = rows_out(place, in_p, n * in_counts[0] * chunk, ff, model, near)
-    out_total = rows_out(place, qkv_q, split, part, model, far)
+    down_total = rows_out(place, down_pair, 0, ff, model, far)
+    out_total = rows_out(place, att_q, split, part, model, far)
     qkv_total, ln1_total = columns_out(
         place,
-        [tiles_of(qkv_p, qkv_counts[0]), tiles_of(qkv_q, qkv_counts[1])],
+        [tiles_of(att_p, qkv_counts[0]), tiles_of(att_q, qkv_counts[1])],
         qkv_counts,
         orders,
         w_qkv,

time: 395 us -> 355 us (0.90); the launches traced: 388 us -> 352 us
  waiting for transfers between devices: 188 us -> 148 us
  Pallas kernels: 94.9 us -> 109 us
  other arithmetic: 30.1 us -> 18.6 us
    ppermute x71 -> x56, waiting for transfers between devices: 188 us -> 148 us  [swap(): return lax.ppermute(x, axis, [(i, i ^ 1 << bit) for i in range(size)])]
    pallas_call x6 -> x10, Pallas kernels: 59.5 us -> 71.4 us  [the longest x1 18.3 us: shards(): pl.pallas_call(ordered(functools.partial(down_kernel, held_of(cots), n, f...]
    convert_element_type x12 -> x13, other arithmetic: 10.2 us -> 3.67 us  [total(): return (keep[a:b].astype(F32) + got[a:b].astype(F32)).astype(BF16)]
    concatenate x4 -> x11, other arithmetic: 0.06 us -> 4.5 us  [the longest x7 3.51 us: join(): jnp.concatenate(arrays, axis=axis)]
    ppermute x71 -> x56, starting transfers between devices: 51 us -> 53.6 us  [swap(): return lax.ppermute(x, axis, [(i, i ^ 1 << bit) for i in range(size)])]
    unnamed x84 -> x90, local copies, waits for them, and re-layouts: 11.5 us -> 13.7 us
  transfers between devices with their start and end apart: 71 -> 56, of which waited for: 25 -> 27; matrix products, arithmetic and copies ran while one was open for 10% -> 7% of each run, Pallas kernels for 18% -> 24%
where the time goes in v3:
time: 355 us; the launch traced here: 352 us
  waiting for transfers between devices  148 us (42%)
  Pallas kernels  109 us (31%)
  starting transfers between devices  53.6 us (15%)
  local copies, waits for them, and re-layouts  21.3 us (6%)
  other arithmetic  18.6 us (5%)
    ppermute x56, waiting for transfers between devices, swap(): return lax.ppermute(x, axis, [(i, i ^ 1 << bit) for i in range(size)])  148 us
    ppermute x56, starting transfers between devices, swap(): return lax.ppermute(x, axis, [(i, i ^ 1 << bit) for i in range(size)])  53.6 us
    pallas_call x1, Pallas kernels, shards(): pl.pallas_call(ordered(functools.partial(down_kernel, held_of(cots), n, f...  18.3 us
    unnamed x90, local copies, waits for them, and re-layouts  13.7 us
    pallas_call x1, Pallas kernels, shards(): pl.pallas_call(ordered(functools.partial(attention_back_kernel, held_of(d...  13.4 us
    pallas_call x1, Pallas kernels, shards(): pl.pallas_call(ordered(functools.partial(attention_kernel, held_of(toks),...  12.5 us
    pallas_call x1, Pallas kernels, shards(): pl.pallas_call(functools.partial(dup_kernel, held_of(cots), n), in_specs=...  12 us
    pallas_call x2, Pallas kernels, columns_out(): pl.pallas_call(functools.partial(columns_out_kernel, n, ff, head_cols, wi...  12 us
  transfers between devices with their start and end apart: 56, of which 27 were waited for; matrix products, arithmetic and copies ran while one was open for 7% of the time, Pallas kernels for 24%

profile of v3, /device:TPU:0, one launch (start us, length us, event | category | flops | bytes accessed | tf_op | source)
XLA Modules:
  0.0 352.0 jit_solution(7321103379204521850)
XLA Ops:
  4.4 2.9 collective-permute-start.2
  10.1 4.8 %sine_multiply_fusion = (f32[1024,256]{1,0:T(8,128)}, f32[1024,256]{1,0:T(8,128)}) fusion(f32[256]{0:T(256)S(1)} %get-tuple-element.168, f32[256]{0:T(256)S(1)} %get-tuple-element.169), kind=kLoop, calls=%fused_computation.6 | loop fusion | flops 524288 | bytes 2099200 | tf_op jit(solution)/shard_map/mul | solution.py:877
  21.3 12.3 %collective-permute-done.refs_6_.refs_1_ = bf16[256,1024]{1,0:T(8,128)(2,1)} collective-permute-done((bf16[256,1024]{1,0:T(8,128)(2,1)S(1)}, bf16[256,1024]{1,0:T(8,128)(2,1)}, u32[]{:S(2)}, u32[]{:S(2)}) %collective-permute-start) | collective-permute-done | bytes 524320 | tf_op jit(solution)/shard_map/ppermute | solution.py:36
  48.4 12.5 %attention.1 = (bf16[1024,256]{1,0:T(8,128)(2,1)S(1)}, bf16[1152,256]{1,0:T(8,128)(2,1)}, bf16[1152,256]{1,0:T(8,128)(2,1)}, bf16[1024,256]{1,0:T(8,128)(2,1)}, ...) custom-call(s32[2]{0:T(128)S(1)} %pad_add_fusion.refs_0_.place_ref, ...), custom_call_target="tpu_custom_call" | custom-call | flops 10737418240 | bytes 4194304 | tf_op jit(solution)/shard_map/attention/pallas_call | solution.py:882
  65.8 6.9 %collective-permute-done.14.refs_14_ = bf16[2,64,1536]{2,1,0:T(8,128)(2,1)S(1)} collective-permute-done((bf16[2,64,1536]{2,1,0:T(8,128)(2,1)S(1)}, bf16[2,64,1536]{2,1,0:T(8,128)(2,1)S(1)}, u32[]{:S(2)}, u32[]{:S(2)}) %collective-permute-start.14) | collective-permute-done | bytes 393248 | tf_op jit(solution)/shard_map/ppermute | solution.py:36
  80.7 11.9 %up_projection.1 = (f32[256,1024]{1,0:T(8,128)}, bf16[1024,1024]{1,0:T(8,128)(2,1)}, f32[1024,1536]{1,0:T(8,128)}, bf16[1024,1536]{1,0:T(8,128)(2,1)}) custom-call(s32[2]{0:T(128)S(1)} %pad_add_fusion.refs_0_.place_ref, bf16[256,1024]{1,0:T(8,128)(2,1)S(1)} %copy-done.10, bf16[256,1024]{1,0:T(8,128)(2,1)} %collective-permute-done.refs_6_.refs_1_, ...), custom_call_target="tpu_custom_call" | custom-call | flops 9663676416 | bytes 4194304 | tf_op jit(solution)/shard_map/up_projection/pallas_call | solution.py:909
  96.3 12.0 %dup.1 = (bf16[1024,768]{1,0:T(8,128)(2,1)}, bf16[1024,1536]{1,0:T(8,128)(2,1)}, bf16[2,256,1024]{2,1,0:T(8,128)(2,1)}, bf16[2,256,1024]{2,1,0:T(8,128)(2,1)}) custom-call(f32[1024,1536]{1,0:T(8,128)} %get-tuple-element.69.up_ref, bf16[1024,1536]{1,0:T(8,128)(2,1)} %get-tuple-element.70.w_in_ref, bf16[656,1024]{1,0:T(8,128)(2,1)} %refs_2_.1, ...), custom_call_target="tpu_custom_call" | custom-call | flops 11274289152 | bytes 4194304 | tf_op jit(solution)/shard_map/dup/pallas_call | solution.py:941
  108.5 2.7 collective-permute-done.18.got_ref
  114.3 7.5 %in_gradient.1 = (bf16[4,24,32,128]{3,2,1,0:T(8,128)(2,1)}, bf16[4,24,32,128]{3,2,1,0:T(8,128)(2,1)}, bf16[4,20,32,128]{3,2,1,0:T(8,128)(2,1)S(1)}, bf16[4,20,32,128]{3,2,1,0:T(8,128)(2,1)S(1)}) custom-call(s32[2]{0:T(128)S(1)} %pad_add_fusion.refs_0_.place_ref, bf16[1024,1024]{1,0:T(8,128)(2,1)} %get-tuple-element.79.refs_1_, ...), custom_call_target="tpu_custom_call" | custom-call | flops 6442450944 | bytes 4194304 | tf_op jit(solution)/shard_map/in_gradient/pallas_call | solution.py:979
  124.1 2.7 collective-permute-done.19.refs_1_
  130.2 18.3 %down_gradient.1 = (bf16[4,656,128]{2,1,0:T(8,128)(2,1)}, bf16[4,656,128]{2,1,0:T(8,128)(2,1)}, bf16[2,256,1024]{2,1,0:T(8,128)(2,1)}, bf16[2,256,1024]{2,1,0:T(8,128)(2,1)}) custom-call(s32[2]{0:T(128)S(1)} %pad_add_fusion.refs_0_.place_ref, bf16[1024,768]{1,0:T(8,128)(2,1)} %get-tuple-element.73.refs_1_, bf16[656,1024]{1,0:T(8,128)(2,1)} %refs_2_.1, ...), custom_call_target="tpu_custom_call" | custom-call | flops 6442450944 | bytes 4194304 | tf_op jit(solution)/shard_map/down_gradient/pallas_call | solution.py:997
  155.2 13.4 %attention_back.1 = (bf16[1024,768]{1,0:T(8,128)(2,1)}, bf16[4,256,128]{2,1,0:T(8,128)(2,1)S(1)}, bf16[4,256,128]{2,1,0:T(8,128)(2,1)S(1)}) custom-call(s32[2]{0:T(128)S(1)} %pad_add_fusion.refs_0_.place_ref, bf16[256,1024]{1,0:T(8,128)(2,1)S(1)} %get-tuple-element.82.refs_6_.refs_1_, bf16[256,1024]{1,0:T(8,128)(2,1)} %copy-done.35, ...), custom_call_target="tpu_custom_call" | custom-call | flops 10737418240 | bytes 4194304 | tf_op jit(solution)/shard_map/attention_back/pallas_call | solution.py:1011
  168.6 7.0 %collective-permute-done.26 = bf16[2,768,128]{2,1,0:T(8,128)(2,1)S(1)} collective-permute-done((bf16[2,768,128]{2,1,0:T(8,128)(2,1)S(1)}, bf16[2,768,128]{2,1,0:T(8,128)(2,1)S(1)}, u32[]{:S(2)}, u32[]{:S(2)}) %collective-permute-start.26) | collective-permute-done | bytes 393248 | tf_op jit(solution)/shard_map/ppermute | solution.py:36
  178.0 4.8 %qkv_gradient.1 = (bf16[4,16,32,128]{3,2,1,0:T(8,128)(2,1)S(1)}, bf16[4,16,32,128]{3,2,1,0:T(8,128)(2,1)}, bf16[4,8,32,128]{3,2,1,0:T(8,128)(2,1)S(1)}, bf16[4,8,32,128]{3,2,1,0:T(8,128)(2,1)S(1)}) custom-call(s32[2]{0:T(128)S(1)} %pad_add_fusion.refs_0_.place_ref, bf16[1024,1024]{1,0:T(8,128)(2,1)} %get-tuple-element.87.refs_1_, ...), custom_call_target="tpu_custom_call" | custom-call | flops 3221225472 | bytes 4194304 | tf_op jit(solution)/shard_map/qkv_gradient/pallas_call | solution.py:1046
  184.8 4.8 %project_back.1 = (bf16[2,256,1024]{2,1,0:T(8,128)(2,1)S(1)}, bf16[2,256,1024]{2,1,0:T(8,128)(2,1)}) custom-call(s32[2]{0:T(128)S(1)} %pad_add_fusion.refs_0_.place_ref, bf16[1024,768]{1,0:T(8,128)(2,1)} %get-tuple-element.96.refs_2_.refs_1_, bf16[1024,768]{1,0:T(8,128)(2,1)} %get-tuple-element.103.refs_2_, bf16[256,1024]{1,0:T(8,128)(2,1)S(1)} %copy-done.16), custom_call_target="tpu_custom_call" | custom-call | flops 1610612736 | bytes 4194304 | tf_op jit(solution)/shard_map/project_back/pallas_call | solution.py:1063
  196.2 13.6 %collective-permute-done.43 = bf16[1,1408,128]{2,1,0:T(8,128)(2,1)S(1)} collective-permute-done((bf16[1,1408,128]{2,1,0:T(8,128)(2,1)S(1)}, bf16[1,1408,128]{2,1,0:T(8,128)(2,1)S(1)}, u32[]{:S(2)}, u32[]{:S(2)}) %collective-permute-start.43) | collective-permute-done | bytes 360480 | tf_op jit(solution)/shard_map/ppermute | solution.py:36
  216.2 10.9 %collective-permute-done.44 = bf16[2,1,352,128]{3,2,0,1:T(8,128)(2,1)S(1)} collective-permute-done((bf16[2,1,352,128]{3,2,0,1:T(8,128)(2,1)S(1)}, bf16[2,1,352,128]{3,2,0,1:T(8,128)(2,1)S(1)}, u32[]{:S(2)}, u32[]{:S(2)}) %collective-permute-start.44) | collective-permute-done | bytes 180256 | tf_op jit(solution)/shard_map/ppermute | solution.py:36
  229.3 3.0 collective-permute-start.52
  232.3 16.1 %collective-permute-done.35 = bf16[1,1024,128]{2,1,0:T(8,128)(2,1)S(1)} collective-permute-done((bf16[1,1024,128]{2,1,0:T(8,128)(2,1)S(1)}, bf16[1,1024,128]{2,1,0:T(8,128)(2,1)S(1)}, u32[]{:S(2)}, u32[]{:S(2)}) %collective-permute-start.35) | collective-permute-done | bytes 262176 | tf_op jit(solution)/shard_map/ppermute | solution.py:36
  249.3 4.0 %collective-permute-done.36 = bf16[2,1,192,128]{3,2,0,1:T(8,128)(2,1)S(1)} collective-permute-done((bf16[2,1,192,128]{3,2,0,1:T(8,128)(2,1)S(1)}, bf16[2,1,192,128]{3,2,0,1:T(8,128)(2,1)S(1)}, u32[]{:S(2)}, u32[]{:S(2)}) %collective-permute-start.36) | collective-permute-done | bytes 98336 | tf_op jit(solution)/shard_map/ppermute | solution.py:36
  253.3 15.6 %collective-permute-done.52 = bf16[1,656,128]{2,1,0:T(8,128)(2,1)S(1)} collective-permute-done((bf16[1,656,128]{2,1,0:T(8,128)(2,1)S(1)}, bf16[1,656,128]{2,1,0:T(8,128)(2,1)S(1)}, u32[]{:S(2)}, u32[]{:S(2)}) %collective-permute-start.52) | collective-permute-done | bytes 167968 | tf_op jit(solution)/shard_map/ppermute | solution.py:36
  269.2 3.0 collective-permute-start.38
  272.2 8.1 %collective-permute-done.53 = bf16[1,656,128]{2,1,0:T(8,128)(2,1)S(1)} collective-permute-done((bf16[1,656,128]{2,1,0:T(8,128)(2,1)S(1)}, bf16[1,656,128]{2,1,0:T(8,128)(2,1)S(1)}, u32[]{:S(2)}, u32[]{:S(2)}) %collective-permute-start.53) | collective-permute-done | bytes 167968 | tf_op jit(solution)/shard_map/ppermute | solution.py:36
  282.6 3.0 collective-permute-done.38
  286.9 4.3 %collective-permute-done.54 = bf16[2,656,128]{2,1,0:T(8,128)(2,1)S(1)} collective-permute-done((bf16[2,656,128]{2,1,0:T(8,128)(2,1)S(1)}, bf16[2,656,128]{2,1,0:T(8,128)(2,1)S(1)}, u32[]{:S(2)}, u32[]{:S(2)}) %collective-permute-start.54) | collective-permute-done | bytes 335904 | tf_op jit(solution)/shard_map/ppermute | solution.py:36
  295.5 2.7 collective-permute-done.49
  299.1 4.7 %collective-permute-done.41 = bf16[2,512,128]{2,1,0:T(8,128)(2,1)S(1)} collective-permute-done((bf16[2,512,128]{2,1,0:T(8,128)(2,1)S(1)}, bf16[2,512,128]{2,1,0:T(8,128)(2,1)S(1)}, u32[]{:S(2)}, u32[]{:S(2)}) %collective-permute-start.41) | collective-permute-done | bytes 262176 | tf_op jit(solution)/shard_map/ppermute | solution.py:36
  304.7 11.2 %collective-permute-done.39 = bf16[2,512,128]{2,1,0:T(8,128)(2,1)S(1)} collective-permute-done((bf16[2,512,128]{2,1,0:T(8,128)(2,1)S(1)}, bf16[2,512,128]{2,1,0:T(8,128)(2,1)S(1)}, u32[]{:S(2)}, u32[]{:S(2)}) %collective-permute-start.39) | collective-permute-done | bytes 262176 | tf_op jit(solution)/shard_map/ppermute | solution.py:36
  319.7 3.3 rows_out.3
  323.7 6.4 %collective-permute-done.50 = bf16[4,640,128]{2,1,0:T(8,128)(2,1)} collective-permute-done((bf16[4,640,128]{2,1,0:T(8,128)(2,1)}, bf16[4,640,128]{2,1,0:T(8,128)(2,1)}, u32[]{:S(2)}, u32[]{:S(2)}) %collective-permute-start.50) | collective-permute-done | bytes 655392 | tf_op jit(solution)/shard_map/ppermute | solution.py:36
  330.1 6.9 %columns_out.3 = (f32[8,32,5248]{2,1,0:T(8,128)}, f32[8,32,1]{2,1,0:T(8,128)S(1)}) custom-call(s32[2]{0:T(128)S(1)} %pad_add_fusion.refs_0_.place_ref, f32[8,32,1]{2,1,0:T(8,128)S(1)} %copy-done.18, bf16[8,32,5248]{2,1,0:T(8,128)(2,1)S(1)} %bitcast.77, bf16[4,24,32,128]{3,2,1,0:T(8,128)(2,1)S(1)} %bitcast.80, bf16[4,24,32,128]{3,2,1,0:T(8,128)(2,1)} %bitcast.49.refs_1_, ...), custom_call_target="tpu_custom_call" | custom-call | tf_op jit(solution)/shard_map/columns_out/pallas_call | solution.py:756
  343.6 5.1 %columns_out.2 = (f32[8,32,3072]{2,1,0:T(8,128)}, f32[8,32,1]{2,1,0:T(8,128)S(1)}) custom-call(s32[2]{0:T(128)S(1)} %pad_add_fusion.refs_0_.place_ref, f32[8,32,1]{2,1,0:T(8,128)S(1)} %copy-done.17, bf16[8,32,3072]{2,1,0:T(8,128)(2,1)S(1)} %bitcast.78, bf16[4,16,32,128]{3,2,1,0:T(8,128)(2,1)} %bitcast.34.refs_0_, bf16[4,16,32,128]{3,2,1,0:T(8,128)(2,1)} %bitcast.35.refs_1_, ...), custom_call_target="tpu_custom_call" | custom-call | tf_op jit(solution)/shard_map/columns_out/pallas_call | solution.py:756
  (275 shorter events, 104.0 us)
Async XLA Ops:
  8.1 32.3 %collective-permute-start.6 = (bf16[128,1024]{1,0:T(8,128)(2,1)}, bf16[128,1024]{1,0:T(8,128)(2,1)S(1)}, u32[]{:S(2)}, u32[]{:S(2)}) collective-permute-start(bf16[128,1024]{1,0:T(8,128)(2,1)} %dynamic-slice_bitcast_fusion.2), channel_id=1, source_target_pairs={{0,2},{1,3},{2,0},{3,1},{4,6},{5,7},{6,4},{7,5},{8,10},{9,11},{10,... | collective-permute-start | bytes 786440 | tf_op jit(solution)/shard_map/ppermute | solution.py:36
  8.1 25.5 %collective-permute-start = (bf16[256,1024]{1,0:T(8,128)(2,1)S(1)}, bf16[256,1024]{1,0:T(8,128)(2,1)}, u32[]{:S(2)}, u32[]{:S(2)}) collective-permute-start(bf16[256,1024]{1,0:T(8,128)(2,1)S(1)} %copy-done.9), channel_id=1, source_target_pairs={{0,2},{1,3},{2,0},{3,1},{4,6},{5,7},{6,4},{7,5},{8,10},{9,11},{10,... | collective-permute-start | bytes 1572872 | tf_op jit(solution)/shard_map/ppermute | solution.py:36
  17.5 18.3 %collective-permute-start.4 = (bf16[2,64,768]{2,1,0:T(8,128)(2,1)S(1)}, bf16[2,64,768]{2,1,0:T(8,128)(2,1)S(1)}, u32[]{:S(2)}, u32[]{:S(2)}) collective-permute-start(bf16[2,64,768]{2,1,0:T(8,128)(2,1)S(1)} %get-tuple-element.152), channel_id=1, source_target_pairs={{0,8},{4,12},{8,0},{12,4},{16,24},{20,28},{24,16},{28,20},{1,9},{5... | collective-permute-start | bytes 589832 | tf_op jit(solution)/shard_map/ppermute | solution.py:36
  19.7 16.8 %collective-permute-start.3 = (bf16[2,64,768]{2,1,0:T(8,128)(2,1)S(1)}, bf16[2,64,768]{2,1,0:T(8,128)(2,1)S(1)}, u32[]{:S(2)}, u32[]{:S(2)}) collective-permute-start(bf16[2,64,768]{2,1,0:T(8,128)(2,1)S(1)} %get-tuple-element.153), channel_id=1, source_target_pairs={{0,4},{4,0},{8,12},{12,8},{16,20},{20,16},{24,28},{28,24},{1,5},{5... | collective-permute-start | bytes 589832 | tf_op jit(solution)/shard_map/ppermute | solution.py:36
  44.0 19.0 %collective-permute-start.12 = (bf16[2,128,1536]{2,1,0:T(8,128)(2,1)S(1)}, bf16[2,128,1536]{2,1,0:T(8,128)(2,1)S(1)}, u32[]{:S(2)}, u32[]{:S(2)}) collective-permute-start(bf16[2,128,1536]{2,1,0:T(8,128)(2,1)S(1)} %dynamic-slice_bitcast_fusion), channel_id=1, source_target_pairs={{0,2},{1,3},{2,0},{3,1},{4,6},{5,7},{6,4},{7,5},{8,10},{9,11},{10,... | collective-permute-start | bytes 2359304 | tf_op jit(solution)/shard_map/ppermute | solution.py:36
  76.5 16.1 %collective-permute-start.16 = (bf16[256,1024]{1,0:T(8,128)(2,1)S(1)}, bf16[256,1024]{1,0:T(8,128)(2,1)S(1)}, u32[]{:S(2)}, u32[]{:S(2)}) collective-permute-start(bf16[256,1024]{1,0:T(8,128)(2,1)S(1)} %copy-done.8), channel_id=1, source_target_pairs={{0,2},{1,3},{2,0},{3,1},{4,6},{5,7},{6,4},{7,5},{8,10},{9,11},{10,... | collective-permute-start | bytes 1572872 | tf_op jit(solution)/shard_map/ppermute | solution.py:36
  121.8 29.6 %collective-permute-start.25 = (bf16[4,640,128]{2,1,0:T(8,128)(2,1)S(1)}, bf16[4,640,128]{2,1,0:T(8,128)(2,1)S(1)}, u32[]{:S(2)}, u32[]{:S(2)}) collective-permute-start(bf16[4,640,128]{2,1,0:T(8,128)(2,1)S(1)} %bitcast.86), channel_id=1, source_target_pairs={{0,8},{4,12},{8,0},{12,4},{16,24},{20,28},{24,16},{28,20},{1,9},{5... | collective-permute-start | bytes 1966088 | tf_op jit(solution)/shard_map/ppermute | solution.py:36
  123.3 28.1 %collective-permute-start.24 = (bf16[4,768,128]{2,1,0:T(8,128)(2,1)}, bf16[4,768,128]{2,1,0:T(8,128)(2,1)S(1)}, u32[]{:S(2)}, u32[]{:S(2)}) collective-permute-start(bf16[4,768,128]{2,1,0:T(8,128)(2,1)} %bitcast.104), channel_id=1, source_target_pairs={{0,4},{4,0},{8,12},{12,8},{16,20},{20,16},{24,28},{28,24},{1,5},{5... | collective-permute-start | bytes 2359304 | tf_op jit(solution)/shard_map/ppermute | solution.py:36
  128.6 19.9 %collective-permute-start.22 = (bf16[256,1024]{1,0:T(8,128)(2,1)S(1)}, bf16[256,1024]{1,0:T(8,128)(2,1)S(1)}, u32[]{:S(2)}, u32[]{:S(2)}) collective-permute-start(bf16[256,1024]{1,0:T(8,128)(2,1)S(1)} %get-tuple-element.82.refs_6_.refs_1_), channel_id=1, source_target_pairs={{0,2},{1,3},{2,0},{3,1},{4,6},{5,7},{6,4},{7,5},{8,10},{9,11},{10,... | collective-permute-start | bytes 1572872 | tf_op jit(solution)/shard_map/ppermute | solution.py:36
  149.8 18.8 %collective-permute-start.28 = (bf16[4,656,128]{2,1,0:T(8,128)(2,1)}, bf16[4,656,128]{2,1,0:T(8,128)(2,1)}, u32[]{:S(2)}, u32[]{:S(2)}) collective-permute-start(bf16[4,656,128]{2,1,0:T(8,128)(2,1)} %get-tuple-element.100), channel_id=1, source_target_pairs={{0,8},{4,12},{8,0},{12,4},{16,24},{20,28},{24,16},{28,20},{1,9},{5... | collective-permute-start | bytes 2015240 | tf_op jit(solution)/shard_map/ppermute | solution.py:36
  151.6 17.0 %collective-permute-start.27 = (bf16[2,640,128]{2,1,0:T(8,128)(2,1)S(1)}, bf16[2,640,128]{2,1,0:T(8,128)(2,1)}, u32[]{:S(2)}, u32[]{:S(2)}) collective-permute-start(bf16[2,640,128]{2,1,0:T(8,128)(2,1)S(1)} %get-tuple-element.139.refs_15_), channel_id=1, source_target_pairs={{0,4},{4,0},{8,12},{12,8},{16,20},{20,16},{24,28},{28,24},{1,5},{5... | collective-permute-start | bytes 983048 | tf_op jit(solution)/shard_map/ppermute | solution.py:36
  152.8 22.8 %collective-permute-start.26 = (bf16[2,768,128]{2,1,0:T(8,128)(2,1)S(1)}, bf16[2,768,128]{2,1,0:T(8,128)(2,1)S(1)}, u32[]{:S(2)}, u32[]{:S(2)}) collective-permute-start(bf16[2,768,128]{2,1,0:T(8,128)(2,1)S(1)} %get-tuple-element.131.refs_14_), channel_id=1, source_target_pairs={{0,8},{4,12},{8,0},{12,4},{16,24},{20,28},{24,16},{28,20},{1,9},{5... | collective-permute-start | bytes 1179656 | tf_op jit(solution)/shard_map/ppermute | solution.py:36
  153.6 29.3 %collective-permute-start.21 = (bf16[256,1024]{1,0:T(8,128)(2,1)S(1)}, bf16[256,1024]{1,0:T(8,128)(2,1)S(1)}, u32[]{:S(2)}, u32[]{:S(2)}) collective-permute-start(bf16[256,1024]{1,0:T(8,128)(2,1)S(1)} %get-tuple-element.86.refs_13_), channel_id=1, source_target_pairs={{0,2},{1,3},{2,0},{3,1},{4,6},{5,7},{6,4},{7,5},{8,10},{9,11},{10,... | collective-permute-start | bytes 1572872 | tf_op jit(solution)/shard_map/ppermute | solution.py:36
  189.7 26.6 %collective-permute-start.51 = (bf16[2,656,128]{2,1,0:T(8,128)(2,1)S(1)}, bf16[2,656,128]{2,1,0:T(8,128)(2,1)S(1)}, u32[]{:S(2)}, u32[]{:S(2)}) collective-permute-start(bf16[2,656,128]{2,1,0:T(8,128)(2,1)S(1)} %get-tuple-element.125.refs_5_), channel_id=1, source_target_pairs={{0,4},{4,0},{8,12},{12,8},{16,20},{20,16},{24,28},{28,24},{1,5},{5... | collective-permute-start | bytes 1007624 | tf_op jit(solution)/shard_map/ppermute | solution.py:36
  190.5 19.3 %collective-permute-start.43 = (bf16[1,1408,128]{2,1,0:T(8,128)(2,1)S(1)}, bf16[1,1408,128]{2,1,0:T(8,128)(2,1)S(1)}, u32[]{:S(2)}, u32[]{:S(2)}) collective-permute-start(bf16[1,1408,128]{2,1,0:T(8,128)(2,1)S(1)} %pad_maximum_fusion.13), channel_id=1, source_target_pairs={{0,16},{4,20},{8,24},{12,28},{16,0},{20,4},{24,8},{28,12},{1,17},{... | collective-permute-start | bytes 1081352 | tf_op jit(solution)/shard_map/ppermute | solution.py:36
  193.2 19.0 %collective-permute-start.31 = (bf16[4,512,128]{2,1,0:T(8,128)(2,1)S(1)}, bf16[4,512,128]{2,1,0:T(8,128)(2,1)S(1)}, u32[]{:S(2)}, u32[]{:S(2)}) collective-permute-start(bf16[4,512,128]{2,1,0:T(8,128)(2,1)S(1)} %bitcast.105), channel_id=1, source_target_pairs={{0,4},{4,0},{8,12},{12,8},{16,20},{20,16},{24,28},{28,24},{1,5},{5... | collective-permute-start | bytes 1572872 | tf_op jit(solution)/shard_map/ppermute | solution.py:36
  194.4 21.1 %collective-permute-start.33 = (bf16[4,512,128]{2,1,0:T(8,128)(2,1)S(1)}, bf16[4,512,128]{2,1,0:T(8,128)(2,1)S(1)}, u32[]{:S(2)}, u32[]{:S(2)}) collective-permute-start(bf16[4,512,128]{2,1,0:T(8,128)(2,1)S(1)} %pad_maximum_fusion.11), channel_id=1, source_target_pairs={{0,8},{4,12},{8,0},{12,4},{16,24},{20,28},{24,16},{28,20},{1,9},{5... | collective-permute-start | bytes 1572872 | tf_op jit(solution)/shard_map/ppermute | solution.py:36
  210.0 17.2 %collective-permute-start.30 = (bf16[256,1024]{1,0:T(8,128)(2,1)S(1)}, bf16[256,1024]{1,0:T(8,128)(2,1)S(1)}, u32[]{:S(2)}, u32[]{:S(2)}) collective-permute-start(bf16[256,1024]{1,0:T(8,128)(2,1)S(1)} %get-tuple-element.107), channel_id=1, source_target_pairs={{0,2},{1,3},{2,0},{3,1},{4,6},{5,7},{6,4},{7,5},{8,10},{9,11},{10,... | collective-permute-start | bytes 1572872 | tf_op jit(solution)/shard_map/ppermute | solution.py:36
  210.7 16.5 %collective-permute-start.44 = (bf16[2,1,352,128]{3,2,0,1:T(8,128)(2,1)S(1)}, bf16[2,1,352,128]{3,2,0,1:T(8,128)(2,1)S(1)}, u32[]{:S(2)}, u32[]{:S(2)}) collective-permute-start(bf16[2,1,352,128]{3,2,0,1:T(8,128)(2,1)S(1)} %get-tuple-element.157), channel_id=1, source_target_pairs={{0,2},{1,3},{2,0},{3,1},{4,6},{5,7},{6,4},{7,5},{8,10},{9,11},{10,... | collective-permute-start | bytes 540680 | tf_op jit(solution)/shard_map/ppermute | solution.py:36
  212.4 16.6 %collective-permute-start.32 = (bf16[2,512,128]{2,1,0:T(8,128)(2,1)S(1)}, bf16[2,512,128]{2,1,0:T(8,128)(2,1)S(1)}, u32[]{:S(2)}, u32[]{:S(2)}) collective-permute-start(bf16[2,512,128]{2,1,0:T(8,128)(2,1)S(1)} %get-tuple-element.148), channel_id=1, source_target_pairs={{0,8},{4,12},{8,0},{12,4},{16,24},{20,28},{24,16},{28,20},{1,9},{5... | collective-permute-start | bytes 786440 | tf_op jit(solution)/shard_map/ppermute | solution.py:36
  229.1 19.3 %collective-permute-start.35 = (bf16[1,1024,128]{2,1,0:T(8,128)(2,1)S(1)}, bf16[1,1024,128]{2,1,0:T(8,128)(2,1)S(1)}, u32[]{:S(2)}, u32[]{:S(2)}) collective-permute-start(bf16[1,1024,128]{2,1,0:T(8,128)(2,1)S(1)} %pad_maximum_fusion.18), channel_id=1, source_target_pairs={{0,16},{4,20},{8,24},{12,28},{16,0},{20,4},{24,8},{28,12},{1,17},{... | collective-permute-start | bytes 786440 | tf_op jit(solution)/shard_map/ppermute | solution.py:36
  229.3 39.7 %collective-permute-start.52 = (bf16[1,656,128]{2,1,0:T(8,128)(2,1)S(1)}, bf16[1,656,128]{2,1,0:T(8,128)(2,1)S(1)}, u32[]{:S(2)}, u32[]{:S(2)}) collective-permute-start(bf16[1,656,128]{2,1,0:T(8,128)(2,1)S(1)} %add_convert_fusion.9), channel_id=1, source_target_pairs={{0,16},{4,20},{8,24},{12,28},{16,0},{20,4},{24,8},{28,12},{1,17},{... | collective-permute-start | bytes 503816 | tf_op jit(solution)/shard_map/ppermute | solution.py:36
  249.2 32.4 %collective-permute-start.46 = (bf16[1,1408,128]{2,1,0:T(8,128)(2,1)S(1)}, bf16[1,1408,128]{2,1,0:T(8,128)(2,1)S(1)}, u32[]{:S(2)}, u32[]{:S(2)}) collective-permute-start(bf16[1,1408,128]{2,1,0:T(8,128)(2,1)S(1)} %maximum_bitcast_fusion.1), channel_id=1, source_target_pairs={{0,16},{4,20},{8,24},{12,28},{16,0},{20,4},{24,8},{28,12},{1,17},{... | collective-permute-start | bytes 1081352 | tf_op jit(solution)/shard_map/ppermute | solution.py:36
  269.2 16.4 %collective-permute-start.38 = (bf16[1,1024,128]{2,1,0:T(8,128)(2,1)S(1)}, bf16[1,1024,128]{2,1,0:T(8,128)(2,1)S(1)}, u32[]{:S(2)}, u32[]{:S(2)}) collective-permute-start(bf16[1,1024,128]{2,1,0:T(8,128)(2,1)S(1)} %maximum_bitcast_fusion.2), channel_id=1, source_target_pairs={{0,16},{4,20},{8,24},{12,28},{16,0},{20,4},{24,8},{28,12},{1,17},{... | collective-permute-start | bytes 786440 | tf_op jit(solution)/shard_map/ppermute | solution.py:36
  281.7 16.5 %collective-permute-start.49 = (bf16[2,640,128]{2,1,0:T(8,128)(2,1)S(1)}, bf16[2,640,128]{2,1,0:T(8,128)(2,1)S(1)}, u32[]{:S(2)}, u32[]{:S(2)}) collective-permute-start(bf16[2,640,128]{2,1,0:T(8,128)(2,1)S(1)} %pad_maximum_fusion.15), channel_id=1, source_target_pairs={{0,4},{4,0},{8,12},{12,8},{16,20},{20,16},{24,28},{28,24},{1,5},{5... | collective-permute-start | bytes 983048 | tf_op jit(solution)/shard_map/ppermute | solution.py:36
  285.7 18.2 %collective-permute-start.41 = (bf16[2,512,128]{2,1,0:T(8,128)(2,1)S(1)}, bf16[2,512,128]{2,1,0:T(8,128)(2,1)S(1)}, u32[]{:S(2)}, u32[]{:S(2)}) collective-permute-start(bf16[2,512,128]{2,1,0:T(8,128)(2,1)S(1)} %get-tuple-element.142), channel_id=1, source_target_pairs={{0,4},{4,0},{8,12},{12,8},{16,20},{20,16},{24,28},{28,24},{1,5},{5... | collective-permute-start | bytes 786440 | tf_op jit(solution)/shard_map/ppermute | solution.py:36
  292.1 27.6 %collective-permute-start.55 = (bf16[4,656,128]{2,1,0:T(8,128)(2,1)}, bf16[4,656,128]{2,1,0:T(8,128)(2,1)}, u32[]{:S(2)}, u32[]{:S(2)}) collective-permute-start(bf16[4,656,128]{2,1,0:T(8,128)(2,1)} %pad_maximum_fusion.8.refs_0_), channel_id=1, source_target_pairs={{0,8},{4,12},{8,0},{12,4},{16,24},{20,28},{24,16},{28,20},{1,9},{5... | collective-permute-start | bytes 2015240 | tf_op jit(solution)/shard_map/ppermute | solution.py:36
  292.1 23.8 %collective-permute-start.39 = (bf16[2,512,128]{2,1,0:T(8,128)(2,1)S(1)}, bf16[2,512,128]{2,1,0:T(8,128)(2,1)S(1)}, u32[]{:S(2)}, u32[]{:S(2)}) collective-permute-start(bf16[2,512,128]{2,1,0:T(8,128)(2,1)S(1)} %get-tuple-element.143), channel_id=1, source_target_pairs={{0,8},{4,12},{8,0},{12,4},{16,24},{20,28},{24,16},{28,20},{1,9},{5... | collective-permute-start | bytes 786440 | tf_op jit(solution)/shard_map/ppermute | solution.py:36
  294.2 35.9 %collective-permute-start.48 = (bf16[4,768,128]{2,1,0:T(8,128)(2,1)S(1)}, bf16[4,768,128]{2,1,0:T(8,128)(2,1)}, u32[]{:S(2)}, u32[]{:S(2)}) collective-permute-start(bf16[4,768,128]{2,1,0:T(8,128)(2,1)S(1)} %pad_maximum_fusion.7), channel_id=1, source_target_pairs={{0,4},{4,0},{8,12},{12,8},{16,20},{20,16},{24,28},{28,24},{1,5},{5... | collective-permute-start | bytes 2359304 | tf_op jit(solution)/shard_map/ppermute | solution.py:36
  299.1 31.0 %collective-permute-start.50 = (bf16[4,640,128]{2,1,0:T(8,128)(2,1)}, bf16[4,640,128]{2,1,0:T(8,128)(2,1)}, u32[]{:S(2)}, u32[]{:S(2)}) collective-permute-start(bf16[4,640,128]{2,1,0:T(8,128)(2,1)} %pad_maximum_fusion.9), channel_id=1, source_target_pairs={{0,8},{4,12},{8,0},{12,4},{16,24},{20,28},{24,16},{28,20},{1,9},{5... | collective-permute-start | bytes 1966088 | tf_op jit(solution)/shard_map/ppermute | solution.py:36
  304.7 34.6 %collective-permute-start.42 = (bf16[4,512,128]{2,1,0:T(8,128)(2,1)}, bf16[4,512,128]{2,1,0:T(8,128)(2,1)}, u32[]{:S(2)}, u32[]{:S(2)}) collective-permute-start(bf16[4,512,128]{2,1,0:T(8,128)(2,1)} %pad_maximum_fusion.10.refs_0_), channel_id=1, source_target_pairs={{0,8},{4,12},{8,0},{12,4},{16,24},{20,28},{24,16},{28,20},{1,9},{5... | collective-permute-start | bytes 1572872 | tf_op jit(solution)/shard_map/ppermute | solution.py:36
  316.8 23.5 %collective-permute-start.40 = (bf16[4,512,128]{2,1,0:T(8,128)(2,1)}, bf16[4,512,128]{2,1,0:T(8,128)(2,1)}, u32[]{:S(2)}, u32[]{:S(2)}) collective-permute-start(bf16[4,512,128]{2,1,0:T(8,128)(2,1)} %pad_maximum_fusion.12), channel_id=1, source_target_pairs={{0,4},{4,0},{8,12},{12,8},{16,20},{20,16},{24,28},{28,24},{1,5},{5... | collective-permute-start | bytes 1572872 | tf_op jit(solution)/shard_map/ppermute | solution.py:36
  (69 other events, 481.3 us)

commit v4 on v3

--- a/solution.py
+++ b/solution.py
@@ -65,14 +65,17 @@
     return Group(swap(array, "shard", bit), held)
 
 
-def gather_rows(x, gate=None):
+def gather_rows(x, gate=None, apart=False):
     rows = x.shape[0]
     groups = [Group(x, [(0, None, 0, rows)])]
     for bit in reversed(range(bits_of("shard"))):
         arrays = [g.array for g in groups]
         if gate is not None and len(arrays) > 1:
             arrays[-1] = after(arrays[-1], *gate())
-        groups = groups + [join(groups, bit, arrays, 0)]
+        if apart:
+            groups = groups + [join([g], bit, [a], 0) for g, a in zip(groups, arrays)]
+        else:
+            groups = groups + [join(groups, bit, arrays, 0)]
     return groups
 
 
@@ -862,9 +865,9 @@
     gain2 = ln2_gain.astype(F32)[:, None]
     qkv_to = split_columns(w_qkv, gain1, n, 3, head_cols, width)
     in_to = split_columns(w_in, gain2, n, 2, ff, padded)
-    toks = gather_rows(tokens)
     qkv_groups = split_weight(qkv_to)
     out_groups = gather_weight(w_out)
+    toks = gather_rows(tokens, lambda: (out_groups[1].array,), apart=True)
 
     lane = jnp.arange(width, dtype=jnp.int32) % HEAD_DIM
     half = HEAD_DIM // 2
@@ -902,7 +905,7 @@
         name="attention",
     )(place, *tables, *arrays_of(toks + qkv_groups + out_groups[2:4]))
 
-    far_done = [toks[1].array, qkv_groups[1].array, out_groups[1].array]
+    far_done = [toks[1].array, qkv_groups[1].array]
     in_groups = split_weight(after(in_to, *far_done), attended)
     atts = gather_rows(attended[:, :head_cols])
     block_shape = shape((n // 2, rows, model), BF16)
@@ -1053,6 +1056,11 @@
         name="qkv_gradient",
     )(place, normed1, dqkv, in_reduce.p[1], in_reduce.q[1], down_reduce[1])
     qkv_flows = [flow_rows(a) for a in qkv_flows]
+    split = qkv_flows[2].shape[1]
+    qkv_q = [jnp.concatenate(x, axis=1) for x in zip(qkv_flows[2:], (out_keep, out_send))]
+    att_reduce = PairReduce(qkv_flows[:2], qkv_q, orders)
+    att_reduce.step(0)
+    att_first = att_reduce.p[1]
     output = pl.pallas_call(
         ordered(output_kernel, 3, 1),
         in_specs=[VMEM_SPEC] * 3 + [ANY_SPEC],
@@ -1061,13 +1069,13 @@
         name="output",
     )(mlp_mine, swap(mlp_other, "shard", top), hidden, qkv_flows[0])
     dnormed1_keep, dnormed1_send = pl.pallas_call(
-        ordered(functools.partial(project_back_kernel, n), 3, 1),
-        in_specs=[SMEM_SPEC] + [VMEM_SPEC] * 2 + [ANY_SPEC],
+        ordered(functools.partial(project_back_kernel, n), 3, 3),
+        in_specs=[SMEM_SPEC] + [VMEM_SPEC] * 2 + [ANY_SPEC] * 3,
         out_shape=[block_shape] * 2,
         compiler_params=params,
         cost_estimate=work(6 * seq * model * width),
         name="project_back",
-    )(place, dqkv, qkv_w, output)
+    )(place, dqkv, qkv_w, output, att_first, att_reduce.q[1])
     mine, other = near_sums(dnormed1_keep, dnormed1_send, "near_sum_1")
     input_grad = pl.pallas_call(
         input_kernel,
@@ -1086,17 +1094,13 @@
         size = n * count * chunk
         return [a[:, :size].reshape(a.shape[0], n * count, chunk, LANES) for a in pair]
 
-    in_p, in_q = turned(*in_reduce.finish([[other]]), in_counts)
+    in_p, in_q = turned(*in_reduce.finish([[qkv_flows[0]]]), in_counts)
     in_p, in_q = pair_gather(in_p, in_q, orders)
-    down_share = replica_reduce(*down_reduce, far[1:], [[other]])
-    down_pair = replica_spread(down_share, far)
-
-    split = qkv_flows[2].shape[1]
-    qkv_q = [jnp.concatenate(x, axis=1) for x in zip(qkv_flows[2:], (out_keep, out_send))]
-    att_reduce = PairReduce(qkv_flows[:2], qkv_q, orders)
-    att_reduce.step(0, [other])
-    att_reduce.step(1, [input_grad])
-    att_p, att_q = att_reduce.finish()
+    down_share = replica_reduce(*down_reduce, far[1:], [[att_first]])
+
+    att_reduce.step(1, [dnormed1_keep])
+    att_p, att_q = att_reduce.finish([[other]])
+    down_pair = replica_spread(after(down_share, att_p), far)
     qkv_p, qkv_q = turned(att_p, att_q[:split], qkv_counts)
     att_p, att_q = pair_gather(qkv_p, jnp.concatenate([qkv_q, att_q[split:]]), orders)
 

time: 355 us -> 331 us (0.932)
  waiting for transfers between devices: 148 us -> 111 us
  starting transfers between devices: 53.6 us -> 61.2 us
  local copies, waits for them, and re-layouts: 21.3 us -> 26.3 us
    ppermute x56 -> x57, waiting for transfers between devices: 148 us -> 111 us  [swap(): return lax.ppermute(x, axis, [(i, i ^ 1 << bit) for i in range(size)])]
    ppermute x56 -> x57, starting transfers between devices: 53.6 us -> 61.2 us  [swap(): return lax.ppermute(x, axis, [(i, i ^ 1 << bit) for i in range(size)])]
    unnamed x90 -> x100, local copies, waits for them, and re-layouts: 13.7 us -> 17.7 us
  transfers between devices with their start and end apart: 56 -> 57, of which waited for: 27 -> 22; matrix products, arithmetic and copies ran while one was open for 7% -> 8% of each run, Pallas kernels for 24% -> 28%
where the time goes in v4:
time: 331 us; the launch traced here: 327 us
  waiting for transfers between devices  111 us (34%)
  Pallas kernels  110 us (33%)
  starting transfers between devices  61.2 us (18%)
  local copies, waits for them, and re-layouts  26.3 us (8%)
  other arithmetic  17 us (5%)
    ppermute x57, waiting for transfers between devices, swap(): return lax.ppermute(x, axis, [(i, i ^ 1 << bit) for i in range(size)])  111 us
    ppermute x57, starting transfers between devices, swap(): return lax.ppermute(x, axis, [(i, i ^ 1 << bit) for i in range(size)])  61.2 us
    pallas_call x1, Pallas kernels, shards(): pl.pallas_call(ordered(functools.partial(down_kernel, held_of(cots), n, f...  18.3 us
    unnamed x100, local copies, waits for them, and re-layouts  17.7 us
    pallas_call x1, Pallas kernels, shards(): pl.pallas_call(ordered(functools.partial(attention_back_kernel, held_of(d...  13.4 us
    pallas_call x1, Pallas kernels, shards(): pl.pallas_call(ordered(functools.partial(attention_kernel, held_of(toks),...  12.6 us
    pallas_call x1, Pallas kernels, shards(): pl.pallas_call(functools.partial(dup_kernel, held_of(cots), n), in_specs=...  12 us
    pallas_call x2, Pallas kernels, columns_out(): pl.pallas_call(functools.partial(columns_out_kernel, n, ff, head_cols, wi...  12 us
  transfers between devices with their start and end apart: 57, of which 22 were waited for; matrix products, arithmetic and copies ran while one was open for 8% of the time, Pallas kernels for 28%

profile of v4, /device:TPU:0, one launch (start us, length us, event | category | flops | bytes accessed | tf_op | source)
XLA Modules:
  0.0 326.9 jit_solution(10748524446608273798)
XLA Ops:
  0.6 3.0 collective-permute-start
  11.3 4.8 %sine_multiply_fusion = (f32[1024,256]{1,0:T(8,128)}, f32[1024,256]{1,0:T(8,128)}) fusion(f32[256]{0:T(256)S(1)} %get-tuple-element.168, f32[256]{0:T(256)S(1)} %get-tuple-element.169), kind=kLoop, calls=%fused_computation.5 | loop fusion | flops 524288 | bytes 2099200 | tf_op jit(solution)/shard_map/mul | solution.py:880
  16.1 8.9 %collective-permute-done.4.refs_10_ = bf16[2,128,768]{2,1,0:T(8,128)(2,1)S(1)} collective-permute-done((bf16[2,128,768]{2,1,0:T(8,128)(2,1)}, bf16[2,128,768]{2,1,0:T(8,128)(2,1)S(1)}, u32[]{:S(2)}, u32[]{:S(2)}) %collective-permute-start.4) | collective-permute-done | bytes 393248 | tf_op jit(solution)/shard_map/ppermute | solution.py:36
  39.6 3.8 %collective-permute-done.8.refs_14_.refs_9_ = bf16[64,1024]{1,0:T(8,128)(2,1)S(1)} collective-permute-done((bf16[64,1024]{1,0:T(8,128)(2,1)S(1)}, bf16[64,1024]{1,0:T(8,128)(2,1)S(1)}, u32[]{:S(2)}, u32[]{:S(2)}) %collective-permute-start.8) | collective-permute-done | bytes 131104 | tf_op jit(solution)/shard_map/ppermute | solution.py:36
  45.9 12.6 %attention.1 = (bf16[1024,256]{1,0:T(8,128)(2,1)S(1)}, bf16[1152,256]{1,0:T(8,128)(2,1)}, bf16[1152,256]{1,0:T(8,128)(2,1)}, bf16[1024,256]{1,0:T(8,128)(2,1)}, ...) custom-call(s32[2]{0:T(128)S(1)} %pad_add_fusion.refs_0_.place_ref, ...), custom_call_target="tpu_custom_call" | custom-call | flops 10737418240 | bytes 4194304 | tf_op jit(solution)/shard_map/attention/pallas_call | solution.py:885
  58.6 4.0 %collective-permute-done.13.refs_13_ = bf16[2,128,1536]{2,1,0:T(8,128)(2,1)S(1)} collective-permute-done((bf16[2,128,1536]{2,1,0:T(8,128)(2,1)S(1)}, bf16[2,128,1536]{2,1,0:T(8,128)(2,1)S(1)}, u32[]{:S(2)}, u32[]{:S(2)}) %collective-permute-start.13) | collective-permute-done | bytes 786464 | tf_op jit(solution)/shard_map/ppermute | solution.py:36
  66.4 6.2 %collective-permute-done.15.refs_15_ = bf16[2,64,1536]{2,1,0:T(8,128)(2,1)S(1)} collective-permute-done((bf16[2,64,1536]{2,1,0:T(8,128)(2,1)S(1)}, bf16[2,64,1536]{2,1,0:T(8,128)(2,1)S(1)}, u32[]{:S(2)}, u32[]{:S(2)}) %collective-permute-start.15) | collective-permute-done | bytes 393248 | tf_op jit(solution)/shard_map/ppermute | solution.py:36
  73.8 3.2 collective-permute-done.10.refs_5_
  80.8 11.9 %up_projection.1 = (f32[256,1024]{1,0:T(8,128)}, bf16[1024,1024]{1,0:T(8,128)(2,1)}, f32[1024,1536]{1,0:T(8,128)}, bf16[1024,1536]{1,0:T(8,128)(2,1)}) custom-call(s32[2]{0:T(128)S(1)} %pad_add_fusion.refs_0_.place_ref, bf16[256,1024]{1,0:T(8,128)(2,1)S(1)} %copy-done.23, bf16[256,1024]{1,0:T(8,128)(2,1)} %collective-permute-done.refs_6_.refs_1_, ...), custom_call_target="tpu_custom_call" | custom-call | flops 9663676416 | bytes 4194304 | tf_op jit(solution)/shard_map/up_projection/pallas_call | solution.py:912
  93.0 2.5 collective-permute-done.18.refs_2_.refs_5_
  96.5 12.0 %dup.1 = (bf16[1024,768]{1,0:T(8,128)(2,1)}, bf16[1024,1536]{1,0:T(8,128)(2,1)}, bf16[2,256,1024]{2,1,0:T(8,128)(2,1)}, bf16[2,256,1024]{2,1,0:T(8,128)(2,1)}) custom-call(f32[1024,1536]{1,0:T(8,128)} %get-tuple-element.70.up_ref, bf16[1024,1536]{1,0:T(8,128)(2,1)} %get-tuple-element.71.w_in_ref, bf16[656,1024]{1,0:T(8,128)(2,1)} %refs_2_.1, ...), custom_call_target="tpu_custom_call" | custom-call | flops 11274289152 | bytes 4194304 | tf_op jit(solution)/shard_map/dup/pallas_call | solution.py:944
  108.7 2.7 collective-permute-done.19.got_ref
  114.5 7.5 %in_gradient.1 = (bf16[4,24,32,128]{3,2,1,0:T(8,128)(2,1)}, bf16[4,24,32,128]{3,2,1,0:T(8,128)(2,1)}, bf16[4,20,32,128]{3,2,1,0:T(8,128)(2,1)S(1)}, bf16[4,20,32,128]{3,2,1,0:T(8,128)(2,1)S(1)}) custom-call(s32[2]{0:T(128)S(1)} %pad_add_fusion.refs_0_.place_ref, bf16[1024,1024]{1,0:T(8,128)(2,1)} %get-tuple-element.80.refs_1_, ...), custom_call_target="tpu_custom_call" | custom-call | flops 6442450944 | bytes 4194304 | tf_op jit(solution)/shard_map/in_gradient/pallas_call | solution.py:982
  131.2 18.3 %down_gradient.1 = (bf16[4,656,128]{2,1,0:T(8,128)(2,1)}, bf16[4,656,128]{2,1,0:T(8,128)(2,1)}, bf16[2,256,1024]{2,1,0:T(8,128)(2,1)}, bf16[2,256,1024]{2,1,0:T(8,128)(2,1)}) custom-call(s32[2]{0:T(128)S(1)} %pad_add_fusion.refs_0_.place_ref, bf16[1024,768]{1,0:T(8,128)(2,1)} %get-tuple-element.74.refs_1_, bf16[656,1024]{1,0:T(8,128)(2,1)} %refs_2_.1, ...), custom_call_target="tpu_custom_call" | custom-call | flops 6442450944 | bytes 4194304 | tf_op jit(solution)/shard_map/down_gradient/pallas_call | solution.py:1000
  158.6 13.4 %attention_back.1 = (bf16[1024,768]{1,0:T(8,128)(2,1)}, bf16[4,256,128]{2,1,0:T(8,128)(2,1)S(1)}, bf16[4,256,128]{2,1,0:T(8,128)(2,1)S(1)}) custom-call(s32[2]{0:T(128)S(1)} %pad_add_fusion.refs_0_.place_ref, bf16[256,1024]{1,0:T(8,128)(2,1)S(1)} %get-tuple-element.83.refs_6_.refs_1_, bf16[256,1024]{1,0:T(8,128)(2,1)} %copy-done.40, ...), custom_call_target="tpu_custom_call" | custom-call | flops 10737418240 | bytes 4194304 | tf_op jit(solution)/shard_map/attention_back/pallas_call | solution.py:1014
  172.1 4.5 %collective-permute-done.27 = bf16[2,768,128]{2,1,0:T(8,128)(2,1)S(1)} collective-permute-done((bf16[2,768,128]{2,1,0:T(8,128)(2,1)S(1)}, bf16[2,768,128]{2,1,0:T(8,128)(2,1)S(1)}, u32[]{:S(2)}, u32[]{:S(2)}) %collective-permute-start.27) | collective-permute-done | bytes 393248 | tf_op jit(solution)/shard_map/ppermute | solution.py:36
  180.3 4.8 %qkv_gradient.1 = (bf16[4,16,32,128]{3,2,1,0:T(8,128)(2,1)S(1)}, bf16[4,16,32,128]{3,2,1,0:T(8,128)(2,1)}, bf16[4,8,32,128]{3,2,1,0:T(8,128)(2,1)S(1)}, bf16[4,8,32,128]{3,2,1,0:T(8,128)(2,1)S(1)}) custom-call(s32[2]{0:T(128)S(1)} %pad_add_fusion.refs_0_.place_ref, bf16[1024,1024]{1,0:T(8,128)(2,1)} %get-tuple-element.88.refs_1_, ...), custom_call_target="tpu_custom_call" | custom-call | flops 3221225472 | bytes 4194304 | tf_op jit(solution)/shard_map/qkv_gradient/pallas_call | solution.py:1049
  186.0 2.6 collective-permute-start.44
  191.3 12.2 %collective-permute-done.44 = bf16[1,1408,128]{2,1,0:T(8,128)(2,1)S(1)} collective-permute-done((bf16[1,1408,128]{2,1,0:T(8,128)(2,1)S(1)}, bf16[1,1408,128]{2,1,0:T(8,128)(2,1)S(1)}, u32[]{:S(2)}, u32[]{:S(2)}) %collective-permute-start.44) | collective-permute-done | bytes 360480 | tf_op jit(solution)/shard_map/ppermute | solution.py:36
  205.2 3.5 %collective-permute-start.53 = (bf16[1,656,128]{2,1,0:T(8,128)(2,1)S(1)}, bf16[1,656,128]{2,1,0:T(8,128)(2,1)S(1)}, u32[]{:S(2)}, u32[]{:S(2)}) collective-permute-start(bf16[1,656,128]{2,1,0:T(8,128)(2,1)S(1)} %add_convert_fusion.9), channel_id=1, source_target_pairs={{0,16},{4,20},{8,24},{12,28},{16,0},{20,4},{24,8},{28,12},{1,17},{... | collective-permute-start | bytes 503816 | tf_op jit(solution)/shard_map/ppermute | solution.py:36
  210.2 4.8 %project_back.1 = (bf16[2,256,1024]{2,1,0:T(8,128)(2,1)}, bf16[2,256,1024]{2,1,0:T(8,128)(2,1)}) custom-call(s32[2]{0:T(128)S(1)} %pad_add_fusion.refs_0_.place_ref, bf16[1024,768]{1,0:T(8,128)(2,1)} %get-tuple-element.97.refs_2_.refs_1_, bf16[1024,768]{1,0:T(8,128)(2,1)} %get-tuple-element.104.refs_2_, bf16[256,1024]{1,0:T(8,128)(2,1)S(1)} %copy-done.20, ...), custom_call_target="tpu_custom_call" | custom-call | flops 1610612736 | bytes 4194304 | tf_op jit(solution)/shard_map/project_back/pallas_call | solution.py:1071
  215.6 3.3 %collective-permute-start.54 = (bf16[1,656,128]{2,1,0:T(8,128)(2,1)S(1)}, bf16[1,656,128]{2,1,0:T(8,128)(2,1)S(1)}, u32[]{:S(2)}, u32[]{:S(2)}) collective-permute-start(bf16[1,656,128]{2,1,0:T(8,128)(2,1)S(1)} %bitcast.92), channel_id=1, source_target_pairs={{0,16},{4,20},{8,24},{12,28},{16,0},{20,4},{24,8},{28,12},{1,17},{... | collective-permute-start | bytes 503816 | tf_op jit(solution)/shard_map/ppermute | solution.py:36
  219.3 3.0 collective-permute-start.47
  223.2 23.4 %collective-permute-done.36 = bf16[1,1024,128]{2,1,0:T(8,128)(2,1)S(1)} collective-permute-done((bf16[1,1024,128]{2,1,0:T(8,128)(2,1)S(1)}, bf16[1,1024,128]{2,1,0:T(8,128)(2,1)S(1)}, u32[]{:S(2)}, u32[]{:S(2)}) %collective-permute-start.36) | collective-permute-done | bytes 262176 | tf_op jit(solution)/shard_map/ppermute | solution.py:36
  248.9 2.6 collective-permute-done.37
  257.0 11.4 %collective-permute-done.39 = bf16[1,1024,128]{2,1,0:T(8,128)(2,1)S(1)} collective-permute-done((bf16[1,1024,128]{2,1,0:T(8,128)(2,1)S(1)}, bf16[1,1024,128]{2,1,0:T(8,128)(2,1)S(1)}, u32[]{:S(2)}, u32[]{:S(2)}) %collective-permute-start.39) | collective-permute-done | bytes 262176 | tf_op jit(solution)/shard_map/ppermute | solution.py:36
  269.4 3.0 collective-permute-start.40
  274.2 3.5 %collective-permute-done.42 = bf16[2,512,128]{2,1,0:T(8,128)(2,1)S(1)} collective-permute-done((bf16[2,512,128]{2,1,0:T(8,128)(2,1)S(1)}, bf16[2,512,128]{2,1,0:T(8,128)(2,1)S(1)}, u32[]{:S(2)}, u32[]{:S(2)}) %collective-permute-start.42) | collective-permute-done | bytes 262176 | tf_op jit(solution)/shard_map/ppermute | solution.py:36
  280.0 10.9 %collective-permute-done.40 = bf16[2,512,128]{2,1,0:T(8,128)(2,1)S(1)} collective-permute-done((bf16[2,512,128]{2,1,0:T(8,128)(2,1)S(1)}, bf16[2,512,128]{2,1,0:T(8,128)(2,1)S(1)}, u32[]{:S(2)}, u32[]{:S(2)}) %collective-permute-start.40) | collective-permute-done | bytes 262176 | tf_op jit(solution)/shard_map/ppermute | solution.py:36
  299.9 2.8 input_grad.1
  305.0 6.9 %columns_out.3 = (f32[8,32,5248]{2,1,0:T(8,128)}, f32[8,32,1]{2,1,0:T(8,128)S(1)}) custom-call(s32[2]{0:T(128)S(1)} %pad_add_fusion.refs_0_.place_ref, f32[8,32,1]{2,1,0:T(8,128)S(1)} %copy-done.22, bf16[8,32,5248]{2,1,0:T(8,128)(2,1)S(1)} %bitcast.80, bf16[4,24,32,128]{3,2,1,0:T(8,128)(2,1)S(1)} %bitcast.82, bf16[4,24,32,128]{3,2,1,0:T(8,128)(2,1)} %bitcast.49.refs_1_, ...), custom_call_target="tpu_custom_call" | custom-call | tf_op jit(solution)/shard_map/columns_out/pallas_call | solution.py:759
  318.5 5.1 %columns_out.2 = (f32[8,32,3072]{2,1,0:T(8,128)}, f32[8,32,1]{2,1,0:T(8,128)S(1)}) custom-call(s32[2]{0:T(128)S(1)} %pad_add_fusion.refs_0_.place_ref, f32[8,32,1]{2,1,0:T(8,128)S(1)} %copy-done.21, bf16[8,32,3072]{2,1,0:T(8,128)(2,1)S(1)} %bitcast.81, bf16[4,16,32,128]{3,2,1,0:T(8,128)(2,1)} %bitcast.34.refs_0_, bf16[4,16,32,128]{3,2,1,0:T(8,128)(2,1)} %bitcast.35.refs_1_, ...), custom_call_target="tpu_custom_call" | custom-call | tf_op jit(solution)/shard_map/columns_out/pallas_call | solution.py:759
  (286 shorter events, 102.3 us)
Async XLA Ops:
  0.6 38.8 %collective-permute-start = (bf16[256,1024]{1,0:T(8,128)(2,1)}, bf16[256,1024]{1,0:T(8,128)(2,1)}, u32[]{:S(2)}, u32[]{:S(2)}) collective-permute-start(bf16[256,1024]{1,0:T(8,128)(2,1)} %tokens.1), channel_id=1, source_target_pairs={{0,2},{1,3},{2,0},{3,1},{4,6},{5,7},{6,4},{7,5},{8,10},{9,11},{10,... | collective-permute-start | bytes 1572872 | tf_op jit(solution)/shard_map/ppermute | solution.py:36
  3.6 41.3 %collective-permute-start.1 = (bf16[256,1024]{1,0:T(8,128)(2,1)}, bf16[256,1024]{1,0:T(8,128)(2,1)}, u32[]{:S(2)}, u32[]{:S(2)}) collective-permute-start(bf16[256,1024]{1,0:T(8,128)(2,1)} %tokens.1), channel_id=1, source_target_pairs={{0,1},{1,0},{2,3},{3,2},{4,5},{5,4},{6,7},{7,6},{8,9},{9,8},{10,11... | collective-permute-start | bytes 1572872 | tf_op jit(solution)/shard_map/ppermute | solution.py:36
  8.5 16.5 %collective-permute-start.4 = (bf16[2,128,768]{2,1,0:T(8,128)(2,1)}, bf16[2,128,768]{2,1,0:T(8,128)(2,1)S(1)}, u32[]{:S(2)}, u32[]{:S(2)}) collective-permute-start(bf16[2,128,768]{2,1,0:T(8,128)(2,1)} %dynamic-slice_bitcast_fusion.1), channel_id=1, source_target_pairs={{0,2},{1,3},{2,0},{3,1},{4,6},{5,7},{6,4},{7,5},{8,10},{9,11},{10,... | collective-permute-start | bytes 1179656 | tf_op jit(solution)/shard_map/ppermute | solution.py:36
  9.4 28.0 %collective-permute-start.2 = (bf16[128,1024]{1,0:T(8,128)(2,1)}, bf16[128,1024]{1,0:T(8,128)(2,1)S(1)}, u32[]{:S(2)}, u32[]{:S(2)}) collective-permute-start(bf16[128,1024]{1,0:T(8,128)(2,1)} %dynamic-slice_bitcast_fusion.2), channel_id=1, source_target_pairs={{0,2},{1,3},{2,0},{3,1},{4,6},{5,7},{6,4},{7,5},{8,10},{9,11},{10,... | collective-permute-start | bytes 786440 | tf_op jit(solution)/shard_map/ppermute | solution.py:36
  43.4 19.2 %collective-permute-start.13 = (bf16[2,128,1536]{2,1,0:T(8,128)(2,1)S(1)}, bf16[2,128,1536]{2,1,0:T(8,128)(2,1)S(1)}, u32[]{:S(2)}, u32[]{:S(2)}) collective-permute-start(bf16[2,128,1536]{2,1,0:T(8,128)(2,1)S(1)} %dynamic-slice_bitcast_fusion), channel_id=1, source_target_pairs={{0,2},{1,3},{2,0},{3,1},{4,6},{5,7},{6,4},{7,5},{8,10},{9,11},{10,... | collective-permute-start | bytes 2359304 | tf_op jit(solution)/shard_map/ppermute | solution.py:36
  77.2 15.5 %collective-permute-start.17 = (bf16[256,1024]{1,0:T(8,128)(2,1)S(1)}, bf16[256,1024]{1,0:T(8,128)(2,1)S(1)}, u32[]{:S(2)}, u32[]{:S(2)}) collective-permute-start(bf16[256,1024]{1,0:T(8,128)(2,1)S(1)} %copy-done.10), channel_id=1, source_target_pairs={{0,2},{1,3},{2,0},{3,1},{4,6},{5,7},{6,4},{7,5},{8,10},{9,11},{10,... | collective-permute-start | bytes 1572872 | tf_op jit(solution)/shard_map/ppermute | solution.py:36
  112.9 14.0 %collective-permute-start.20 = (bf16[256,1024]{1,0:T(8,128)(2,1)S(1)}, bf16[256,1024]{1,0:T(8,128)(2,1)S(1)}, u32[]{:S(2)}, u32[]{:S(2)}) collective-permute-start(bf16[256,1024]{1,0:T(8,128)(2,1)S(1)} %get-tuple-element.78.refs_3_), channel_id=1, source_target_pairs={{0,2},{1,3},{2,0},{3,1},{4,6},{5,7},{6,4},{7,5},{8,10},{9,11},{10,... | collective-permute-start | bytes 1572872 | tf_op jit(solution)/shard_map/ppermute | solution.py:36
  121.9 30.7 %collective-permute-start.26 = (bf16[4,640,128]{2,1,0:T(8,128)(2,1)S(1)}, bf16[4,640,128]{2,1,0:T(8,128)(2,1)S(1)}, u32[]{:S(2)}, u32[]{:S(2)}) collective-permute-start(bf16[4,640,128]{2,1,0:T(8,128)(2,1)S(1)} %bitcast.89), channel_id=1, source_target_pairs={{0,8},{4,12},{8,0},{12,4},{16,24},{20,28},{24,16},{28,20},{1,9},{5... | collective-permute-start | bytes 1966088 | tf_op jit(solution)/shard_map/ppermute | solution.py:36
  123.5 29.2 %collective-permute-start.25 = (bf16[4,768,128]{2,1,0:T(8,128)(2,1)}, bf16[4,768,128]{2,1,0:T(8,128)(2,1)S(1)}, u32[]{:S(2)}, u32[]{:S(2)}) collective-permute-start(bf16[4,768,128]{2,1,0:T(8,128)(2,1)} %bitcast.110), channel_id=1, source_target_pairs={{0,4},{4,0},{8,12},{12,8},{16,20},{20,16},{24,28},{28,24},{1,5},{5... | collective-permute-start | bytes 2359304 | tf_op jit(solution)/shard_map/ppermute | solution.py:36
  129.7 19.9 %collective-permute-start.23 = (bf16[256,1024]{1,0:T(8,128)(2,1)S(1)}, bf16[256,1024]{1,0:T(8,128)(2,1)S(1)}, u32[]{:S(2)}, u32[]{:S(2)}) collective-permute-start(bf16[256,1024]{1,0:T(8,128)(2,1)S(1)} %get-tuple-element.83.refs_6_.refs_1_), channel_id=1, source_target_pairs={{0,2},{1,3},{2,0},{3,1},{4,6},{5,7},{6,4},{7,5},{8,10},{9,11},{10,... | collective-permute-start | bytes 1572872 | tf_op jit(solution)/shard_map/ppermute | solution.py:36
  151.0 21.0 %collective-permute-start.29 = (bf16[4,656,128]{2,1,0:T(8,128)(2,1)}, bf16[4,656,128]{2,1,0:T(8,128)(2,1)}, u32[]{:S(2)}, u32[]{:S(2)}) collective-permute-start(bf16[4,656,128]{2,1,0:T(8,128)(2,1)} %get-tuple-element.101), channel_id=1, source_target_pairs={{0,8},{4,12},{8,0},{12,4},{16,24},{20,28},{24,16},{28,20},{1,9},{5... | collective-permute-start | bytes 2015240 | tf_op jit(solution)/shard_map/ppermute | solution.py:36
  154.8 17.2 %collective-permute-start.28 = (bf16[2,640,128]{2,1,0:T(8,128)(2,1)S(1)}, bf16[2,640,128]{2,1,0:T(8,128)(2,1)}, u32[]{:S(2)}, u32[]{:S(2)}) collective-permute-start(bf16[2,640,128]{2,1,0:T(8,128)(2,1)S(1)} %get-tuple-element.139.refs_15_), channel_id=1, source_target_pairs={{0,4},{4,0},{8,12},{12,8},{16,20},{20,16},{24,28},{28,24},{1,5},{5... | collective-permute-start | bytes 983048 | tf_op jit(solution)/shard_map/ppermute | solution.py:36
  156.3 20.2 %collective-permute-start.27 = (bf16[2,768,128]{2,1,0:T(8,128)(2,1)S(1)}, bf16[2,768,128]{2,1,0:T(8,128)(2,1)S(1)}, u32[]{:S(2)}, u32[]{:S(2)}) collective-permute-start(bf16[2,768,128]{2,1,0:T(8,128)(2,1)S(1)} %get-tuple-element.131.refs_14_), channel_id=1, source_target_pairs={{0,8},{4,12},{8,0},{12,4},{16,24},{20,28},{24,16},{28,20},{1,9},{5... | collective-permute-start | bytes 1179656 | tf_op jit(solution)/shard_map/ppermute | solution.py:36
  157.1 33.3 %collective-permute-start.22 = (bf16[256,1024]{1,0:T(8,128)(2,1)S(1)}, bf16[256,1024]{1,0:T(8,128)(2,1)S(1)}, u32[]{:S(2)}, u32[]{:S(2)}) collective-permute-start(bf16[256,1024]{1,0:T(8,128)(2,1)S(1)} %get-tuple-element.87.refs_13_), channel_id=1, source_target_pairs={{0,2},{1,3},{2,0},{3,1},{4,6},{5,7},{6,4},{7,5},{8,10},{9,11},{10,... | collective-permute-start | bytes 1572872 | tf_op jit(solution)/shard_map/ppermute | solution.py:36
  177.8 27.4 %collective-permute-start.52 = (bf16[2,656,128]{2,1,0:T(8,128)(2,1)S(1)}, bf16[2,656,128]{2,1,0:T(8,128)(2,1)S(1)}, u32[]{:S(2)}, u32[]{:S(2)}) collective-permute-start(bf16[2,656,128]{2,1,0:T(8,128)(2,1)S(1)} %get-tuple-element.125.refs_5_), channel_id=1, source_target_pairs={{0,4},{4,0},{8,12},{12,8},{16,20},{20,16},{24,28},{28,24},{1,5},{5... | collective-permute-start | bytes 1007624 | tf_op jit(solution)/shard_map/ppermute | solution.py:36
  185.1 19.2 %collective-permute-start.30 = (bf16[4,512,128]{2,1,0:T(8,128)(2,1)}, bf16[4,512,128]{2,1,0:T(8,128)(2,1)S(1)}, u32[]{:S(2)}, u32[]{:S(2)}) collective-permute-start(bf16[4,512,128]{2,1,0:T(8,128)(2,1)} %bitcast.111), channel_id=1, source_target_pairs={{0,4},{4,0},{8,12},{12,8},{16,20},{20,16},{24,28},{28,24},{1,5},{5... | collective-permute-start | bytes 1572872 | tf_op jit(solution)/shard_map/ppermute | solution.py:36
  186.0 17.5 %collective-permute-start.44 = (bf16[1,1408,128]{2,1,0:T(8,128)(2,1)S(1)}, bf16[1,1408,128]{2,1,0:T(8,128)(2,1)S(1)}, u32[]{:S(2)}, u32[]{:S(2)}) collective-permute-start(bf16[1,1408,128]{2,1,0:T(8,128)(2,1)S(1)} %pad_maximum_fusion.12), channel_id=1, source_target_pairs={{0,16},{4,20},{8,24},{12,28},{16,0},{20,4},{24,8},{28,12},{1,17},{... | collective-permute-start | bytes 1081352 | tf_op jit(solution)/shard_map/ppermute | solution.py:36
  188.7 20.1 %collective-permute-start.31 = (bf16[4,512,128]{2,1,0:T(8,128)(2,1)S(1)}, bf16[4,512,128]{2,1,0:T(8,128)(2,1)S(1)}, u32[]{:S(2)}, u32[]{:S(2)}) collective-permute-start(bf16[4,512,128]{2,1,0:T(8,128)(2,1)S(1)} %pad_maximum_fusion.10), channel_id=1, source_target_pairs={{0,8},{4,12},{8,0},{12,4},{16,24},{20,28},{24,16},{28,20},{1,9},{5... | collective-permute-start | bytes 1572872 | tf_op jit(solution)/shard_map/ppermute | solution.py:36
  204.5 14.4 %collective-permute-start.34 = (bf16[2,512,128]{2,1,0:T(8,128)(2,1)S(1)}, bf16[2,512,128]{2,1,0:T(8,128)(2,1)S(1)}, u32[]{:S(2)}, u32[]{:S(2)}) collective-permute-start(bf16[2,512,128]{2,1,0:T(8,128)(2,1)S(1)} %get-tuple-element.149.refs_4_), channel_id=1, source_target_pairs={{0,8},{4,12},{8,0},{12,4},{16,24},{20,28},{24,16},{28,20},{1,9},{5... | collective-permute-start | bytes 786440 | tf_op jit(solution)/shard_map/ppermute | solution.py:36
  215.6 32.3 %collective-permute-start.54 = (bf16[1,656,128]{2,1,0:T(8,128)(2,1)S(1)}, bf16[1,656,128]{2,1,0:T(8,128)(2,1)S(1)}, u32[]{:S(2)}, u32[]{:S(2)}) collective-permute-start(bf16[1,656,128]{2,1,0:T(8,128)(2,1)S(1)} %bitcast.92), channel_id=1, source_target_pairs={{0,16},{4,20},{8,24},{12,28},{16,0},{20,4},{24,8},{28,12},{1,17},{... | collective-permute-start | bytes 503816 | tf_op jit(solution)/shard_map/ppermute | solution.py:36
  219.1 27.5 %collective-permute-start.36 = (bf16[1,1024,128]{2,1,0:T(8,128)(2,1)S(1)}, bf16[1,1024,128]{2,1,0:T(8,128)(2,1)S(1)}, u32[]{:S(2)}, u32[]{:S(2)}) collective-permute-start(bf16[1,1024,128]{2,1,0:T(8,128)(2,1)S(1)} %pad_maximum_fusion.17), channel_id=1, source_target_pairs={{0,16},{4,20},{8,24},{12,28},{16,0},{20,4},{24,8},{28,12},{1,17},{... | collective-permute-start | bytes 786440 | tf_op jit(solution)/shard_map/ppermute | solution.py:36
  219.3 33.8 %collective-permute-start.47 = (bf16[1,1408,128]{2,1,0:T(8,128)(2,1)S(1)}, bf16[1,1408,128]{2,1,0:T(8,128)(2,1)S(1)}, u32[]{:S(2)}, u32[]{:S(2)}) collective-permute-start(bf16[1,1408,128]{2,1,0:T(8,128)(2,1)S(1)} %maximum_bitcast_fusion.1), channel_id=1, source_target_pairs={{0,16},{4,20},{8,24},{12,28},{16,0},{20,4},{24,8},{28,12},{1,17},{... | collective-permute-start | bytes 1081352 | tf_op jit(solution)/shard_map/ppermute | solution.py:36
  253.1 19.2 %collective-permute-start.48 = (bf16[2,768,128]{2,1,0:T(8,128)(2,1)S(1)}, bf16[2,768,128]{2,1,0:T(8,128)(2,1)S(1)}, u32[]{:S(2)}, u32[]{:S(2)}) collective-permute-start(bf16[2,768,128]{2,1,0:T(8,128)(2,1)S(1)} %fusion.7), channel_id=1, source_target_pairs={{0,8},{4,12},{8,0},{12,4},{16,24},{20,28},{24,16},{28,20},{1,9},{5... | collective-permute-start | bytes 1179656 | tf_op jit(solution)/shard_map/ppermute | solution.py:36
  253.3 15.1 %collective-permute-start.39 = (bf16[1,1024,128]{2,1,0:T(8,128)(2,1)S(1)}, bf16[1,1024,128]{2,1,0:T(8,128)(2,1)S(1)}, u32[]{:S(2)}, u32[]{:S(2)}) collective-permute-start(bf16[1,1024,128]{2,1,0:T(8,128)(2,1)S(1)} %maximum_bitcast_fusion.2), channel_id=1, source_target_pairs={{0,16},{4,20},{8,24},{12,28},{16,0},{20,4},{24,8},{28,12},{1,17},{... | collective-permute-start | bytes 786440 | tf_op jit(solution)/shard_map/ppermute | solution.py:36
  255.6 17.7 %collective-permute-start.50 = (bf16[2,640,128]{2,1,0:T(8,128)(2,1)S(1)}, bf16[2,640,128]{2,1,0:T(8,128)(2,1)S(1)}, u32[]{:S(2)}, u32[]{:S(2)}) collective-permute-start(bf16[2,640,128]{2,1,0:T(8,128)(2,1)S(1)} %pad_maximum_fusion.14), channel_id=1, source_target_pairs={{0,4},{4,0},{8,12},{12,8},{16,20},{20,16},{24,28},{28,24},{1,5},{5... | collective-permute-start | bytes 983048 | tf_op jit(solution)/shard_map/ppermute | solution.py:36
  256.9 34.9 %collective-permute-start.56 = (bf16[4,656,128]{2,1,0:T(8,128)(2,1)S(1)}, bf16[4,656,128]{2,1,0:T(8,128)(2,1)S(1)}, u32[]{:S(2)}, u32[]{:S(2)}) collective-permute-start(bf16[4,656,128]{2,1,0:T(8,128)(2,1)S(1)} %pad_maximum_fusion.7.refs_0_), channel_id=1, source_target_pairs={{0,8},{4,12},{8,0},{12,4},{16,24},{20,28},{24,16},{28,20},{1,9},{5... | collective-permute-start | bytes 2015240 | tf_op jit(solution)/shard_map/ppermute | solution.py:36
  269.4 21.5 %collective-permute-start.40 = (bf16[2,512,128]{2,1,0:T(8,128)(2,1)S(1)}, bf16[2,512,128]{2,1,0:T(8,128)(2,1)S(1)}, u32[]{:S(2)}, u32[]{:S(2)}) collective-permute-start(bf16[2,512,128]{2,1,0:T(8,128)(2,1)S(1)} %get-tuple-element.143), channel_id=1, source_target_pairs={{0,8},{4,12},{8,0},{12,4},{16,24},{20,28},{24,16},{28,20},{1,9},{5... | collective-permute-start | bytes 786440 | tf_op jit(solution)/shard_map/ppermute | solution.py:36
  272.4 32.6 %collective-permute-start.49 = (bf16[4,768,128]{2,1,0:T(8,128)(2,1)S(1)}, bf16[4,768,128]{2,1,0:T(8,128)(2,1)}, u32[]{:S(2)}, u32[]{:S(2)}) collective-permute-start(bf16[4,768,128]{2,1,0:T(8,128)(2,1)S(1)} %pad_maximum_fusion.6), channel_id=1, source_target_pairs={{0,4},{4,0},{8,12},{12,8},{16,20},{20,16},{24,28},{28,24},{1,5},{5... | collective-permute-start | bytes 2359304 | tf_op jit(solution)/shard_map/ppermute | solution.py:36
  274.2 30.8 %collective-permute-start.51 = (bf16[4,640,128]{2,1,0:T(8,128)(2,1)}, bf16[4,640,128]{2,1,0:T(8,128)(2,1)}, u32[]{:S(2)}, u32[]{:S(2)}) collective-permute-start(bf16[4,640,128]{2,1,0:T(8,128)(2,1)} %pad_maximum_fusion.8), channel_id=1, source_target_pairs={{0,8},{4,12},{8,0},{12,4},{16,24},{20,28},{24,16},{28,20},{1,9},{5... | collective-permute-start | bytes 1966088 | tf_op jit(solution)/shard_map/ppermute | solution.py:36
  277.7 22.1 %collective-permute-start.33 = (bf16[256,1024]{1,0:T(8,128)(2,1)}, bf16[256,1024]{1,0:T(8,128)(2,1)}, u32[]{:S(2)}, u32[]{:S(2)}) collective-permute-start(bf16[256,1024]{1,0:T(8,128)(2,1)} %get-tuple-element.113), channel_id=1, source_target_pairs={{0,2},{1,3},{2,0},{3,1},{4,6},{5,7},{6,4},{7,5},{8,10},{9,11},{10,... | collective-permute-start | bytes 1572872 | tf_op jit(solution)/shard_map/ppermute | solution.py:36
  290.9 24.3 %collective-permute-start.43 = (bf16[4,512,128]{2,1,0:T(8,128)(2,1)}, bf16[4,512,128]{2,1,0:T(8,128)(2,1)}, u32[]{:S(2)}, u32[]{:S(2)}) collective-permute-start(bf16[4,512,128]{2,1,0:T(8,128)(2,1)} %pad_maximum_fusion.9.refs_0_), channel_id=1, source_target_pairs={{0,8},{4,12},{8,0},{12,4},{16,24},{20,28},{24,16},{28,20},{1,9},{5... | collective-permute-start | bytes 1572872 | tf_op jit(solution)/shard_map/ppermute | solution.py:36
  292.6 23.6 %collective-permute-start.41 = (bf16[4,512,128]{2,1,0:T(8,128)(2,1)}, bf16[4,512,128]{2,1,0:T(8,128)(2,1)}, u32[]{:S(2)}, u32[]{:S(2)}) collective-permute-start(bf16[4,512,128]{2,1,0:T(8,128)(2,1)} %pad_maximum_fusion.11), channel_id=1, source_target_pairs={{0,4},{4,0},{8,12},{12,8},{16,20},{20,16},{24,28},{28,24},{1,5},{5... | collective-permute-start | bytes 1572872 | tf_op jit(solution)/shard_map/ppermute | solution.py:36
  (75 other events, 512.4 us)

commit v5 on v4

--- a/solution.py
+++ b/solution.py
@@ -79,37 +79,37 @@
     return groups
 
 
-def parity():
-    return bit_of("rep", 0) ^ bit_of("rep", 1)
-
-
-def half_by_replica(x, dim):
+def parity(bits):
+    return functools.reduce(lambda a, b: a ^ b, [bit_of("rep", bit) for bit in bits])
+
+
+def half_by_replica(x, dim, bits):
     shape = x.shape
     x = x.reshape(shape[:dim] + (2, shape[dim] // 2) + shape[dim + 1 :])
-    return lax.dynamic_index_in_dim(x, parity(), dim, keepdims=False)
-
-
-def fetch_far(send, dim, top, gate):
-    got = swap(half_by_replica(send, dim), "shard", top)
+    return lax.dynamic_index_in_dim(x, parity(bits), dim, keepdims=False)
+
+
+def fetch_far(send, dim, top, gate, bits):
+    got = swap(half_by_replica(send, dim, bits), "shard", top)
     kept = got if gate is None else after(got, gate)
-    first, second = jnp.split(kept, 2, axis=dim)
     size = got.shape[dim]
-    return [
-        Group(got, [(1 << top, 0, 0, size)]),
-        Group(swap(first, "rep", 0), [(1 << top, 1, 0, size // 2)]),
-        Group(swap(second, "rep", 1), [(1 << top, 2, 0, size // 2)]),
+    count = len(bits)
+    parts = jnp.split(kept, count, axis=dim)
+    return [Group(got, [(1 << top, (0, bits), 0, size)])] + [
+        Group(swap(part, "rep", bit), [(1 << top, (1 + k, bits), 0, size // count)])
+        for k, (part, bit) in enumerate(zip(parts, bits))
     ]
 
 
-def gather_weight(x, gate=None):
+def gather_weight(x, gate, bits):
     top = bits_of("shard") - 1
-    groups = [Group(x, [(0, None, 0, x.shape[0])])] + fetch_far(x, 0, top, gate)
+    groups = [Group(x, [(0, None, 0, x.shape[0])])] + fetch_far(x, 0, top, gate, bits)
     for bit in reversed(range(top)):
         groups = groups + [join(groups, bit, [g.array for g in groups], 0)]
     return groups
 
 
-def split_weight(x, gate=None):
+def split_weight(x, gate, bits):
     me = lax.axis_index("shard")
     top = bits_of("shard") - 1
 
@@ -117,7 +117,8 @@
         start = ((me & (a.shape[0] - 1)) >> bit ^ 1) << bit
         return lax.dynamic_slice_in_dim(a, start, 1 << bit)
 
-    groups = [Group(x, [(0, None, 0, x.shape[1])])] + fetch_far(part_for(x, top), 1, top, gate)
+    groups = [Group(x, [(0, None, 0, x.shape[1])])]
+    groups += fetch_far(part_for(x, top), 1, top, gate, bits)
     for bit in reversed(range(top)):
         groups = groups + [join(groups, bit, [part_for(g.array, bit) for g in groups], 1)]
     return groups
@@ -226,14 +227,15 @@
 
 def weight_copies(held, refs, target, me, sems, rep, by_owner, rows):
     copies = []
-    own = (rep ^ (rep >> 1)) & 1
     for (pieces, shape), ref in zip(held, refs):
         source = ref.at[me & (shape[0] - 1)] if len(shape) == 3 else ref
         for j, code, first, count in pieces:
             start = (me ^ j if by_owner else j) * rows
             if code is not None:
-                start = start + (own if code == 0 else 1 - own) * (rows // 2)
-                start = start + (rows // 4 if code == 2 else 0)
+                place, bits = code
+                own = functools.reduce(lambda a, b: a ^ b, [(rep >> bit) & 1 for bit in bits])
+                start = start + (own if place == 0 else 1 - own) * (rows // 2)
+                start = start + max(place - 1, 0) * (rows // 2 // len(bits))
             place = target.at[pl.ds(pl.multiple_of(start, count), count), :]
             sem = sems.at[len(copies)]
             copies.append(pltpu.make_async_copy(source.at[first : first + count, :], place, sem))
@@ -576,11 +578,14 @@
     other_ref[...] = (keep_ref[1].astype(F32) + got_ref[1].astype(F32)).astype(BF16)
 
 
-def near_sums(keep, send, name):
+def near_sums(keep, send, name, gate=None):
     bits = bits_of("shard")
     for bit in range(bits - 2):
         keep, send = add_halves(keep, swap(send, "shard", bit))
     _, rows, model = keep.shape
+    got = swap(send, "shard", bits - 2)
+    if gate is not None:
+        got = after(got, gate)
     return pl.pallas_call(
         add_kernel,
         out_shape=[
@@ -589,7 +594,7 @@
         ],
         compiler_params=pltpu.CompilerParams(vmem_limit_bytes=16 << 20),
         name=name,
-    )(keep, swap(send, "shard", bits - 2))
+    )(keep, got)
 
 
 def output_kernel(mine, got, hidden, out_ref):
@@ -865,9 +870,8 @@
     gain2 = ln2_gain.astype(F32)[:, None]
     qkv_to = split_columns(w_qkv, gain1, n, 3, head_cols, width)
     in_to = split_columns(w_in, gain2, n, 2, ff, padded)
-    qkv_groups = split_weight(qkv_to)
-    out_groups = gather_weight(w_out)
-    toks = gather_rows(tokens, lambda: (out_groups[1].array,), apart=True)
+    qkv_groups = split_weight(qkv_to, None, (0, 1))
+    toks = gather_rows(tokens, apart=True)
 
     lane = jnp.arange(width, dtype=jnp.int32) % HEAD_DIM
     half = HEAD_DIM // 2
@@ -886,11 +890,11 @@
         ordered(
             functools.partial(attention_kernel, held_of(toks), held_of(qkv_groups), n, heads),
             5 + len(toks) + len(qkv_groups),
-            2,
+            0,
         ),
         in_specs=[SMEM_SPEC]
         + [VMEM_SPEC] * (4 + len(toks))
-        + [ANY_SPEC] * (len(qkv_groups) + 2),
+        + [ANY_SPEC] * len(qkv_groups),
         out_shape=(
             shape((seq, width), BF16),
             shape((seq + 2 * HALF, width), BF16),
@@ -903,10 +907,11 @@
         compiler_params=params,
         cost_estimate=work(40 * seq * model * width),
         name="attention",
-    )(place, *tables, *arrays_of(toks + qkv_groups + out_groups[2:4]))
+    )(place, *tables, *arrays_of(toks + qkv_groups))
 
     far_done = [toks[1].array, qkv_groups[1].array]
-    in_groups = split_weight(after(in_to, *far_done), attended)
+    out_groups = gather_weight(after(w_out, *far_done), attended, (2,))
+    in_groups = split_weight(after(in_to, *far_done), attended, (0, 1))
     atts = gather_rows(attended[:, :head_cols])
     block_shape = shape((n // 2, rows, model), BF16)
     hidden, normed2, up, in_w = pl.pallas_call(
@@ -1006,8 +1011,7 @@
         cost_estimate=work(8 * seq * model * padded),
         name="down_gradient",
     )(place, act, down_w, *arrays_of(cots), dproj)
-    dprojs = gather_rows(dproj)
-    mlp_mine, mlp_other = near_sums(mlp_keep, mlp_send, "near_sum_mlp")
+    dprojs = gather_rows(dproj, lambda: (down_keep,))
     in_reduce.step(0, [dprojs[1].array])
 
     out_shape = shape((slots, part, lanes), BF16)
@@ -1015,9 +1019,9 @@
         ordered(
             functools.partial(attention_back_kernel, held_of(dprojs), n, heads, far),
             len(dprojs) + 10,
-            3,
+            2,
         ),
-        in_specs=[SMEM_SPEC] + [VMEM_SPEC] * (len(dprojs) + 9) + [ANY_SPEC] * 3,
+        in_specs=[SMEM_SPEC] + [VMEM_SPEC] * (len(dprojs) + 9) + [ANY_SPEC] * 2,
         out_shape=[shape((seq, 3 * width), BF16), out_shape, out_shape],
         scratch_shapes=[
             pltpu.VMEM((seq, width), BF16),
@@ -1037,24 +1041,24 @@
         keys,
         values,
         *tables,
-        mlp_other,
         in_reduce.p[1],
         in_reduce.q[1],
     )
 
+    mlp_mine, mlp_other = near_sums(mlp_keep, mlp_send, "near_sum_mlp", dqkv)
     qkv_tiles = 3 * width // LANES
     qkv_counts = [qkv_tiles - qkv_tiles // 3, qkv_tiles // 3]
     in_reduce.step(1, [dqkv])
     down_reduce = add_halves(down_keep, after(swap(down_send, "rep", far[0]), dqkv))
     qkv_flows = pl.pallas_call(
-        ordered(functools.partial(qkv_kernel, n, qkv_counts, orders), 3, 3),
-        in_specs=[SMEM_SPEC] + [VMEM_SPEC] * 2 + [ANY_SPEC] * 3,
+        ordered(functools.partial(qkv_kernel, n, qkv_counts, orders), 3, 4),
+        in_specs=[SMEM_SPEC] + [VMEM_SPEC] * 2 + [ANY_SPEC] * 4,
         out_shape=[shape((slots, n * c, chunk, LANES), BF16) for c in qkv_counts for _ in range(2)],
         scratch_shapes=[pltpu.VMEM((part, 3 * width), F32)],
         compiler_params=params,
         cost_estimate=work(12 * seq * model * width),
         name="qkv_gradient",
-    )(place, normed1, dqkv, in_reduce.p[1], in_reduce.q[1], down_reduce[1])
+    )(place, normed1, dqkv, in_reduce.p[1], in_reduce.q[1], down_reduce[1], mlp_other)
     qkv_flows = [flow_rows(a) for a in qkv_flows]
     split = qkv_flows[2].shape[1]
     qkv_q = [jnp.concatenate(x, axis=1) for x in zip(qkv_flows[2:], (out_keep, out_send))]
@@ -1095,12 +1099,13 @@
         return [a[:, :size].reshape(a.shape[0], n * count, chunk, LANES) for a in pair]
 
     in_p, in_q = turned(*in_reduce.finish([[qkv_flows[0]]]), in_counts)
-    in_p, in_q = pair_gather(in_p, in_q, orders)
     down_share = replica_reduce(*down_reduce, far[1:], [[att_first]])
 
     att_reduce.step(1, [dnormed1_keep])
     att_p, att_q = att_reduce.finish([[other]])
-    down_pair = replica_spread(after(down_share, att_p), far)
+    att_done = att_p[:16]
+    in_p, in_q = pair_gather(after(in_p, att_done), after(in_q, att_done), orders)
+    down_pair = replica_spread(after(down_share, att_done), far)
     qkv_p, qkv_q = turned(att_p, att_q[:split], qkv_counts)
     att_p, att_q = pair_gather(qkv_p, jnp.concatenate([qkv_q, att_q[split:]]), orders)
 

time: 331 us -> 350 us (1.057)
  waiting for transfers between devices: 111 us -> 138 us
  starting transfers between devices: 61.2 us -> 50.3 us
    ppermute x57 -> x56, waiting for transfers between devices: 111 us -> 138 us  [swap(): return lax.ppermute(x, axis, [(i, i ^ 1 << bit) for i in range(size)])]
    ppermute x57 -> x56, starting transfers between devices: 61.2 us -> 50.3 us  [swap(): return lax.ppermute(x, axis, [(i, i ^ 1 << bit) for i in range(size)])]
    unnamed x100 -> x94, local copies, waits for them, and re-layouts: 17.7 us -> 19.2 us
  transfers between devices with their start and end apart: 57 -> 56, of which waited for: 22 -> 25; matrix products, arithmetic and copies ran while one was open for 8% -> 7% of each run, Pallas kernels for 28% -> 26%
where the time goes in v5:
time: 350 us; the launch traced here: 346 us
  waiting for transfers between devices  138 us (39%)
  Pallas kernels  110 us (31%)
  starting transfers between devices  50.3 us (14%)
  local copies, waits for them, and re-layouts  28.9 us (8%)
  other arithmetic  17.4 us (5%)
    ppermute x56, waiting for transfers between devices, swap(): return lax.ppermute(x, axis, [(i, i ^ 1 << bit) for i in range(size)])  138 us
    ppermute x56, starting transfers between devices, swap(): return lax.ppermute(x, axis, [(i, i ^ 1 << bit) for i in range(size)])  50.3 us
    unnamed x94, local copies, waits for them, and re-layouts  19.2 us
    pallas_call x1, Pallas kernels, shards(): pl.pallas_call(ordered(functools.partial(down_kernel, held_of(cots), n, f...  18.3 us
    pallas_call x1, Pallas kernels, shards(): pl.pallas_call(ordered(functools.partial(attention_back_kernel, held_of(d...  13.2 us
    pallas_call x1, Pallas kernels, shards(): pl.pallas_call(ordered(functools.partial(attention_kernel, held_of(toks),...  12.3 us
    pallas_call x2, Pallas kernels, columns_out(): pl.pallas_call(functools.partial(columns_out_kernel, n, ff, head_cols, wi...  12 us
    pallas_call x1, Pallas kernels, shards(): pl.pallas_call(functools.partial(dup_kernel, held_of(cots), n), in_specs=...  12 us
  transfers between devices with their start and end apart: 56, of which 25 were waited for; matrix products, arithmetic and copies ran while one was open for 7% of the time, Pallas kernels for 26%

profile of v5, /device:TPU:0, one launch (start us, length us, event | category | flops | bytes accessed | tf_op | source)
XLA Modules:
  0.0 345.5 jit_solution(2913921718600368792)
XLA Ops:
  4.8 3.0 collective-permute-start.3
  8.9 8.8 %collective-permute-done.3.refs_10_ = bf16[2,128,768]{2,1,0:T(8,128)(2,1)S(1)} collective-permute-done((bf16[2,128,768]{2,1,0:T(8,128)(2,1)S(1)}, bf16[2,128,768]{2,1,0:T(8,128)(2,1)S(1)}, u32[]{:S(2)}, u32[]{:S(2)}) %collective-permute-start.3) | collective-permute-done | bytes 393248 | tf_op jit(solution)/shard_map/ppermute | solution.py:36
  27.3 4.8 %sine_multiply_fusion = (f32[1024,256]{1,0:T(8,128)}, f32[1024,256]{1,0:T(8,128)}) fusion(f32[256]{0:T(256)S(1)} %get-tuple-element.178, f32[256]{0:T(256)S(1)} %get-tuple-element.179), kind=kLoop, calls=%fused_computation.5 | loop fusion | flops 524288 | bytes 2099200 | tf_op jit(solution)/shard_map/mul | solution.py:884
  40.8 12.3 %attention.1 = (bf16[1024,256]{1,0:T(8,128)(2,1)S(1)}, bf16[1152,256]{1,0:T(8,128)(2,1)}, bf16[1152,256]{1,0:T(8,128)(2,1)}, bf16[1024,256]{1,0:T(8,128)(2,1)S(1...) custom-call(s32[2]{0:T(128)S(1)} %pad_add_fusion.refs_0_.place_ref, ...), custom_call_target="tpu_custom_call" | custom-call | flops 10737418240 | bytes 4194304 | tf_op jit(solution)/shard_map/attention/pallas_call | solution.py:889
  53.1 4.9 %collective-permute-done.12.refs_12_ = bf16[2,128,1536]{2,1,0:T(8,128)(2,1)S(1)} collective-permute-done((bf16[2,128,1536]{2,1,0:T(8,128)(2,1)S(1)}, bf16[2,128,1536]{2,1,0:T(8,128)(2,1)S(1)}, u32[]{:S(2)}, u32[]{:S(2)}) %collective-permute-start.12) | collective-permute-done | bytes 786464 | tf_op jit(solution)/shard_map/ppermute | solution.py:36
  63.6 2.6 collective-permute-start.10
  66.2 4.6 %collective-permute-done.14.refs_14_ = bf16[2,64,1536]{2,1,0:T(8,128)(2,1)S(1)} collective-permute-done((bf16[2,64,1536]{2,1,0:T(8,128)(2,1)S(1)}, bf16[2,64,1536]{2,1,0:T(8,128)(2,1)S(1)}, u32[]{:S(2)}, u32[]{:S(2)}) %collective-permute-start.14) | collective-permute-done | bytes 393248 | tf_op jit(solution)/shard_map/ppermute | solution.py:36
  71.1 5.6 %collective-permute-done.10.refs_9_ = bf16[128,1024]{1,0:T(8,128)(2,1)S(1)} collective-permute-done((bf16[128,1024]{1,0:T(8,128)(2,1)S(1)}, bf16[128,1024]{1,0:T(8,128)(2,1)S(1)}, u32[]{:S(2)}, u32[]{:S(2)}) %collective-permute-start.10) | collective-permute-done | bytes 262176 | tf_op jit(solution)/shard_map/ppermute | solution.py:36
  82.1 11.9 %up_projection.1 = (f32[256,1024]{1,0:T(8,128)}, bf16[1024,1024]{1,0:T(8,128)(2,1)}, f32[1024,1536]{1,0:T(8,128)}, bf16[1024,1536]{1,0:T(8,128)(2,1)}) custom-call(s32[2]{0:T(128)S(1)} %pad_add_fusion.refs_0_.place_ref, bf16[256,1024]{1,0:T(8,128)(2,1)} %tokens.1, bf16[256,1024]{1,0:T(8,128)(2,1)} %collective-permute-done.refs_6_.refs_1_, ...), custom_call_target="tpu_custom_call" | custom-call | flops 9663676416 | bytes 4194304 | tf_op jit(solution)/shard_map/up_projection/pallas_call | solution.py:917
  94.3 2.5 collective-permute-done.17.refs_2_.refs_5_
  97.8 12.0 %dup.1 = (bf16[1024,768]{1,0:T(8,128)(2,1)}, bf16[1024,1536]{1,0:T(8,128)(2,1)}, bf16[2,256,1024]{2,1,0:T(8,128)(2,1)}, bf16[2,256,1024]{2,1,0:T(8,128)(2,1)}) custom-call(f32[1024,1536]{1,0:T(8,128)} %get-tuple-element.77.up_ref, bf16[1024,1536]{1,0:T(8,128)(2,1)} %get-tuple-element.78.w_in_ref, bf16[656,1024]{1,0:T(8,128)(2,1)} %refs_2_.1, ...), custom_call_target="tpu_custom_call" | custom-call | flops 11274289152 | bytes 4194304 | tf_op jit(solution)/shard_map/dup/pallas_call | solution.py:949
  110.0 2.7 collective-permute-done.18.got_ref
  115.7 7.5 %in_gradient.1 = (bf16[4,24,32,128]{3,2,1,0:T(8,128)(2,1)}, bf16[4,24,32,128]{3,2,1,0:T(8,128)(2,1)}, bf16[4,20,32,128]{3,2,1,0:T(8,128)(2,1)S(1)}, bf16[4,20,32,128]{3,2,1,0:T(8,128)(2,1)S(1)}) custom-call(s32[2]{0:T(128)S(1)} %pad_add_fusion.refs_0_.place_ref, bf16[1024,1024]{1,0:T(8,128)(2,1)} %get-tuple-element.87.refs_1_, ...), custom_call_target="tpu_custom_call" | custom-call | flops 6442450944 | bytes 4194304 | tf_op jit(solution)/shard_map/in_gradient/pallas_call | solution.py:987
  124.7 3.5 %collective-permute-done.19.refs_1_ = bf16[256,1024]{1,0:T(8,128)(2,1)S(1)} collective-permute-done((bf16[256,1024]{1,0:T(8,128)(2,1)S(1)}, bf16[256,1024]{1,0:T(8,128)(2,1)S(1)}, u32[]{:S(2)}, u32[]{:S(2)}) %collective-permute-start.19) | collective-permute-done | bytes 524320 | tf_op jit(solution)/shard_map/ppermute | solution.py:36
  132.5 18.3 %down_gradient.1 = (bf16[4,656,128]{2,1,0:T(8,128)(2,1)}, bf16[4,656,128]{2,1,0:T(8,128)(2,1)}, bf16[2,256,1024]{2,1,0:T(8,128)(2,1)}, bf16[2,256,1024]{2,1,0:T(8,128)(2,1)}) custom-call(s32[2]{0:T(128)S(1)} %pad_add_fusion.refs_0_.place_ref, bf16[1024,768]{1,0:T(8,128)(2,1)} %get-tuple-element.81.refs_1_, bf16[656,1024]{1,0:T(8,128)(2,1)} %refs_2_.1, ...), custom_call_target="tpu_custom_call" | custom-call | flops 6442450944 | bytes 4194304 | tf_op jit(solution)/shard_map/down_gradient/pallas_call | solution.py:1005
  158.6 13.2 %attention_back.1 = (bf16[1024,768]{1,0:T(8,128)(2,1)}, bf16[4,256,128]{2,1,0:T(8,128)(2,1)S(1)}, bf16[4,256,128]{2,1,0:T(8,128)(2,1)S(1)}) custom-call(s32[2]{0:T(128)S(1)} %pad_add_fusion.refs_0_.place_ref, bf16[256,1024]{1,0:T(8,128)(2,1)S(1)} %get-tuple-element.90.refs_6_.refs_1_, bf16[256,1024]{1,0:T(8,128)(2,1)} %copy-done.35, ...), custom_call_target="tpu_custom_call" | custom-call | flops 10737418240 | bytes 4194304 | tf_op jit(solution)/shard_map/attention_back/pallas_call | solution.py:1018
  171.8 5.6 %collective-permute-done.26 = bf16[2,768,128]{2,1,0:T(8,128)(2,1)S(1)} collective-permute-done((bf16[2,768,128]{2,1,0:T(8,128)(2,1)S(1)}, bf16[2,768,128]{2,1,0:T(8,128)(2,1)S(1)}, u32[]{:S(2)}, u32[]{:S(2)}) %collective-permute-start.26) | collective-permute-done | bytes 393248 | tf_op jit(solution)/shard_map/ppermute | solution.py:36
  180.4 4.8 %qkv_gradient.1 = (bf16[4,16,32,128]{3,2,1,0:T(8,128)(2,1)S(1)}, bf16[4,16,32,128]{3,2,1,0:T(8,128)(2,1)}, bf16[4,8,32,128]{3,2,1,0:T(8,128)(2,1)S(1)}, bf16[4,8,32,128]{3,2,1,0:T(8,128)(2,1)S(1)}) custom-call(s32[2]{0:T(128)S(1)} %pad_add_fusion.refs_0_.place_ref, bf16[1024,1024]{1,0:T(8,128)(2,1)} %get-tuple-element.107.refs_1_, ...), custom_call_target="tpu_custom_call" | custom-call | flops 3221225472 | bytes 4194304 | tf_op jit(solution)/shard_map/qkv_gradient/pallas_call | solution.py:1053
  188.9 13.8 %collective-permute-done.43 = bf16[1,1408,128]{2,1,0:T(8,128)(2,1)S(1)} collective-permute-done((bf16[1,1408,128]{2,1,0:T(8,128)(2,1)S(1)}, bf16[1,1408,128]{2,1,0:T(8,128)(2,1)S(1)}, u32[]{:S(2)}, u32[]{:S(2)}) %collective-permute-start.43) | collective-permute-done | bytes 360480 | tf_op jit(solution)/shard_map/ppermute | solution.py:36
  210.2 4.7 %project_back.1 = (bf16[2,256,1024]{2,1,0:T(8,128)(2,1)}, bf16[2,256,1024]{2,1,0:T(8,128)(2,1)}) custom-call(s32[2]{0:T(128)S(1)} %pad_add_fusion.refs_0_.place_ref, bf16[1024,768]{1,0:T(8,128)(2,1)} %get-tuple-element.103.refs_2_.refs_1_, bf16[1024,768]{1,0:T(8,128)(2,1)} %get-tuple-element.113.refs_2_, bf16[256,1024]{1,0:T(8,128)(2,1)S(1)} %copy-done.16, ...), custom_call_target="tpu_custom_call" | custom-call | flops 1610612736 | bytes 4194304 | tf_op jit(solution)/shard_map/project_back/pallas_call | solution.py:1075
  220.1 13.9 %collective-permute-done.35 = bf16[1,1024,128]{2,1,0:T(8,128)(2,1)S(1)} collective-permute-done((bf16[1,1024,128]{2,1,0:T(8,128)(2,1)S(1)}, bf16[1,1024,128]{2,1,0:T(8,128)(2,1)S(1)}, u32[]{:S(2)}, u32[]{:S(2)}) %collective-permute-start.35) | collective-permute-done | bytes 262176 | tf_op jit(solution)/shard_map/ppermute | solution.py:36
  235.6 3.2 collective-permute-done.36
  240.3 2.8 collective-permute-start.38
  243.1 22.8 %collective-permute-done.53 = bf16[1,656,128]{2,1,0:T(8,128)(2,1)S(1)} collective-permute-done((bf16[1,656,128]{2,1,0:T(8,128)(2,1)S(1)}, bf16[1,656,128]{2,1,0:T(8,128)(2,1)S(1)}, u32[]{:S(2)}, u32[]{:S(2)}) %collective-permute-start.53) | collective-permute-done | bytes 167968 | tf_op jit(solution)/shard_map/ppermute | solution.py:36
  272.1 4.6 %collective-permute-done.54 = bf16[2,656,128]{2,1,0:T(8,128)(2,1)S(1)} collective-permute-done((bf16[2,656,128]{2,1,0:T(8,128)(2,1)S(1)}, bf16[2,656,128]{2,1,0:T(8,128)(2,1)S(1)}, u32[]{:S(2)}, u32[]{:S(2)}) %collective-permute-start.54) | collective-permute-done | bytes 335904 | tf_op jit(solution)/shard_map/ppermute | solution.py:36
  280.0 3.8 %collective-permute-done.49 = bf16[2,640,128]{2,1,0:T(8,128)(2,1)S(1)} collective-permute-done((bf16[2,640,128]{2,1,0:T(8,128)(2,1)S(1)}, bf16[2,640,128]{2,1,0:T(8,128)(2,1)S(1)}, u32[]{:S(2)}, u32[]{:S(2)}) %collective-permute-start.49) | collective-permute-done | bytes 327712 | tf_op jit(solution)/shard_map/ppermute | solution.py:36
  285.2 4.2 %collective-permute-done.41 = bf16[2,512,128]{2,1,0:T(8,128)(2,1)S(1)} collective-permute-done((bf16[2,512,128]{2,1,0:T(8,128)(2,1)S(1)}, bf16[2,512,128]{2,1,0:T(8,128)(2,1)S(1)}, u32[]{:S(2)}, u32[]{:S(2)}) %collective-permute-start.41) | collective-permute-done | bytes 262176 | tf_op jit(solution)/shard_map/ppermute | solution.py:36
  299.6 2.8 input_grad.1
  302.5 3.3 rows_out.3
  305.8 19.5 %collective-permute-done.42.refs_1_ = bf16[4,512,128]{2,1,0:T(8,128)(2,1)} collective-permute-done((bf16[4,512,128]{2,1,0:T(8,128)(2,1)}, bf16[4,512,128]{2,1,0:T(8,128)(2,1)}, u32[]{:S(2)}, u32[]{:S(2)}) %collective-permute-start.42) | collective-permute-done | bytes 524320 | tf_op jit(solution)/shard_map/ppermute | solution.py:36
  326.2 5.2 %columns_out.2 = (f32[8,32,3072]{2,1,0:T(8,128)}, f32[8,32,1]{2,1,0:T(8,128)S(1)}) custom-call(s32[2]{0:T(128)S(1)} %pad_add_fusion.refs_0_.place_ref, f32[8,32,1]{2,1,0:T(8,128)S(1)} %copy-done.18, bf16[8,32,3072]{2,1,0:T(8,128)(2,1)S(1)} %bitcast.83, bf16[4,16,32,128]{3,2,1,0:T(8,128)(2,1)} %bitcast.34.refs_0_, bf16[4,16,32,128]{3,2,1,0:T(8,128)(2,1)} %bitcast.35.refs_1_, ...), custom_call_target="tpu_custom_call" | custom-call | tf_op jit(solution)/shard_map/columns_out/pallas_call | solution.py:764
  336.2 6.8 %columns_out.3 = (f32[8,32,5248]{2,1,0:T(8,128)}, f32[8,32,1]{2,1,0:T(8,128)S(1)}) custom-call(s32[2]{0:T(128)S(1)} %pad_add_fusion.refs_0_.place_ref, f32[8,32,1]{2,1,0:T(8,128)S(1)} %copy-done.17, bf16[8,32,5248]{2,1,0:T(8,128)(2,1)S(1)} %bitcast.82, bf16[4,24,32,128]{3,2,1,0:T(8,128)(2,1)S(1)} %bitcast.84, bf16[4,24,32,128]{3,2,1,0:T(8,128)(2,1)} %bitcast.50.refs_1_, ...), custom_call_target="tpu_custom_call" | custom-call | tf_op jit(solution)/shard_map/columns_out/pallas_call | solution.py:764
  (277 shorter events, 103.7 us)
Async XLA Ops:
  7.8 27.7 %collective-permute-start = (bf16[256,1024]{1,0:T(8,128)(2,1)}, bf16[256,1024]{1,0:T(8,128)(2,1)}, u32[]{:S(2)}, u32[]{:S(2)}) collective-permute-start(bf16[256,1024]{1,0:T(8,128)(2,1)} %tokens.1), channel_id=1, source_target_pairs={{0,2},{1,3},{2,0},{3,1},{4,6},{5,7},{6,4},{7,5},{8,10},{9,11},{10,... | collective-permute-start | bytes 1572872 | tf_op jit(solution)/shard_map/ppermute | solution.py:36
  7.9 31.9 %collective-permute-start.1 = (bf16[256,1024]{1,0:T(8,128)(2,1)}, bf16[256,1024]{1,0:T(8,128)(2,1)}, u32[]{:S(2)}, u32[]{:S(2)}) collective-permute-start(bf16[256,1024]{1,0:T(8,128)(2,1)} %tokens.1), channel_id=1, source_target_pairs={{0,1},{1,0},{2,3},{3,2},{4,5},{5,4},{6,7},{7,6},{8,9},{9,8},{10,11... | collective-permute-start | bytes 1572872 | tf_op jit(solution)/shard_map/ppermute | solution.py:36
  37.6 20.5 %collective-permute-start.12 = (bf16[2,128,1536]{2,1,0:T(8,128)(2,1)S(1)}, bf16[2,128,1536]{2,1,0:T(8,128)(2,1)S(1)}, u32[]{:S(2)}, u32[]{:S(2)}) collective-permute-start(bf16[2,128,1536]{2,1,0:T(8,128)(2,1)S(1)} %dynamic-slice_bitcast_fusion), channel_id=1, source_target_pairs={{0,2},{1,3},{2,0},{3,1},{4,6},{5,7},{6,4},{7,5},{8,10},{9,11},{10,... | collective-permute-start | bytes 2359304 | tf_op jit(solution)/shard_map/ppermute | solution.py:36
  39.1 24.5 %collective-permute-start.9 = (bf16[128,1024]{1,0:T(8,128)(2,1)S(1)}, bf16[128,1024]{1,0:T(8,128)(2,1)S(1)}, u32[]{:S(2)}, u32[]{:S(2)}) collective-permute-start(bf16[128,1024]{1,0:T(8,128)(2,1)S(1)} %dynamic-slice_bitcast_fusion.2), channel_id=1, source_target_pairs={{0,2},{1,3},{2,0},{3,1},{4,6},{5,7},{6,4},{7,5},{8,10},{9,11},{10,... | collective-permute-start | bytes 786440 | tf_op jit(solution)/shard_map/ppermute | solution.py:36
  61.4 15.5 %collective-permute-start.7 = (bf16[1024,256]{1,0:T(8,128)(2,1)S(1)}, bf16[1024,256]{1,0:T(8,128)(2,1)S(1)}, u32[]{:S(2)}, u32[]{:S(2)}) collective-permute-start(bf16[1024,256]{1,0:T(8,128)(2,1)S(1)} %get-tuple-element.72.refs_4_.refs_5_), channel_id=1, source_target_pairs={{0,2},{1,3},{2,0},{3,1},{4,6},{5,7},{6,4},{7,5},{8,10},{9,11},{10,... | collective-permute-start | bytes 1572872 | tf_op jit(solution)/shard_map/ppermute | solution.py:36
  77.6 16.4 %collective-permute-start.16 = (bf16[256,1024]{1,0:T(8,128)(2,1)S(1)}, bf16[256,1024]{1,0:T(8,128)(2,1)S(1)}, u32[]{:S(2)}, u32[]{:S(2)}) collective-permute-start(bf16[256,1024]{1,0:T(8,128)(2,1)S(1)} %copy-done.8), channel_id=1, source_target_pairs={{0,2},{1,3},{2,0},{3,1},{4,6},{5,7},{6,4},{7,5},{8,10},{9,11},{10,... | collective-permute-start | bytes 1572872 | tf_op jit(solution)/shard_map/ppermute | solution.py:36
  114.2 14.0 %collective-permute-start.19 = (bf16[256,1024]{1,0:T(8,128)(2,1)S(1)}, bf16[256,1024]{1,0:T(8,128)(2,1)S(1)}, u32[]{:S(2)}, u32[]{:S(2)}) collective-permute-start(bf16[256,1024]{1,0:T(8,128)(2,1)S(1)} %get-tuple-element.85.refs_3_), channel_id=1, source_target_pairs={{0,2},{1,3},{2,0},{3,1},{4,6},{5,7},{6,4},{7,5},{8,10},{9,11},{10,... | collective-permute-start | bytes 1572872 | tf_op jit(solution)/shard_map/ppermute | solution.py:36
  123.2 29.2 %collective-permute-start.24 = (bf16[4,640,128]{2,1,0:T(8,128)(2,1)S(1)}, bf16[4,640,128]{2,1,0:T(8,128)(2,1)}, u32[]{:S(2)}, u32[]{:S(2)}) collective-permute-start(bf16[4,640,128]{2,1,0:T(8,128)(2,1)S(1)} %bitcast.91), channel_id=1, source_target_pairs={{0,8},{4,12},{8,0},{12,4},{16,24},{20,28},{24,16},{28,20},{1,9},{5... | collective-permute-start | bytes 1966088 | tf_op jit(solution)/shard_map/ppermute | solution.py:36
  123.2 29.2 %collective-permute-start.23 = (bf16[4,768,128]{2,1,0:T(8,128)(2,1)}, bf16[4,768,128]{2,1,0:T(8,128)(2,1)S(1)}, u32[]{:S(2)}, u32[]{:S(2)}) collective-permute-start(bf16[4,768,128]{2,1,0:T(8,128)(2,1)} %bitcast.112), channel_id=1, source_target_pairs={{0,4},{4,0},{8,12},{12,8},{16,20},{20,16},{24,28},{28,24},{1,5},{5... | collective-permute-start | bytes 2359304 | tf_op jit(solution)/shard_map/ppermute | solution.py:36
  131.1 19.8 %collective-permute-start.21 = (bf16[256,1024]{1,0:T(8,128)(2,1)S(1)}, bf16[256,1024]{1,0:T(8,128)(2,1)S(1)}, u32[]{:S(2)}, u32[]{:S(2)}) collective-permute-start(bf16[256,1024]{1,0:T(8,128)(2,1)S(1)} %get-tuple-element.90.refs_6_.refs_1_), channel_id=1, source_target_pairs={{0,2},{1,3},{2,0},{3,1},{4,6},{5,7},{6,4},{7,5},{8,10},{9,11},{10,... | collective-permute-start | bytes 1572872 | tf_op jit(solution)/shard_map/ppermute | solution.py:36
  152.2 19.5 %collective-permute-start.28 = (bf16[4,656,128]{2,1,0:T(8,128)(2,1)}, bf16[4,656,128]{2,1,0:T(8,128)(2,1)S(1)}, u32[]{:S(2)}, u32[]{:S(2)}) collective-permute-start(bf16[4,656,128]{2,1,0:T(8,128)(2,1)} %get-tuple-element.110), channel_id=1, source_target_pairs={{0,8},{4,12},{8,0},{12,4},{16,24},{20,28},{24,16},{28,20},{1,9},{5... | collective-permute-start | bytes 2015240 | tf_op jit(solution)/shard_map/ppermute | solution.py:36
  152.3 25.2 %collective-permute-start.20 = (bf16[2,256,1024]{2,1,0:T(8,128)(2,1)}, bf16[2,256,1024]{2,1,0:T(8,128)(2,1)S(1)}, u32[]{:S(2)}, u32[]{:S(2)}) collective-permute-start(bf16[2,256,1024]{2,1,0:T(8,128)(2,1)} %get-tuple-element.92), channel_id=1, source_target_pairs={{0,1},{1,0},{2,3},{3,2},{4,5},{5,4},{6,7},{7,6},{8,9},{9,8},{10,11... | collective-permute-start | bytes 3145736 | tf_op jit(solution)/shard_map/ppermute | solution.py:36
  153.7 18.1 %collective-permute-start.27 = (bf16[2,640,128]{2,1,0:T(8,128)(2,1)S(1)}, bf16[2,640,128]{2,1,0:T(8,128)(2,1)S(1)}, u32[]{:S(2)}, u32[]{:S(2)}) collective-permute-start(bf16[2,640,128]{2,1,0:T(8,128)(2,1)S(1)} %get-tuple-element.151.refs_14_), channel_id=1, source_target_pairs={{0,4},{4,0},{8,12},{12,8},{16,20},{20,16},{24,28},{28,24},{1,5},{5... | collective-permute-start | bytes 983048 | tf_op jit(solution)/shard_map/ppermute | solution.py:36
  155.6 21.8 %collective-permute-start.26 = (bf16[2,768,128]{2,1,0:T(8,128)(2,1)S(1)}, bf16[2,768,128]{2,1,0:T(8,128)(2,1)S(1)}, u32[]{:S(2)}, u32[]{:S(2)}) collective-permute-start(bf16[2,768,128]{2,1,0:T(8,128)(2,1)S(1)} %get-tuple-element.143.refs_13_), channel_id=1, source_target_pairs={{0,8},{4,12},{8,0},{12,4},{16,24},{20,28},{24,16},{28,20},{1,9},{5... | collective-permute-start | bytes 1179656 | tf_op jit(solution)/shard_map/ppermute | solution.py:36
  177.6 29.1 %collective-permute-start.51 = (bf16[2,656,128]{2,1,0:T(8,128)(2,1)S(1)}, bf16[2,656,128]{2,1,0:T(8,128)(2,1)}, u32[]{:S(2)}, u32[]{:S(2)}) collective-permute-start(bf16[2,656,128]{2,1,0:T(8,128)(2,1)S(1)} %get-tuple-element.137.refs_5_), channel_id=1, source_target_pairs={{0,4},{4,0},{8,12},{12,8},{16,20},{20,16},{24,28},{28,24},{1,5},{5... | collective-permute-start | bytes 1007624 | tf_op jit(solution)/shard_map/ppermute | solution.py:36
  179.5 28.8 %collective-permute-start.25 = (bf16[256,1024]{1,0:T(8,128)(2,1)S(1)}, bf16[256,1024]{1,0:T(8,128)(2,1)S(1)}, u32[]{:S(2)}, u32[]{:S(2)}) collective-permute-start(bf16[256,1024]{1,0:T(8,128)(2,1)S(1)} %get-tuple-element.106.refs_6_), channel_id=1, source_target_pairs={{0,2},{1,3},{2,0},{3,1},{4,6},{5,7},{6,4},{7,5},{8,10},{9,11},{10,... | collective-permute-start | bytes 1572872 | tf_op jit(solution)/shard_map/ppermute | solution.py:36
  185.2 18.9 %collective-permute-start.29 = (bf16[4,512,128]{2,1,0:T(8,128)(2,1)}, bf16[4,512,128]{2,1,0:T(8,128)(2,1)S(1)}, u32[]{:S(2)}, u32[]{:S(2)}) collective-permute-start(bf16[4,512,128]{2,1,0:T(8,128)(2,1)} %bitcast.113), channel_id=1, source_target_pairs={{0,4},{4,0},{8,12},{12,8},{16,20},{20,16},{24,28},{28,24},{1,5},{5... | collective-permute-start | bytes 1572872 | tf_op jit(solution)/shard_map/ppermute | solution.py:36
  185.7 17.0 %collective-permute-start.43 = (bf16[1,1408,128]{2,1,0:T(8,128)(2,1)S(1)}, bf16[1,1408,128]{2,1,0:T(8,128)(2,1)S(1)}, u32[]{:S(2)}, u32[]{:S(2)}) collective-permute-start(bf16[1,1408,128]{2,1,0:T(8,128)(2,1)S(1)} %pad_maximum_fusion.12), channel_id=1, source_target_pairs={{0,16},{4,20},{8,24},{12,28},{16,0},{20,4},{24,8},{28,12},{1,17},{... | collective-permute-start | bytes 1081352 | tf_op jit(solution)/shard_map/ppermute | solution.py:36
  187.0 19.4 %collective-permute-start.30 = (bf16[4,512,128]{2,1,0:T(8,128)(2,1)S(1)}, bf16[4,512,128]{2,1,0:T(8,128)(2,1)S(1)}, u32[]{:S(2)}, u32[]{:S(2)}) collective-permute-start(bf16[4,512,128]{2,1,0:T(8,128)(2,1)S(1)} %pad_maximum_fusion.10), channel_id=1, source_target_pairs={{0,8},{4,12},{8,0},{12,4},{16,24},{20,28},{24,16},{28,20},{1,9},{5... | collective-permute-start | bytes 1572872 | tf_op jit(solution)/shard_map/ppermute | solution.py:36
  215.7 18.3 %collective-permute-start.35 = (bf16[1,1024,128]{2,1,0:T(8,128)(2,1)S(1)}, bf16[1,1024,128]{2,1,0:T(8,128)(2,1)S(1)}, u32[]{:S(2)}, u32[]{:S(2)}) collective-permute-start(bf16[1,1024,128]{2,1,0:T(8,128)(2,1)S(1)} %pad_maximum_fusion.17), channel_id=1, source_target_pairs={{0,16},{4,20},{8,24},{12,28},{16,0},{20,4},{24,8},{28,12},{1,17},{... | collective-permute-start | bytes 786440 | tf_op jit(solution)/shard_map/ppermute | solution.py:36
  217.6 21.4 %collective-permute-start.52 = (bf16[1,656,128]{2,1,0:T(8,128)(2,1)S(1)}, bf16[1,656,128]{2,1,0:T(8,128)(2,1)S(1)}, u32[]{:S(2)}, u32[]{:S(2)}) collective-permute-start(bf16[1,656,128]{2,1,0:T(8,128)(2,1)S(1)} %add_convert_fusion.9), channel_id=1, source_target_pairs={{0,16},{4,20},{8,24},{12,28},{16,0},{20,4},{24,8},{28,12},{1,17},{... | collective-permute-start | bytes 503816 | tf_op jit(solution)/shard_map/ppermute | solution.py:36
  235.5 31.0 %collective-permute-start.46 = (bf16[1,1408,128]{2,1,0:T(8,128)(2,1)S(1)}, bf16[1,1408,128]{2,1,0:T(8,128)(2,1)S(1)}, u32[]{:S(2)}, u32[]{:S(2)}) collective-permute-start(bf16[1,1408,128]{2,1,0:T(8,128)(2,1)S(1)} %maximum_bitcast_fusion.1), channel_id=1, source_target_pairs={{0,16},{4,20},{8,24},{12,28},{16,0},{20,4},{24,8},{28,12},{1,17},{... | collective-permute-start | bytes 1081352 | tf_op jit(solution)/shard_map/ppermute | solution.py:36
  239.9 26.0 %collective-permute-start.53 = (bf16[1,656,128]{2,1,0:T(8,128)(2,1)S(1)}, bf16[1,656,128]{2,1,0:T(8,128)(2,1)S(1)}, u32[]{:S(2)}, u32[]{:S(2)}) collective-permute-start(bf16[1,656,128]{2,1,0:T(8,128)(2,1)S(1)} %bitcast.94), channel_id=1, source_target_pairs={{0,16},{4,20},{8,24},{12,28},{16,0},{20,4},{24,8},{28,12},{1,17},{... | collective-permute-start | bytes 503816 | tf_op jit(solution)/shard_map/ppermute | solution.py:36
  240.3 31.2 %collective-permute-start.38 = (bf16[1,1024,128]{2,1,0:T(8,128)(2,1)S(1)}, bf16[1,1024,128]{2,1,0:T(8,128)(2,1)S(1)}, u32[]{:S(2)}, u32[]{:S(2)}) collective-permute-start(bf16[1,1024,128]{2,1,0:T(8,128)(2,1)S(1)} %maximum_bitcast_fusion.2), channel_id=1, source_target_pairs={{0,16},{4,20},{8,24},{12,28},{16,0},{20,4},{24,8},{28,12},{1,17},{... | collective-permute-start | bytes 786440 | tf_op jit(solution)/shard_map/ppermute | solution.py:36
  266.6 26.5 %collective-permute-start.32 = (bf16[256,1024]{1,0:T(8,128)(2,1)S(1)}, bf16[256,1024]{1,0:T(8,128)(2,1)S(1)}, u32[]{:S(2)}, u32[]{:S(2)}) collective-permute-start(bf16[256,1024]{1,0:T(8,128)(2,1)S(1)} %get-tuple-element.122), channel_id=1, source_target_pairs={{0,2},{1,3},{2,0},{3,1},{4,6},{5,7},{6,4},{7,5},{8,10},{9,11},{10,... | collective-permute-start | bytes 1572872 | tf_op jit(solution)/shard_map/ppermute | solution.py:36
  268.0 15.8 %collective-permute-start.49 = (bf16[2,640,128]{2,1,0:T(8,128)(2,1)S(1)}, bf16[2,640,128]{2,1,0:T(8,128)(2,1)S(1)}, u32[]{:S(2)}, u32[]{:S(2)}) collective-permute-start(bf16[2,640,128]{2,1,0:T(8,128)(2,1)S(1)} %pad_maximum_fusion.14), channel_id=1, source_target_pairs={{0,4},{4,0},{8,12},{12,8},{16,20},{20,16},{24,28},{28,24},{1,5},{5... | collective-permute-start | bytes 983048 | tf_op jit(solution)/shard_map/ppermute | solution.py:36
  271.6 17.8 %collective-permute-start.41 = (bf16[2,512,128]{2,1,0:T(8,128)(2,1)S(1)}, bf16[2,512,128]{2,1,0:T(8,128)(2,1)S(1)}, u32[]{:S(2)}, u32[]{:S(2)}) collective-permute-start(bf16[2,512,128]{2,1,0:T(8,128)(2,1)S(1)} %get-tuple-element.154), channel_id=1, source_target_pairs={{0,4},{4,0},{8,12},{12,8},{16,20},{20,16},{24,28},{28,24},{1,5},{5... | collective-permute-start | bytes 786440 | tf_op jit(solution)/shard_map/ppermute | solution.py:36
  279.9 22.5 %collective-permute-start.55 = (bf16[4,656,128]{2,1,0:T(8,128)(2,1)}, bf16[4,656,128]{2,1,0:T(8,128)(2,1)}, u32[]{:S(2)}, u32[]{:S(2)}) collective-permute-start(bf16[4,656,128]{2,1,0:T(8,128)(2,1)} %pad_maximum_fusion.7.refs_0_), channel_id=1, source_target_pairs={{0,8},{4,12},{8,0},{12,4},{16,24},{20,28},{24,16},{28,20},{1,9},{5... | collective-permute-start | bytes 2015240 | tf_op jit(solution)/shard_map/ppermute | solution.py:36
  283.8 52.4 %collective-permute-start.48 = (bf16[4,768,128]{2,1,0:T(8,128)(2,1)S(1)}, bf16[4,768,128]{2,1,0:T(8,128)(2,1)}, u32[]{:S(2)}, u32[]{:S(2)}) collective-permute-start(bf16[4,768,128]{2,1,0:T(8,128)(2,1)S(1)} %pad_maximum_fusion.6), channel_id=1, source_target_pairs={{0,4},{4,0},{8,12},{12,8},{16,20},{20,16},{24,28},{28,24},{1,5},{5... | collective-permute-start | bytes 2359304 | tf_op jit(solution)/shard_map/ppermute | solution.py:36
  289.4 46.7 %collective-permute-start.50 = (bf16[4,640,128]{2,1,0:T(8,128)(2,1)}, bf16[4,640,128]{2,1,0:T(8,128)(2,1)}, u32[]{:S(2)}, u32[]{:S(2)}) collective-permute-start(bf16[4,640,128]{2,1,0:T(8,128)(2,1)} %pad_maximum_fusion.8), channel_id=1, source_target_pairs={{0,8},{4,12},{8,0},{12,4},{16,24},{20,28},{24,16},{28,20},{1,9},{5... | collective-permute-start | bytes 1966088 | tf_op jit(solution)/shard_map/ppermute | solution.py:36
  290.3 35.0 %collective-permute-start.42 = (bf16[4,512,128]{2,1,0:T(8,128)(2,1)}, bf16[4,512,128]{2,1,0:T(8,128)(2,1)}, u32[]{:S(2)}, u32[]{:S(2)}) collective-permute-start(bf16[4,512,128]{2,1,0:T(8,128)(2,1)} %pad_maximum_fusion.9.refs_0_), channel_id=1, source_target_pairs={{0,8},{4,12},{8,0},{12,4},{16,24},{20,28},{24,16},{28,20},{1,9},{5... | collective-permute-start | bytes 1572872 | tf_op jit(solution)/shard_map/ppermute | solution.py:36
  293.9 32.3 %collective-permute-start.40 = (bf16[4,512,128]{2,1,0:T(8,128)(2,1)}, bf16[4,512,128]{2,1,0:T(8,128)(2,1)}, u32[]{:S(2)}, u32[]{:S(2)}) collective-permute-start(bf16[4,512,128]{2,1,0:T(8,128)(2,1)} %pad_maximum_fusion.11), channel_id=1, source_target_pairs={{0,4},{4,0},{8,12},{12,8},{16,20},{20,16},{24,28},{28,24},{1,5},{5... | collective-permute-start | bytes 1572872 | tf_op jit(solution)/shard_map/ppermute | solution.py:36
  (71 other events, 488.8 us)

commit v6 on v5

--- a/solution.py
+++ b/solution.py
@@ -91,7 +91,7 @@
 
 def fetch_far(send, dim, top, gate, bits):
     got = swap(half_by_replica(send, dim, bits), "shard", top)
-    kept = got if gate is None else after(got, gate)
+    kept = after(got, *gate) if gate else got
     size = got.shape[dim]
     count = len(bits)
     parts = jnp.split(kept, count, axis=dim)
@@ -870,9 +870,6 @@
     gain2 = ln2_gain.astype(F32)[:, None]
     qkv_to = split_columns(w_qkv, gain1, n, 3, head_cols, width)
     in_to = split_columns(w_in, gain2, n, 2, ff, padded)
-    qkv_groups = split_weight(qkv_to, None, (0, 1))
-    toks = gather_rows(tokens, apart=True)
-
     lane = jnp.arange(width, dtype=jnp.int32) % HEAD_DIM
     half = HEAD_DIM // 2
     frequency = jnp.exp(-math.log(rope_base) * 2.0 * (lane % half).astype(F32) / HEAD_DIM)
@@ -885,6 +882,9 @@
         jnp.broadcast_to(ids[:, None], (seq, LANES)),
         jnp.pad(ids, (HALF, HALF), constant_values=-1)[None],
     )
+
+    qkv_groups = split_weight(qkv_to, (tables[0], tables[1], in_to), (0, 1))
+    toks = gather_rows(tokens, apart=True)
 
     queries, keys, values, attended, normed1, qkv_w = pl.pallas_call(
         ordered(
@@ -909,9 +909,8 @@
         name="attention",
     )(place, *tables, *arrays_of(toks + qkv_groups))
 
-    far_done = [toks[1].array, qkv_groups[1].array]
-    out_groups = gather_weight(after(w_out, *far_done), attended, (2,))
-    in_groups = split_weight(after(in_to, *far_done), attended, (0, 1))
+    out_groups = gather_weight(after(w_out, toks[1].array), (attended,), (2,))
+    in_groups = split_weight(after(in_to, qkv_groups[1].array), (attended,), (0, 1))
     atts = gather_rows(attended[:, :head_cols])
     block_shape = shape((n // 2, rows, model), BF16)
     hidden, normed2, up, in_w = pl.pallas_call(
@@ -1104,7 +1103,7 @@
     att_reduce.step(1, [dnormed1_keep])
     att_p, att_q = att_reduce.finish([[other]])
     att_done = att_p[:16]
-    in_p, in_q = pair_gather(after(in_p, att_done), after(in_q, att_done), orders)
+    in_p, in_q = pair_gather(in_p, in_q, orders)
     down_pair = replica_spread(after(down_share, att_done), far)
     qkv_p, qkv_q = turned(att_p, att_q[:split], qkv_counts)
     att_p, att_q = pair_gather(qkv_p, jnp.concatenate([qkv_q, att_q[split:]]), orders)

time: 350 us -> 328 us (0.937)
  waiting for transfers between devices: 138 us -> 111 us
  starting transfers between devices: 50.3 us -> 57.5 us
  other arithmetic: 17.4 us -> 13.8 us
    ppermute x56, waiting for transfers between devices: 138 us -> 111 us  [swap(): return lax.ppermute(x, axis, [(i, i ^ 1 << bit) for i in range(size)])]
    ppermute x56, starting transfers between devices: 50.3 us -> 57.5 us  [swap(): return lax.ppermute(x, axis, [(i, i ^ 1 << bit) for i in range(size)])]
    unnamed x94 -> x86, local copies, waits for them, and re-layouts: 19.2 us -> 19.8 us
  transfers between devices with their start and end apart: 56 -> 56, of which waited for: 25 -> 22; matrix products, arithmetic and copies ran while one was open for 7% -> 7% of each run, Pallas kernels for 26% -> 28%
where the time goes in v6:
time: 328 us; the launch traced here: 324 us
  waiting for transfers between devices  111 us (34%)
  Pallas kernels  110 us (34%)
  starting transfers between devices  57.5 us (18%)
  local copies, waits for them, and re-layouts  30.2 us (9%)
  other arithmetic  13.8 us (4%)
    ppermute x56, waiting for transfers between devices, swap(): return lax.ppermute(x, axis, [(i, i ^ 1 << bit) for i in range(size)])  111 us
    ppermute x56, starting transfers between devices, swap(): return lax.ppermute(x, axis, [(i, i ^ 1 << bit) for i in range(size)])  57.5 us
    unnamed x86, local copies, waits for them, and re-layouts  19.8 us
    pallas_call x1, Pallas kernels, shards(): pl.pallas_call(ordered(functools.partial(down_kernel, held_of(cots), n, f...  18.4 us
    pallas_call x1, Pallas kernels, shards(): pl.pallas_call(ordered(functools.partial(attention_back_kernel, held_of(d...  13.4 us
    pallas_call x1, Pallas kernels, shards(): pl.pallas_call(ordered(functools.partial(attention_kernel, held_of(toks),...  12.4 us
    pallas_call x2, Pallas kernels, columns_out(): pl.pallas_call(functools.partial(columns_out_kernel, n, ff, head_cols, wi...  12 us
    pallas_call x1, Pallas kernels, shards(): pl.pallas_call(functools.partial(dup_kernel, held_of(cots), n), in_specs=...  12 us
  transfers between devices with their start and end apart: 56, of which 22 were waited for; matrix products, arithmetic and copies ran while one was open for 7% of the time, Pallas kernels for 28%

profile of v6, /device:TPU:0, one launch (start us, length us, event | category | flops | bytes accessed | tf_op | source)
XLA Modules:
  0.0 324.0 jit_solution(9749063993311275550)
XLA Ops:
  5.5 2.9 collective-permute-start.3
  11.7 4.8 %sine_multiply_fusion = (f32[1024,256]{1,0:T(8,128)}, f32[1024,256]{1,0:T(8,128)}) fusion(f32[256]{0:T(256)S(1)} %get-tuple-element.174, f32[256]{0:T(256)S(1)} %get-tuple-element.175), kind=kLoop, calls=%fused_computation.5 | loop fusion | flops 524288 | bytes 2099200 | tf_op jit(solution)/shard_map/mul | solution.py:881
  24.5 3.1 collective-permute-done.4.refs_11_
  34.1 12.4 %attention.1 = (bf16[1024,256]{1,0:T(8,128)(2,1)S(1)}, bf16[1152,256]{1,0:T(8,128)(2,1)}, bf16[1152,256]{1,0:T(8,128)(2,1)}, bf16[1024,256]{1,0:T(8,128)(2,1)S(1...) custom-call(s32[2]{0:T(128)S(1)} %pad_add_fusion.refs_0_.place_ref, ...), custom_call_target="tpu_custom_call" | custom-call | flops 10737418240 | bytes 4194304 | tf_op jit(solution)/shard_map/attention/pallas_call | solution.py:889
  46.5 4.8 %collective-permute-done.12.refs_12_ = bf16[2,128,1536]{2,1,0:T(8,128)(2,1)S(1)} collective-permute-done((bf16[2,128,1536]{2,1,0:T(8,128)(2,1)S(1)}, bf16[2,128,1536]{2,1,0:T(8,128)(2,1)S(1)}, u32[]{:S(2)}, u32[]{:S(2)}) %collective-permute-start.12) | collective-permute-done | bytes 786464 | tf_op jit(solution)/shard_map/ppermute | solution.py:36
  57.4 2.6 collective-permute-start.10
  60.0 5.8 %collective-permute-done.14.refs_14_ = bf16[2,64,1536]{2,1,0:T(8,128)(2,1)S(1)} collective-permute-done((bf16[2,64,1536]{2,1,0:T(8,128)(2,1)S(1)}, bf16[2,64,1536]{2,1,0:T(8,128)(2,1)S(1)}, u32[]{:S(2)}, u32[]{:S(2)}) %collective-permute-start.14) | collective-permute-done | bytes 393248 | tf_op jit(solution)/shard_map/ppermute | solution.py:36
  66.1 4.9 %collective-permute-done.10.refs_9_ = bf16[128,1024]{1,0:T(8,128)(2,1)S(1)} collective-permute-done((bf16[128,1024]{1,0:T(8,128)(2,1)S(1)}, bf16[128,1024]{1,0:T(8,128)(2,1)S(1)}, u32[]{:S(2)}, u32[]{:S(2)}) %collective-permute-start.10) | collective-permute-done | bytes 262176 | tf_op jit(solution)/shard_map/ppermute | solution.py:36
  77.4 11.9 %up_projection.1 = (f32[256,1024]{1,0:T(8,128)}, bf16[1024,1024]{1,0:T(8,128)(2,1)}, f32[1024,1536]{1,0:T(8,128)}, bf16[1024,1536]{1,0:T(8,128)(2,1)}) custom-call(s32[2]{0:T(128)S(1)} %pad_add_fusion.refs_0_.place_ref, bf16[256,1024]{1,0:T(8,128)(2,1)} %tokens.1, bf16[256,1024]{1,0:T(8,128)(2,1)} %collective-permute-done.refs_6_.refs_1_, ...), custom_call_target="tpu_custom_call" | custom-call | flops 9663676416 | bytes 4194304 | tf_op jit(solution)/shard_map/up_projection/pallas_call | solution.py:916
  89.7 2.5 collective-permute-done.17.refs_2_.refs_5_
  93.1 12.0 %dup.1 = (bf16[1024,768]{1,0:T(8,128)(2,1)}, bf16[1024,1536]{1,0:T(8,128)(2,1)}, bf16[2,256,1024]{2,1,0:T(8,128)(2,1)}, bf16[2,256,1024]{2,1,0:T(8,128)(2,1)}) custom-call(f32[1024,1536]{1,0:T(8,128)} %get-tuple-element.76.up_ref, bf16[1024,1536]{1,0:T(8,128)(2,1)} %get-tuple-element.77.w_in_ref, bf16[656,1024]{1,0:T(8,128)(2,1)} %refs_2_.1, ...), custom_call_target="tpu_custom_call" | custom-call | flops 11274289152 | bytes 4194304 | tf_op jit(solution)/shard_map/dup/pallas_call | solution.py:948
  105.3 2.7 collective-permute-done.18.got_ref
  111.1 7.5 %in_gradient.1 = (bf16[4,24,32,128]{3,2,1,0:T(8,128)(2,1)}, bf16[4,24,32,128]{3,2,1,0:T(8,128)(2,1)}, bf16[4,20,32,128]{3,2,1,0:T(8,128)(2,1)S(1)}, bf16[4,20,32,128]{3,2,1,0:T(8,128)(2,1)S(1)}) custom-call(s32[2]{0:T(128)S(1)} %pad_add_fusion.refs_0_.place_ref, bf16[1024,1024]{1,0:T(8,128)(2,1)} %get-tuple-element.86.refs_1_, ...), custom_call_target="tpu_custom_call" | custom-call | flops 6442450944 | bytes 4194304 | tf_op jit(solution)/shard_map/in_gradient/pallas_call | solution.py:986
  120.9 2.6 collective-permute-done.19.refs_1_
  127.9 18.4 %down_gradient.1 = (bf16[4,656,128]{2,1,0:T(8,128)(2,1)}, bf16[4,656,128]{2,1,0:T(8,128)(2,1)}, bf16[2,256,1024]{2,1,0:T(8,128)(2,1)}, bf16[2,256,1024]{2,1,0:T(8,128)(2,1)}) custom-call(s32[2]{0:T(128)S(1)} %pad_add_fusion.refs_0_.place_ref, bf16[1024,768]{1,0:T(8,128)(2,1)} %get-tuple-element.80.refs_1_, bf16[656,1024]{1,0:T(8,128)(2,1)} %refs_2_.1, ...), custom_call_target="tpu_custom_call" | custom-call | flops 6442450944 | bytes 4194304 | tf_op jit(solution)/shard_map/down_gradient/pallas_call | solution.py:1004
  153.0 13.4 %attention_back.1 = (bf16[1024,768]{1,0:T(8,128)(2,1)}, bf16[4,256,128]{2,1,0:T(8,128)(2,1)S(1)}, bf16[4,256,128]{2,1,0:T(8,128)(2,1)S(1)}) custom-call(s32[2]{0:T(128)S(1)} %pad_add_fusion.refs_0_.place_ref, bf16[256,1024]{1,0:T(8,128)(2,1)S(1)} %get-tuple-element.89.refs_6_.refs_1_, bf16[256,1024]{1,0:T(8,128)(2,1)} %copy-done.32, ...), custom_call_target="tpu_custom_call" | custom-call | flops 10737418240 | bytes 4194304 | tf_op jit(solution)/shard_map/attention_back/pallas_call | solution.py:1017
  166.4 6.4 %collective-permute-done.26 = bf16[2,768,128]{2,1,0:T(8,128)(2,1)S(1)} collective-permute-done((bf16[2,768,128]{2,1,0:T(8,128)(2,1)S(1)}, bf16[2,768,128]{2,1,0:T(8,128)(2,1)S(1)}, u32[]{:S(2)}, u32[]{:S(2)}) %collective-permute-start.26) | collective-permute-done | bytes 393248 | tf_op jit(solution)/shard_map/ppermute | solution.py:36
  175.7 4.8 %qkv_gradient.1 = (bf16[4,16,32,128]{3,2,1,0:T(8,128)(2,1)S(1)}, bf16[4,16,32,128]{3,2,1,0:T(8,128)(2,1)}, bf16[4,8,32,128]{3,2,1,0:T(8,128)(2,1)S(1)}, bf16[4,8,32,128]{3,2,1,0:T(8,128)(2,1)S(1)}) custom-call(s32[2]{0:T(128)S(1)} %pad_add_fusion.refs_0_.place_ref, bf16[1024,1024]{1,0:T(8,128)(2,1)} %get-tuple-element.106.refs_1_, ...), custom_call_target="tpu_custom_call" | custom-call | flops 3221225472 | bytes 4194304 | tf_op jit(solution)/shard_map/qkv_gradient/pallas_call | solution.py:1052
  180.9 2.5 collective-permute-start.43
  185.3 12.7 %collective-permute-done.43 = bf16[1,1408,128]{2,1,0:T(8,128)(2,1)S(1)} collective-permute-done((bf16[1,1408,128]{2,1,0:T(8,128)(2,1)S(1)}, bf16[1,1408,128]{2,1,0:T(8,128)(2,1)S(1)}, u32[]{:S(2)}, u32[]{:S(2)}) %collective-permute-start.43) | collective-permute-done | bytes 360480 | tf_op jit(solution)/shard_map/ppermute | solution.py:36
  200.5 3.5 %collective-permute-start.52 = (bf16[1,656,128]{2,1,0:T(8,128)(2,1)S(1)}, bf16[1,656,128]{2,1,0:T(8,128)(2,1)S(1)}, u32[]{:S(2)}, u32[]{:S(2)}) collective-permute-start(bf16[1,656,128]{2,1,0:T(8,128)(2,1)S(1)} %add_convert_fusion.9), channel_id=1, source_target_pairs={{0,16},{4,20},{8,24},{12,28},{16,0},{20,4},{24,8},{28,12},{1,17},{... | collective-permute-start | bytes 503816 | tf_op jit(solution)/shard_map/ppermute | solution.py:36
  207.7 4.7 %project_back.1 = (bf16[2,256,1024]{2,1,0:T(8,128)(2,1)}, bf16[2,256,1024]{2,1,0:T(8,128)(2,1)}) custom-call(s32[2]{0:T(128)S(1)} %pad_add_fusion.refs_0_.place_ref, bf16[1024,768]{1,0:T(8,128)(2,1)} %get-tuple-element.102.refs_2_.refs_1_, bf16[1024,768]{1,0:T(8,128)(2,1)} %get-tuple-element.112.refs_2_, bf16[256,1024]{1,0:T(8,128)(2,1)S(1)} %copy-done.20, ...), custom_call_target="tpu_custom_call" | custom-call | flops 1610612736 | bytes 4194304 | tf_op jit(solution)/shard_map/project_back/pallas_call | solution.py:1074
  213.6 2.8 collective-permute-start.35
  217.8 24.7 %collective-permute-done.35 = bf16[1,1024,128]{2,1,0:T(8,128)(2,1)S(1)} collective-permute-done((bf16[1,1024,128]{2,1,0:T(8,128)(2,1)S(1)}, bf16[1,1024,128]{2,1,0:T(8,128)(2,1)S(1)}, u32[]{:S(2)}, u32[]{:S(2)}) %collective-permute-start.35) | collective-permute-done | bytes 262176 | tf_op jit(solution)/shard_map/ppermute | solution.py:36
  244.7 2.6 collective-permute-done.36
  247.4 2.7 collective-permute-done.46
  253.8 11.5 %collective-permute-done.38 = bf16[1,1024,128]{2,1,0:T(8,128)(2,1)S(1)} collective-permute-done((bf16[1,1024,128]{2,1,0:T(8,128)(2,1)S(1)}, bf16[1,1024,128]{2,1,0:T(8,128)(2,1)S(1)}, u32[]{:S(2)}, u32[]{:S(2)}) %collective-permute-start.38) | collective-permute-done | bytes 262176 | tf_op jit(solution)/shard_map/ppermute | solution.py:36
  270.5 4.1 %collective-permute-done.41 = bf16[2,512,128]{2,1,0:T(8,128)(2,1)S(1)} collective-permute-done((bf16[2,512,128]{2,1,0:T(8,128)(2,1)S(1)}, bf16[2,512,128]{2,1,0:T(8,128)(2,1)S(1)}, u32[]{:S(2)}, u32[]{:S(2)}) %collective-permute-start.41) | collective-permute-done | bytes 262176 | tf_op jit(solution)/shard_map/ppermute | solution.py:36
  276.8 11.0 %collective-permute-done.39 = bf16[2,512,128]{2,1,0:T(8,128)(2,1)S(1)} collective-permute-done((bf16[2,512,128]{2,1,0:T(8,128)(2,1)S(1)}, bf16[2,512,128]{2,1,0:T(8,128)(2,1)S(1)}, u32[]{:S(2)}, u32[]{:S(2)}) %collective-permute-start.39) | collective-permute-done | bytes 262176 | tf_op jit(solution)/shard_map/ppermute | solution.py:36
  296.9 3.0 input_grad.1
  302.0 6.9 %columns_out.3 = (f32[8,32,5248]{2,1,0:T(8,128)}, f32[8,32,1]{2,1,0:T(8,128)S(1)}) custom-call(s32[2]{0:T(128)S(1)} %pad_add_fusion.refs_0_.place_ref, f32[8,32,1]{2,1,0:T(8,128)S(1)} %copy-done.22, bf16[8,32,5248]{2,1,0:T(8,128)(2,1)S(1)} %bitcast.80, bf16[4,24,32,128]{3,2,1,0:T(8,128)(2,1)S(1)} %bitcast.82, bf16[4,24,32,128]{3,2,1,0:T(8,128)(2,1)} %bitcast.49.refs_1_, ...), custom_call_target="tpu_custom_call" | custom-call | tf_op jit(solution)/shard_map/columns_out/pallas_call | solution.py:764
  315.5 5.2 %columns_out.2 = (f32[8,32,3072]{2,1,0:T(8,128)}, f32[8,32,1]{2,1,0:T(8,128)S(1)}) custom-call(s32[2]{0:T(128)S(1)} %pad_add_fusion.refs_0_.place_ref, f32[8,32,1]{2,1,0:T(8,128)S(1)} %copy-done.21, bf16[8,32,3072]{2,1,0:T(8,128)(2,1)S(1)} %bitcast.81, bf16[4,16,32,128]{3,2,1,0:T(8,128)(2,1)} %bitcast.34.refs_0_, bf16[4,16,32,128]{3,2,1,0:T(8,128)(2,1)} %bitcast.35.refs_1_, ...), custom_call_target="tpu_custom_call" | custom-call | tf_op jit(solution)/shard_map/columns_out/pallas_call | solution.py:764
  (269 shorter events, 101.0 us)
Async XLA Ops:
  8.5 20.8 %collective-permute-start = (bf16[256,1024]{1,0:T(8,128)(2,1)}, bf16[256,1024]{1,0:T(8,128)(2,1)}, u32[]{:S(2)}, u32[]{:S(2)}) collective-permute-start(bf16[256,1024]{1,0:T(8,128)(2,1)} %tokens.1), channel_id=1, source_target_pairs={{0,2},{1,3},{2,0},{3,1},{4,6},{5,7},{6,4},{7,5},{8,10},{9,11},{10,... | collective-permute-start | bytes 1572872 | tf_op jit(solution)/shard_map/ppermute | solution.py:36
  30.9 20.4 %collective-permute-start.12 = (bf16[2,128,1536]{2,1,0:T(8,128)(2,1)S(1)}, bf16[2,128,1536]{2,1,0:T(8,128)(2,1)S(1)}, u32[]{:S(2)}, u32[]{:S(2)}) collective-permute-start(bf16[2,128,1536]{2,1,0:T(8,128)(2,1)S(1)} %dynamic-slice_bitcast_fusion), channel_id=1, source_target_pairs={{0,2},{1,3},{2,0},{3,1},{4,6},{5,7},{6,4},{7,5},{8,10},{9,11},{10,... | collective-permute-start | bytes 2359304 | tf_op jit(solution)/shard_map/ppermute | solution.py:36
  32.6 24.9 %collective-permute-start.9 = (bf16[128,1024]{1,0:T(8,128)(2,1)S(1)}, bf16[128,1024]{1,0:T(8,128)(2,1)S(1)}, u32[]{:S(2)}, u32[]{:S(2)}) collective-permute-start(bf16[128,1024]{1,0:T(8,128)(2,1)S(1)} %dynamic-slice_bitcast_fusion.2), channel_id=1, source_target_pairs={{0,2},{1,3},{2,0},{3,1},{4,6},{5,7},{6,4},{7,5},{8,10},{9,11},{10,... | collective-permute-start | bytes 786440 | tf_op jit(solution)/shard_map/ppermute | solution.py:36
  51.4 14.5 %collective-permute-start.14 = (bf16[2,64,1536]{2,1,0:T(8,128)(2,1)S(1)}, bf16[2,64,1536]{2,1,0:T(8,128)(2,1)S(1)}, u32[]{:S(2)}, u32[]{:S(2)}) collective-permute-start(bf16[2,64,1536]{2,1,0:T(8,128)(2,1)S(1)} %get-tuple-element.142), channel_id=1, source_target_pairs={{0,8},{4,12},{8,0},{12,4},{16,24},{20,28},{24,16},{28,20},{1,9},{5... | collective-permute-start | bytes 1179656 | tf_op jit(solution)/shard_map/ppermute | solution.py:36
  55.9 15.3 %collective-permute-start.7 = (bf16[1024,256]{1,0:T(8,128)(2,1)S(1)}, bf16[1024,256]{1,0:T(8,128)(2,1)S(1)}, u32[]{:S(2)}, u32[]{:S(2)}) collective-permute-start(bf16[1024,256]{1,0:T(8,128)(2,1)S(1)} %get-tuple-element.71.refs_4_.refs_5_), channel_id=1, source_target_pairs={{0,2},{1,3},{2,0},{3,1},{4,6},{5,7},{6,4},{7,5},{8,10},{9,11},{10,... | collective-permute-start | bytes 1572872 | tf_op jit(solution)/shard_map/ppermute | solution.py:36
  71.8 17.6 %collective-permute-start.16 = (bf16[256,1024]{1,0:T(8,128)(2,1)S(1)}, bf16[256,1024]{1,0:T(8,128)(2,1)S(1)}, u32[]{:S(2)}, u32[]{:S(2)}) collective-permute-start(bf16[256,1024]{1,0:T(8,128)(2,1)S(1)} %copy-done.10), channel_id=1, source_target_pairs={{0,2},{1,3},{2,0},{3,1},{4,6},{5,7},{6,4},{7,5},{8,10},{9,11},{10,... | collective-permute-start | bytes 1572872 | tf_op jit(solution)/shard_map/ppermute | solution.py:36
  118.6 29.9 %collective-permute-start.24 = (bf16[4,640,128]{2,1,0:T(8,128)(2,1)S(1)}, bf16[4,640,128]{2,1,0:T(8,128)(2,1)S(1)}, u32[]{:S(2)}, u32[]{:S(2)}) collective-permute-start(bf16[4,640,128]{2,1,0:T(8,128)(2,1)S(1)} %bitcast.89), channel_id=1, source_target_pairs={{0,8},{4,12},{8,0},{12,4},{16,24},{20,28},{24,16},{28,20},{1,9},{5... | collective-permute-start | bytes 1966088 | tf_op jit(solution)/shard_map/ppermute | solution.py:36
  119.4 29.1 %collective-permute-start.23 = (bf16[4,768,128]{2,1,0:T(8,128)(2,1)}, bf16[4,768,128]{2,1,0:T(8,128)(2,1)S(1)}, u32[]{:S(2)}, u32[]{:S(2)}) collective-permute-start(bf16[4,768,128]{2,1,0:T(8,128)(2,1)} %bitcast.110), channel_id=1, source_target_pairs={{0,4},{4,0},{8,12},{12,8},{16,20},{20,16},{24,28},{28,24},{1,5},{5... | collective-permute-start | bytes 2359304 | tf_op jit(solution)/shard_map/ppermute | solution.py:36
  126.4 19.9 %collective-permute-start.21 = (bf16[256,1024]{1,0:T(8,128)(2,1)S(1)}, bf16[256,1024]{1,0:T(8,128)(2,1)S(1)}, u32[]{:S(2)}, u32[]{:S(2)}) collective-permute-start(bf16[256,1024]{1,0:T(8,128)(2,1)S(1)} %get-tuple-element.89.refs_6_.refs_1_), channel_id=1, source_target_pairs={{0,2},{1,3},{2,0},{3,1},{4,6},{5,7},{6,4},{7,5},{8,10},{9,11},{10,... | collective-permute-start | bytes 1572872 | tf_op jit(solution)/shard_map/ppermute | solution.py:36
  147.7 18.7 %collective-permute-start.28 = (bf16[4,656,128]{2,1,0:T(8,128)(2,1)}, bf16[4,656,128]{2,1,0:T(8,128)(2,1)S(1)}, u32[]{:S(2)}, u32[]{:S(2)}) collective-permute-start(bf16[4,656,128]{2,1,0:T(8,128)(2,1)} %get-tuple-element.109), channel_id=1, source_target_pairs={{0,8},{4,12},{8,0},{12,4},{16,24},{20,28},{24,16},{28,20},{1,9},{5... | collective-permute-start | bytes 2015240 | tf_op jit(solution)/shard_map/ppermute | solution.py:36
  148.5 24.5 %collective-permute-start.20 = (bf16[2,256,1024]{2,1,0:T(8,128)(2,1)}, bf16[2,256,1024]{2,1,0:T(8,128)(2,1)S(1)}, u32[]{:S(2)}, u32[]{:S(2)}) collective-permute-start(bf16[2,256,1024]{2,1,0:T(8,128)(2,1)} %get-tuple-element.91), channel_id=1, source_target_pairs={{0,1},{1,0},{2,3},{3,2},{4,5},{5,4},{6,7},{7,6},{8,9},{9,8},{10,11... | collective-permute-start | bytes 3145736 | tf_op jit(solution)/shard_map/ppermute | solution.py:36
  148.8 17.6 %collective-permute-start.27 = (bf16[2,640,128]{2,1,0:T(8,128)(2,1)S(1)}, bf16[2,640,128]{2,1,0:T(8,128)(2,1)S(1)}, u32[]{:S(2)}, u32[]{:S(2)}) collective-permute-start(bf16[2,640,128]{2,1,0:T(8,128)(2,1)S(1)} %get-tuple-element.147.refs_14_), channel_id=1, source_target_pairs={{0,4},{4,0},{8,12},{12,8},{16,20},{20,16},{24,28},{28,24},{1,5},{5... | collective-permute-start | bytes 983048 | tf_op jit(solution)/shard_map/ppermute | solution.py:36
  150.7 22.1 %collective-permute-start.26 = (bf16[2,768,128]{2,1,0:T(8,128)(2,1)S(1)}, bf16[2,768,128]{2,1,0:T(8,128)(2,1)S(1)}, u32[]{:S(2)}, u32[]{:S(2)}) collective-permute-start(bf16[2,768,128]{2,1,0:T(8,128)(2,1)S(1)} %get-tuple-element.139.refs_13_), channel_id=1, source_target_pairs={{0,8},{4,12},{8,0},{12,4},{16,24},{20,28},{24,16},{28,20},{1,9},{5... | collective-permute-start | bytes 1179656 | tf_op jit(solution)/shard_map/ppermute | solution.py:36
  173.0 27.4 %collective-permute-start.51 = (bf16[2,656,128]{2,1,0:T(8,128)(2,1)S(1)}, bf16[2,656,128]{2,1,0:T(8,128)(2,1)S(1)}, u32[]{:S(2)}, u32[]{:S(2)}) collective-permute-start(bf16[2,656,128]{2,1,0:T(8,128)(2,1)S(1)} %get-tuple-element.133.refs_5_), channel_id=1, source_target_pairs={{0,4},{4,0},{8,12},{12,8},{16,20},{20,16},{24,28},{28,24},{1,5},{5... | collective-permute-start | bytes 1007624 | tf_op jit(solution)/shard_map/ppermute | solution.py:36
  174.8 30.9 %collective-permute-start.25 = (bf16[256,1024]{1,0:T(8,128)(2,1)S(1)}, bf16[256,1024]{1,0:T(8,128)(2,1)S(1)}, u32[]{:S(2)}, u32[]{:S(2)}) collective-permute-start(bf16[256,1024]{1,0:T(8,128)(2,1)S(1)} %get-tuple-element.105.refs_6_), channel_id=1, source_target_pairs={{0,2},{1,3},{2,0},{3,1},{4,6},{5,7},{6,4},{7,5},{8,10},{9,11},{10,... | collective-permute-start | bytes 1572872 | tf_op jit(solution)/shard_map/ppermute | solution.py:36
  180.5 19.0 %collective-permute-start.29 = (bf16[4,512,128]{2,1,0:T(8,128)(2,1)}, bf16[4,512,128]{2,1,0:T(8,128)(2,1)S(1)}, u32[]{:S(2)}, u32[]{:S(2)}) collective-permute-start(bf16[4,512,128]{2,1,0:T(8,128)(2,1)} %bitcast.111), channel_id=1, source_target_pairs={{0,4},{4,0},{8,12},{12,8},{16,20},{20,16},{24,28},{28,24},{1,5},{5... | collective-permute-start | bytes 1572872 | tf_op jit(solution)/shard_map/ppermute | solution.py:36
  180.9 17.0 %collective-permute-start.43 = (bf16[1,1408,128]{2,1,0:T(8,128)(2,1)S(1)}, bf16[1,1408,128]{2,1,0:T(8,128)(2,1)S(1)}, u32[]{:S(2)}, u32[]{:S(2)}) collective-permute-start(bf16[1,1408,128]{2,1,0:T(8,128)(2,1)S(1)} %pad_maximum_fusion.12), channel_id=1, source_target_pairs={{0,16},{4,20},{8,24},{12,28},{16,0},{20,4},{24,8},{28,12},{1,17},{... | collective-permute-start | bytes 1081352 | tf_op jit(solution)/shard_map/ppermute | solution.py:36
  183.4 20.5 %collective-permute-start.30 = (bf16[4,512,128]{2,1,0:T(8,128)(2,1)S(1)}, bf16[4,512,128]{2,1,0:T(8,128)(2,1)S(1)}, u32[]{:S(2)}, u32[]{:S(2)}) collective-permute-start(bf16[4,512,128]{2,1,0:T(8,128)(2,1)S(1)} %pad_maximum_fusion.10), channel_id=1, source_target_pairs={{0,8},{4,12},{8,0},{12,4},{16,24},{20,28},{24,16},{28,20},{1,9},{5... | collective-permute-start | bytes 1572872 | tf_op jit(solution)/shard_map/ppermute | solution.py:36
  198.2 14.3 %collective-permute-start.44 = (bf16[2,1,352,128]{3,2,0,1:T(8,128)(2,1)S(1)}, bf16[2,1,352,128]{3,2,0,1:T(8,128)(2,1)S(1)}, u32[]{:S(2)}, u32[]{:S(2)}) collective-permute-start(bf16[2,1,352,128]{3,2,0,1:T(8,128)(2,1)S(1)} %get-tuple-element.165), channel_id=1, source_target_pairs={{0,2},{1,3},{2,0},{3,1},{4,6},{5,7},{6,4},{7,5},{8,10},{9,11},{10,... | collective-permute-start | bytes 540680 | tf_op jit(solution)/shard_map/ppermute | solution.py:36
  213.2 30.9 %collective-permute-start.53 = (bf16[1,656,128]{2,1,0:T(8,128)(2,1)S(1)}, bf16[1,656,128]{2,1,0:T(8,128)(2,1)S(1)}, u32[]{:S(2)}, u32[]{:S(2)}) collective-permute-start(bf16[1,656,128]{2,1,0:T(8,128)(2,1)S(1)} %bitcast.92), channel_id=1, source_target_pairs={{0,16},{4,20},{8,24},{12,28},{16,0},{20,4},{24,8},{28,12},{1,17},{... | collective-permute-start | bytes 503816 | tf_op jit(solution)/shard_map/ppermute | solution.py:36
  213.6 28.8 %collective-permute-start.35 = (bf16[1,1024,128]{2,1,0:T(8,128)(2,1)S(1)}, bf16[1,1024,128]{2,1,0:T(8,128)(2,1)S(1)}, u32[]{:S(2)}, u32[]{:S(2)}) collective-permute-start(bf16[1,1024,128]{2,1,0:T(8,128)(2,1)S(1)} %pad_maximum_fusion.17), channel_id=1, source_target_pairs={{0,16},{4,20},{8,24},{12,28},{16,0},{20,4},{24,8},{28,12},{1,17},{... | collective-permute-start | bytes 786440 | tf_op jit(solution)/shard_map/ppermute | solution.py:36
  216.5 33.6 %collective-permute-start.46 = (bf16[1,1408,128]{2,1,0:T(8,128)(2,1)S(1)}, bf16[1,1408,128]{2,1,0:T(8,128)(2,1)S(1)}, u32[]{:S(2)}, u32[]{:S(2)}) collective-permute-start(bf16[1,1408,128]{2,1,0:T(8,128)(2,1)S(1)} %maximum_bitcast_fusion.1), channel_id=1, source_target_pairs={{0,16},{4,20},{8,24},{12,28},{16,0},{20,4},{24,8},{28,12},{1,17},{... | collective-permute-start | bytes 1081352 | tf_op jit(solution)/shard_map/ppermute | solution.py:36
  250.1 18.3 %collective-permute-start.47 = (bf16[2,768,128]{2,1,0:T(8,128)(2,1)S(1)}, bf16[2,768,128]{2,1,0:T(8,128)(2,1)S(1)}, u32[]{:S(2)}, u32[]{:S(2)}) collective-permute-start(bf16[2,768,128]{2,1,0:T(8,128)(2,1)S(1)} %fusion.7), channel_id=1, source_target_pairs={{0,8},{4,12},{8,0},{12,4},{16,24},{20,28},{24,16},{28,20},{1,9},{5... | collective-permute-start | bytes 1179656 | tf_op jit(solution)/shard_map/ppermute | solution.py:36
  250.3 15.0 %collective-permute-start.38 = (bf16[1,1024,128]{2,1,0:T(8,128)(2,1)S(1)}, bf16[1,1024,128]{2,1,0:T(8,128)(2,1)S(1)}, u32[]{:S(2)}, u32[]{:S(2)}) collective-permute-start(bf16[1,1024,128]{2,1,0:T(8,128)(2,1)S(1)} %maximum_bitcast_fusion.2), channel_id=1, source_target_pairs={{0,16},{4,20},{8,24},{12,28},{16,0},{20,4},{24,8},{28,12},{1,17},{... | collective-permute-start | bytes 786440 | tf_op jit(solution)/shard_map/ppermute | solution.py:36
  251.8 17.9 %collective-permute-start.49 = (bf16[2,640,128]{2,1,0:T(8,128)(2,1)S(1)}, bf16[2,640,128]{2,1,0:T(8,128)(2,1)S(1)}, u32[]{:S(2)}, u32[]{:S(2)}) collective-permute-start(bf16[2,640,128]{2,1,0:T(8,128)(2,1)S(1)} %pad_maximum_fusion.14), channel_id=1, source_target_pairs={{0,4},{4,0},{8,12},{12,8},{16,20},{20,16},{24,28},{28,24},{1,5},{5... | collective-permute-start | bytes 983048 | tf_op jit(solution)/shard_map/ppermute | solution.py:36
  253.7 34.9 %collective-permute-start.55 = (bf16[4,656,128]{2,1,0:T(8,128)(2,1)S(1)}, bf16[4,656,128]{2,1,0:T(8,128)(2,1)S(1)}, u32[]{:S(2)}, u32[]{:S(2)}) collective-permute-start(bf16[4,656,128]{2,1,0:T(8,128)(2,1)S(1)} %pad_maximum_fusion.7.refs_0_), channel_id=1, source_target_pairs={{0,8},{4,12},{8,0},{12,4},{16,24},{20,28},{24,16},{28,20},{1,9},{5... | collective-permute-start | bytes 2015240 | tf_op jit(solution)/shard_map/ppermute | solution.py:36
  266.4 21.4 %collective-permute-start.39 = (bf16[2,512,128]{2,1,0:T(8,128)(2,1)S(1)}, bf16[2,512,128]{2,1,0:T(8,128)(2,1)S(1)}, u32[]{:S(2)}, u32[]{:S(2)}) collective-permute-start(bf16[2,512,128]{2,1,0:T(8,128)(2,1)S(1)} %get-tuple-element.151), channel_id=1, source_target_pairs={{0,8},{4,12},{8,0},{12,4},{16,24},{20,28},{24,16},{28,20},{1,9},{5... | collective-permute-start | bytes 786440 | tf_op jit(solution)/shard_map/ppermute | solution.py:36
  268.5 33.4 %collective-permute-start.48 = (bf16[4,768,128]{2,1,0:T(8,128)(2,1)S(1)}, bf16[4,768,128]{2,1,0:T(8,128)(2,1)}, u32[]{:S(2)}, u32[]{:S(2)}) collective-permute-start(bf16[4,768,128]{2,1,0:T(8,128)(2,1)S(1)} %pad_maximum_fusion.6), channel_id=1, source_target_pairs={{0,4},{4,0},{8,12},{12,8},{16,20},{20,16},{24,28},{28,24},{1,5},{5... | collective-permute-start | bytes 2359304 | tf_op jit(solution)/shard_map/ppermute | solution.py:36
  270.5 31.4 %collective-permute-start.50 = (bf16[4,640,128]{2,1,0:T(8,128)(2,1)}, bf16[4,640,128]{2,1,0:T(8,128)(2,1)}, u32[]{:S(2)}, u32[]{:S(2)}) collective-permute-start(bf16[4,640,128]{2,1,0:T(8,128)(2,1)} %pad_maximum_fusion.8), channel_id=1, source_target_pairs={{0,8},{4,12},{8,0},{12,4},{16,24},{20,28},{24,16},{28,20},{1,9},{5... | collective-permute-start | bytes 1966088 | tf_op jit(solution)/shard_map/ppermute | solution.py:36
  274.6 22.2 %collective-permute-start.32 = (bf16[256,1024]{1,0:T(8,128)(2,1)}, bf16[256,1024]{1,0:T(8,128)(2,1)}, u32[]{:S(2)}, u32[]{:S(2)}) collective-permute-start(bf16[256,1024]{1,0:T(8,128)(2,1)} %get-tuple-element.121), channel_id=1, source_target_pairs={{0,2},{1,3},{2,0},{3,1},{4,6},{5,7},{6,4},{7,5},{8,10},{9,11},{10,... | collective-permute-start | bytes 1572872 | tf_op jit(solution)/shard_map/ppermute | solution.py:36
  287.8 24.5 %collective-permute-start.42 = (bf16[4,512,128]{2,1,0:T(8,128)(2,1)}, bf16[4,512,128]{2,1,0:T(8,128)(2,1)}, u32[]{:S(2)}, u32[]{:S(2)}) collective-permute-start(bf16[4,512,128]{2,1,0:T(8,128)(2,1)} %pad_maximum_fusion.9.refs_0_), channel_id=1, source_target_pairs={{0,8},{4,12},{8,0},{12,4},{16,24},{20,28},{24,16},{28,20},{1,9},{5... | collective-permute-start | bytes 1572872 | tf_op jit(solution)/shard_map/ppermute | solution.py:36
  289.5 23.7 %collective-permute-start.40 = (bf16[4,512,128]{2,1,0:T(8,128)(2,1)}, bf16[4,512,128]{2,1,0:T(8,128)(2,1)}, u32[]{:S(2)}, u32[]{:S(2)}) collective-permute-start(bf16[4,512,128]{2,1,0:T(8,128)(2,1)} %pad_maximum_fusion.11), channel_id=1, source_target_pairs={{0,4},{4,0},{8,12},{12,8},{16,20},{20,16},{24,28},{28,24},{1,5},{5... | collective-permute-start | bytes 1572872 | tf_op jit(solution)/shard_map/ppermute | solution.py:36
  (67 other events, 458.0 us)

commit v7 on v6

--- a/solution.py
+++ b/solution.py
@@ -1048,22 +1048,22 @@
     qkv_tiles = 3 * width // LANES
     qkv_counts = [qkv_tiles - qkv_tiles // 3, qkv_tiles // 3]
     in_reduce.step(1, [dqkv])
-    down_reduce = add_halves(down_keep, after(swap(down_send, "rep", far[0]), dqkv))
     qkv_flows = pl.pallas_call(
-        ordered(functools.partial(qkv_kernel, n, qkv_counts, orders), 3, 4),
-        in_specs=[SMEM_SPEC] + [VMEM_SPEC] * 2 + [ANY_SPEC] * 4,
+        ordered(functools.partial(qkv_kernel, n, qkv_counts, orders), 3, 3),
+        in_specs=[SMEM_SPEC] + [VMEM_SPEC] * 2 + [ANY_SPEC] * 3,
         out_shape=[shape((slots, n * c, chunk, LANES), BF16) for c in qkv_counts for _ in range(2)],
         scratch_shapes=[pltpu.VMEM((part, 3 * width), F32)],
         compiler_params=params,
         cost_estimate=work(12 * seq * model * width),
         name="qkv_gradient",
-    )(place, normed1, dqkv, in_reduce.p[1], in_reduce.q[1], down_reduce[1], mlp_other)
+    )(place, normed1, dqkv, in_reduce.p[1], in_reduce.q[1], mlp_other)
     qkv_flows = [flow_rows(a) for a in qkv_flows]
     split = qkv_flows[2].shape[1]
     qkv_q = [jnp.concatenate(x, axis=1) for x in zip(qkv_flows[2:], (out_keep, out_send))]
     att_reduce = PairReduce(qkv_flows[:2], qkv_q, orders)
     att_reduce.step(0)
     att_first = att_reduce.p[1]
+    att_reduce.step(1)
     output = pl.pallas_call(
         ordered(output_kernel, 3, 1),
         in_specs=[VMEM_SPEC] * 3 + [ANY_SPEC],
@@ -1072,13 +1072,13 @@
         name="output",
     )(mlp_mine, swap(mlp_other, "shard", top), hidden, qkv_flows[0])
     dnormed1_keep, dnormed1_send = pl.pallas_call(
-        ordered(functools.partial(project_back_kernel, n), 3, 3),
-        in_specs=[SMEM_SPEC] + [VMEM_SPEC] * 2 + [ANY_SPEC] * 3,
+        ordered(functools.partial(project_back_kernel, n), 3, 1),
+        in_specs=[SMEM_SPEC] + [VMEM_SPEC] * 2 + [ANY_SPEC],
         out_shape=[block_shape] * 2,
         compiler_params=params,
         cost_estimate=work(6 * seq * model * width),
         name="project_back",
-    )(place, dqkv, qkv_w, output, att_first, att_reduce.q[1])
+    )(place, dqkv, qkv_w, att_first)
     mine, other = near_sums(dnormed1_keep, dnormed1_send, "near_sum_1")
     input_grad = pl.pallas_call(
         input_kernel,
@@ -1098,10 +1098,10 @@
         return [a[:, :size].reshape(a.shape[0], n * count, chunk, LANES) for a in pair]
 
     in_p, in_q = turned(*in_reduce.finish([[qkv_flows[0]]]), in_counts)
-    down_share = replica_reduce(*down_reduce, far[1:], [[att_first]])
-
-    att_reduce.step(1, [dnormed1_keep])
-    att_p, att_q = att_reduce.finish([[other]])
+    down_send = after(down_send, dqkv)
+    down_share = replica_reduce(down_keep, down_send, far, [[qkv_flows[0]], [att_first]])
+
+    att_p, att_q = att_reduce.finish()
     att_done = att_p[:16]
     in_p, in_q = pair_gather(in_p, in_q, orders)
     down_pair = replica_spread(after(down_share, att_done), far)

time: 328 us -> 346 us (1.055)
  waiting for transfers between devices: 111 us -> 120 us
  local copies, waits for them, and re-layouts: 30.2 us -> 35.8 us
  starting transfers between devices: 57.5 us -> 62.1 us
    ppermute x56, waiting for transfers between devices: 111 us -> 120 us  [swap(): return lax.ppermute(x, axis, [(i, i ^ 1 << bit) for i in range(size)])]
    unnamed x86 -> x104, local copies, waits for them, and re-layouts: 19.8 us -> 25.4 us
    ppermute x56, starting transfers between devices: 57.5 us -> 62.1 us  [swap(): return lax.ppermute(x, axis, [(i, i ^ 1 << bit) for i in range(size)])]
  transfers between devices with their start and end apart: 56 -> 56, of which waited for: 22 -> 23; matrix products, arithmetic and copies ran while one was open for 7% -> 7% of each run, Pallas kernels for 28% -> 27%
where the time goes in v7:
time: 346 us; the launch traced here: 342 us
  waiting for transfers between devices  120 us (35%)
  Pallas kernels  108 us (31%)
  starting transfers between devices  62.1 us (18%)
  local copies, waits for them, and re-layouts  35.8 us (10%)
  other arithmetic  14.3 us (4%)
    ppermute x56, waiting for transfers between devices, swap(): return lax.ppermute(x, axis, [(i, i ^ 1 << bit) for i in range(size)])  120 us
    ppermute x56, starting transfers between devices, swap(): return lax.ppermute(x, axis, [(i, i ^ 1 << bit) for i in range(size)])  62.1 us
    unnamed x104, local copies, waits for them, and re-layouts  25.4 us
    pallas_call x1, Pallas kernels, shards(): pl.pallas_call(ordered(functools.partial(down_kernel, held_of(cots), n, f...  18.3 us
    pallas_call x1, Pallas kernels, shards(): pl.pallas_call(ordered(functools.partial(attention_back_kernel, held_of(d...  13.2 us
    pallas_call x1, Pallas kernels, shards(): pl.pallas_call(ordered(functools.partial(attention_kernel, held_of(toks),...  12.3 us
    pallas_call x1, Pallas kernels, shards(): pl.pallas_call(functools.partial(dup_kernel, held_of(cots), n), in_specs=...  12 us
    pallas_call x2, Pallas kernels, columns_out(): pl.pallas_call(functools.partial(columns_out_kernel, n, ff, head_cols, wi...  12 us
  transfers between devices with their start and end apart: 56, of which 23 were waited for; matrix products, arithmetic and copies ran while one was open for 7% of the time, Pallas kernels for 27%

profile of v7, /device:TPU:0, one launch (start us, length us, event | category | flops | bytes accessed | tf_op | source)
XLA Modules:
  0.0 342.3 jit_solution(3666245255960506664)
XLA Ops:
  11.7 4.8 %sine_multiply_fusion = (f32[1024,256]{1,0:T(8,128)}, f32[1024,256]{1,0:T(8,128)}) fusion(f32[256]{0:T(256)S(1)} %get-tuple-element.170, f32[256]{0:T(256)S(1)} %get-tuple-element.171), kind=kLoop, calls=%fused_computation.5 | loop fusion | flops 524288 | bytes 2099200 | tf_op jit(solution)/shard_map/mul | solution.py:881
  24.5 3.1 collective-permute-done.4.refs_11_
  34.1 12.3 %attention.1 = (bf16[1024,256]{1,0:T(8,128)(2,1)S(1)}, bf16[1152,256]{1,0:T(8,128)(2,1)}, bf16[1152,256]{1,0:T(8,128)(2,1)}, bf16[1024,256]{1,0:T(8,128)(2,1)S(1...) custom-call(s32[2]{0:T(128)S(1)} %pad_add_fusion.refs_0_.place_ref, ...), custom_call_target="tpu_custom_call" | custom-call | flops 10737418240 | bytes 4194304 | tf_op jit(solution)/shard_map/attention/pallas_call | solution.py:889
  46.5 4.9 %collective-permute-done.12.refs_12_ = bf16[2,128,1536]{2,1,0:T(8,128)(2,1)S(1)} collective-permute-done((bf16[2,128,1536]{2,1,0:T(8,128)(2,1)S(1)}, bf16[2,128,1536]{2,1,0:T(8,128)(2,1)S(1)}, u32[]{:S(2)}, u32[]{:S(2)}) %collective-permute-start.12) | collective-permute-done | bytes 786464 | tf_op jit(solution)/shard_map/ppermute | solution.py:36
  60.0 5.8 %collective-permute-done.14.refs_14_ = bf16[2,64,1536]{2,1,0:T(8,128)(2,1)S(1)} collective-permute-done((bf16[2,64,1536]{2,1,0:T(8,128)(2,1)S(1)}, bf16[2,64,1536]{2,1,0:T(8,128)(2,1)S(1)}, u32[]{:S(2)}, u32[]{:S(2)}) %collective-permute-start.14) | collective-permute-done | bytes 393248 | tf_op jit(solution)/shard_map/ppermute | solution.py:36
  66.1 4.9 %collective-permute-done.10.refs_9_ = bf16[128,1024]{1,0:T(8,128)(2,1)S(1)} collective-permute-done((bf16[128,1024]{1,0:T(8,128)(2,1)S(1)}, bf16[128,1024]{1,0:T(8,128)(2,1)S(1)}, u32[]{:S(2)}, u32[]{:S(2)}) %collective-permute-start.10) | collective-permute-done | bytes 262176 | tf_op jit(solution)/shard_map/ppermute | solution.py:36
  77.5 11.9 %up_projection.1 = (f32[256,1024]{1,0:T(8,128)}, bf16[1024,1024]{1,0:T(8,128)(2,1)}, f32[1024,1536]{1,0:T(8,128)}, bf16[1024,1536]{1,0:T(8,128)(2,1)}) custom-call(s32[2]{0:T(128)S(1)} %pad_add_fusion.refs_0_.place_ref, bf16[256,1024]{1,0:T(8,128)(2,1)} %tokens.1, bf16[256,1024]{1,0:T(8,128)(2,1)} %collective-permute-done.refs_6_.refs_1_, ...), custom_call_target="tpu_custom_call" | custom-call | flops 9663676416 | bytes 4194304 | tf_op jit(solution)/shard_map/up_projection/pallas_call | solution.py:916
  93.2 12.0 %dup.1 = (bf16[1024,768]{1,0:T(8,128)(2,1)}, bf16[1024,1536]{1,0:T(8,128)(2,1)}, bf16[2,256,1024]{2,1,0:T(8,128)(2,1)}, bf16[2,256,1024]{2,1,0:T(8,128)(2,1)}) custom-call(f32[1024,1536]{1,0:T(8,128)} %get-tuple-element.74.up_ref, bf16[1024,1536]{1,0:T(8,128)(2,1)} %get-tuple-element.75.w_in_ref, bf16[656,1024]{1,0:T(8,128)(2,1)} %refs_2_.1, ...), custom_call_target="tpu_custom_call" | custom-call | flops 11274289152 | bytes 4194304 | tf_op jit(solution)/shard_map/dup/pallas_call | solution.py:948
  111.2 7.4 %in_gradient.1 = (bf16[4,24,32,128]{3,2,1,0:T(8,128)(2,1)}, bf16[4,24,32,128]{3,2,1,0:T(8,128)(2,1)}, bf16[4,20,32,128]{3,2,1,0:T(8,128)(2,1)S(1)}, bf16[4,20,32,128]{3,2,1,0:T(8,128)(2,1)S(1)}) custom-call(s32[2]{0:T(128)S(1)} %pad_add_fusion.refs_0_.place_ref, bf16[1024,1024]{1,0:T(8,128)(2,1)} %get-tuple-element.84.refs_1_, ...), custom_call_target="tpu_custom_call" | custom-call | flops 6442450944 | bytes 4194304 | tf_op jit(solution)/shard_map/in_gradient/pallas_call | solution.py:986
  128.0 18.3 %down_gradient.1 = (bf16[4,656,128]{2,1,0:T(8,128)(2,1)}, bf16[4,656,128]{2,1,0:T(8,128)(2,1)}, bf16[2,256,1024]{2,1,0:T(8,128)(2,1)}, bf16[2,256,1024]{2,1,0:T(8,128)(2,1)}) custom-call(s32[2]{0:T(128)S(1)} %pad_add_fusion.refs_0_.place_ref, bf16[1024,768]{1,0:T(8,128)(2,1)} %get-tuple-element.78.refs_1_, bf16[656,1024]{1,0:T(8,128)(2,1)} %refs_2_.1, ...), custom_call_target="tpu_custom_call" | custom-call | flops 6442450944 | bytes 4194304 | tf_op jit(solution)/shard_map/down_gradient/pallas_call | solution.py:1004
  151.8 13.2 %attention_back.1 = (bf16[1024,768]{1,0:T(8,128)(2,1)}, bf16[4,256,128]{2,1,0:T(8,128)(2,1)S(1)}, bf16[4,256,128]{2,1,0:T(8,128)(2,1)S(1)}) custom-call(s32[2]{0:T(128)S(1)} %pad_add_fusion.refs_0_.place_ref, bf16[256,1024]{1,0:T(8,128)(2,1)S(1)} %get-tuple-element.87.refs_6_.refs_1_, bf16[256,1024]{1,0:T(8,128)(2,1)} %copy-done.39, ...), custom_call_target="tpu_custom_call" | custom-call | flops 10737418240 | bytes 4194304 | tf_op jit(solution)/shard_map/attention_back/pallas_call | solution.py:1017
  168.6 4.0 %qkv_gradient.1 = (bf16[4,16,32,128]{3,2,1,0:T(8,128)(2,1)S(1)}, bf16[4,16,32,128]{3,2,1,0:T(8,128)(2,1)S(1)}, bf16[4,8,32,128]{3,2,1,0:T(8,128)(2,1)S(1)}, bf16[4,8,32,128]{3,2,1,0:T(8,128)(2,1)S(1)}) custom-call(s32[2]{0:T(128)S(1)} %pad_add_fusion.refs_0_.place_ref, bf16[1024,1024]{1,0:T(8,128)(2,1)} %get-tuple-element.104.refs_1_, ...), custom_call_target="tpu_custom_call" | custom-call | flops 3221225472 | bytes 4194304 | tf_op jit(solution)/shard_map/qkv_gradient/pallas_call | solution.py:1051
  173.2 3.0 collective-permute-start.42
  177.5 12.1 %collective-permute-done.42 = bf16[1,1408,128]{2,1,0:T(8,128)(2,1)S(1)} collective-permute-done((bf16[1,1408,128]{2,1,0:T(8,128)(2,1)S(1)}, bf16[1,1408,128]{2,1,0:T(8,128)(2,1)S(1)}, u32[]{:S(2)}, u32[]{:S(2)}) %collective-permute-start.42) | collective-permute-done | bytes 360480 | tf_op jit(solution)/shard_map/ppermute | solution.py:36
  190.5 4.7 %collective-permute-start.31 = (bf16[2,512,128]{2,1,0:T(8,128)(2,1)S(1)}, bf16[2,512,128]{2,1,0:T(8,128)(2,1)S(1)}, u32[]{:S(2)}, u32[]{:S(2)}) collective-permute-start(bf16[2,512,128]{2,1,0:T(8,128)(2,1)S(1)} %get-tuple-element.153.refs_3_), channel_id=1, source_target_pairs={{0,8},{4,12},{8,0},{12,4},{16,24},{20,28},{24,16},{28,20},{1,9},{5... | collective-permute-start | bytes 786440 | tf_op jit(solution)/shard_map/ppermute | solution.py:36
  195.2 6.8 %collective-permute-done.32 = bf16[4,512,128]{2,1,0:T(8,128)(2,1)S(1)} collective-permute-done((bf16[4,512,128]{2,1,0:T(8,128)(2,1)S(1)}, bf16[4,512,128]{2,1,0:T(8,128)(2,1)S(1)}, u32[]{:S(2)}, u32[]{:S(2)}) %collective-permute-start.32) | collective-permute-done | bytes 524320 | tf_op jit(solution)/shard_map/ppermute | solution.py:36
  202.7 4.8 %project_back.1 = (bf16[2,256,1024]{2,1,0:T(8,128)(2,1)S(1)}, bf16[2,256,1024]{2,1,0:T(8,128)(2,1)}) custom-call(s32[2]{0:T(128)S(1)} %pad_add_fusion.refs_0_.place_ref, bf16[1024,768]{1,0:T(8,128)(2,1)} %get-tuple-element.100.refs_2_.refs_1_, bf16[1024,768]{1,0:T(8,128)(2,1)} %get-tuple-element.108.refs_2_, bf16[2,512,128]{2,1,0:T(8,128)(2,1)S(1)} %get-tuple-element.153.refs_3_), custom_call_target="tpu_custom_call" | custom-call | flops 1610612736 | bytes 4194304 | tf_op jit(solution)/shard_map/project_back/pallas_call | solution.py:1074
  210.6 3.5 %collective-permute-start.34 = (bf16[1,1024,128]{2,1,0:T(8,128)(2,1)S(1)}, bf16[1,1024,128]{2,1,0:T(8,128)(2,1)S(1)}, u32[]{:S(2)}, u32[]{:S(2)}) collective-permute-start(bf16[1,1024,128]{2,1,0:T(8,128)(2,1)S(1)} %pad_maximum_fusion.17), channel_id=1, source_target_pairs={{0,16},{4,20},{8,24},{12,28},{16,0},{20,4},{24,8},{28,12},{1,17},{... | collective-permute-start | bytes 786440 | tf_op jit(solution)/shard_map/ppermute | solution.py:36
  214.2 4.0 %collective-permute-done.51 = bf16[2,656,128]{2,1,0:T(8,128)(2,1)S(1)} collective-permute-done((bf16[2,656,128]{2,1,0:T(8,128)(2,1)S(1)}, bf16[2,656,128]{2,1,0:T(8,128)(2,1)S(1)}, u32[]{:S(2)}, u32[]{:S(2)}) %collective-permute-start.51) | collective-permute-done | bytes 335904 | tf_op jit(solution)/shard_map/ppermute | solution.py:36
  218.2 3.5 %collective-permute-start.52 = (bf16[1,656,128]{2,1,0:T(8,128)(2,1)S(1)}, bf16[1,656,128]{2,1,0:T(8,128)(2,1)S(1)}, u32[]{:S(2)}, u32[]{:S(2)}) collective-permute-start(bf16[1,656,128]{2,1,0:T(8,128)(2,1)S(1)} %add_convert_fusion.9), channel_id=1, source_target_pairs={{0,16},{4,20},{8,24},{12,28},{16,0},{20,4},{24,8},{28,12},{1,17},{... | collective-permute-start | bytes 503816 | tf_op jit(solution)/shard_map/ppermute | solution.py:36
  221.7 15.9 %collective-permute-done.34 = bf16[1,1024,128]{2,1,0:T(8,128)(2,1)S(1)} collective-permute-done((bf16[1,1024,128]{2,1,0:T(8,128)(2,1)S(1)}, bf16[1,1024,128]{2,1,0:T(8,128)(2,1)S(1)}, u32[]{:S(2)}, u32[]{:S(2)}) %collective-permute-start.34) | collective-permute-done | bytes 262176 | tf_op jit(solution)/shard_map/ppermute | solution.py:36
  238.3 7.0 %collective-permute-done.45 = bf16[1,1408,128]{2,1,0:T(8,128)(2,1)S(1)} collective-permute-done((bf16[1,1408,128]{2,1,0:T(8,128)(2,1)S(1)}, bf16[1,1408,128]{2,1,0:T(8,128)(2,1)S(1)}, u32[]{:S(2)}, u32[]{:S(2)}) %collective-permute-start.45) | collective-permute-done | bytes 360480 | tf_op jit(solution)/shard_map/ppermute | solution.py:36
  245.6 3.4 collective-permute-done.52
  249.2 3.0 collective-permute-start.37
  253.8 12.6 %collective-permute-done.53 = bf16[1,656,128]{2,1,0:T(8,128)(2,1)S(1)} collective-permute-done((bf16[1,656,128]{2,1,0:T(8,128)(2,1)S(1)}, bf16[1,656,128]{2,1,0:T(8,128)(2,1)S(1)}, u32[]{:S(2)}, u32[]{:S(2)}) %collective-permute-start.53) | collective-permute-done | bytes 167968 | tf_op jit(solution)/shard_map/ppermute | solution.py:36
  266.9 4.2 %collective-permute-done.37 = bf16[1,1024,128]{2,1,0:T(8,128)(2,1)S(1)} collective-permute-done((bf16[1,1024,128]{2,1,0:T(8,128)(2,1)S(1)}, bf16[1,1024,128]{2,1,0:T(8,128)(2,1)S(1)}, u32[]{:S(2)}, u32[]{:S(2)}) %collective-permute-start.37) | collective-permute-done | bytes 262176 | tf_op jit(solution)/shard_map/ppermute | solution.py:36
  275.0 6.8 %collective-permute-done.54 = bf16[2,656,128]{2,1,0:T(8,128)(2,1)S(1)} collective-permute-done((bf16[2,656,128]{2,1,0:T(8,128)(2,1)S(1)}, bf16[2,656,128]{2,1,0:T(8,128)(2,1)S(1)}, u32[]{:S(2)}, u32[]{:S(2)}) %collective-permute-start.54) | collective-permute-done | bytes 335904 | tf_op jit(solution)/shard_map/ppermute | solution.py:36
  284.3 3.2 collective-permute-done.40
  305.6 6.8 %columns_out.3 = (f32[8,32,5248]{2,1,0:T(8,128)}, f32[8,32,1]{2,1,0:T(8,128)S(1)}) custom-call(s32[2]{0:T(128)S(1)} %pad_add_fusion.refs_0_.place_ref, f32[8,32,1]{2,1,0:T(8,128)S(1)} %copy-done.24, bf16[8,32,5248]{2,1,0:T(8,128)(2,1)S(1)} %bitcast.80, bf16[4,24,32,128]{3,2,1,0:T(8,128)(2,1)S(1)} %bitcast.82, bf16[4,24,32,128]{3,2,1,0:T(8,128)(2,1)} %bitcast.49.refs_1_, ...), custom_call_target="tpu_custom_call" | custom-call | tf_op jit(solution)/shard_map/columns_out/pallas_call | solution.py:764
  314.8 11.6 %collective-permute-done.41.refs_1_ = bf16[4,512,128]{2,1,0:T(8,128)(2,1)} collective-permute-done((bf16[4,512,128]{2,1,0:T(8,128)(2,1)}, bf16[4,512,128]{2,1,0:T(8,128)(2,1)}, u32[]{:S(2)}, u32[]{:S(2)}) %collective-permute-start.41) | collective-permute-done | bytes 524320 | tf_op jit(solution)/shard_map/ppermute | solution.py:36
  330.6 5.1 %columns_out.2 = (f32[8,32,3072]{2,1,0:T(8,128)}, f32[8,32,1]{2,1,0:T(8,128)S(1)}) custom-call(s32[2]{0:T(128)S(1)} %pad_add_fusion.refs_0_.place_ref, f32[8,32,1]{2,1,0:T(8,128)S(1)} %copy-done.23, bf16[8,32,3072]{2,1,0:T(8,128)(2,1)S(1)} %bitcast.81, bf16[4,16,32,128]{3,2,1,0:T(8,128)(2,1)} %bitcast.34.refs_0_, bf16[4,16,32,128]{3,2,1,0:T(8,128)(2,1)} %bitcast.35.refs_1_, ...), custom_call_target="tpu_custom_call" | custom-call | tf_op jit(solution)/shard_map/columns_out/pallas_call | solution.py:764
  338.9 3.2 rows_out.3
  (287 shorter events, 112.8 us)
Async XLA Ops:
  8.5 20.8 %collective-permute-start = (bf16[256,1024]{1,0:T(8,128)(2,1)}, bf16[256,1024]{1,0:T(8,128)(2,1)}, u32[]{:S(2)}, u32[]{:S(2)}) collective-permute-start(bf16[256,1024]{1,0:T(8,128)(2,1)} %tokens.1), channel_id=1, source_target_pairs={{0,2},{1,3},{2,0},{3,1},{4,6},{5,7},{6,4},{7,5},{8,10},{9,11},{10,... | collective-permute-start | bytes 1572872 | tf_op jit(solution)/shard_map/ppermute | solution.py:36
  30.9 20.4 %collective-permute-start.12 = (bf16[2,128,1536]{2,1,0:T(8,128)(2,1)S(1)}, bf16[2,128,1536]{2,1,0:T(8,128)(2,1)S(1)}, u32[]{:S(2)}, u32[]{:S(2)}) collective-permute-start(bf16[2,128,1536]{2,1,0:T(8,128)(2,1)S(1)} %dynamic-slice_bitcast_fusion), channel_id=1, source_target_pairs={{0,2},{1,3},{2,0},{3,1},{4,6},{5,7},{6,4},{7,5},{8,10},{9,11},{10,... | collective-permute-start | bytes 2359304 | tf_op jit(solution)/shard_map/ppermute | solution.py:36
  32.6 24.9 %collective-permute-start.9 = (bf16[128,1024]{1,0:T(8,128)(2,1)S(1)}, bf16[128,1024]{1,0:T(8,128)(2,1)S(1)}, u32[]{:S(2)}, u32[]{:S(2)}) collective-permute-start(bf16[128,1024]{1,0:T(8,128)(2,1)S(1)} %dynamic-slice_bitcast_fusion.2), channel_id=1, source_target_pairs={{0,2},{1,3},{2,0},{3,1},{4,6},{5,7},{6,4},{7,5},{8,10},{9,11},{10,... | collective-permute-start | bytes 786440 | tf_op jit(solution)/shard_map/ppermute | solution.py:36
  55.9 15.3 %collective-permute-start.7 = (bf16[1024,256]{1,0:T(8,128)(2,1)S(1)}, bf16[1024,256]{1,0:T(8,128)(2,1)S(1)}, u32[]{:S(2)}, u32[]{:S(2)}) collective-permute-start(bf16[1024,256]{1,0:T(8,128)(2,1)S(1)} %get-tuple-element.69.refs_4_.refs_5_), channel_id=1, source_target_pairs={{0,2},{1,3},{2,0},{3,1},{4,6},{5,7},{6,4},{7,5},{8,10},{9,11},{10,... | collective-permute-start | bytes 1572872 | tf_op jit(solution)/shard_map/ppermute | solution.py:36
  71.8 17.6 %collective-permute-start.16 = (bf16[256,1024]{1,0:T(8,128)(2,1)S(1)}, bf16[256,1024]{1,0:T(8,128)(2,1)S(1)}, u32[]{:S(2)}, u32[]{:S(2)}) collective-permute-start(bf16[256,1024]{1,0:T(8,128)(2,1)S(1)} %copy-done.11), channel_id=1, source_target_pairs={{0,2},{1,3},{2,0},{3,1},{4,6},{5,7},{6,4},{7,5},{8,10},{9,11},{10,... | collective-permute-start | bytes 1572872 | tf_op jit(solution)/shard_map/ppermute | solution.py:36
  118.6 29.4 %collective-permute-start.24 = (bf16[4,640,128]{2,1,0:T(8,128)(2,1)S(1)}, bf16[4,640,128]{2,1,0:T(8,128)(2,1)S(1)}, u32[]{:S(2)}, u32[]{:S(2)}) collective-permute-start(bf16[4,640,128]{2,1,0:T(8,128)(2,1)S(1)} %bitcast.89), channel_id=1, source_target_pairs={{0,8},{4,12},{8,0},{12,4},{16,24},{20,28},{24,16},{28,20},{1,9},{5... | collective-permute-start | bytes 1966088 | tf_op jit(solution)/shard_map/ppermute | solution.py:36
  119.4 28.6 %collective-permute-start.23 = (bf16[4,768,128]{2,1,0:T(8,128)(2,1)}, bf16[4,768,128]{2,1,0:T(8,128)(2,1)S(1)}, u32[]{:S(2)}, u32[]{:S(2)}) collective-permute-start(bf16[4,768,128]{2,1,0:T(8,128)(2,1)} %bitcast.111), channel_id=1, source_target_pairs={{0,4},{4,0},{8,12},{12,8},{16,20},{20,16},{24,28},{28,24},{1,5},{5... | collective-permute-start | bytes 2359304 | tf_op jit(solution)/shard_map/ppermute | solution.py:36
  126.5 19.8 %collective-permute-start.21 = (bf16[256,1024]{1,0:T(8,128)(2,1)S(1)}, bf16[256,1024]{1,0:T(8,128)(2,1)S(1)}, u32[]{:S(2)}, u32[]{:S(2)}) collective-permute-start(bf16[256,1024]{1,0:T(8,128)(2,1)S(1)} %get-tuple-element.87.refs_6_.refs_1_), channel_id=1, source_target_pairs={{0,2},{1,3},{2,0},{3,1},{4,6},{5,7},{6,4},{7,5},{8,10},{9,11},{10,... | collective-permute-start | bytes 1572872 | tf_op jit(solution)/shard_map/ppermute | solution.py:36
  147.9 18.4 %collective-permute-start.20 = (bf16[2,256,1024]{2,1,0:T(8,128)(2,1)S(1)}, bf16[2,256,1024]{2,1,0:T(8,128)(2,1)S(1)}, u32[]{:S(2)}, u32[]{:S(2)}) collective-permute-start(bf16[2,256,1024]{2,1,0:T(8,128)(2,1)S(1)} %copy-done.45), channel_id=1, source_target_pairs={{0,1},{1,0},{2,3},{3,2},{4,5},{5,4},{6,7},{7,6},{8,9},{9,8},{10,11... | collective-permute-start | bytes 3145736 | tf_op jit(solution)/shard_map/ppermute | solution.py:36
  148.2 18.2 %collective-permute-start.27 = (bf16[2,640,128]{2,1,0:T(8,128)(2,1)S(1)}, bf16[2,640,128]{2,1,0:T(8,128)(2,1)S(1)}, u32[]{:S(2)}, u32[]{:S(2)}) collective-permute-start(bf16[2,640,128]{2,1,0:T(8,128)(2,1)S(1)} %get-tuple-element.143.refs_14_), channel_id=1, source_target_pairs={{0,4},{4,0},{8,12},{12,8},{16,20},{20,16},{24,28},{28,24},{1,5},{5... | collective-permute-start | bytes 983048 | tf_op jit(solution)/shard_map/ppermute | solution.py:36
  150.0 16.3 %collective-permute-start.26 = (bf16[2,768,128]{2,1,0:T(8,128)(2,1)S(1)}, bf16[2,768,128]{2,1,0:T(8,128)(2,1)S(1)}, u32[]{:S(2)}, u32[]{:S(2)}) collective-permute-start(bf16[2,768,128]{2,1,0:T(8,128)(2,1)S(1)} %get-tuple-element.135.refs_13_), channel_id=1, source_target_pairs={{0,8},{4,12},{8,0},{12,4},{16,24},{20,28},{24,16},{28,20},{1,9},{5... | collective-permute-start | bytes 1179656 | tf_op jit(solution)/shard_map/ppermute | solution.py:36
  165.0 43.1 %collective-permute-start.50 = (bf16[4,656,128]{2,1,0:T(8,128)(2,1)S(1)}, bf16[4,656,128]{2,1,0:T(8,128)(2,1)S(1)}, u32[]{:S(2)}, u32[]{:S(2)}) collective-permute-start(bf16[4,656,128]{2,1,0:T(8,128)(2,1)S(1)} %copy-done.50), channel_id=1, source_target_pairs={{0,8},{4,12},{8,0},{12,4},{16,24},{20,28},{24,16},{28,20},{1,9},{5... | collective-permute-start | bytes 2015240 | tf_op jit(solution)/shard_map/ppermute | solution.py:36
  172.6 17.8 %collective-permute-start.28 = (bf16[4,512,128]{2,1,0:T(8,128)(2,1)S(1)}, bf16[4,512,128]{2,1,0:T(8,128)(2,1)S(1)}, u32[]{:S(2)}, u32[]{:S(2)}) collective-permute-start(bf16[4,512,128]{2,1,0:T(8,128)(2,1)S(1)} %bitcast.90), channel_id=1, source_target_pairs={{0,4},{4,0},{8,12},{12,8},{16,20},{20,16},{24,28},{28,24},{1,5},{5... | collective-permute-start | bytes 1572872 | tf_op jit(solution)/shard_map/ppermute | solution.py:36
  173.2 16.4 %collective-permute-start.42 = (bf16[1,1408,128]{2,1,0:T(8,128)(2,1)S(1)}, bf16[1,1408,128]{2,1,0:T(8,128)(2,1)S(1)}, u32[]{:S(2)}, u32[]{:S(2)}) collective-permute-start(bf16[1,1408,128]{2,1,0:T(8,128)(2,1)S(1)} %pad_maximum_fusion.12), channel_id=1, source_target_pairs={{0,16},{4,20},{8,24},{12,28},{16,0},{20,4},{24,8},{28,12},{1,17},{... | collective-permute-start | bytes 1081352 | tf_op jit(solution)/shard_map/ppermute | solution.py:36
  176.2 25.8 %collective-permute-start.32 = (bf16[4,512,128]{2,1,0:T(8,128)(2,1)S(1)}, bf16[4,512,128]{2,1,0:T(8,128)(2,1)S(1)}, u32[]{:S(2)}, u32[]{:S(2)}) collective-permute-start(bf16[4,512,128]{2,1,0:T(8,128)(2,1)S(1)} %pad_maximum_fusion.10), channel_id=1, source_target_pairs={{0,8},{4,12},{8,0},{12,4},{16,24},{20,28},{24,16},{28,20},{1,9},{5... | collective-permute-start | bytes 1572872 | tf_op jit(solution)/shard_map/ppermute | solution.py:36
  189.8 17.8 %collective-permute-start.43 = (bf16[2,1,352,128]{3,2,0,1:T(8,128)(2,1)S(1)}, bf16[2,1,352,128]{3,2,0,1:T(8,128)(2,1)S(1)}, u32[]{:S(2)}, u32[]{:S(2)}) collective-permute-start(bf16[2,1,352,128]{3,2,0,1:T(8,128)(2,1)S(1)} %get-tuple-element.161), channel_id=1, source_target_pairs={{0,2},{1,3},{2,0},{3,1},{4,6},{5,7},{6,4},{7,5},{8,10},{9,11},{10,... | collective-permute-start | bytes 540680 | tf_op jit(solution)/shard_map/ppermute | solution.py:36
  190.5 19.9 %collective-permute-start.31 = (bf16[2,512,128]{2,1,0:T(8,128)(2,1)S(1)}, bf16[2,512,128]{2,1,0:T(8,128)(2,1)S(1)}, u32[]{:S(2)}, u32[]{:S(2)}) collective-permute-start(bf16[2,512,128]{2,1,0:T(8,128)(2,1)S(1)} %get-tuple-element.153.refs_3_), channel_id=1, source_target_pairs={{0,8},{4,12},{8,0},{12,4},{16,24},{20,28},{24,16},{28,20},{1,9},{5... | collective-permute-start | bytes 786440 | tf_op jit(solution)/shard_map/ppermute | solution.py:36
  207.5 65.1 %collective-permute-start.29 = (bf16[2,256,1024]{2,1,0:T(8,128)(2,1)}, bf16[2,256,1024]{2,1,0:T(8,128)(2,1)S(1)}, u32[]{:S(2)}, u32[]{:S(2)}) collective-permute-start(bf16[2,256,1024]{2,1,0:T(8,128)(2,1)} %get-tuple-element.111), channel_id=1, source_target_pairs={{0,1},{1,0},{2,3},{3,2},{4,5},{5,4},{6,7},{7,6},{8,9},{9,8},{10,11... | collective-permute-start | bytes 3145736 | tf_op jit(solution)/shard_map/ppermute | solution.py:36
  210.6 27.0 %collective-permute-start.34 = (bf16[1,1024,128]{2,1,0:T(8,128)(2,1)S(1)}, bf16[1,1024,128]{2,1,0:T(8,128)(2,1)S(1)}, u32[]{:S(2)}, u32[]{:S(2)}) collective-permute-start(bf16[1,1024,128]{2,1,0:T(8,128)(2,1)S(1)} %pad_maximum_fusion.17), channel_id=1, source_target_pairs={{0,16},{4,20},{8,24},{12,28},{16,0},{20,4},{24,8},{28,12},{1,17},{... | collective-permute-start | bytes 786440 | tf_op jit(solution)/shard_map/ppermute | solution.py:36
  214.1 31.2 %collective-permute-start.45 = (bf16[1,1408,128]{2,1,0:T(8,128)(2,1)S(1)}, bf16[1,1408,128]{2,1,0:T(8,128)(2,1)S(1)}, u32[]{:S(2)}, u32[]{:S(2)}) collective-permute-start(bf16[1,1408,128]{2,1,0:T(8,128)(2,1)S(1)} %maximum_bitcast_fusion.1), channel_id=1, source_target_pairs={{0,16},{4,20},{8,24},{12,28},{16,0},{20,4},{24,8},{28,12},{1,17},{... | collective-permute-start | bytes 1081352 | tf_op jit(solution)/shard_map/ppermute | solution.py:36
  218.2 30.7 %collective-permute-start.52 = (bf16[1,656,128]{2,1,0:T(8,128)(2,1)S(1)}, bf16[1,656,128]{2,1,0:T(8,128)(2,1)S(1)}, u32[]{:S(2)}, u32[]{:S(2)}) collective-permute-start(bf16[1,656,128]{2,1,0:T(8,128)(2,1)S(1)} %add_convert_fusion.9), channel_id=1, source_target_pairs={{0,16},{4,20},{8,24},{12,28},{16,0},{20,4},{24,8},{28,12},{1,17},{... | collective-permute-start | bytes 503816 | tf_op jit(solution)/shard_map/ppermute | solution.py:36
  245.4 28.2 %collective-permute-start.46 = (bf16[2,768,128]{2,1,0:T(8,128)(2,1)S(1)}, bf16[2,768,128]{2,1,0:T(8,128)(2,1)S(1)}, u32[]{:S(2)}, u32[]{:S(2)}) collective-permute-start(bf16[2,768,128]{2,1,0:T(8,128)(2,1)S(1)} %fusion.7), channel_id=1, source_target_pairs={{0,8},{4,12},{8,0},{12,4},{16,24},{20,28},{24,16},{28,20},{1,9},{5... | collective-permute-start | bytes 1179656 | tf_op jit(solution)/shard_map/ppermute | solution.py:36
  249.0 17.4 %collective-permute-start.53 = (bf16[1,656,128]{2,1,0:T(8,128)(2,1)S(1)}, bf16[1,656,128]{2,1,0:T(8,128)(2,1)S(1)}, u32[]{:S(2)}, u32[]{:S(2)}) collective-permute-start(bf16[1,656,128]{2,1,0:T(8,128)(2,1)S(1)} %bitcast.93), channel_id=1, source_target_pairs={{0,16},{4,20},{8,24},{12,28},{16,0},{20,4},{24,8},{28,12},{1,17},{... | collective-permute-start | bytes 503816 | tf_op jit(solution)/shard_map/ppermute | solution.py:36
  249.2 21.8 %collective-permute-start.37 = (bf16[1,1024,128]{2,1,0:T(8,128)(2,1)S(1)}, bf16[1,1024,128]{2,1,0:T(8,128)(2,1)S(1)}, u32[]{:S(2)}, u32[]{:S(2)}) collective-permute-start(bf16[1,1024,128]{2,1,0:T(8,128)(2,1)S(1)} %maximum_bitcast_fusion.2), channel_id=1, source_target_pairs={{0,16},{4,20},{8,24},{12,28},{16,0},{20,4},{24,8},{28,12},{1,17},{... | collective-permute-start | bytes 786440 | tf_op jit(solution)/shard_map/ppermute | solution.py:36
  252.2 21.2 %collective-permute-start.48 = (bf16[2,640,128]{2,1,0:T(8,128)(2,1)S(1)}, bf16[2,640,128]{2,1,0:T(8,128)(2,1)S(1)}, u32[]{:S(2)}, u32[]{:S(2)}) collective-permute-start(bf16[2,640,128]{2,1,0:T(8,128)(2,1)S(1)} %pad_maximum_fusion.14), channel_id=1, source_target_pairs={{0,4},{4,0},{8,12},{12,8},{16,20},{20,16},{24,28},{28,24},{1,5},{5... | collective-permute-start | bytes 983048 | tf_op jit(solution)/shard_map/ppermute | solution.py:36
  266.4 24.9 %collective-permute-start.25 = (bf16[256,1024]{1,0:T(8,128)(2,1)S(1)}, bf16[256,1024]{1,0:T(8,128)(2,1)S(1)}, u32[]{:S(2)}, u32[]{:S(2)}) collective-permute-start(bf16[256,1024]{1,0:T(8,128)(2,1)S(1)} %copy-done.30), channel_id=1, source_target_pairs={{0,2},{1,3},{2,0},{3,1},{4,6},{5,7},{6,4},{7,5},{8,10},{9,11},{10,... | collective-permute-start | bytes 1572872 | tf_op jit(solution)/shard_map/ppermute | solution.py:36
  273.5 18.6 %collective-permute-start.30 = (bf16[256,1024]{1,0:T(8,128)(2,1)S(1)}, bf16[256,1024]{1,0:T(8,128)(2,1)S(1)}, u32[]{:S(2)}, u32[]{:S(2)}) collective-permute-start(bf16[256,1024]{1,0:T(8,128)(2,1)S(1)} %get-tuple-element.113), channel_id=1, source_target_pairs={{0,2},{1,3},{2,0},{3,1},{4,6},{5,7},{6,4},{7,5},{8,10},{9,11},{10,... | collective-permute-start | bytes 1572872 | tf_op jit(solution)/shard_map/ppermute | solution.py:36
  281.9 23.7 %collective-permute-start.47 = (bf16[4,768,128]{2,1,0:T(8,128)(2,1)S(1)}, bf16[4,768,128]{2,1,0:T(8,128)(2,1)}, u32[]{:S(2)}, u32[]{:S(2)}) collective-permute-start(bf16[4,768,128]{2,1,0:T(8,128)(2,1)S(1)} %pad_maximum_fusion.6), channel_id=1, source_target_pairs={{0,4},{4,0},{8,12},{12,8},{16,20},{20,16},{24,28},{28,24},{1,5},{5... | collective-permute-start | bytes 2359304 | tf_op jit(solution)/shard_map/ppermute | solution.py:36
  287.5 18.1 %collective-permute-start.49 = (bf16[4,640,128]{2,1,0:T(8,128)(2,1)}, bf16[4,640,128]{2,1,0:T(8,128)(2,1)}, u32[]{:S(2)}, u32[]{:S(2)}) collective-permute-start(bf16[4,640,128]{2,1,0:T(8,128)(2,1)} %pad_maximum_fusion.8), channel_id=1, source_target_pairs={{0,8},{4,12},{8,0},{12,4},{16,24},{20,28},{24,16},{28,20},{1,9},{5... | collective-permute-start | bytes 1966088 | tf_op jit(solution)/shard_map/ppermute | solution.py:36
  287.5 51.4 %collective-permute-start.55 = (bf16[4,656,128]{2,1,0:T(8,128)(2,1)}, bf16[4,656,128]{2,1,0:T(8,128)(2,1)}, u32[]{:S(2)}, u32[]{:S(2)}) collective-permute-start(bf16[4,656,128]{2,1,0:T(8,128)(2,1)} %pad_maximum_fusion.7.refs_0_), channel_id=1, source_target_pairs={{0,8},{4,12},{8,0},{12,4},{16,24},{20,28},{24,16},{28,20},{1,9},{5... | collective-permute-start | bytes 2015240 | tf_op jit(solution)/shard_map/ppermute | solution.py:36
  292.1 34.3 %collective-permute-start.41 = (bf16[4,512,128]{2,1,0:T(8,128)(2,1)}, bf16[4,512,128]{2,1,0:T(8,128)(2,1)}, u32[]{:S(2)}, u32[]{:S(2)}) collective-permute-start(bf16[4,512,128]{2,1,0:T(8,128)(2,1)} %pad_maximum_fusion.9.refs_0_), channel_id=1, source_target_pairs={{0,8},{4,12},{8,0},{12,4},{16,24},{20,28},{24,16},{28,20},{1,9},{5... | collective-permute-start | bytes 1572872 | tf_op jit(solution)/shard_map/ppermute | solution.py:36
  293.0 34.4 %collective-permute-start.39 = (bf16[4,512,128]{2,1,0:T(8,128)(2,1)}, bf16[4,512,128]{2,1,0:T(8,128)(2,1)}, u32[]{:S(2)}, u32[]{:S(2)}) collective-permute-start(bf16[4,512,128]{2,1,0:T(8,128)(2,1)} %pad_maximum_fusion.11), channel_id=1, source_target_pairs={{0,4},{4,0},{8,12},{12,8},{16,20},{20,16},{24,28},{28,24},{1,5},{5... | collective-permute-start | bytes 1572872 | tf_op jit(solution)/shard_map/ppermute | solution.py:36
  (76 other events, 459.4 us)

commit v8 on v7

--- a/solution.py
+++ b/solution.py
@@ -943,7 +943,7 @@
         cost_estimate=work(12 * seq * model * padded),
         name="up_projection",
     )(place, *arrays_of(toks + atts + out_groups + in_groups))
-    cots = gather_rows(after(cotangent, atts[1].array), lambda: (up,))
+    cots = gather_rows(after(cotangent, atts[1].array), lambda: (up,), apart=True)
     down_w = jnp.pad(w_down, ((0, -ff % 16), (0, 0)))
     act, dup, dnormed2_keep, dnormed2_send = pl.pallas_call(
         functools.partial(dup_kernel, held_of(cots), n),
@@ -974,7 +974,7 @@
     lanes = max(LANES, model // replicas)
     tiles = up_tiles(ff)
     orders = [near, far]
-    in_counts = [tiles - tiles // 2, tiles // 2]
+    in_counts = [tiles // 2, tiles - tiles // 2]
     in_shapes = [shape((slots, n * c, chunk, LANES), BF16) for c in in_counts for _ in range(2)]
     down_shape = shape((slots, ff, lanes), BF16)
     top = bits_of("shard") - 1
@@ -1002,7 +1002,7 @@
         name="norm_back",
     )(mine, swap(other, "shard", top), hidden, cotangent, in_flows[0])
     down_keep, down_send, mlp_keep, mlp_send = pl.pallas_call(
-        ordered(functools.partial(down_kernel, held_of(cots), n, ff, far), 3 + len(cots), 1),
+        ordered(functools.partial(down_kernel, held_of(cots), n, ff, near), 3 + len(cots), 1),
         in_specs=[SMEM_SPEC] + [VMEM_SPEC] * (2 + len(cots)) + [ANY_SPEC],
         out_shape=[down_shape] * 2 + [block_shape] * 2,
         scratch_shapes=[pltpu.VMEM((padded, model), F32)],
@@ -1059,7 +1059,9 @@
     )(place, normed1, dqkv, in_reduce.p[1], in_reduce.q[1], mlp_other)
     qkv_flows = [flow_rows(a) for a in qkv_flows]
     split = qkv_flows[2].shape[1]
+    down_first = add_halves(down_keep, after(swap(down_send, "rep", near[0]), dqkv))
     qkv_q = [jnp.concatenate(x, axis=1) for x in zip(qkv_flows[2:], (out_keep, out_send))]
+    qkv_q[1] = after(qkv_q[1], down_first[1])
     att_reduce = PairReduce(qkv_flows[:2], qkv_q, orders)
     att_reduce.step(0)
     att_first = att_reduce.p[1]
@@ -1098,13 +1100,12 @@
         return [a[:, :size].reshape(a.shape[0], n * count, chunk, LANES) for a in pair]
 
     in_p, in_q = turned(*in_reduce.finish([[qkv_flows[0]]]), in_counts)
-    down_send = after(down_send, dqkv)
-    down_share = replica_reduce(down_keep, down_send, far, [[qkv_flows[0]], [att_first]])
+    down_share = replica_reduce(*down_first, near[1:], [[att_first]])
 
     att_p, att_q = att_reduce.finish()
     att_done = att_p[:16]
     in_p, in_q = pair_gather(in_p, in_q, orders)
-    down_pair = replica_spread(after(down_share, att_done), far)
+    down_pair = replica_spread(after(down_share, att_done), near)
     qkv_p, qkv_q = turned(att_p, att_q[:split], qkv_counts)
     att_p, att_q = pair_gather(qkv_p, jnp.concatenate([qkv_q, att_q[split:]]), orders)
 
@@ -1118,7 +1119,7 @@
         n,
         ff=ff,
     )
-    down_total = rows_out(place, down_pair, 0, ff, model, far)
+    down_total = rows_out(place, down_pair, 0, ff, model, near)
     out_total = rows_out(place, att_q, split, part, model, far)
     qkv_total, ln1_total = columns_out(
         place,

time: 346 us -> 325 us (0.939)
  waiting for transfers between devices: 120 us -> 109 us
  starting transfers between devices: 62.1 us -> 54.2 us
    ppermute x56 -> x57, waiting for transfers between devices: 120 us -> 109 us  [swap(): return lax.ppermute(x, axis, [(i, i ^ 1 << bit) for i in range(size)])]
    ppermute x56 -> x57, starting transfers between devices: 62.1 us -> 54.2 us  [swap(): return lax.ppermute(x, axis, [(i, i ^ 1 << bit) for i in range(size)])]
  transfers between devices with their start and end apart: 56 -> 57, of which waited for: 23 -> 21; matrix products, arithmetic and copies ran while one was open for 7% -> 7% of each run, Pallas kernels for 27% -> 27%
where the time goes in v8:
time: 325 us; the launch traced here: 321 us
  waiting for transfers between devices  109 us (34%)
  Pallas kernels  108 us (33%)
  starting transfers between devices  54.2 us (17%)
  local copies, waits for them, and re-layouts  32.4 us (10%)
  other arithmetic  14.6 us (4%)
    ppermute x57, waiting for transfers between devices, swap(): return lax.ppermute(x, axis, [(i, i ^ 1 << bit) for i in range(size)])  109 us
    ppermute x57, starting transfers between devices, swap(): return lax.ppermute(x, axis, [(i, i ^ 1 << bit) for i in range(size)])  54.2 us
    unnamed x104, local copies, waits for them, and re-layouts  22 us
    pallas_call x1, Pallas kernels, shards(): pl.pallas_call(ordered(functools.partial(down_kernel, held_of(cots), n, f...  18.1 us
    pallas_call x1, Pallas kernels, shards(): pl.pallas_call(ordered(functools.partial(attention_back_kernel, held_of(d...  13.2 us
    pallas_call x1, Pallas kernels, shards(): pl.pallas_call(ordered(functools.partial(attention_kernel, held_of(toks),...  12.4 us
    pallas_call x1, Pallas kernels, shards(): pl.pallas_call(functools.partial(dup_kernel, held_of(cots), n), in_specs=...  12 us
    pallas_call x2, Pallas kernels, columns_out(): pl.pallas_call(functools.partial(columns_out_kernel, n, ff, head_cols, wi...  12 us
  transfers between devices with their start and end apart: 57, of which 21 were waited for; matrix products, arithmetic and copies ran while one was open for 7% of the time, Pallas kernels for 27%

profile of v8, /device:TPU:0, one launch (start us, length us, event | category | flops | bytes accessed | tf_op | source)
XLA Modules:
  0.0 320.6 jit_solution(16819159183619230047)
XLA Ops:
  5.5 2.9 collective-permute-start.3
  11.7 4.8 %sine_multiply_fusion = (f32[1024,256]{1,0:T(8,128)}, f32[1024,256]{1,0:T(8,128)}) fusion(f32[256]{0:T(256)S(1)} %get-tuple-element.170, f32[256]{0:T(256)S(1)} %get-tuple-element.171), kind=kLoop, calls=%fused_computation.4 | loop fusion | flops 524288 | bytes 2099200 | tf_op jit(solution)/shard_map/mul | solution.py:881
  24.5 3.1 collective-permute-done.4.refs_11_
  34.1 12.4 %attention.1 = (bf16[1024,256]{1,0:T(8,128)(2,1)S(1)}, bf16[1152,256]{1,0:T(8,128)(2,1)}, bf16[1152,256]{1,0:T(8,128)(2,1)}, bf16[1024,256]{1,0:T(8,128)(2,1)S(1...) custom-call(s32[2]{0:T(128)S(1)} %pad_add_fusion.refs_0_.place_ref, ...), custom_call_target="tpu_custom_call" | custom-call | flops 10737418240 | bytes 4194304 | tf_op jit(solution)/shard_map/attention/pallas_call | solution.py:889
  46.5 4.8 %collective-permute-done.12.refs_12_ = bf16[2,128,1536]{2,1,0:T(8,128)(2,1)S(1)} collective-permute-done((bf16[2,128,1536]{2,1,0:T(8,128)(2,1)S(1)}, bf16[2,128,1536]{2,1,0:T(8,128)(2,1)S(1)}, u32[]{:S(2)}, u32[]{:S(2)}) %collective-permute-start.12) | collective-permute-done | bytes 786464 | tf_op jit(solution)/shard_map/ppermute | solution.py:36
  57.4 2.6 collective-permute-start.10
  60.0 5.8 %collective-permute-done.14.refs_14_ = bf16[2,64,1536]{2,1,0:T(8,128)(2,1)S(1)} collective-permute-done((bf16[2,64,1536]{2,1,0:T(8,128)(2,1)S(1)}, bf16[2,64,1536]{2,1,0:T(8,128)(2,1)S(1)}, u32[]{:S(2)}, u32[]{:S(2)}) %collective-permute-start.14) | collective-permute-done | bytes 393248 | tf_op jit(solution)/shard_map/ppermute | solution.py:36
  66.2 4.9 %collective-permute-done.10.refs_9_ = bf16[128,1024]{1,0:T(8,128)(2,1)S(1)} collective-permute-done((bf16[128,1024]{1,0:T(8,128)(2,1)S(1)}, bf16[128,1024]{1,0:T(8,128)(2,1)S(1)}, u32[]{:S(2)}, u32[]{:S(2)}) %collective-permute-start.10) | collective-permute-done | bytes 262176 | tf_op jit(solution)/shard_map/ppermute | solution.py:36
  76.3 11.9 %up_projection.1 = (f32[256,1024]{1,0:T(8,128)}, bf16[1024,1024]{1,0:T(8,128)(2,1)}, f32[1024,1536]{1,0:T(8,128)}, bf16[1024,1536]{1,0:T(8,128)(2,1)}) custom-call(s32[2]{0:T(128)S(1)} %pad_add_fusion.refs_0_.place_ref, bf16[256,1024]{1,0:T(8,128)(2,1)} %tokens.1, bf16[256,1024]{1,0:T(8,128)(2,1)} %collective-permute-done.refs_6_.refs_1_, ...), custom_call_target="tpu_custom_call" | custom-call | flops 9663676416 | bytes 4194304 | tf_op jit(solution)/shard_map/up_projection/pallas_call | solution.py:916
  91.0 12.0 %dup.1 = (bf16[1024,768]{1,0:T(8,128)(2,1)}, bf16[1024,1536]{1,0:T(8,128)(2,1)}, bf16[2,256,1024]{2,1,0:T(8,128)(2,1)}, bf16[2,256,1024]{2,1,0:T(8,128)(2,1)}) custom-call(f32[1024,1536]{1,0:T(8,128)} %get-tuple-element.74.up_ref, bf16[1024,1536]{1,0:T(8,128)(2,1)} %get-tuple-element.75.w_in_ref, bf16[656,1024]{1,0:T(8,128)(2,1)} %refs_2_.1, ...), custom_call_target="tpu_custom_call" | custom-call | flops 11274289152 | bytes 4194304 | tf_op jit(solution)/shard_map/dup/pallas_call | solution.py:948
  103.3 2.7 collective-permute-done.19.got_ref
  109.0 7.4 %in_gradient.1 = (bf16[4,20,32,128]{3,2,1,0:T(8,128)(2,1)S(1)}, bf16[4,20,32,128]{3,2,1,0:T(8,128)(2,1)S(1)}, bf16[4,24,32,128]{3,2,1,0:T(8,128)(2,1)}, bf16[4,24,32,128]{3,2,1,0:T(8,128)(2,1)}) custom-call(s32[2]{0:T(128)S(1)} %pad_add_fusion.refs_0_.place_ref, bf16[1024,1024]{1,0:T(8,128)(2,1)} %get-tuple-element.84.refs_1_, ...), custom_call_target="tpu_custom_call" | custom-call | flops 6442450944 | bytes 4194304 | tf_op jit(solution)/shard_map/in_gradient/pallas_call | solution.py:986
  118.7 2.8 collective-permute-done.20.refs_1_
  124.6 18.1 %down_gradient.1 = (bf16[4,656,128]{2,1,0:T(8,128)(2,1)}, bf16[4,656,128]{2,1,0:T(8,128)(2,1)}, bf16[2,256,1024]{2,1,0:T(8,128)(2,1)}, bf16[2,256,1024]{2,1,0:T(8,128)(2,1)}) custom-call(s32[2]{0:T(128)S(1)} %pad_add_fusion.refs_0_.place_ref, bf16[1024,768]{1,0:T(8,128)(2,1)} %get-tuple-element.78.refs_1_, bf16[656,1024]{1,0:T(8,128)(2,1)} %refs_2_.1, ...), custom_call_target="tpu_custom_call" | custom-call | flops 6442450944 | bytes 4194304 | tf_op jit(solution)/shard_map/down_gradient/pallas_call | solution.py:1004
  149.1 13.2 %attention_back.1 = (bf16[1024,768]{1,0:T(8,128)(2,1)}, bf16[4,256,128]{2,1,0:T(8,128)(2,1)S(1)}, bf16[4,256,128]{2,1,0:T(8,128)(2,1)S(1)}) custom-call(s32[2]{0:T(128)S(1)} %pad_add_fusion.refs_0_.place_ref, bf16[256,1024]{1,0:T(8,128)(2,1)S(1)} %copy-done.28, bf16[256,1024]{1,0:T(8,128)(2,1)} %copy-done.42, bf16[512,1024]{1,0:T(8,128)(2,1)} %copy-done.47, ...), custom_call_target="tpu_custom_call" | custom-call | flops 10737418240 | bytes 4194304 | tf_op jit(solution)/shard_map/attention_back/pallas_call | solution.py:1017
  163.7 6.8 %collective-permute-done.28 = bf16[2,768,128]{2,1,0:T(8,128)(2,1)S(1)} collective-permute-done((bf16[2,768,128]{2,1,0:T(8,128)(2,1)S(1)}, bf16[2,768,128]{2,1,0:T(8,128)(2,1)S(1)}, u32[]{:S(2)}, u32[]{:S(2)}) %collective-permute-start.28) | collective-permute-done | bytes 393248 | tf_op jit(solution)/shard_map/ppermute | solution.py:36
  172.7 4.0 %qkv_gradient.1 = (bf16[4,16,32,128]{3,2,1,0:T(8,128)(2,1)S(1)}, bf16[4,16,32,128]{3,2,1,0:T(8,128)(2,1)S(1)}, bf16[4,8,32,128]{3,2,1,0:T(8,128)(2,1)S(1)}, bf16[4,8,32,128]{3,2,1,0:T(8,128)(2,1)S(1)}) custom-call(s32[2]{0:T(128)S(1)} %pad_add_fusion.refs_0_.place_ref, bf16[1024,1024]{1,0:T(8,128)(2,1)} %get-tuple-element.104.refs_1_, ...), custom_call_target="tpu_custom_call" | custom-call | flops 3221225472 | bytes 4194304 | tf_op jit(solution)/shard_map/qkv_gradient/pallas_call | solution.py:1051
  178.4 4.2 %collective-permute-start.34 = (bf16[4,512,128]{2,1,0:T(8,128)(2,1)S(1)}, bf16[4,512,128]{2,1,0:T(8,128)(2,1)S(1)}, u32[]{:S(2)}, u32[]{:S(2)}) collective-permute-start(bf16[4,512,128]{2,1,0:T(8,128)(2,1)S(1)} %pad_maximum_fusion.9), channel_id=1, source_target_pairs={{0,8},{4,12},{8,0},{12,4},{16,24},{20,28},{24,16},{28,20},{1,9},{5... | collective-permute-start | bytes 1572872 | tf_op jit(solution)/shard_map/ppermute | solution.py:36
  182.6 14.2 %collective-permute-done.44 = bf16[1,1408,128]{2,1,0:T(8,128)(2,1)S(1)} collective-permute-done((bf16[1,1408,128]{2,1,0:T(8,128)(2,1)S(1)}, bf16[1,1408,128]{2,1,0:T(8,128)(2,1)S(1)}, u32[]{:S(2)}, u32[]{:S(2)}) %collective-permute-start.44) | collective-permute-done | bytes 360480 | tf_op jit(solution)/shard_map/ppermute | solution.py:36
  200.0 5.3 %collective-permute-done.34 = bf16[4,512,128]{2,1,0:T(8,128)(2,1)S(1)} collective-permute-done((bf16[4,512,128]{2,1,0:T(8,128)(2,1)S(1)}, bf16[4,512,128]{2,1,0:T(8,128)(2,1)S(1)}, u32[]{:S(2)}, u32[]{:S(2)}) %collective-permute-start.34) | collective-permute-done | bytes 524320 | tf_op jit(solution)/shard_map/ppermute | solution.py:36
  206.0 4.7 %project_back.1 = (bf16[2,256,1024]{2,1,0:T(8,128)(2,1)S(1)}, bf16[2,256,1024]{2,1,0:T(8,128)(2,1)}) custom-call(s32[2]{0:T(128)S(1)} %pad_add_fusion.refs_0_.place_ref, bf16[1024,768]{1,0:T(8,128)(2,1)} %get-tuple-element.100.refs_2_.refs_1_, bf16[1024,768]{1,0:T(8,128)(2,1)} %get-tuple-element.108.refs_2_, bf16[2,512,128]{2,1,0:T(8,128)(2,1)S(1)} %get-tuple-element.153.refs_3_), custom_call_target="tpu_custom_call" | custom-call | flops 1610612736 | bytes 4194304 | tf_op jit(solution)/shard_map/project_back/pallas_call | solution.py:1076
  215.4 25.8 %collective-permute-done.36 = bf16[1,1024,128]{2,1,0:T(8,128)(2,1)S(1)} collective-permute-done((bf16[1,1024,128]{2,1,0:T(8,128)(2,1)S(1)}, bf16[1,1024,128]{2,1,0:T(8,128)(2,1)S(1)}, u32[]{:S(2)}, u32[]{:S(2)}) %collective-permute-start.36) | collective-permute-done | bytes 262176 | tf_op jit(solution)/shard_map/ppermute | solution.py:36
  241.6 4.5 %collective-permute-done.37 = bf16[2,1,192,128]{3,2,0,1:T(8,128)(2,1)S(1)} collective-permute-done((bf16[2,1,192,128]{3,2,0,1:T(8,128)(2,1)S(1)}, bf16[2,1,192,128]{3,2,0,1:T(8,128)(2,1)S(1)}, u32[]{:S(2)}, u32[]{:S(2)}) %collective-permute-start.37) | collective-permute-done | bytes 98336 | tf_op jit(solution)/shard_map/ppermute | solution.py:36
  246.2 2.7 collective-permute-done.47
  253.0 3.2 %collective-permute-done.55 = bf16[2,656,128]{2,1,0:T(8,128)(2,1)S(1)} collective-permute-done((bf16[2,656,128]{2,1,0:T(8,128)(2,1)S(1)}, bf16[2,656,128]{2,1,0:T(8,128)(2,1)S(1)}, u32[]{:S(2)}, u32[]{:S(2)}) %collective-permute-start.55) | collective-permute-done | bytes 335904 | tf_op jit(solution)/shard_map/ppermute | solution.py:36
  257.8 6.4 %collective-permute-done.39 = bf16[1,1024,128]{2,1,0:T(8,128)(2,1)S(1)} collective-permute-done((bf16[1,1024,128]{2,1,0:T(8,128)(2,1)S(1)}, bf16[1,1024,128]{2,1,0:T(8,128)(2,1)S(1)}, u32[]{:S(2)}, u32[]{:S(2)}) %collective-permute-start.39) | collective-permute-done | bytes 262176 | tf_op jit(solution)/shard_map/ppermute | solution.py:36
  264.3 4.4 %collective-permute-done.48 = bf16[2,640,128]{2,1,0:T(8,128)(2,1)S(1)} collective-permute-done((bf16[2,640,128]{2,1,0:T(8,128)(2,1)S(1)}, bf16[2,640,128]{2,1,0:T(8,128)(2,1)S(1)}, u32[]{:S(2)}, u32[]{:S(2)}) %collective-permute-start.48) | collective-permute-done | bytes 327712 | tf_op jit(solution)/shard_map/ppermute | solution.py:36
  274.2 5.7 %collective-permute-done.42 = bf16[2,512,128]{2,1,0:T(8,128)(2,1)S(1)} collective-permute-done((bf16[2,512,128]{2,1,0:T(8,128)(2,1)S(1)}, bf16[2,512,128]{2,1,0:T(8,128)(2,1)S(1)}, u32[]{:S(2)}, u32[]{:S(2)}) %collective-permute-start.42) | collective-permute-done | bytes 262176 | tf_op jit(solution)/shard_map/ppermute | solution.py:36
  293.4 2.4 rows_out.3
  295.9 2.9 input_grad.1
  298.8 6.8 %columns_out.3 = (f32[8,32,5248]{2,1,0:T(8,128)}, f32[8,32,1]{2,1,0:T(8,128)S(1)}) custom-call(s32[2]{0:T(128)S(1)} %pad_add_fusion.refs_0_.place_ref, f32[8,32,1]{2,1,0:T(8,128)S(1)} %copy-done.25, bf16[8,32,5248]{2,1,0:T(8,128)(2,1)S(1)} %bitcast.80, bf16[4,20,32,128]{3,2,1,0:T(8,128)(2,1)} %bitcast.48.refs_0_, bf16[4,20,32,128]{3,2,1,0:T(8,128)(2,1)} %bitcast.49.refs_1_, ...), custom_call_target="tpu_custom_call" | custom-call | tf_op jit(solution)/shard_map/columns_out/pallas_call | solution.py:764
  312.2 5.1 %columns_out.2 = (f32[8,32,3072]{2,1,0:T(8,128)}, f32[8,32,1]{2,1,0:T(8,128)S(1)}) custom-call(s32[2]{0:T(128)S(1)} %pad_add_fusion.refs_0_.place_ref, f32[8,32,1]{2,1,0:T(8,128)S(1)} %copy-done.24, bf16[8,32,3072]{2,1,0:T(8,128)(2,1)S(1)} %bitcast.81, bf16[4,16,32,128]{3,2,1,0:T(8,128)(2,1)} %bitcast.34.refs_0_, bf16[4,16,32,128]{3,2,1,0:T(8,128)(2,1)} %bitcast.35.refs_1_, ...), custom_call_target="tpu_custom_call" | custom-call | tf_op jit(solution)/shard_map/columns_out/pallas_call | solution.py:764
  (288 shorter events, 100.4 us)
Async XLA Ops:
  8.5 20.8 %collective-permute-start = (bf16[256,1024]{1,0:T(8,128)(2,1)}, bf16[256,1024]{1,0:T(8,128)(2,1)}, u32[]{:S(2)}, u32[]{:S(2)}) collective-permute-start(bf16[256,1024]{1,0:T(8,128)(2,1)} %tokens.1), channel_id=1, source_target_pairs={{0,2},{1,3},{2,0},{3,1},{4,6},{5,7},{6,4},{7,5},{8,10},{9,11},{10,... | collective-permute-start | bytes 1572872 | tf_op jit(solution)/shard_map/ppermute | solution.py:36
  30.9 20.4 %collective-permute-start.12 = (bf16[2,128,1536]{2,1,0:T(8,128)(2,1)S(1)}, bf16[2,128,1536]{2,1,0:T(8,128)(2,1)S(1)}, u32[]{:S(2)}, u32[]{:S(2)}) collective-permute-start(bf16[2,128,1536]{2,1,0:T(8,128)(2,1)S(1)} %dynamic-slice_bitcast_fusion), channel_id=1, source_target_pairs={{0,2},{1,3},{2,0},{3,1},{4,6},{5,7},{6,4},{7,5},{8,10},{9,11},{10,... | collective-permute-start | bytes 2359304 | tf_op jit(solution)/shard_map/ppermute | solution.py:36
  32.6 24.9 %collective-permute-start.9 = (bf16[128,1024]{1,0:T(8,128)(2,1)S(1)}, bf16[128,1024]{1,0:T(8,128)(2,1)S(1)}, u32[]{:S(2)}, u32[]{:S(2)}) collective-permute-start(bf16[128,1024]{1,0:T(8,128)(2,1)S(1)} %dynamic-slice_bitcast_fusion.2), channel_id=1, source_target_pairs={{0,2},{1,3},{2,0},{3,1},{4,6},{5,7},{6,4},{7,5},{8,10},{9,11},{10,... | collective-permute-start | bytes 786440 | tf_op jit(solution)/shard_map/ppermute | solution.py:36
  51.4 14.5 %collective-permute-start.14 = (bf16[2,64,1536]{2,1,0:T(8,128)(2,1)S(1)}, bf16[2,64,1536]{2,1,0:T(8,128)(2,1)S(1)}, u32[]{:S(2)}, u32[]{:S(2)}) collective-permute-start(bf16[2,64,1536]{2,1,0:T(8,128)(2,1)S(1)} %get-tuple-element.138), channel_id=1, source_target_pairs={{0,8},{4,12},{8,0},{12,4},{16,24},{20,28},{24,16},{28,20},{1,9},{5... | collective-permute-start | bytes 1179656 | tf_op jit(solution)/shard_map/ppermute | solution.py:36
  55.9 15.3 %collective-permute-start.7 = (bf16[1024,256]{1,0:T(8,128)(2,1)S(1)}, bf16[1024,256]{1,0:T(8,128)(2,1)S(1)}, u32[]{:S(2)}, u32[]{:S(2)}) collective-permute-start(bf16[1024,256]{1,0:T(8,128)(2,1)S(1)} %get-tuple-element.69.refs_4_.refs_5_), channel_id=1, source_target_pairs={{0,2},{1,3},{2,0},{3,1},{4,6},{5,7},{6,4},{7,5},{8,10},{9,11},{10,... | collective-permute-start | bytes 1572872 | tf_op jit(solution)/shard_map/ppermute | solution.py:36
  72.5 15.7 %collective-permute-start.16 = (bf16[256,1024]{1,0:T(8,128)(2,1)S(1)}, bf16[256,1024]{1,0:T(8,128)(2,1)S(1)}, u32[]{:S(2)}, u32[]{:S(2)}) collective-permute-start(bf16[256,1024]{1,0:T(8,128)(2,1)S(1)} %copy-done.29), channel_id=1, source_target_pairs={{0,2},{1,3},{2,0},{3,1},{4,6},{5,7},{6,4},{7,5},{8,10},{9,11},{10,... | collective-permute-start | bytes 1572872 | tf_op jit(solution)/shard_map/ppermute | solution.py:36
  74.0 14.5 %collective-permute-start.17 = (bf16[256,1024]{1,0:T(8,128)(2,1)S(1)}, bf16[256,1024]{1,0:T(8,128)(2,1)S(1)}, u32[]{:S(2)}, u32[]{:S(2)}) collective-permute-start(bf16[256,1024]{1,0:T(8,128)(2,1)S(1)} %copy-done.29), channel_id=1, source_target_pairs={{0,1},{1,0},{2,3},{3,2},{4,5},{5,4},{6,7},{7,6},{8,9},{9,8},{10,11... | collective-permute-start | bytes 1572872 | tf_op jit(solution)/shard_map/ppermute | solution.py:36
  107.4 14.1 %collective-permute-start.20 = (bf16[256,1024]{1,0:T(8,128)(2,1)S(1)}, bf16[256,1024]{1,0:T(8,128)(2,1)S(1)}, u32[]{:S(2)}, u32[]{:S(2)}) collective-permute-start(bf16[256,1024]{1,0:T(8,128)(2,1)S(1)} %get-tuple-element.82.refs_3_), channel_id=1, source_target_pairs={{0,2},{1,3},{2,0},{3,1},{4,6},{5,7},{6,4},{7,5},{8,10},{9,11},{10,... | collective-permute-start | bytes 1572872 | tf_op jit(solution)/shard_map/ppermute | solution.py:36
  116.4 29.7 %collective-permute-start.25 = (bf16[4,768,128]{2,1,0:T(8,128)(2,1)}, bf16[4,768,128]{2,1,0:T(8,128)(2,1)S(1)}, u32[]{:S(2)}, u32[]{:S(2)}) collective-permute-start(bf16[4,768,128]{2,1,0:T(8,128)(2,1)} %bitcast.111), channel_id=1, source_target_pairs={{0,8},{4,12},{8,0},{12,4},{16,24},{20,28},{24,16},{28,20},{1,9},{5... | collective-permute-start | bytes 2359304 | tf_op jit(solution)/shard_map/ppermute | solution.py:36
  117.2 29.0 %collective-permute-start.24 = (bf16[4,640,128]{2,1,0:T(8,128)(2,1)S(1)}, bf16[4,640,128]{2,1,0:T(8,128)(2,1)S(1)}, u32[]{:S(2)}, u32[]{:S(2)}) collective-permute-start(bf16[4,640,128]{2,1,0:T(8,128)(2,1)S(1)} %bitcast.89), channel_id=1, source_target_pairs={{0,4},{4,0},{8,12},{12,8},{16,20},{20,16},{24,28},{28,24},{1,5},{5... | collective-permute-start | bytes 1966088 | tf_op jit(solution)/shard_map/ppermute | solution.py:36
  123.2 19.6 %collective-permute-start.22 = (bf16[256,1024]{1,0:T(8,128)(2,1)S(1)}, bf16[256,1024]{1,0:T(8,128)(2,1)S(1)}, u32[]{:S(2)}, u32[]{:S(2)}) collective-permute-start(bf16[256,1024]{1,0:T(8,128)(2,1)S(1)} %get-tuple-element.87.refs_7_.refs_1_), channel_id=1, source_target_pairs={{0,2},{1,3},{2,0},{3,1},{4,6},{5,7},{6,4},{7,5},{8,10},{9,11},{10,... | collective-permute-start | bytes 1572872 | tf_op jit(solution)/shard_map/ppermute | solution.py:36
  144.3 18.2 %collective-permute-start.33 = (bf16[4,656,128]{2,1,0:T(8,128)(2,1)}, bf16[4,656,128]{2,1,0:T(8,128)(2,1)S(1)}, u32[]{:S(2)}, u32[]{:S(2)}) collective-permute-start(bf16[4,656,128]{2,1,0:T(8,128)(2,1)} %get-tuple-element.119), channel_id=1, source_target_pairs={{0,4},{4,0},{8,12},{12,8},{16,20},{20,16},{24,28},{28,24},{1,5},{5... | collective-permute-start | bytes 2015240 | tf_op jit(solution)/shard_map/ppermute | solution.py:36
  145.9 24.6 %collective-permute-start.21 = (bf16[2,256,1024]{2,1,0:T(8,128)(2,1)}, bf16[2,256,1024]{2,1,0:T(8,128)(2,1)S(1)}, u32[]{:S(2)}, u32[]{:S(2)}) collective-permute-start(bf16[2,256,1024]{2,1,0:T(8,128)(2,1)} %get-tuple-element.89), channel_id=1, source_target_pairs={{0,1},{1,0},{2,3},{3,2},{4,5},{5,4},{6,7},{7,6},{8,9},{9,8},{10,11... | collective-permute-start | bytes 3145736 | tf_op jit(solution)/shard_map/ppermute | solution.py:36
  146.4 24.1 %collective-permute-start.28 = (bf16[2,768,128]{2,1,0:T(8,128)(2,1)S(1)}, bf16[2,768,128]{2,1,0:T(8,128)(2,1)S(1)}, u32[]{:S(2)}, u32[]{:S(2)}) collective-permute-start(bf16[2,768,128]{2,1,0:T(8,128)(2,1)S(1)} %get-tuple-element.135.refs_14_), channel_id=1, source_target_pairs={{0,4},{4,0},{8,12},{12,8},{16,20},{20,16},{24,28},{28,24},{1,5},{5... | collective-permute-start | bytes 1179656 | tf_op jit(solution)/shard_map/ppermute | solution.py:36
  147.2 23.3 %collective-permute-start.27 = (bf16[2,640,128]{2,1,0:T(8,128)(2,1)S(1)}, bf16[2,640,128]{2,1,0:T(8,128)(2,1)S(1)}, u32[]{:S(2)}, u32[]{:S(2)}) collective-permute-start(bf16[2,640,128]{2,1,0:T(8,128)(2,1)S(1)} %get-tuple-element.143.refs_13_), channel_id=1, source_target_pairs={{0,8},{4,12},{8,0},{12,4},{16,24},{20,28},{24,16},{28,20},{1,9},{5... | collective-permute-start | bytes 983048 | tf_op jit(solution)/shard_map/ppermute | solution.py:36
  162.6 35.5 %collective-permute-start.52 = (bf16[2,656,128]{2,1,0:T(8,128)(2,1)S(1)}, bf16[2,656,128]{2,1,0:T(8,128)(2,1)S(1)}, u32[]{:S(2)}, u32[]{:S(2)}) collective-permute-start(bf16[2,656,128]{2,1,0:T(8,128)(2,1)S(1)} %get-tuple-element.129), channel_id=1, source_target_pairs={{0,8},{4,12},{8,0},{12,4},{16,24},{20,28},{24,16},{28,20},{1,9},{5... | collective-permute-start | bytes 1007624 | tf_op jit(solution)/shard_map/ppermute | solution.py:36
  176.7 21.1 %collective-permute-start.29 = (bf16[4,512,128]{2,1,0:T(8,128)(2,1)S(1)}, bf16[4,512,128]{2,1,0:T(8,128)(2,1)S(1)}, u32[]{:S(2)}, u32[]{:S(2)}) collective-permute-start(bf16[4,512,128]{2,1,0:T(8,128)(2,1)S(1)} %bitcast.90), channel_id=1, source_target_pairs={{0,4},{4,0},{8,12},{12,8},{16,20},{20,16},{24,28},{28,24},{1,5},{5... | collective-permute-start | bytes 1572872 | tf_op jit(solution)/shard_map/ppermute | solution.py:36
  178.3 18.5 %collective-permute-start.44 = (bf16[1,1408,128]{2,1,0:T(8,128)(2,1)S(1)}, bf16[1,1408,128]{2,1,0:T(8,128)(2,1)S(1)}, u32[]{:S(2)}, u32[]{:S(2)}) collective-permute-start(bf16[1,1408,128]{2,1,0:T(8,128)(2,1)S(1)} %pad_maximum_fusion.12), channel_id=1, source_target_pairs={{0,16},{4,20},{8,24},{12,28},{16,0},{20,4},{24,8},{28,12},{1,17},{... | collective-permute-start | bytes 1081352 | tf_op jit(solution)/shard_map/ppermute | solution.py:36
  178.4 26.8 %collective-permute-start.34 = (bf16[4,512,128]{2,1,0:T(8,128)(2,1)S(1)}, bf16[4,512,128]{2,1,0:T(8,128)(2,1)S(1)}, u32[]{:S(2)}, u32[]{:S(2)}) collective-permute-start(bf16[4,512,128]{2,1,0:T(8,128)(2,1)S(1)} %pad_maximum_fusion.9), channel_id=1, source_target_pairs={{0,8},{4,12},{8,0},{12,4},{16,24},{20,28},{24,16},{28,20},{1,9},{5... | collective-permute-start | bytes 1572872 | tf_op jit(solution)/shard_map/ppermute | solution.py:36
  210.6 59.6 %collective-permute-start.30 = (bf16[2,256,1024]{2,1,0:T(8,128)(2,1)}, bf16[2,256,1024]{2,1,0:T(8,128)(2,1)S(1)}, u32[]{:S(2)}, u32[]{:S(2)}) collective-permute-start(bf16[2,256,1024]{2,1,0:T(8,128)(2,1)} %get-tuple-element.111), channel_id=1, source_target_pairs={{0,1},{1,0},{2,3},{3,2},{4,5},{5,4},{6,7},{7,6},{8,9},{9,8},{10,11... | collective-permute-start | bytes 3145736 | tf_op jit(solution)/shard_map/ppermute | solution.py:36
  211.3 30.1 %collective-permute-start.54 = (bf16[1,656,128]{2,1,0:T(8,128)(2,1)S(1)}, bf16[1,656,128]{2,1,0:T(8,128)(2,1)S(1)}, u32[]{:S(2)}, u32[]{:S(2)}) collective-permute-start(bf16[1,656,128]{2,1,0:T(8,128)(2,1)S(1)} %bitcast.93), channel_id=1, source_target_pairs={{0,16},{4,20},{8,24},{12,28},{16,0},{20,4},{24,8},{28,12},{1,17},{... | collective-permute-start | bytes 503816 | tf_op jit(solution)/shard_map/ppermute | solution.py:36
  212.3 29.0 %collective-permute-start.36 = (bf16[1,1024,128]{2,1,0:T(8,128)(2,1)S(1)}, bf16[1,1024,128]{2,1,0:T(8,128)(2,1)S(1)}, u32[]{:S(2)}, u32[]{:S(2)}) collective-permute-start(bf16[1,1024,128]{2,1,0:T(8,128)(2,1)S(1)} %pad_maximum_fusion.17), channel_id=1, source_target_pairs={{0,16},{4,20},{8,24},{12,28},{16,0},{20,4},{24,8},{28,12},{1,17},{... | collective-permute-start | bytes 786440 | tf_op jit(solution)/shard_map/ppermute | solution.py:36
  214.7 34.2 %collective-permute-start.47 = (bf16[1,1408,128]{2,1,0:T(8,128)(2,1)S(1)}, bf16[1,1408,128]{2,1,0:T(8,128)(2,1)S(1)}, u32[]{:S(2)}, u32[]{:S(2)}) collective-permute-start(bf16[1,1408,128]{2,1,0:T(8,128)(2,1)S(1)} %maximum_bitcast_fusion.1), channel_id=1, source_target_pairs={{0,16},{4,20},{8,24},{12,28},{16,0},{20,4},{24,8},{28,12},{1,17},{... | collective-permute-start | bytes 1081352 | tf_op jit(solution)/shard_map/ppermute | solution.py:36
  241.5 14.7 %collective-permute-start.55 = (bf16[2,656,128]{2,1,0:T(8,128)(2,1)S(1)}, bf16[2,656,128]{2,1,0:T(8,128)(2,1)S(1)}, u32[]{:S(2)}, u32[]{:S(2)}) collective-permute-start(bf16[2,656,128]{2,1,0:T(8,128)(2,1)S(1)} %pad_maximum_fusion.13), channel_id=1, source_target_pairs={{0,8},{4,12},{8,0},{12,4},{16,24},{20,28},{24,16},{28,20},{1,9},{5... | collective-permute-start | bytes 1007624 | tf_op jit(solution)/shard_map/ppermute | solution.py:36
  248.9 21.2 %collective-permute-start.50 = (bf16[2,768,128]{2,1,0:T(8,128)(2,1)S(1)}, bf16[2,768,128]{2,1,0:T(8,128)(2,1)S(1)}, u32[]{:S(2)}, u32[]{:S(2)}) collective-permute-start(bf16[2,768,128]{2,1,0:T(8,128)(2,1)S(1)} %pad_maximum_fusion.11), channel_id=1, source_target_pairs={{0,4},{4,0},{8,12},{12,8},{16,20},{20,16},{24,28},{28,24},{1,5},{5... | collective-permute-start | bytes 1179656 | tf_op jit(solution)/shard_map/ppermute | solution.py:36
  250.7 17.9 %collective-permute-start.48 = (bf16[2,640,128]{2,1,0:T(8,128)(2,1)S(1)}, bf16[2,640,128]{2,1,0:T(8,128)(2,1)S(1)}, u32[]{:S(2)}, u32[]{:S(2)}) collective-permute-start(bf16[2,640,128]{2,1,0:T(8,128)(2,1)S(1)} %pad_maximum_fusion.14), channel_id=1, source_target_pairs={{0,8},{4,12},{8,0},{12,4},{16,24},{20,28},{24,16},{28,20},{1,9},{5... | collective-permute-start | bytes 983048 | tf_op jit(solution)/shard_map/ppermute | solution.py:36
  256.3 27.6 %collective-permute-start.56 = (bf16[4,656,128]{2,1,0:T(8,128)(2,1)S(1)}, bf16[4,656,128]{2,1,0:T(8,128)(2,1)S(1)}, u32[]{:S(2)}, u32[]{:S(2)}) collective-permute-start(bf16[4,656,128]{2,1,0:T(8,128)(2,1)S(1)} %pad_maximum_fusion.6.refs_0_), channel_id=1, source_target_pairs={{0,4},{4,0},{8,12},{12,8},{16,20},{20,16},{24,28},{28,24},{1,5},{5... | collective-permute-start | bytes 2015240 | tf_op jit(solution)/shard_map/ppermute | solution.py:36
  264.2 18.9 %collective-permute-start.26 = (bf16[256,1024]{1,0:T(8,128)(2,1)S(1)}, bf16[256,1024]{1,0:T(8,128)(2,1)S(1)}, u32[]{:S(2)}, u32[]{:S(2)}) collective-permute-start(bf16[256,1024]{1,0:T(8,128)(2,1)S(1)} %copy-done.32), channel_id=1, source_target_pairs={{0,2},{1,3},{2,0},{3,1},{4,6},{5,7},{6,4},{7,5},{8,10},{9,11},{10,... | collective-permute-start | bytes 1572872 | tf_op jit(solution)/shard_map/ppermute | solution.py:36
  270.2 28.5 %collective-permute-start.51 = (bf16[4,768,128]{2,1,0:T(8,128)(2,1)S(1)}, bf16[4,768,128]{2,1,0:T(8,128)(2,1)}, u32[]{:S(2)}, u32[]{:S(2)}) collective-permute-start(bf16[4,768,128]{2,1,0:T(8,128)(2,1)S(1)} %pad_maximum_fusion.5), channel_id=1, source_target_pairs={{0,8},{4,12},{8,0},{12,4},{16,24},{20,28},{24,16},{28,20},{1,9},{5... | collective-permute-start | bytes 2359304 | tf_op jit(solution)/shard_map/ppermute | solution.py:36
  279.9 18.9 %collective-permute-start.49 = (bf16[4,640,128]{2,1,0:T(8,128)(2,1)}, bf16[4,640,128]{2,1,0:T(8,128)(2,1)}, u32[]{:S(2)}, u32[]{:S(2)}) collective-permute-start(bf16[4,640,128]{2,1,0:T(8,128)(2,1)} %pad_maximum_fusion.7), channel_id=1, source_target_pairs={{0,4},{4,0},{8,12},{12,8},{16,20},{20,16},{24,28},{28,24},{1,5},{5... | collective-permute-start | bytes 1966088 | tf_op jit(solution)/shard_map/ppermute | solution.py:36
  283.9 24.1 %collective-permute-start.43 = (bf16[4,512,128]{2,1,0:T(8,128)(2,1)}, bf16[4,512,128]{2,1,0:T(8,128)(2,1)}, u32[]{:S(2)}, u32[]{:S(2)}) collective-permute-start(bf16[4,512,128]{2,1,0:T(8,128)(2,1)} %pad_maximum_fusion.8.refs_0_), channel_id=1, source_target_pairs={{0,8},{4,12},{8,0},{12,4},{16,24},{20,28},{24,16},{28,20},{1,9},{5... | collective-permute-start | bytes 1572872 | tf_op jit(solution)/shard_map/ppermute | solution.py:36
  284.7 24.2 %collective-permute-start.41 = (bf16[4,512,128]{2,1,0:T(8,128)(2,1)}, bf16[4,512,128]{2,1,0:T(8,128)(2,1)}, u32[]{:S(2)}, u32[]{:S(2)}) collective-permute-start(bf16[4,512,128]{2,1,0:T(8,128)(2,1)} %pad_maximum_fusion.10), channel_id=1, source_target_pairs={{0,4},{4,0},{8,12},{12,8},{16,20},{20,16},{24,28},{28,24},{1,5},{5... | collective-permute-start | bytes 1572872 | tf_op jit(solution)/shard_map/ppermute | solution.py:36
  (77 other events, 468.2 us)

commit v9 on v8

--- a/solution.py
+++ b/solution.py
@@ -1049,14 +1049,14 @@
     qkv_counts = [qkv_tiles - qkv_tiles // 3, qkv_tiles // 3]
     in_reduce.step(1, [dqkv])
     qkv_flows = pl.pallas_call(
-        ordered(functools.partial(qkv_kernel, n, qkv_counts, orders), 3, 3),
-        in_specs=[SMEM_SPEC] + [VMEM_SPEC] * 2 + [ANY_SPEC] * 3,
+        ordered(functools.partial(qkv_kernel, n, qkv_counts, orders), 3, 1),
+        in_specs=[SMEM_SPEC] + [VMEM_SPEC] * 2 + [ANY_SPEC],
         out_shape=[shape((slots, n * c, chunk, LANES), BF16) for c in qkv_counts for _ in range(2)],
         scratch_shapes=[pltpu.VMEM((part, 3 * width), F32)],
         compiler_params=params,
         cost_estimate=work(12 * seq * model * width),
         name="qkv_gradient",
-    )(place, normed1, dqkv, in_reduce.p[1], in_reduce.q[1], mlp_other)
+    )(place, normed1, dqkv, mlp_other)
     qkv_flows = [flow_rows(a) for a in qkv_flows]
     split = qkv_flows[2].shape[1]
     down_first = add_halves(down_keep, after(swap(down_send, "rep", near[0]), dqkv))

time: 325 us -> 319 us (0.982)
  waiting for transfers between devices: 109 us -> 96.8 us
  starting transfers between devices: 54.2 us -> 60.5 us
    ppermute x57, waiting for transfers between devices: 109 us -> 96.8 us  [swap(): return lax.ppermute(x, axis, [(i, i ^ 1 << bit) for i in range(size)])]
    ppermute x57, starting transfers between devices: 54.2 us -> 60.5 us  [swap(): return lax.ppermute(x, axis, [(i, i ^ 1 << bit) for i in range(size)])]
  transfers between devices with their start and end apart: 57 -> 57, of which waited for: 21 -> 20; matrix products, arithmetic and copies ran while one was open for 7% -> 7% of each run, Pallas kernels for 27% -> 28%
where the time goes in v9:
time: 319 us; the launch traced here: 314 us
  Pallas kernels  108 us (34%)
  waiting for transfers between devices  96.8 us (30%)
  starting transfers between devices  60.5 us (19%)
  local copies, waits for them, and re-layouts  32.4 us (10%)
  other arithmetic  14.6 us (5%)
    ppermute x57, waiting for transfers between devices, swap(): return lax.ppermute(x, axis, [(i, i ^ 1 << bit) for i in range(size)])  96.8 us
    ppermute x57, starting transfers between devices, swap(): return lax.ppermute(x, axis, [(i, i ^ 1 << bit) for i in range(size)])  60.5 us
    unnamed x104, local copies, waits for them, and re-layouts  22 us
    pallas_call x1, Pallas kernels, shards(): pl.pallas_call(ordered(functools.partial(down_kernel, held_of(cots), n, f...  18.1 us
    pallas_call x1, Pallas kernels, shards(): pl.pallas_call(ordered(functools.partial(attention_back_kernel, held_of(d...  13.2 us
    pallas_call x1, Pallas kernels, shards(): pl.pallas_call(ordered(functools.partial(attention_kernel, held_of(toks),...  12.4 us
    pallas_call x1, Pallas kernels, shards(): pl.pallas_call(functools.partial(dup_kernel, held_of(cots), n), in_specs=...  12 us
    pallas_call x2, Pallas kernels, columns_out(): pl.pallas_call(functools.partial(columns_out_kernel, n, ff, head_cols, wi...  12 us
  transfers between devices with their start and end apart: 57, of which 20 were waited for; matrix products, arithmetic and copies ran while one was open for 7% of the time, Pallas kernels for 28%

profile of v9, /device:TPU:0, one launch (start us, length us, event | category | flops | bytes accessed | tf_op | source)
XLA Modules:
  0.0 314.4 jit_solution(15391447326045962326)
XLA Ops:
  5.5 2.9 collective-permute-start.3
  11.7 4.8 %sine_multiply_fusion = (f32[1024,256]{1,0:T(8,128)}, f32[1024,256]{1,0:T(8,128)}) fusion(f32[256]{0:T(256)S(1)} %get-tuple-element.170, f32[256]{0:T(256)S(1)} %get-tuple-element.171), kind=kLoop, calls=%fused_computation.4 | loop fusion | flops 524288 | bytes 2099200 | tf_op jit(solution)/shard_map/mul | solution.py:881
  24.5 3.1 collective-permute-done.4.refs_11_
  34.1 12.4 %attention.1 = (bf16[1024,256]{1,0:T(8,128)(2,1)S(1)}, bf16[1152,256]{1,0:T(8,128)(2,1)}, bf16[1152,256]{1,0:T(8,128)(2,1)}, bf16[1024,256]{1,0:T(8,128)(2,1)S(1...) custom-call(s32[2]{0:T(128)S(1)} %pad_add_fusion.refs_0_.place_ref, ...), custom_call_target="tpu_custom_call" | custom-call | flops 10737418240 | bytes 4194304 | tf_op jit(solution)/shard_map/attention/pallas_call | solution.py:889
  46.5 4.8 %collective-permute-done.12.refs_12_ = bf16[2,128,1536]{2,1,0:T(8,128)(2,1)S(1)} collective-permute-done((bf16[2,128,1536]{2,1,0:T(8,128)(2,1)S(1)}, bf16[2,128,1536]{2,1,0:T(8,128)(2,1)S(1)}, u32[]{:S(2)}, u32[]{:S(2)}) %collective-permute-start.12) | collective-permute-done | bytes 786464 | tf_op jit(solution)/shard_map/ppermute | solution.py:36
  57.4 2.6 collective-permute-start.10
  60.0 5.8 %collective-permute-done.14.refs_14_ = bf16[2,64,1536]{2,1,0:T(8,128)(2,1)S(1)} collective-permute-done((bf16[2,64,1536]{2,1,0:T(8,128)(2,1)S(1)}, bf16[2,64,1536]{2,1,0:T(8,128)(2,1)S(1)}, u32[]{:S(2)}, u32[]{:S(2)}) %collective-permute-start.14) | collective-permute-done | bytes 393248 | tf_op jit(solution)/shard_map/ppermute | solution.py:36
  66.2 4.9 %collective-permute-done.10.refs_9_ = bf16[128,1024]{1,0:T(8,128)(2,1)S(1)} collective-permute-done((bf16[128,1024]{1,0:T(8,128)(2,1)S(1)}, bf16[128,1024]{1,0:T(8,128)(2,1)S(1)}, u32[]{:S(2)}, u32[]{:S(2)}) %collective-permute-start.10) | collective-permute-done | bytes 262176 | tf_op jit(solution)/shard_map/ppermute | solution.py:36
  76.3 11.9 %up_projection.1 = (f32[256,1024]{1,0:T(8,128)}, bf16[1024,1024]{1,0:T(8,128)(2,1)}, f32[1024,1536]{1,0:T(8,128)}, bf16[1024,1536]{1,0:T(8,128)(2,1)}) custom-call(s32[2]{0:T(128)S(1)} %pad_add_fusion.refs_0_.place_ref, bf16[256,1024]{1,0:T(8,128)(2,1)} %tokens.1, bf16[256,1024]{1,0:T(8,128)(2,1)} %collective-permute-done.refs_6_.refs_1_, ...), custom_call_target="tpu_custom_call" | custom-call | flops 9663676416 | bytes 4194304 | tf_op jit(solution)/shard_map/up_projection/pallas_call | solution.py:916
  91.0 12.0 %dup.1 = (bf16[1024,768]{1,0:T(8,128)(2,1)}, bf16[1024,1536]{1,0:T(8,128)(2,1)}, bf16[2,256,1024]{2,1,0:T(8,128)(2,1)}, bf16[2,256,1024]{2,1,0:T(8,128)(2,1)}) custom-call(f32[1024,1536]{1,0:T(8,128)} %get-tuple-element.74.up_ref, bf16[1024,1536]{1,0:T(8,128)(2,1)} %get-tuple-element.75.w_in_ref, bf16[656,1024]{1,0:T(8,128)(2,1)} %refs_2_.1, ...), custom_call_target="tpu_custom_call" | custom-call | flops 11274289152 | bytes 4194304 | tf_op jit(solution)/shard_map/dup/pallas_call | solution.py:948
  103.3 2.7 collective-permute-done.19.got_ref
  109.0 7.4 %in_gradient.1 = (bf16[4,20,32,128]{3,2,1,0:T(8,128)(2,1)S(1)}, bf16[4,20,32,128]{3,2,1,0:T(8,128)(2,1)S(1)}, bf16[4,24,32,128]{3,2,1,0:T(8,128)(2,1)}, bf16[4,24,32,128]{3,2,1,0:T(8,128)(2,1)}) custom-call(s32[2]{0:T(128)S(1)} %pad_add_fusion.refs_0_.place_ref, bf16[1024,1024]{1,0:T(8,128)(2,1)} %get-tuple-element.84.refs_1_, ...), custom_call_target="tpu_custom_call" | custom-call | flops 6442450944 | bytes 4194304 | tf_op jit(solution)/shard_map/in_gradient/pallas_call | solution.py:986
  118.7 2.8 collective-permute-done.20.refs_1_
  124.6 18.1 %down_gradient.1 = (bf16[4,656,128]{2,1,0:T(8,128)(2,1)}, bf16[4,656,128]{2,1,0:T(8,128)(2,1)}, bf16[2,256,1024]{2,1,0:T(8,128)(2,1)}, bf16[2,256,1024]{2,1,0:T(8,128)(2,1)}) custom-call(s32[2]{0:T(128)S(1)} %pad_add_fusion.refs_0_.place_ref, bf16[1024,768]{1,0:T(8,128)(2,1)} %get-tuple-element.78.refs_1_, bf16[656,1024]{1,0:T(8,128)(2,1)} %refs_2_.1, ...), custom_call_target="tpu_custom_call" | custom-call | flops 6442450944 | bytes 4194304 | tf_op jit(solution)/shard_map/down_gradient/pallas_call | solution.py:1004
  149.1 13.2 %attention_back.1 = (bf16[1024,768]{1,0:T(8,128)(2,1)}, bf16[4,256,128]{2,1,0:T(8,128)(2,1)S(1)}, bf16[4,256,128]{2,1,0:T(8,128)(2,1)S(1)}) custom-call(s32[2]{0:T(128)S(1)} %pad_add_fusion.refs_0_.place_ref, bf16[256,1024]{1,0:T(8,128)(2,1)S(1)} %copy-done.28, bf16[256,1024]{1,0:T(8,128)(2,1)} %copy-done.42, bf16[512,1024]{1,0:T(8,128)(2,1)} %copy-done.47, ...), custom_call_target="tpu_custom_call" | custom-call | flops 10737418240 | bytes 4194304 | tf_op jit(solution)/shard_map/attention_back/pallas_call | solution.py:1017
  165.7 4.0 %qkv_gradient.1 = (bf16[4,16,32,128]{3,2,1,0:T(8,128)(2,1)S(1)}, bf16[4,16,32,128]{3,2,1,0:T(8,128)(2,1)S(1)}, bf16[4,8,32,128]{3,2,1,0:T(8,128)(2,1)S(1)}, bf16[4,8,32,128]{3,2,1,0:T(8,128)(2,1)S(1)}) custom-call(s32[2]{0:T(128)S(1)} %pad_add_fusion.refs_0_.place_ref, bf16[1024,1024]{1,0:T(8,128)(2,1)} %get-tuple-element.104.refs_1_, ...), custom_call_target="tpu_custom_call" | custom-call | flops 3221225472 | bytes 4194304 | tf_op jit(solution)/shard_map/qkv_gradient/pallas_call | solution.py:1051
  171.6 3.2 %collective-permute-start.44 = (bf16[1,1408,128]{2,1,0:T(8,128)(2,1)S(1)}, bf16[1,1408,128]{2,1,0:T(8,128)(2,1)S(1)}, u32[]{:S(2)}, u32[]{:S(2)}) collective-permute-start(bf16[1,1408,128]{2,1,0:T(8,128)(2,1)S(1)} %pad_maximum_fusion.12), channel_id=1, source_target_pairs={{0,16},{4,20},{8,24},{12,28},{16,0},{20,4},{24,8},{28,12},{1,17},{... | collective-permute-start | bytes 1081352 | tf_op jit(solution)/shard_map/ppermute | solution.py:36
  176.0 14.6 %collective-permute-done.44 = bf16[1,1408,128]{2,1,0:T(8,128)(2,1)S(1)} collective-permute-done((bf16[1,1408,128]{2,1,0:T(8,128)(2,1)S(1)}, bf16[1,1408,128]{2,1,0:T(8,128)(2,1)S(1)}, u32[]{:S(2)}, u32[]{:S(2)}) %collective-permute-start.44) | collective-permute-done | bytes 360480 | tf_op jit(solution)/shard_map/ppermute | solution.py:36
  192.0 3.5 %collective-permute-start.53 = (bf16[1,656,128]{2,1,0:T(8,128)(2,1)S(1)}, bf16[1,656,128]{2,1,0:T(8,128)(2,1)S(1)}, u32[]{:S(2)}, u32[]{:S(2)}) collective-permute-start(bf16[1,656,128]{2,1,0:T(8,128)(2,1)S(1)} %add_convert_fusion.9), channel_id=1, source_target_pairs={{0,16},{4,20},{8,24},{12,28},{16,0},{20,4},{24,8},{28,12},{1,17},{... | collective-permute-start | bytes 503816 | tf_op jit(solution)/shard_map/ppermute | solution.py:36
  195.5 4.6 %collective-permute-done.32 = bf16[4,512,128]{2,1,0:T(8,128)(2,1)S(1)} collective-permute-done((bf16[4,512,128]{2,1,0:T(8,128)(2,1)S(1)}, bf16[4,512,128]{2,1,0:T(8,128)(2,1)S(1)}, u32[]{:S(2)}, u32[]{:S(2)}) %collective-permute-start.32) | collective-permute-done | bytes 524320 | tf_op jit(solution)/shard_map/ppermute | solution.py:36
  200.3 4.7 %project_back.1 = (bf16[2,256,1024]{2,1,0:T(8,128)(2,1)S(1)}, bf16[2,256,1024]{2,1,0:T(8,128)(2,1)}) custom-call(s32[2]{0:T(128)S(1)} %pad_add_fusion.refs_0_.place_ref, bf16[1024,768]{1,0:T(8,128)(2,1)} %get-tuple-element.100.refs_2_.refs_1_, bf16[1024,768]{1,0:T(8,128)(2,1)} %get-tuple-element.106.refs_2_, bf16[2,512,128]{2,1,0:T(8,128)(2,1)S(1)} %get-tuple-element.153.refs_3_), custom_call_target="tpu_custom_call" | custom-call | flops 1610612736 | bytes 4194304 | tf_op jit(solution)/shard_map/project_back/pallas_call | solution.py:1076
  209.9 24.6 %collective-permute-done.34 = bf16[1,1024,128]{2,1,0:T(8,128)(2,1)S(1)} collective-permute-done((bf16[1,1024,128]{2,1,0:T(8,128)(2,1)S(1)}, bf16[1,1024,128]{2,1,0:T(8,128)(2,1)S(1)}, u32[]{:S(2)}, u32[]{:S(2)}) %collective-permute-start.34) | collective-permute-done | bytes 262176 | tf_op jit(solution)/shard_map/ppermute | solution.py:36
  234.8 4.5 %collective-permute-done.35 = bf16[2,1,192,128]{3,2,0,1:T(8,128)(2,1)S(1)} collective-permute-done((bf16[2,1,192,128]{3,2,0,1:T(8,128)(2,1)S(1)}, bf16[2,1,192,128]{3,2,0,1:T(8,128)(2,1)S(1)}, u32[]{:S(2)}, u32[]{:S(2)}) %collective-permute-start.35) | collective-permute-done | bytes 98336 | tf_op jit(solution)/shard_map/ppermute | solution.py:36
  239.4 2.8 collective-permute-done.47
  245.4 4.4 %collective-permute-done.55 = bf16[2,656,128]{2,1,0:T(8,128)(2,1)S(1)} collective-permute-done((bf16[2,656,128]{2,1,0:T(8,128)(2,1)S(1)}, bf16[2,656,128]{2,1,0:T(8,128)(2,1)S(1)}, u32[]{:S(2)}, u32[]{:S(2)}) %collective-permute-start.55) | collective-permute-done | bytes 335904 | tf_op jit(solution)/shard_map/ppermute | solution.py:36
  249.9 7.3 %collective-permute-start.56 = (bf16[4,656,128]{2,1,0:T(8,128)(2,1)S(1)}, bf16[4,656,128]{2,1,0:T(8,128)(2,1)S(1)}, u32[]{:S(2)}, u32[]{:S(2)}) collective-permute-start(bf16[4,656,128]{2,1,0:T(8,128)(2,1)S(1)} %pad_maximum_fusion.6.refs_0_), channel_id=1, source_target_pairs={{0,4},{4,0},{8,12},{12,8},{16,20},{20,16},{24,28},{28,24},{1,5},{5... | collective-permute-start | bytes 2015240 | tf_op jit(solution)/shard_map/ppermute | solution.py:36
  257.2 4.7 %collective-permute-done.48 = bf16[2,640,128]{2,1,0:T(8,128)(2,1)S(1)} collective-permute-done((bf16[2,640,128]{2,1,0:T(8,128)(2,1)S(1)}, bf16[2,640,128]{2,1,0:T(8,128)(2,1)S(1)}, u32[]{:S(2)}, u32[]{:S(2)}) %collective-permute-start.48) | collective-permute-done | bytes 327712 | tf_op jit(solution)/shard_map/ppermute | solution.py:36
  268.0 5.7 %collective-permute-done.40 = bf16[2,512,128]{2,1,0:T(8,128)(2,1)S(1)} collective-permute-done((bf16[2,512,128]{2,1,0:T(8,128)(2,1)S(1)}, bf16[2,512,128]{2,1,0:T(8,128)(2,1)S(1)}, u32[]{:S(2)}, u32[]{:S(2)}) %collective-permute-start.40) | collective-permute-done | bytes 262176 | tf_op jit(solution)/shard_map/ppermute | solution.py:36
  287.2 2.4 rows_out.3
  289.6 2.9 input_grad.1
  292.5 6.8 %columns_out.3 = (f32[8,32,5248]{2,1,0:T(8,128)}, f32[8,32,1]{2,1,0:T(8,128)S(1)}) custom-call(s32[2]{0:T(128)S(1)} %pad_add_fusion.refs_0_.place_ref, f32[8,32,1]{2,1,0:T(8,128)S(1)} %copy-done.25, bf16[8,32,5248]{2,1,0:T(8,128)(2,1)S(1)} %bitcast.80, bf16[4,20,32,128]{3,2,1,0:T(8,128)(2,1)} %bitcast.48.refs_0_, bf16[4,20,32,128]{3,2,1,0:T(8,128)(2,1)} %bitcast.49.refs_1_, ...), custom_call_target="tpu_custom_call" | custom-call | tf_op jit(solution)/shard_map/columns_out/pallas_call | solution.py:764
  306.0 5.1 %columns_out.2 = (f32[8,32,3072]{2,1,0:T(8,128)}, f32[8,32,1]{2,1,0:T(8,128)S(1)}) custom-call(s32[2]{0:T(128)S(1)} %pad_add_fusion.refs_0_.place_ref, f32[8,32,1]{2,1,0:T(8,128)S(1)} %copy-done.24, bf16[8,32,3072]{2,1,0:T(8,128)(2,1)S(1)} %bitcast.81, bf16[4,16,32,128]{3,2,1,0:T(8,128)(2,1)} %bitcast.32.refs_0_, bf16[4,16,32,128]{3,2,1,0:T(8,128)(2,1)} %bitcast.33.refs_1_, ...), custom_call_target="tpu_custom_call" | custom-call | tf_op jit(solution)/shard_map/columns_out/pallas_call | solution.py:764
  (288 shorter events, 97.5 us)
Async XLA Ops:
  8.5 20.8 %collective-permute-start = (bf16[256,1024]{1,0:T(8,128)(2,1)}, bf16[256,1024]{1,0:T(8,128)(2,1)}, u32[]{:S(2)}, u32[]{:S(2)}) collective-permute-start(bf16[256,1024]{1,0:T(8,128)(2,1)} %tokens.1), channel_id=1, source_target_pairs={{0,2},{1,3},{2,0},{3,1},{4,6},{5,7},{6,4},{7,5},{8,10},{9,11},{10,... | collective-permute-start | bytes 1572872 | tf_op jit(solution)/shard_map/ppermute | solution.py:36
  30.9 20.4 %collective-permute-start.12 = (bf16[2,128,1536]{2,1,0:T(8,128)(2,1)S(1)}, bf16[2,128,1536]{2,1,0:T(8,128)(2,1)S(1)}, u32[]{:S(2)}, u32[]{:S(2)}) collective-permute-start(bf16[2,128,1536]{2,1,0:T(8,128)(2,1)S(1)} %dynamic-slice_bitcast_fusion), channel_id=1, source_target_pairs={{0,2},{1,3},{2,0},{3,1},{4,6},{5,7},{6,4},{7,5},{8,10},{9,11},{10,... | collective-permute-start | bytes 2359304 | tf_op jit(solution)/shard_map/ppermute | solution.py:36
  32.6 24.9 %collective-permute-start.9 = (bf16[128,1024]{1,0:T(8,128)(2,1)S(1)}, bf16[128,1024]{1,0:T(8,128)(2,1)S(1)}, u32[]{:S(2)}, u32[]{:S(2)}) collective-permute-start(bf16[128,1024]{1,0:T(8,128)(2,1)S(1)} %dynamic-slice_bitcast_fusion.2), channel_id=1, source_target_pairs={{0,2},{1,3},{2,0},{3,1},{4,6},{5,7},{6,4},{7,5},{8,10},{9,11},{10,... | collective-permute-start | bytes 786440 | tf_op jit(solution)/shard_map/ppermute | solution.py:36
  51.4 14.5 %collective-permute-start.14 = (bf16[2,64,1536]{2,1,0:T(8,128)(2,1)S(1)}, bf16[2,64,1536]{2,1,0:T(8,128)(2,1)S(1)}, u32[]{:S(2)}, u32[]{:S(2)}) collective-permute-start(bf16[2,64,1536]{2,1,0:T(8,128)(2,1)S(1)} %get-tuple-element.138), channel_id=1, source_target_pairs={{0,8},{4,12},{8,0},{12,4},{16,24},{20,28},{24,16},{28,20},{1,9},{5... | collective-permute-start | bytes 1179656 | tf_op jit(solution)/shard_map/ppermute | solution.py:36
  55.9 15.3 %collective-permute-start.7 = (bf16[1024,256]{1,0:T(8,128)(2,1)S(1)}, bf16[1024,256]{1,0:T(8,128)(2,1)S(1)}, u32[]{:S(2)}, u32[]{:S(2)}) collective-permute-start(bf16[1024,256]{1,0:T(8,128)(2,1)S(1)} %get-tuple-element.69.refs_4_.refs_5_), channel_id=1, source_target_pairs={{0,2},{1,3},{2,0},{3,1},{4,6},{5,7},{6,4},{7,5},{8,10},{9,11},{10,... | collective-permute-start | bytes 1572872 | tf_op jit(solution)/shard_map/ppermute | solution.py:36
  72.5 15.7 %collective-permute-start.16 = (bf16[256,1024]{1,0:T(8,128)(2,1)S(1)}, bf16[256,1024]{1,0:T(8,128)(2,1)S(1)}, u32[]{:S(2)}, u32[]{:S(2)}) collective-permute-start(bf16[256,1024]{1,0:T(8,128)(2,1)S(1)} %copy-done.29), channel_id=1, source_target_pairs={{0,2},{1,3},{2,0},{3,1},{4,6},{5,7},{6,4},{7,5},{8,10},{9,11},{10,... | collective-permute-start | bytes 1572872 | tf_op jit(solution)/shard_map/ppermute | solution.py:36
  74.0 14.5 %collective-permute-start.17 = (bf16[256,1024]{1,0:T(8,128)(2,1)S(1)}, bf16[256,1024]{1,0:T(8,128)(2,1)S(1)}, u32[]{:S(2)}, u32[]{:S(2)}) collective-permute-start(bf16[256,1024]{1,0:T(8,128)(2,1)S(1)} %copy-done.29), channel_id=1, source_target_pairs={{0,1},{1,0},{2,3},{3,2},{4,5},{5,4},{6,7},{7,6},{8,9},{9,8},{10,11... | collective-permute-start | bytes 1572872 | tf_op jit(solution)/shard_map/ppermute | solution.py:36
  116.4 29.7 %collective-permute-start.25 = (bf16[4,768,128]{2,1,0:T(8,128)(2,1)}, bf16[4,768,128]{2,1,0:T(8,128)(2,1)S(1)}, u32[]{:S(2)}, u32[]{:S(2)}) collective-permute-start(bf16[4,768,128]{2,1,0:T(8,128)(2,1)} %bitcast.111), channel_id=1, source_target_pairs={{0,8},{4,12},{8,0},{12,4},{16,24},{20,28},{24,16},{28,20},{1,9},{5... | collective-permute-start | bytes 2359304 | tf_op jit(solution)/shard_map/ppermute | solution.py:36
  117.2 28.9 %collective-permute-start.24 = (bf16[4,640,128]{2,1,0:T(8,128)(2,1)S(1)}, bf16[4,640,128]{2,1,0:T(8,128)(2,1)S(1)}, u32[]{:S(2)}, u32[]{:S(2)}) collective-permute-start(bf16[4,640,128]{2,1,0:T(8,128)(2,1)S(1)} %bitcast.89), channel_id=1, source_target_pairs={{0,4},{4,0},{8,12},{12,8},{16,20},{20,16},{24,28},{28,24},{1,5},{5... | collective-permute-start | bytes 1966088 | tf_op jit(solution)/shard_map/ppermute | solution.py:36
  123.2 19.6 %collective-permute-start.22 = (bf16[256,1024]{1,0:T(8,128)(2,1)S(1)}, bf16[256,1024]{1,0:T(8,128)(2,1)S(1)}, u32[]{:S(2)}, u32[]{:S(2)}) collective-permute-start(bf16[256,1024]{1,0:T(8,128)(2,1)S(1)} %get-tuple-element.87.refs_7_.refs_1_), channel_id=1, source_target_pairs={{0,2},{1,3},{2,0},{3,1},{4,6},{5,7},{6,4},{7,5},{8,10},{9,11},{10,... | collective-permute-start | bytes 1572872 | tf_op jit(solution)/shard_map/ppermute | solution.py:36
  144.3 18.2 %collective-permute-start.31 = (bf16[4,656,128]{2,1,0:T(8,128)(2,1)}, bf16[4,656,128]{2,1,0:T(8,128)(2,1)S(1)}, u32[]{:S(2)}, u32[]{:S(2)}) collective-permute-start(bf16[4,656,128]{2,1,0:T(8,128)(2,1)} %get-tuple-element.117), channel_id=1, source_target_pairs={{0,4},{4,0},{8,12},{12,8},{16,20},{20,16},{24,28},{28,24},{1,5},{5... | collective-permute-start | bytes 2015240 | tf_op jit(solution)/shard_map/ppermute | solution.py:36
  145.9 17.8 %collective-permute-start.21 = (bf16[2,256,1024]{2,1,0:T(8,128)(2,1)}, bf16[2,256,1024]{2,1,0:T(8,128)(2,1)S(1)}, u32[]{:S(2)}, u32[]{:S(2)}) collective-permute-start(bf16[2,256,1024]{2,1,0:T(8,128)(2,1)} %get-tuple-element.89), channel_id=1, source_target_pairs={{0,1},{1,0},{2,3},{3,2},{4,5},{5,4},{6,7},{7,6},{8,9},{9,8},{10,11... | collective-permute-start | bytes 3145736 | tf_op jit(solution)/shard_map/ppermute | solution.py:36
  146.3 25.0 %collective-permute-start.42 = (bf16[2,640,128]{2,1,0:T(8,128)(2,1)S(1)}, bf16[2,640,128]{2,1,0:T(8,128)(2,1)S(1)}, u32[]{:S(2)}, u32[]{:S(2)}) collective-permute-start(bf16[2,640,128]{2,1,0:T(8,128)(2,1)S(1)} %get-tuple-element.143.refs_13_), channel_id=1, source_target_pairs={{0,8},{4,12},{8,0},{12,4},{16,24},{20,28},{24,16},{28,20},{1,9},{5... | collective-permute-start | bytes 983048 | tf_op jit(solution)/shard_map/ppermute | solution.py:36
  147.5 23.9 %collective-permute-start.43 = (bf16[2,768,128]{2,1,0:T(8,128)(2,1)S(1)}, bf16[2,768,128]{2,1,0:T(8,128)(2,1)S(1)}, u32[]{:S(2)}, u32[]{:S(2)}) collective-permute-start(bf16[2,768,128]{2,1,0:T(8,128)(2,1)S(1)} %get-tuple-element.135.refs_14_), channel_id=1, source_target_pairs={{0,4},{4,0},{8,12},{12,8},{16,20},{20,16},{24,28},{28,24},{1,5},{5... | collective-permute-start | bytes 1179656 | tf_op jit(solution)/shard_map/ppermute | solution.py:36
  162.6 29.3 %collective-permute-start.52 = (bf16[2,656,128]{2,1,0:T(8,128)(2,1)S(1)}, bf16[2,656,128]{2,1,0:T(8,128)(2,1)S(1)}, u32[]{:S(2)}, u32[]{:S(2)}) collective-permute-start(bf16[2,656,128]{2,1,0:T(8,128)(2,1)S(1)} %get-tuple-element.129), channel_id=1, source_target_pairs={{0,8},{4,12},{8,0},{12,4},{16,24},{20,28},{24,16},{28,20},{1,9},{5... | collective-permute-start | bytes 1007624 | tf_op jit(solution)/shard_map/ppermute | solution.py:36
  169.7 22.0 %collective-permute-start.27 = (bf16[4,512,128]{2,1,0:T(8,128)(2,1)S(1)}, bf16[4,512,128]{2,1,0:T(8,128)(2,1)S(1)}, u32[]{:S(2)}, u32[]{:S(2)}) collective-permute-start(bf16[4,512,128]{2,1,0:T(8,128)(2,1)S(1)} %bitcast.90), channel_id=1, source_target_pairs={{0,4},{4,0},{8,12},{12,8},{16,20},{20,16},{24,28},{28,24},{1,5},{5... | collective-permute-start | bytes 1572872 | tf_op jit(solution)/shard_map/ppermute | solution.py:36
  171.6 19.0 %collective-permute-start.44 = (bf16[1,1408,128]{2,1,0:T(8,128)(2,1)S(1)}, bf16[1,1408,128]{2,1,0:T(8,128)(2,1)S(1)}, u32[]{:S(2)}, u32[]{:S(2)}) collective-permute-start(bf16[1,1408,128]{2,1,0:T(8,128)(2,1)S(1)} %pad_maximum_fusion.12), channel_id=1, source_target_pairs={{0,16},{4,20},{8,24},{12,28},{16,0},{20,4},{24,8},{28,12},{1,17},{... | collective-permute-start | bytes 1081352 | tf_op jit(solution)/shard_map/ppermute | solution.py:36
  174.8 25.2 %collective-permute-start.32 = (bf16[4,512,128]{2,1,0:T(8,128)(2,1)S(1)}, bf16[4,512,128]{2,1,0:T(8,128)(2,1)S(1)}, u32[]{:S(2)}, u32[]{:S(2)}) collective-permute-start(bf16[4,512,128]{2,1,0:T(8,128)(2,1)S(1)} %pad_maximum_fusion.9), channel_id=1, source_target_pairs={{0,8},{4,12},{8,0},{12,4},{16,24},{20,28},{24,16},{28,20},{1,9},{5... | collective-permute-start | bytes 1572872 | tf_op jit(solution)/shard_map/ppermute | solution.py:36
  190.8 14.2 %collective-permute-start.45 = (bf16[2,1,352,128]{3,2,0,1:T(8,128)(2,1)S(1)}, bf16[2,1,352,128]{3,2,0,1:T(8,128)(2,1)S(1)}, u32[]{:S(2)}, u32[]{:S(2)}) collective-permute-start(bf16[2,1,352,128]{3,2,0,1:T(8,128)(2,1)S(1)} %get-tuple-element.161), channel_id=1, source_target_pairs={{0,2},{1,3},{2,0},{3,1},{4,6},{5,7},{6,4},{7,5},{8,10},{9,11},{10,... | collective-permute-start | bytes 540680 | tf_op jit(solution)/shard_map/ppermute | solution.py:36
  205.0 59.1 %collective-permute-start.28 = (bf16[2,256,1024]{2,1,0:T(8,128)(2,1)}, bf16[2,256,1024]{2,1,0:T(8,128)(2,1)S(1)}, u32[]{:S(2)}, u32[]{:S(2)}) collective-permute-start(bf16[2,256,1024]{2,1,0:T(8,128)(2,1)} %get-tuple-element.109), channel_id=1, source_target_pairs={{0,1},{1,0},{2,3},{3,2},{4,5},{5,4},{6,7},{7,6},{8,9},{9,8},{10,11... | collective-permute-start | bytes 3145736 | tf_op jit(solution)/shard_map/ppermute | solution.py:36
  205.7 29.1 %collective-permute-start.54 = (bf16[1,656,128]{2,1,0:T(8,128)(2,1)S(1)}, bf16[1,656,128]{2,1,0:T(8,128)(2,1)S(1)}, u32[]{:S(2)}, u32[]{:S(2)}) collective-permute-start(bf16[1,656,128]{2,1,0:T(8,128)(2,1)S(1)} %bitcast.93), channel_id=1, source_target_pairs={{0,16},{4,20},{8,24},{12,28},{16,0},{20,4},{24,8},{28,12},{1,17},{... | collective-permute-start | bytes 503816 | tf_op jit(solution)/shard_map/ppermute | solution.py:36
  206.7 27.7 %collective-permute-start.34 = (bf16[1,1024,128]{2,1,0:T(8,128)(2,1)S(1)}, bf16[1,1024,128]{2,1,0:T(8,128)(2,1)S(1)}, u32[]{:S(2)}, u32[]{:S(2)}) collective-permute-start(bf16[1,1024,128]{2,1,0:T(8,128)(2,1)S(1)} %pad_maximum_fusion.17), channel_id=1, source_target_pairs={{0,16},{4,20},{8,24},{12,28},{16,0},{20,4},{24,8},{28,12},{1,17},{... | collective-permute-start | bytes 786440 | tf_op jit(solution)/shard_map/ppermute | solution.py:36
  209.0 33.2 %collective-permute-start.47 = (bf16[1,1408,128]{2,1,0:T(8,128)(2,1)S(1)}, bf16[1,1408,128]{2,1,0:T(8,128)(2,1)S(1)}, u32[]{:S(2)}, u32[]{:S(2)}) collective-permute-start(bf16[1,1408,128]{2,1,0:T(8,128)(2,1)S(1)} %maximum_bitcast_fusion.1), channel_id=1, source_target_pairs={{0,16},{4,20},{8,24},{12,28},{16,0},{20,4},{24,8},{28,12},{1,17},{... | collective-permute-start | bytes 1081352 | tf_op jit(solution)/shard_map/ppermute | solution.py:36
  234.8 15.0 %collective-permute-start.55 = (bf16[2,656,128]{2,1,0:T(8,128)(2,1)S(1)}, bf16[2,656,128]{2,1,0:T(8,128)(2,1)S(1)}, u32[]{:S(2)}, u32[]{:S(2)}) collective-permute-start(bf16[2,656,128]{2,1,0:T(8,128)(2,1)S(1)} %pad_maximum_fusion.13), channel_id=1, source_target_pairs={{0,8},{4,12},{8,0},{12,4},{16,24},{20,28},{24,16},{28,20},{1,9},{5... | collective-permute-start | bytes 1007624 | tf_op jit(solution)/shard_map/ppermute | solution.py:36
  242.3 21.7 %collective-permute-start.50 = (bf16[2,768,128]{2,1,0:T(8,128)(2,1)S(1)}, bf16[2,768,128]{2,1,0:T(8,128)(2,1)S(1)}, u32[]{:S(2)}, u32[]{:S(2)}) collective-permute-start(bf16[2,768,128]{2,1,0:T(8,128)(2,1)S(1)} %pad_maximum_fusion.11), channel_id=1, source_target_pairs={{0,4},{4,0},{8,12},{12,8},{16,20},{20,16},{24,28},{28,24},{1,5},{5... | collective-permute-start | bytes 1179656 | tf_op jit(solution)/shard_map/ppermute | solution.py:36
  244.5 17.4 %collective-permute-start.48 = (bf16[2,640,128]{2,1,0:T(8,128)(2,1)S(1)}, bf16[2,640,128]{2,1,0:T(8,128)(2,1)S(1)}, u32[]{:S(2)}, u32[]{:S(2)}) collective-permute-start(bf16[2,640,128]{2,1,0:T(8,128)(2,1)S(1)} %pad_maximum_fusion.14), channel_id=1, source_target_pairs={{0,8},{4,12},{8,0},{12,4},{16,24},{20,28},{24,16},{28,20},{1,9},{5... | collective-permute-start | bytes 983048 | tf_op jit(solution)/shard_map/ppermute | solution.py:36
  249.9 28.1 %collective-permute-start.56 = (bf16[4,656,128]{2,1,0:T(8,128)(2,1)S(1)}, bf16[4,656,128]{2,1,0:T(8,128)(2,1)S(1)}, u32[]{:S(2)}, u32[]{:S(2)}) collective-permute-start(bf16[4,656,128]{2,1,0:T(8,128)(2,1)S(1)} %pad_maximum_fusion.6.refs_0_), channel_id=1, source_target_pairs={{0,4},{4,0},{8,12},{12,8},{16,20},{20,16},{24,28},{28,24},{1,5},{5... | collective-permute-start | bytes 2015240 | tf_op jit(solution)/shard_map/ppermute | solution.py:36
  257.2 20.0 %collective-permute-start.26 = (bf16[256,1024]{1,0:T(8,128)(2,1)S(1)}, bf16[256,1024]{1,0:T(8,128)(2,1)S(1)}, u32[]{:S(2)}, u32[]{:S(2)}) collective-permute-start(bf16[256,1024]{1,0:T(8,128)(2,1)S(1)} %copy-done.32), channel_id=1, source_target_pairs={{0,2},{1,3},{2,0},{3,1},{4,6},{5,7},{6,4},{7,5},{8,10},{9,11},{10,... | collective-permute-start | bytes 1572872 | tf_op jit(solution)/shard_map/ppermute | solution.py:36
  264.1 28.5 %collective-permute-start.51 = (bf16[4,768,128]{2,1,0:T(8,128)(2,1)S(1)}, bf16[4,768,128]{2,1,0:T(8,128)(2,1)}, u32[]{:S(2)}, u32[]{:S(2)}) collective-permute-start(bf16[4,768,128]{2,1,0:T(8,128)(2,1)S(1)} %pad_maximum_fusion.5), channel_id=1, source_target_pairs={{0,8},{4,12},{8,0},{12,4},{16,24},{20,28},{24,16},{28,20},{1,9},{5... | collective-permute-start | bytes 2359304 | tf_op jit(solution)/shard_map/ppermute | solution.py:36
  273.7 18.9 %collective-permute-start.49 = (bf16[4,640,128]{2,1,0:T(8,128)(2,1)}, bf16[4,640,128]{2,1,0:T(8,128)(2,1)}, u32[]{:S(2)}, u32[]{:S(2)}) collective-permute-start(bf16[4,640,128]{2,1,0:T(8,128)(2,1)} %pad_maximum_fusion.7), channel_id=1, source_target_pairs={{0,4},{4,0},{8,12},{12,8},{16,20},{20,16},{24,28},{28,24},{1,5},{5... | collective-permute-start | bytes 1966088 | tf_op jit(solution)/shard_map/ppermute | solution.py:36
  278.0 23.7 %collective-permute-start.41 = (bf16[4,512,128]{2,1,0:T(8,128)(2,1)}, bf16[4,512,128]{2,1,0:T(8,128)(2,1)}, u32[]{:S(2)}, u32[]{:S(2)}) collective-permute-start(bf16[4,512,128]{2,1,0:T(8,128)(2,1)} %pad_maximum_fusion.8.refs_0_), channel_id=1, source_target_pairs={{0,8},{4,12},{8,0},{12,4},{16,24},{20,28},{24,16},{28,20},{1,9},{5... | collective-permute-start | bytes 1572872 | tf_op jit(solution)/shard_map/ppermute | solution.py:36
  278.8 23.9 %collective-permute-start.39 = (bf16[4,512,128]{2,1,0:T(8,128)(2,1)}, bf16[4,512,128]{2,1,0:T(8,128)(2,1)}, u32[]{:S(2)}, u32[]{:S(2)}) collective-permute-start(bf16[4,512,128]{2,1,0:T(8,128)(2,1)} %pad_maximum_fusion.10), channel_id=1, source_target_pairs={{0,4},{4,0},{8,12},{12,8},{16,20},{20,16},{24,28},{28,24},{1,5},{5... | collective-permute-start | bytes 1572872 | tf_op jit(solution)/shard_map/ppermute | solution.py:36
  (77 other events, 449.7 us)
